TPU v7x, 32 devices: a whole 2x2x4 slice. The times are simulated.
32 devices in a mesh: ckpt: 2 (over x), train: 16 (over z, y, core).
Axes of the slice: x: 2, y: 2, z: 4, core: 2. Of those that a mesh axis runs over, the one named last changes fastest.
Arguments:
- train_feat: bfloat16 [2, 32768, 1024], P('ckpt', 'train'), may hold values from -6 to 6
- test_feat: bfloat16 [2, 1024, 1024], P('ckpt', 'train'), may hold values from -0.375 to 0.375
- kernel_inv: bfloat16 [2, 1024, 1024], P('ckpt', 'train'), may hold values from -0.1875 to 0.1875
- bucket_weight: float32 [2, 16], P('ckpt'), may hold values from 0.2 to 2
- bucket: int32 [32768], P('train'), may hold values from 0 to 15
- test_order: int32 [1024], replicated, may hold values from 0 to 1023, each once
Outputs:
- scores: float32 [32768, 1024], P('train', 'ckpt')
Inputs may be any that keep to these rules, and one draw needn't show every extreme that they name: `test_order`: each of 0 to 1023 once.
All inputs are finite; a program needn't handle non-finite values.
Results may differ from a plain program's by a relative error of at most 0.012.
Values may be sent and summed in bfloat16 or wider, within the bound.
No kernel may reach another device: no remote copies, remote signals or barrier semaphores. Data moves between devices by JAX's collectives and lax.ppermute only.
A program may use at most 64 MiB of HBM per device.

v0:
```python
import jax
import jax.numpy as jnp
from jax import lax
from jax.sharding import PartitionSpec as P


def shards(train_feat, test_feat, kernel_inv, bucket_weight, bucket, test_order):
    local_ck = train_feat.shape[0]
    full_inverse = lax.all_gather(kernel_inv, "train", axis=1, tiled=True)
    local_rows = jnp.einsum(
        "kjb,kab->kja", test_feat, full_inverse, preferred_element_type=jnp.float32
    ).astype(jnp.bfloat16)
    stored = lax.all_gather(local_rows, "train", axis=1, tiled=True)
    ordered = jnp.zeros_like(stored).at[:, test_order, :].set(stored)
    onehot = (
        bucket[:, None] == jnp.arange(bucket_weight.shape[1], dtype=jnp.int32)[None, :]
    ).astype(jnp.float32)
    weights = jnp.dot(onehot, bucket_weight.T, precision=lax.Precision.HIGHEST)
    total = weights * jnp.dot(train_feat[0], ordered[0].T, preferred_element_type=jnp.float32)
    ensemble = local_ck * lax.axis_size("ckpt")
    summed = lax.psum_scatter(
        total.astype(jnp.bfloat16), "ckpt", scatter_dimension=1, tiled=True
    ).astype(jnp.float32)
    return summed / ensemble


def solution(mesh):
    return jax.shard_map(
        shards,
        mesh=mesh,
        in_specs=(
            P("ckpt", "train", None),
            P("ckpt", "train", None),
            P("ckpt", "train", None),
            P("ckpt", None),
            P("train"),
            P(),
        ),
        out_specs=P("train", "ckpt"),
        check_vma=False,
    )
```

profile of v0, /device:TPU:0, one launch (start us, length us, event | category | flops | bytes accessed | tf_op | source)
XLA Modules:
  0.0 181.2 jit_solution(18101309145878518904)
XLA Ops:
  6.5 0.0 copy-start
  6.5 0.0 copy-start.1
  6.5 0.0 copy-start.2
  6.5 0.0 copy-start.3
  6.5 0.0 all-gather.4.cloned.1.call-start
  6.6 0.7 all-gather.4.cloned.1.call-update
  7.3 0.0 all-gather.6.cloned.1.call-start
  7.3 46.3 %all-gather.4.cloned.1.call-done = bf16[1,1024,1024]{2,1,0:T(8,128)(2,1)} async-done(((bf16[1,64,1024]{2,1,0:T(8,128)(2,1)}), bf16[1,1024,1024]{2,1,0:T(8,128)(2,1)}) %all-gather.4.cloned.1.call-update) | async-done | bytes 2097168 | tf_op jit(solution)/shard_map/all_gather | solution.py:9
  53.7 0.0 copy-done
  53.7 3.0 %fusion.6 = bf16[64,1024]{1,0:T(8,128)(2,1)} fusion(bf16[1,1024,1024]{2,1,0:T(8,128)(2,1)} %all-gather.4.cloned.1.call-done, bf16[1,64,1024]{2,1,0:T(8,128)(2,1)S(1)} %copy-done), kind=kOutput, calls=%fused_computation.7 | convolution fusion | flops 134283264 | bytes 2359296 | tf_op jit(solution)/shard_map/kjb,kab->kja/dot_general | solution.py:10
  56.7 0.0 all-gather.6.cloned.1.call-update
  56.7 0.0 reduce-scatter.2.cloned.1.call-start
  56.8 0.0 copy-done.1
  56.8 0.0 copy-done.2
  56.8 0.0 copy-done.3
  56.8 0.7 fusion.11
  57.5 39.5 %all-gather.6.cloned.1.call-done = bf16[1024,1024]{1,0:T(8,128)(2,1)} async-done(((bf16[64,1024]{1,0:T(8,128)(2,1)}), bf16[1024,1024]{1,0:T(8,128)(2,1)}) %all-gather.6.cloned.1.call-update) | async-done | bytes 2097168 | tf_op jit(solution)/shard_map/all_gather | solution.py:13
  97.0 6.6 %scatter_custom_fusion = bf16[1024,1024]{1,0:T(8,128)(2,1)S(1)} fusion(s32[1024]{0:T(1024)S(1)} %compare_select_fusion, bf16[1024,1024]{1,0:T(8,128)(2,1)} %all-gather.6.cloned.1.call-done, bf16[]{:T(256)} %constant.1.clone.1), kind=kCustom, calls=%fused_computation.8 | custom fusion | bytes 2097664 | tf_op jit(solution)/shard_map/scatter | solution.py:14
  103.6 8.4 %fusion.1 = bf16[2048,1024]{0,1:T(8,128)(2,1)} fusion(bf16[1024,1024]{1,0:T(8,128)(2,1)S(1)} %scatter_custom_fusion, bf16[1,2048,1024]{2,1,0:T(8,128)(2,1)} %param.6, f32[2048]{0:T(1024)S(1)} %bitcast.22), kind=kOutput, calls=%fused_computation.4 | convolution fusion | flops 4299161600 | bytes 10493952 | tf_op jit(solution)/shard_map/dot_general | solution.py:19
  112.0 0.0 reduce-scatter.2.cloned.1.call-update
  112.0 53.2 %reduce-scatter.2.cloned.1.call-done = bf16[2048,512]{0,1:T(8,128)(2,1)} async-done(((bf16[2048,1024]{0,1:T(8,128)(2,1)}), bf16[2048,512]{0,1:T(8,128)(2,1)}) %reduce-scatter.2.cloned.1.call-update) | async-done | bytes 2097168 | tf_op jit(solution)/shard_map/reduce_scatter | solution.py:21
  165.2 4.1 %convert_multiply_fusion = f32[2048,512]{0,1:T(8,128)} fusion(bf16[2048,512]{0,1:T(8,128)(2,1)} %reduce-scatter.2.cloned.1.call-done), kind=kLoop, calls=%fused_computation.3 | loop fusion | flops 2097152 | bytes 6291456 | tf_op jit(solution)/shard_map/div | solution.py:24
  169.3 5.3 %copy.7 = f32[2048,512]{1,0:T(8,128)} copy(f32[2048,512]{0,1:T(8,128)} %convert_multiply_fusion) | data formatting | bytes 8388608 | tf_op jit(solution)/shard_map/div | solution.py:24
  (1 shorter events, 0.0 us)
Async XLA Ops:
  6.5 47.1 %copy-start = (bf16[1,64,1024]{2,1,0:T(8,128)(2,1)S(1)}, bf16[1,64,1024]{2,1,0:T(8,128)(2,1)}, u32[]{:S(2)}) copy-start(bf16[1,64,1024]{2,1,0:T(8,128)(2,1)} %param.7) | copy-start | bytes 393220
  6.5 50.2 %copy-start.1 = (s32[1024]{0:T(1024)S(1)}, s32[1024]{0:T(1024)}, u32[]{:S(2)}) copy-start(s32[1024]{0:T(1024)} %param.11) | copy-start | bytes 12292
  6.5 50.2 %copy-start.2 = (s32[2048]{0:T(1024)S(1)}, s32[2048]{0:T(1024)}, u32[]{:S(2)}) copy-start(s32[2048]{0:T(1024)} %param.10) | copy-start | bytes 24580
  6.5 50.2 %copy-start.3 = (f32[1,16]{1,0:T(1,128)S(1)}, f32[1,16]{1,0:T(1,128)}, u32[]{:S(2)}) copy-start(f32[1,16]{1,0:T(1,128)} %param.9) | copy-start | bytes 196
  6.5 47.1 %all-gather.4.cloned.1.call-start = ((), (), s32[]{:S(2)}) async-start(), calls=%async_computation.1 | async-start | bytes 2228224 | tf_op jit(solution)/shard_map/all_gather | solution.py:9
  7.3 89.8 %all-gather.6.cloned.1.call-start = ((), (), s32[]{:S(2)}) async-start(), calls=%async_computation.3 | async-start | bytes 2228224 | tf_op jit(solution)/shard_map/all_gather | solution.py:13
  56.7 108.5 %reduce-scatter.2.cloned.1.call-start = ((), (), s32[]{:S(2)}) async-start(), calls=%async_computation.2 | async-start | bytes 6291456 | tf_op jit(solution)/shard_map/reduce_scatter | solution.py:21
Sparse Core Ops, SparseCore 0:
  9.5 44.0 all-gather.3
  56.8 40.1 all-gather.5
  112.1 53.0 reduce-scatter.1
where the time goes:
time: 181 us
  waiting for transfers between devices  140 us (77%)
  between operations  13.2 us (7%)
  matrix products  12.1 us (7%)
  local copies, waits for them, and re-layouts  11.9 us (7%)
  other arithmetic  4.09 us (2%)
    reduce_scatter x1, waiting for transfers between devices, shards(): lax.psum_scatter(total.astype(jnp.bfloat16), 'ckpt', scatter_dimension=1,...  53.2 us
    all_gather x1, waiting for transfers between devices, shards(): full_inverse = lax.all_gather(kernel_inv, 'train', axis=1, tiled=True)  46.3 us
    all_gather x1, waiting for transfers between devices, shards(): stored = lax.all_gather(local_rows, 'train', axis=1, tiled=True)  39.5 us
    dot_general x1, matrix products, shards(): jnp.dot(train_feat[0], ordered[0].T, preferred_element_type=jnp.float32)  8.38 us
    scatter x1, local copies, waits for them, and re-layouts, shards(): ordered = jnp.zeros_like(stored).at[:, test_order, :].set(stored)  6.58 us
    div x1, local copies, waits for them, and re-layouts, shards(): return summed / ensemble  5.34 us
    div x1, other arithmetic, shards(): return summed / ensemble  4.08 us
  transfers between devices with their start and end apart: 3, of which 3 were waited for; matrix products, arithmetic and copies ran while one was open for 0% of the time, Pallas kernels for 0%

commit v1 on v0

v1 whole, which is shorter than its diff:
```python
import functools
import jax
import jax.numpy as jnp
from jax import lax
from jax.experimental import pallas as pl
from jax.experimental.pallas import tpu as pltpu
from jax.sharding import PartitionSpec as P

VMEM = pl.BlockSpec(memory_space=pltpu.VMEM)
SMEM = pl.BlockSpec(memory_space=pltpu.SMEM)
F32 = jnp.float32
LIMIT = 40 * 1024 * 1024


def factors(n):
    core = 2 if n % 2 == 0 else 1
    rest = n // core
    outer = 1
    while outer * outer < rest:
        outer *= 2
    if rest % outer:
        outer = rest
    return outer, rest // outer, core


def rotation(dims, axis, k):
    total = dims[0] * dims[1] * dims[2]
    pairs = []
    for dst in range(total):
        digits = [dst // (dims[1] * dims[2]), dst // dims[2] % dims[1], dst % dims[2]]
        digits[axis] = (digits[axis] + k) % dims[axis]
        pairs.append(((digits[0] * dims[1] + digits[1]) * dims[2] + digits[2], dst))
    return pairs


def gather(own, n):
    dims = factors(n)
    held = [((0, 0, 0), own)]
    for axis in range(3):
        arrived = []
        for k in range(1, dims[axis]):
            for offset, block in held:
                moved = list(offset)
                moved[axis] = k
                arrived.append(
                    (tuple(moved), lax.ppermute(block, "train", rotation(dims, axis, k)))
                )
        held = held + arrived
    me = lax.axis_index("train")
    mine = (me // (dims[1] * dims[2]), me // dims[2] % dims[1], me % dims[2])
    places = []
    for offset, _ in held:
        digit = [(mine[a] + offset[a]) % dims[a] for a in range(3)]
        places.append((digit[0] * dims[1] + digit[1]) * dims[2] + digit[2])
    return jnp.stack(places).astype(jnp.int32), [block for _, block in held]


def weights_kernel(bucket, table, out):
    rows = bucket.shape[1]
    onehot = (lax.broadcasted_iota(jnp.int32, (table.shape[0], rows), 0) == bucket[...]).astype(F32)
    out[...] = lax.dot_general(
        onehot, table[...], (((0,), (0,)), ((), ())),
        precision=lax.Precision.HIGHEST, preferred_element_type=F32,
    )


def transform_kernel(ensemble, places, me, order, *rest):
    blocks = rest[: -4]
    out, test, inverse, sorted_test = rest[-4:]
    rows = blocks[0].shape[1]
    for s, block in enumerate(blocks):
        at = pl.ds(pl.multiple_of(places[s] * rows, rows), rows)
        test[at, :] = block[0]
        inverse[at, :] = block[1]
    count = order.shape[1]
    width = count // ensemble
    for k in range(ensemble):
        first = lax.rem(me[0] + k, ensemble) * width
        wanted = lax.broadcasted_iota(jnp.int32, (width, count), 0) + first
        onehot = (wanted == order[...]).astype(jnp.bfloat16)
        sorted_test[...] = jnp.dot(
            onehot, test[...], preferred_element_type=F32
        ).astype(jnp.bfloat16)
        out[k] = lax.dot_general(
            inverse[...], sorted_test[...], (((1,), (1,)), ((), ())), preferred_element_type=F32
        ).astype(jnp.bfloat16)


def scaled(train, matrix, weight):
    tile = jnp.dot(train[...], matrix[...], preferred_element_type=F32)
    wide = jnp.concatenate([weight[...]] * (tile.shape[1] // weight.shape[1]), axis=1)
    return (tile * wide).astype(jnp.bfloat16)


def send_kernel(train, matrix, weight, out):
    out[...] = scaled(train, matrix, weight)


def sum_kernel(ensemble, train, matrix, weight, *rest):
    out = rest[-1]
    total = scaled(train, matrix, weight).astype(F32)
    for other in rest[:-2]:
        total = total + other[...].astype(F32)
    out[...] = total / ensemble


def shards(train_feat, test_feat, kernel_inv, bucket_weight, bucket, test_order):
    ensemble, n = lax.axis_size("ckpt"), lax.axis_size("train")
    train = train_feat[0]
    rows, size = train.shape
    count = test_order.shape[0]
    width = count // ensemble
    bf16 = jnp.bfloat16
    params = pltpu.CompilerParams(vmem_limit_bytes=LIMIT)

    places, blocks = gather(jnp.concatenate([test_feat, kernel_inv], axis=0), n)

    table = jnp.broadcast_to(bucket_weight.reshape(-1, 1), (bucket_weight.shape[1], 128))
    weight = pl.pallas_call(
        weights_kernel,
        out_shape=jax.ShapeDtypeStruct((rows, 128), F32),
        in_specs=[VMEM] * 2, out_specs=VMEM, compiler_params=params,
    )(bucket.reshape(1, rows), table)

    matrices = pl.pallas_call(
        functools.partial(transform_kernel, ensemble),
        out_shape=jax.ShapeDtypeStruct((ensemble, size, width), bf16),
        in_specs=[SMEM, SMEM, VMEM] + [VMEM] * len(blocks),
        out_specs=VMEM,
        scratch_shapes=[
            pltpu.VMEM((count, size), bf16),
            pltpu.VMEM((size, size), bf16),
            pltpu.VMEM((width, size), bf16),
        ],
        compiler_params=params,
        cost_estimate=pl.CostEstimate(
            flops=4 * size * size * count, bytes_accessed=8 * size * count, transcendentals=0
        ),
    )(places, lax.axis_index("ckpt").reshape(1), test_order.reshape(1, count), *blocks)

    parts = [1, 3, 3, 3, 3, 2, 1] if ensemble == 2 else [8, 8]
    unit = rows // sum(parts)
    starts = [sum(parts[:q]) * unit for q in range(len(parts))]

    def specs(first, length):
        step = unit
        at = first // step
        return (
            [
                pl.BlockSpec((step, size), lambda i: (at + i, 0)),
                None,
                pl.BlockSpec((step, 128), lambda i: (at + i, 0)),
            ],
            length // step,
            pl.BlockSpec((step, width), lambda i: (i, 0)),
            pl.BlockSpec((step, width), lambda i: (at + i, 0)),
        )

    received = []
    for first, part in zip(starts, parts):
        length = part * unit
        got = []
        for k in range(1, ensemble):
            ins, steps, moved, _ = specs(first, length)
            ins[1] = pl.BlockSpec((None, size, width), lambda i, k=k: (k, 0, 0))
            tile = pl.pallas_call(
                send_kernel,
                out_shape=jax.ShapeDtypeStruct((length, width), bf16),
                grid=(steps,), in_specs=ins, out_specs=moved, compiler_params=params,
                cost_estimate=pl.CostEstimate(
                    flops=2 * length * size * width,
                    bytes_accessed=2 * (length * size + size * width + length * width),
                    transcendentals=0,
                ),
            )(train, matrices, weight)
            got.append(
                lax.ppermute(tile, "ckpt", [(d, (d + k) % ensemble) for d in range(ensemble)])
            )
        received.append(got)

    out = jnp.zeros((rows, width), F32) if False else None
    for first, part, got in zip(starts, parts, received):
        length = part * unit
        ins, steps, moved, placed = specs(first, length)
        ins[1] = pl.BlockSpec((None, size, width), lambda i: (0, 0, 0))
        held = [] if out is None else [out]
        body = sum_kernel
        if out is None:
            def body(ensemble, *refs):
                sum_kernel(ensemble, *refs[:-1], None, refs[-1])
        out = pl.pallas_call(
            functools.partial(body, ensemble),
            out_shape=jax.ShapeDtypeStruct((rows, width), F32),
            grid=(steps,),
            in_specs=ins + [moved] * len(got) + [pl.BlockSpec(memory_space=pl.ANY)] * len(held),
            out_specs=placed,
            input_output_aliases={3 + len(got): 0} if held else {},
            compiler_params=params,
            cost_estimate=pl.CostEstimate(
                flops=2 * length * size * width,
                bytes_accessed=2 * (length * size + size * width + 3 * length * width),
                transcendentals=0,
            ),
        )(train, matrices, weight, *got, *held)
    return out


def solution(mesh):
    return jax.shard_map(
        shards,
        mesh=mesh,
        in_specs=(
            P("ckpt", "train", None),
            P("ckpt", "train", None),
            P("ckpt", "train", None),
            P("ckpt", None),
            P("train"),
            P(),
        ),
        out_specs=P("train", "ckpt"),
        check_vma=False,
    )
```

time: 181 us -> 110 us (0.61)
  waiting for transfers between devices: 140 us -> 58.3 us
  Pallas kernels: 0 us -> 24.2 us
  starting transfers between devices: 0.11 us -> 20.2 us
  between operations: 13.2 us -> 0.17 us
  matrix products: 12.1 us -> 0 us
  local copies, waits for them, and re-layouts: 11.9 us -> 7.34 us
  other arithmetic: 4.09 us -> 0 us
    all_gather x2 -> x0, waiting for transfers between devices: 85.9 us -> none  [the longest x1 46.3 us: shards(): full_inverse = lax.all_gather(kernel_inv, 'train', axis=1, tiled=True)]
    ppermute x0 -> x22, waiting for transfers between devices: none -> 58.3 us  [the longest x7 29.9 us: shards(): lax.ppermute(tile, 'ckpt', [(d, (d + k) % ensemble) for d in range(ensemb...]
    reduce_scatter x1 -> x0, waiting for transfers between devices: 53.2 us -> none  [shards(): lax.psum_scatter(total.astype(jnp.bfloat16), 'ckpt', scatter_dimension=1,...]
    pallas_call x0 -> x16, Pallas kernels: none -> 24.2 us  [the longest x7 11.8 us: shards(): pl.pallas_call(functools.partial(body, ensemble), out_shape=jax.ShapeDtyp...]
    ppermute x0 -> x22, starting transfers between devices: none -> 20.2 us  [the longest x15 12.3 us: gather(): lax.ppermute(block, 'train', rotation(dims, axis, k))]
    dot_general x3 -> x0, matrix products: 12.1 us -> none  [the longest x1 8.38 us: shards(): jnp.dot(train_feat[0], ordered[0].T, preferred_element_type=jnp.float32)]
    scatter x1 -> x0, local copies, waits for them, and re-layouts: 6.58 us -> none  [shards(): ordered = jnp.zeros_like(stored).at[:, test_order, :].set(stored)]
    unnamed x8 -> x15, local copies, waits for them, and re-layouts: 0.02 us -> 5.61 us
  transfers between devices with their start and end apart: 3 -> 22, of which waited for: 3 -> 5; matrix products, arithmetic and copies ran while one was open for 0% -> 1% of each run, Pallas kernels for 0% -> 15%
where the time goes in v1:
time: 110 us
  waiting for transfers between devices  58.3 us (53%)
  Pallas kernels  24.2 us (22%)
  starting transfers between devices  20.2 us (18%)
  local copies, waits for them, and re-layouts  7.34 us (7%)
    ppermute x7, waiting for transfers between devices, shards(): lax.ppermute(tile, 'ckpt', [(d, (d + k) % ensemble) for d in range(ensemb...  29.9 us
    ppermute x15, waiting for transfers between devices, gather(): lax.ppermute(block, 'train', rotation(dims, axis, k))  28.4 us
    ppermute x15, starting transfers between devices, gather(): lax.ppermute(block, 'train', rotation(dims, axis, k))  12.3 us
    pallas_call x7, Pallas kernels, shards(): pl.pallas_call(functools.partial(body, ensemble), out_shape=jax.ShapeDtyp...  11.8 us
    ppermute x7, starting transfers between devices, shards(): lax.ppermute(tile, 'ckpt', [(d, (d + k) % ensemble) for d in range(ensemb...  7.93 us
    pallas_call x1, Pallas kernels, shards(): pl.pallas_call(functools.partial(transform_kernel, ensemble), out_shape=j...  6.15 us
    unnamed x15, local copies, waits for them, and re-layouts  5.61 us
    pallas_call x7, Pallas kernels, shards(): pl.pallas_call(send_kernel, out_shape=jax.ShapeDtypeStruct((length, width...  5.21 us
  transfers between devices with their start and end apart: 22, of which 5 were waited for; matrix products, arithmetic and copies ran while one was open for 1% of the time, Pallas kernels for 15%

profile of v1, /device:TPU:0, one launch (start us, length us, event | category | flops | bytes accessed | tf_op | source)
XLA Modules:
  0.0 110.2 jit_solution(13309252969477412891)
XLA Ops:
  0.0 0.9 constant_dynamic-update-slice_fusion.1
  0.9 0.9 constant_dynamic-update-slice_fusion.rest_0_
  1.8 5.1 %collective-permute-start = (bf16[2,64,1024]{2,1,0:T(8,128)(2,1)S(1)}, bf16[2,64,1024]{2,1,0:T(8,128)(2,1)S(1)}, u32[]{:S(2)}, u32[]{:S(2)}) collective-permute-start(bf16[2,64,1024]{2,1,0:T(8,128)(2,1)S(1)} %constant_dynamic-update-slice_fusion.rest_0_), channel_id=1, source_target_pairs={{4,0},{5,1},{6,2},{7,3},{8,4},{9,5},{10,6},{11,7},{12,8},{13,9},{1... | collective-permute-start | bytes 786440 | tf_op jit(solution)/shard_map/ppermute | solution.py:46
  6.9 1.0 collective-permute-start.2
  8.0 1.5 %collective-permute-start.3 = (bf16[2,64,1024]{2,1,0:T(8,128)(2,1)S(1)}, bf16[2,64,1024]{2,1,0:T(8,128)(2,1)S(1)}, u32[]{:S(2)}, u32[]{:S(2)}) collective-permute-start(bf16[2,64,1024]{2,1,0:T(8,128)(2,1)S(1)} %constant_dynamic-update-slice_fusion.rest_0_), channel_id=1, source_target_pairs={{2,0},{3,1},{0,2},{1,3},{6,4},{7,5},{4,6},{5,7},{10,8},{11,9},{8,1... | collective-permute-start | bytes 786440 | tf_op jit(solution)/shard_map/ppermute | solution.py:46
  9.5 4.2 %collective-permute-done.rest_1_ = bf16[2,64,1024]{2,1,0:T(8,128)(2,1)S(1)} collective-permute-done((bf16[2,64,1024]{2,1,0:T(8,128)(2,1)S(1)}, bf16[2,64,1024]{2,1,0:T(8,128)(2,1)S(1)}, u32[]{:S(2)}, u32[]{:S(2)}) %collective-permute-start) | collective-permute-done | bytes 262176 | tf_op jit(solution)/shard_map/ppermute | solution.py:46
  13.7 1.5 %collective-permute-start.4 = (bf16[2,64,1024]{2,1,0:T(8,128)(2,1)S(1)}, bf16[2,64,1024]{2,1,0:T(8,128)(2,1)S(1)}, u32[]{:S(2)}, u32[]{:S(2)}) collective-permute-start(bf16[2,64,1024]{2,1,0:T(8,128)(2,1)S(1)} %collective-permute-done.rest_1_), channel_id=1, source_target_pairs={{2,0},{3,1},{0,2},{1,3},{6,4},{7,5},{4,6},{5,7},{10,8},{11,9},{8,1... | collective-permute-start | bytes 786440 | tf_op jit(solution)/shard_map/ppermute | solution.py:46
  15.2 14.0 %collective-permute-done.1.rest_2_ = bf16[2,64,1024]{2,1,0:T(8,128)(2,1)S(1)} collective-permute-done((bf16[2,64,1024]{2,1,0:T(8,128)(2,1)S(1)}, bf16[2,64,1024]{2,1,0:T(8,128)(2,1)S(1)}, u32[]{:S(2)}, u32[]{:S(2)}) %collective-permute-start.1) | collective-permute-done | bytes 262176 | tf_op jit(solution)/shard_map/ppermute | solution.py:46
  29.2 1.5 %collective-permute-start.5 = (bf16[2,64,1024]{2,1,0:T(8,128)(2,1)S(1)}, bf16[2,64,1024]{2,1,0:T(8,128)(2,1)S(1)}, u32[]{:S(2)}, u32[]{:S(2)}) collective-permute-start(bf16[2,64,1024]{2,1,0:T(8,128)(2,1)S(1)} %collective-permute-done.1.rest_2_), channel_id=1, source_target_pairs={{2,0},{3,1},{0,2},{1,3},{6,4},{7,5},{4,6},{5,7},{10,8},{11,9},{8,1... | collective-permute-start | bytes 786440 | tf_op jit(solution)/shard_map/ppermute | solution.py:46
  30.8 0.5 collective-permute-start.6
  31.3 0.5 collective-permute-start.8
  31.8 0.1 collective-permute-start.9
  31.9 6.6 %collective-permute-done.5.rest_6_ = bf16[2,64,1024]{2,1,0:T(8,128)(2,1)S(1)} collective-permute-done((bf16[2,64,1024]{2,1,0:T(8,128)(2,1)S(1)}, bf16[2,64,1024]{2,1,0:T(8,128)(2,1)S(1)}, u32[]{:S(2)}, u32[]{:S(2)}) %collective-permute-start.5) | collective-permute-done | bytes 262176 | tf_op jit(solution)/shard_map/ppermute | solution.py:46
  38.5 3.5 %collective-permute-done.6.rest_7_ = bf16[2,64,1024]{2,1,0:T(8,128)(2,1)S(1)} collective-permute-done((bf16[2,64,1024]{2,1,0:T(8,128)(2,1)S(1)}, bf16[2,64,1024]{2,1,0:T(8,128)(2,1)S(1)}, u32[]{:S(2)}, u32[]{:S(2)}) %collective-permute-start.6) | collective-permute-done | bytes 262176 | tf_op jit(solution)/shard_map/ppermute | solution.py:46
  42.1 0.7 copy-done.2
  42.8 0.5 collective-permute-start.13
  43.3 0.7 copy-done.4
  44.0 0.0 collective-permute-start.14
  44.0 0.7 broadcast_in_dim.8.table
  44.7 0.7 copy-done.1
  45.4 1.0 shard_map.65.weight.refs_2_
  46.4 0.1 stack.67.places
  46.6 0.9 copy-done.3
  47.5 0.9 copy-done.5
  48.5 0.7 copy-done.6
  49.2 6.1 %shard_map.64.matrix.refs_1_ = bf16[2,1024,512]{2,1,0:T(8,128)(2,1)S(1)} custom-call(s32[16]{0:T(128)S(1)} %stack.67.places, s32[1]{0:T(128)} %bitcast.17.me, s32[1,1024]{1,0:T(1,128)S(1)} %bitcast.36, bf16[2,64,1024]{2,1,0:T(8,128)(2,1)S(1)} %constant_dynamic-update-slice_fusion.rest_0_, bf16[2,64,1024]{2,1,0:T(8,128)(2,1)S(1)} %collective-permute-done.rest_1_, ...), custom_call_target="tpu_custom_call" | custom-call | flops 4294967296 | bytes 8388608 | tf_op jit(solution)/shard_map/pallas_call | solution.py:125
  55.3 1.0 shard_map.71
  56.3 1.6 %collective-permute-start.20 = (bf16[384,512]{1,0:T(8,128)(2,1)S(1)}, bf16[384,512]{1,0:T(8,128)(2,1)S(1)}, u32[]{:S(2)}, u32[]{:S(2)}) collective-permute-start(bf16[384,512]{1,0:T(8,128)(2,1)S(1)} %shard_map.71), channel_id=1, source_target_pairs={{0,16},{16,0},{1,17},{17,1},{2,18},{18,2},{3,19},{19,3},{4,20},{20... | collective-permute-start | bytes 1179656 | tf_op jit(solution)/shard_map/ppermute | solution.py:177
  57.9 1.0 shard_map.70
  58.9 0.6 collective-permute-start.19
  59.5 1.0 shard_map.69
  60.5 1.6 %collective-permute-start.18 = (bf16[384,512]{1,0:T(8,128)(2,1)S(1)}, bf16[384,512]{1,0:T(8,128)(2,1)S(1)}, u32[]{:S(2)}, u32[]{:S(2)}) collective-permute-start(bf16[384,512]{1,0:T(8,128)(2,1)S(1)} %shard_map.69), channel_id=1, source_target_pairs={{0,16},{16,0},{1,17},{17,1},{2,18},{18,2},{3,19},{19,3},{4,20},{20... | collective-permute-start | bytes 1179656 | tf_op jit(solution)/shard_map/ppermute | solution.py:177
  62.0 1.0 shard_map.68
  63.0 0.6 collective-permute-start.17
  63.6 0.3 shard_map.72
  63.9 1.6 %collective-permute-start.21 = (bf16[128,512]{1,0:T(8,128)(2,1)S(1)}, bf16[128,512]{1,0:T(8,128)(2,1)S(1)}, u32[]{:S(2)}, u32[]{:S(2)}) collective-permute-start(bf16[128,512]{1,0:T(8,128)(2,1)S(1)} %shard_map.72), channel_id=1, source_target_pairs={{0,16},{16,0},{1,17},{17,1},{2,18},{18,2},{3,19},{19,3},{4,20},{20... | collective-permute-start | bytes 393224 | tf_op jit(solution)/shard_map/ppermute | solution.py:177
  65.5 0.7 shard_map.67
  66.2 29.8 %collective-permute-done.21.refs_3_ = bf16[128,512]{1,0:T(8,128)(2,1)S(1)} collective-permute-done((bf16[128,512]{1,0:T(8,128)(2,1)S(1)}, bf16[128,512]{1,0:T(8,128)(2,1)S(1)}, u32[]{:S(2)}, u32[]{:S(2)}) %collective-permute-start.21) | collective-permute-done | bytes 131104 | tf_op jit(solution)/shard_map/ppermute | solution.py:177
  96.0 1.5 %collective-permute-start.16 = (bf16[256,512]{1,0:T(8,128)(2,1)S(1)}, bf16[256,512]{1,0:T(8,128)(2,1)S(1)}, u32[]{:S(2)}, u32[]{:S(2)}) collective-permute-start(bf16[256,512]{1,0:T(8,128)(2,1)S(1)} %shard_map.67), channel_id=1, source_target_pairs={{0,16},{16,0},{1,17},{17,1},{2,18},{18,2},{3,19},{19,3},{4,20},{20... | collective-permute-start | bytes 786440 | tf_op jit(solution)/shard_map/ppermute | solution.py:177
  97.5 0.3 shard_map.66
  97.8 1.0 shard_map.73.rest_1_
  98.9 0.6 collective-permute-start.15
  99.4 2.1 %shard_map.74.rest_1_ = f32[2048,512]{1,0:T(8,128)} custom-call(bf16[2048,1024]{1,0:T(8,128)(2,1)S(1)} %bitcast.29, bf16[2,1024,512]{2,1,0:T(8,128)(2,1)S(1)} %shard_map.64.matrix.refs_1_, f32[2048,128]{1,0:T(8,128)S(1)} %shard_map.65.weight.refs_2_, bf16[384,512]{1,0:T(8,128)(2,1)S(1)} %collective-permute-done.20.rest_0_, ...), custom_call_target="tpu_custom_call", output_to_operand_aliasing={{}: (4, {})} | custom-call | flops 402653184 | bytes 3014656 | tf_op jit(solution)/shard_map/pallas_call | solution.py:191
  101.5 2.1 %shard_map.75.rest_1_ = f32[2048,512]{1,0:T(8,128)} custom-call(bf16[2048,1024]{1,0:T(8,128)(2,1)S(1)} %bitcast.30, bf16[2,1024,512]{2,1,0:T(8,128)(2,1)S(1)} %shard_map.64.matrix.refs_1_, f32[2048,128]{1,0:T(8,128)S(1)} %shard_map.65.weight.refs_2_, bf16[384,512]{1,0:T(8,128)(2,1)S(1)} %collective-permute-done.19.rest_0_, ...), custom_call_target="tpu_custom_call", output_to_operand_aliasing={{}: (4, {})} | custom-call | flops 402653184 | bytes 3014656 | tf_op jit(solution)/shard_map/pallas_call | solution.py:191
  103.6 2.1 %shard_map.76.rest_1_ = f32[2048,512]{1,0:T(8,128)} custom-call(bf16[2048,1024]{1,0:T(8,128)(2,1)S(1)} %bitcast.31, bf16[2,1024,512]{2,1,0:T(8,128)(2,1)S(1)} %shard_map.64.matrix.refs_1_, f32[2048,128]{1,0:T(8,128)S(1)} %shard_map.65.weight.refs_2_, bf16[384,512]{1,0:T(8,128)(2,1)S(1)} %collective-permute-done.18.rest_0_, ...), custom_call_target="tpu_custom_call", output_to_operand_aliasing={{}: (4, {})} | custom-call | flops 402653184 | bytes 3014656 | tf_op jit(solution)/shard_map/pallas_call | solution.py:191
  105.7 2.1 %shard_map.77.rest_1_ = f32[2048,512]{1,0:T(8,128)} custom-call(bf16[2048,1024]{1,0:T(8,128)(2,1)S(1)} %bitcast.32, bf16[2,1024,512]{2,1,0:T(8,128)(2,1)S(1)} %shard_map.64.matrix.refs_1_, f32[2048,128]{1,0:T(8,128)S(1)} %shard_map.65.weight.refs_2_, bf16[384,512]{1,0:T(8,128)(2,1)S(1)} %collective-permute-done.17.rest_0_, ...), custom_call_target="tpu_custom_call", output_to_operand_aliasing={{}: (4, {})} | custom-call | flops 402653184 | bytes 3014656 | tf_op jit(solution)/shard_map/pallas_call | solution.py:191
  107.8 1.4 %shard_map.78.rest_1_ = f32[2048,512]{1,0:T(8,128)} custom-call(bf16[2048,1024]{1,0:T(8,128)(2,1)S(1)} %bitcast.33, bf16[2,1024,512]{2,1,0:T(8,128)(2,1)S(1)} %shard_map.64.matrix.refs_1_, f32[2048,128]{1,0:T(8,128)S(1)} %shard_map.65.weight.refs_2_, bf16[256,512]{1,0:T(8,128)(2,1)S(1)} %collective-permute-done.16.rest_0_, ...), custom_call_target="tpu_custom_call", output_to_operand_aliasing={{}: (4, {})} | custom-call | flops 268435456 | bytes 2359296 | tf_op jit(solution)/shard_map/pallas_call | solution.py:191
  109.1 1.0 shard_map.79
  (30 shorter events, 0.1 us)
Async XLA Ops:
  1.8 11.9 %collective-permute-start = (bf16[2,64,1024]{2,1,0:T(8,128)(2,1)S(1)}, bf16[2,64,1024]{2,1,0:T(8,128)(2,1)S(1)}, u32[]{:S(2)}, u32[]{:S(2)}) collective-permute-start(bf16[2,64,1024]{2,1,0:T(8,128)(2,1)S(1)} %constant_dynamic-update-slice_fusion.rest_0_), channel_id=1, source_target_pairs={{4,0},{5,1},{6,2},{7,3},{8,4},{9,5},{10,6},{11,7},{12,8},{13,9},{1... | collective-permute-start | bytes 786440 | tf_op jit(solution)/shard_map/ppermute | solution.py:46
  6.9 22.3 %collective-permute-start.1 = (bf16[2,64,1024]{2,1,0:T(8,128)(2,1)S(1)}, bf16[2,64,1024]{2,1,0:T(8,128)(2,1)S(1)}, u32[]{:S(2)}, u32[]{:S(2)}) collective-permute-start(bf16[2,64,1024]{2,1,0:T(8,128)(2,1)S(1)} %constant_dynamic-update-slice_fusion.rest_0_), channel_id=1, source_target_pairs={{8,0},{9,1},{10,2},{11,3},{12,4},{13,5},{14,6},{15,7},{0,8},{1,9},... | collective-permute-start | bytes 786440 | tf_op jit(solution)/shard_map/ppermute | solution.py:46
  6.9 23.8 %collective-permute-start.2 = (bf16[2,64,1024]{2,1,0:T(8,128)(2,1)S(1)}, bf16[2,64,1024]{2,1,0:T(8,128)(2,1)S(1)}, u32[]{:S(2)}, u32[]{:S(2)}) collective-permute-start(bf16[2,64,1024]{2,1,0:T(8,128)(2,1)S(1)} %constant_dynamic-update-slice_fusion.rest_0_), channel_id=1, source_target_pairs={{12,0},{13,1},{14,2},{15,3},{0,4},{1,5},{2,6},{3,7},{4,8},{5,9},{6... | collective-permute-start | bytes 786440 | tf_op jit(solution)/shard_map/ppermute | solution.py:46
  8.0 23.3 %collective-permute-start.3 = (bf16[2,64,1024]{2,1,0:T(8,128)(2,1)S(1)}, bf16[2,64,1024]{2,1,0:T(8,128)(2,1)S(1)}, u32[]{:S(2)}, u32[]{:S(2)}) collective-permute-start(bf16[2,64,1024]{2,1,0:T(8,128)(2,1)S(1)} %constant_dynamic-update-slice_fusion.rest_0_), channel_id=1, source_target_pairs={{2,0},{3,1},{0,2},{1,3},{6,4},{7,5},{4,6},{5,7},{10,8},{11,9},{8,1... | collective-permute-start | bytes 786440 | tf_op jit(solution)/shard_map/ppermute | solution.py:46
  9.5 21.8 %collective-permute-start.7 = (bf16[2,64,1024]{2,1,0:T(8,128)(2,1)S(1)}, bf16[2,64,1024]{2,1,0:T(8,128)(2,1)S(1)}, u32[]{:S(2)}, u32[]{:S(2)}) collective-permute-start(bf16[2,64,1024]{2,1,0:T(8,128)(2,1)S(1)} %constant_dynamic-update-slice_fusion.rest_0_), channel_id=1, source_target_pairs={{1,0},{0,1},{3,2},{2,3},{5,4},{4,5},{7,6},{6,7},{9,8},{8,9},{11,10... | collective-permute-start | bytes 786440 | tf_op jit(solution)/shard_map/ppermute | solution.py:46
  13.7 18.1 %collective-permute-start.4 = (bf16[2,64,1024]{2,1,0:T(8,128)(2,1)S(1)}, bf16[2,64,1024]{2,1,0:T(8,128)(2,1)S(1)}, u32[]{:S(2)}, u32[]{:S(2)}) collective-permute-start(bf16[2,64,1024]{2,1,0:T(8,128)(2,1)S(1)} %collective-permute-done.rest_1_), channel_id=1, source_target_pairs={{2,0},{3,1},{0,2},{1,3},{6,4},{7,5},{4,6},{5,7},{10,8},{11,9},{8,1... | collective-permute-start | bytes 786440 | tf_op jit(solution)/shard_map/ppermute | solution.py:46
  29.2 9.2 %collective-permute-start.5 = (bf16[2,64,1024]{2,1,0:T(8,128)(2,1)S(1)}, bf16[2,64,1024]{2,1,0:T(8,128)(2,1)S(1)}, u32[]{:S(2)}, u32[]{:S(2)}) collective-permute-start(bf16[2,64,1024]{2,1,0:T(8,128)(2,1)S(1)} %collective-permute-done.1.rest_2_), channel_id=1, source_target_pairs={{2,0},{3,1},{0,2},{1,3},{6,4},{7,5},{4,6},{5,7},{10,8},{11,9},{8,1... | collective-permute-start | bytes 786440 | tf_op jit(solution)/shard_map/ppermute | solution.py:46
  30.8 11.3 %collective-permute-start.6 = (bf16[2,64,1024]{2,1,0:T(8,128)(2,1)S(1)}, bf16[2,64,1024]{2,1,0:T(8,128)(2,1)S(1)}, u32[]{:S(2)}, u32[]{:S(2)}) collective-permute-start(bf16[2,64,1024]{2,1,0:T(8,128)(2,1)S(1)} %collective-permute-done.2.rest_3_), channel_id=1, source_target_pairs={{2,0},{3,1},{0,2},{1,3},{6,4},{7,5},{4,6},{5,7},{10,8},{11,9},{8,1... | collective-permute-start | bytes 786440 | tf_op jit(solution)/shard_map/ppermute | solution.py:46
  31.3 10.8 %collective-permute-start.10 = (bf16[2,64,1024]{2,1,0:T(8,128)(2,1)S(1)}, bf16[2,64,1024]{2,1,0:T(8,128)(2,1)S(1)}, u32[]{:S(2)}, u32[]{:S(2)}) collective-permute-start(bf16[2,64,1024]{2,1,0:T(8,128)(2,1)S(1)} %collective-permute-done.2.rest_3_), channel_id=1, source_target_pairs={{1,0},{0,1},{3,2},{2,3},{5,4},{4,5},{7,6},{6,7},{9,8},{8,9},{11,10... | collective-permute-start | bytes 786440 | tf_op jit(solution)/shard_map/ppermute | solution.py:46
  31.3 12.0 %collective-permute-start.8 = (bf16[2,64,1024]{2,1,0:T(8,128)(2,1)S(1)}, bf16[2,64,1024]{2,1,0:T(8,128)(2,1)S(1)}, u32[]{:S(2)}, u32[]{:S(2)}) collective-permute-start(bf16[2,64,1024]{2,1,0:T(8,128)(2,1)S(1)} %collective-permute-done.rest_1_), channel_id=1, source_target_pairs={{1,0},{0,1},{3,2},{2,3},{5,4},{4,5},{7,6},{6,7},{9,8},{8,9},{11,10... | collective-permute-start | bytes 786440 | tf_op jit(solution)/shard_map/ppermute | solution.py:46
  31.8 14.7 %collective-permute-start.9 = (bf16[2,64,1024]{2,1,0:T(8,128)(2,1)S(1)}, bf16[2,64,1024]{2,1,0:T(8,128)(2,1)}, u32[]{:S(2)}, u32[]{:S(2)}) collective-permute-start(bf16[2,64,1024]{2,1,0:T(8,128)(2,1)S(1)} %collective-permute-done.1.rest_2_), channel_id=1, source_target_pairs={{1,0},{0,1},{3,2},{2,3},{5,4},{4,5},{7,6},{6,7},{9,8},{8,9},{11,10... | collective-permute-start | bytes 786440 | tf_op jit(solution)/shard_map/ppermute | solution.py:46
  38.5 8.1 %collective-permute-start.11 = (bf16[2,64,1024]{2,1,0:T(8,128)(2,1)S(1)}, bf16[2,64,1024]{2,1,0:T(8,128)(2,1)}, u32[]{:S(2)}, u32[]{:S(2)}) collective-permute-start(bf16[2,64,1024]{2,1,0:T(8,128)(2,1)S(1)} %collective-permute-done.3.rest_4_), channel_id=1, source_target_pairs={{1,0},{0,1},{3,2},{2,3},{5,4},{4,5},{7,6},{6,7},{9,8},{8,9},{11,10... | collective-permute-start | bytes 786440 | tf_op jit(solution)/shard_map/ppermute | solution.py:46
  42.0 4.5 %collective-permute-start.12 = (bf16[2,64,1024]{2,1,0:T(8,128)(2,1)S(1)}, bf16[2,64,1024]{2,1,0:T(8,128)(2,1)}, u32[]{:S(2)}, u32[]{:S(2)}) collective-permute-start(bf16[2,64,1024]{2,1,0:T(8,128)(2,1)S(1)} %collective-permute-done.4.rest_5_), channel_id=1, source_target_pairs={{1,0},{0,1},{3,2},{2,3},{5,4},{4,5},{7,6},{6,7},{9,8},{8,9},{11,10... | collective-permute-start | bytes 786440 | tf_op jit(solution)/shard_map/ppermute | solution.py:46
  42.0 0.7 copy-start.2
  42.8 3.8 %collective-permute-start.13 = (bf16[2,64,1024]{2,1,0:T(8,128)(2,1)S(1)}, bf16[2,64,1024]{2,1,0:T(8,128)(2,1)}, u32[]{:S(2)}, u32[]{:S(2)}) collective-permute-start(bf16[2,64,1024]{2,1,0:T(8,128)(2,1)S(1)} %collective-permute-done.5.rest_6_), channel_id=1, source_target_pairs={{1,0},{0,1},{3,2},{2,3},{5,4},{4,5},{7,6},{6,7},{9,8},{8,9},{11,10... | collective-permute-start | bytes 786440 | tf_op jit(solution)/shard_map/ppermute | solution.py:46
  43.3 0.7 copy-start.4
  44.0 2.6 %collective-permute-start.14 = (bf16[2,64,1024]{2,1,0:T(8,128)(2,1)S(1)}, bf16[2,64,1024]{2,1,0:T(8,128)(2,1)}, u32[]{:S(2)}, u32[]{:S(2)}) collective-permute-start(bf16[2,64,1024]{2,1,0:T(8,128)(2,1)S(1)} %collective-permute-done.6.rest_7_), channel_id=1, source_target_pairs={{1,0},{0,1},{3,2},{2,3},{5,4},{4,5},{7,6},{6,7},{9,8},{8,9},{11,10... | collective-permute-start | bytes 786440 | tf_op jit(solution)/shard_map/ppermute | solution.py:46
  44.7 0.7 copy-start.1
  46.6 1.0 copy-start.3
  47.5 0.9 copy-start.5
  48.5 0.7 copy-start.6
  49.2 6.2 %copy-start = (bf16[1,2048,1024]{2,1,0:T(8,128)(2,1)S(1)}, bf16[1,2048,1024]{2,1,0:T(8,128)(2,1)}, u32[]{:S(2)}) copy-start(bf16[1,2048,1024]{2,1,0:T(8,128)(2,1)} %param.6) | copy-start | bytes 12582916
  56.3 42.5 %collective-permute-start.20 = (bf16[384,512]{1,0:T(8,128)(2,1)S(1)}, bf16[384,512]{1,0:T(8,128)(2,1)S(1)}, u32[]{:S(2)}, u32[]{:S(2)}) collective-permute-start(bf16[384,512]{1,0:T(8,128)(2,1)S(1)} %shard_map.71), channel_id=1, source_target_pairs={{0,16},{16,0},{1,17},{17,1},{2,18},{18,2},{3,19},{19,3},{4,20},{20... | collective-permute-start | bytes 1179656 | tf_op jit(solution)/shard_map/ppermute | solution.py:177
  58.9 42.6 %collective-permute-start.19 = (bf16[384,512]{1,0:T(8,128)(2,1)S(1)}, bf16[384,512]{1,0:T(8,128)(2,1)S(1)}, u32[]{:S(2)}, u32[]{:S(2)}) collective-permute-start(bf16[384,512]{1,0:T(8,128)(2,1)S(1)} %shard_map.70), channel_id=1, source_target_pairs={{0,16},{16,0},{1,17},{17,1},{2,18},{18,2},{3,19},{19,3},{4,20},{20... | collective-permute-start | bytes 1179656 | tf_op jit(solution)/shard_map/ppermute | solution.py:177
  60.5 43.1 %collective-permute-start.18 = (bf16[384,512]{1,0:T(8,128)(2,1)S(1)}, bf16[384,512]{1,0:T(8,128)(2,1)S(1)}, u32[]{:S(2)}, u32[]{:S(2)}) collective-permute-start(bf16[384,512]{1,0:T(8,128)(2,1)S(1)} %shard_map.69), channel_id=1, source_target_pairs={{0,16},{16,0},{1,17},{17,1},{2,18},{18,2},{3,19},{19,3},{4,20},{20... | collective-permute-start | bytes 1179656 | tf_op jit(solution)/shard_map/ppermute | solution.py:177
  63.0 42.6 %collective-permute-start.17 = (bf16[384,512]{1,0:T(8,128)(2,1)S(1)}, bf16[384,512]{1,0:T(8,128)(2,1)S(1)}, u32[]{:S(2)}, u32[]{:S(2)}) collective-permute-start(bf16[384,512]{1,0:T(8,128)(2,1)S(1)} %shard_map.68), channel_id=1, source_target_pairs={{0,16},{16,0},{1,17},{17,1},{2,18},{18,2},{3,19},{19,3},{4,20},{20... | collective-permute-start | bytes 1179656 | tf_op jit(solution)/shard_map/ppermute | solution.py:177
  63.9 32.1 %collective-permute-start.21 = (bf16[128,512]{1,0:T(8,128)(2,1)S(1)}, bf16[128,512]{1,0:T(8,128)(2,1)S(1)}, u32[]{:S(2)}, u32[]{:S(2)}) collective-permute-start(bf16[128,512]{1,0:T(8,128)(2,1)S(1)} %shard_map.72), channel_id=1, source_target_pairs={{0,16},{16,0},{1,17},{17,1},{2,18},{18,2},{3,19},{19,3},{4,20},{20... | collective-permute-start | bytes 393224 | tf_op jit(solution)/shard_map/ppermute | solution.py:177
  96.0 11.7 %collective-permute-start.16 = (bf16[256,512]{1,0:T(8,128)(2,1)S(1)}, bf16[256,512]{1,0:T(8,128)(2,1)S(1)}, u32[]{:S(2)}, u32[]{:S(2)}) collective-permute-start(bf16[256,512]{1,0:T(8,128)(2,1)S(1)} %shard_map.67), channel_id=1, source_target_pairs={{0,16},{16,0},{1,17},{17,1},{2,18},{18,2},{3,19},{19,3},{4,20},{20... | collective-permute-start | bytes 786440 | tf_op jit(solution)/shard_map/ppermute | solution.py:177
  98.9 10.3 %collective-permute-start.15 = (bf16[128,512]{1,0:T(8,128)(2,1)S(1)}, bf16[128,512]{1,0:T(8,128)(2,1)S(1)}, u32[]{:S(2)}, u32[]{:S(2)}) collective-permute-start(bf16[128,512]{1,0:T(8,128)(2,1)S(1)} %shard_map.66), channel_id=1, source_target_pairs={{0,16},{16,0},{1,17},{17,1},{2,18},{18,2},{3,19},{19,3},{4,20},{20... | collective-permute-start | bytes 393224 | tf_op jit(solution)/shard_map/ppermute | solution.py:177

commit v2 on v0

v2 whole, which is shorter than its diff:
```python
import functools
import jax
import jax.numpy as jnp
from jax import lax
from jax.experimental import pallas as pl
from jax.experimental.pallas import tpu as pltpu
from jax.sharding import PartitionSpec as P

VMEM = pl.BlockSpec(memory_space=pltpu.VMEM)
SMEM = pl.BlockSpec(memory_space=pltpu.SMEM)
ANY = pl.BlockSpec(memory_space=pl.ANY)
F32 = jnp.float32
BF16 = jnp.bfloat16
MIB = 1024 * 1024
LANES = 128


def factors(n):
    core = 2 if n % 2 == 0 else 1
    rest = n // core
    outer = 1
    while outer * outer < rest:
        outer *= 2
    if rest % outer:
        outer = rest
    return outer, rest // outer, core


def turn(block, dims, axis, k):
    pairs = []
    for dst in range(dims[0] * dims[1] * dims[2]):
        digits = [dst // (dims[1] * dims[2]), dst // dims[2] % dims[1], dst % dims[2]]
        digits[axis] = (digits[axis] + k) % dims[axis]
        pairs.append(((digits[0] * dims[1] + digits[1]) * dims[2] + digits[2], dst))
    return lax.ppermute(block, "train", pairs)


def within(block, dims):
    held = [((0, 0), block)]
    held += [((k, 0), turn(block, dims, 1, k)) for k in range(1, dims[1])]
    held += [
        ((i, k), turn(b, dims, 2, k)) for k in range(1, dims[2]) for (i, _), b in held
    ]
    return [offset for offset, _ in held], [b for _, b in held]


def digits_of(me, dims):
    return (
        lax.div(me, dims[1] * dims[2]),
        lax.rem(lax.div(me, dims[2]), dims[1]),
        lax.rem(me, dims[2]),
    )


def inner_place(me, offset, dims):
    _, inner, core = digits_of(me, dims)
    return lax.rem(inner + offset[0], dims[1]) * dims[2] + lax.rem(core + offset[1], dims[2])


def outer_place(me, k, dims):
    return lax.rem(digits_of(me, dims)[0] + k, dims[0])


def ahead(k, n):
    return [(d, (d + k) % n) for d in range(n)]


def aligned(index, rows):
    return pl.ds(pl.multiple_of(index * rows, rows), rows)


def call(kernel, outs, operands, specs, mib=8, flops=0, moved=0, scratch=(), aliases=None, out_specs=None):
    several = isinstance(outs, list)
    shapes = outs if several else [outs]
    out_specs = out_specs or [VMEM] * len(shapes)
    return pl.pallas_call(
        kernel,
        out_shape=outs,
        in_specs=specs,
        out_specs=out_specs if several else out_specs[0],
        scratch_shapes=list(scratch),
        input_output_aliases=aliases or {},
        compiler_params=pltpu.CompilerParams(vmem_limit_bytes=mib * MIB),
        cost_estimate=pl.CostEstimate(flops=flops, bytes_accessed=moved, transcendentals=0),
    )(*operands)


def shape(dims, dtype=BF16):
    return jax.ShapeDtypeStruct(dims, dtype)


def stack_kernel(*refs):
    for i, ref in enumerate(refs[:-1]):
        refs[-1][i] = ref[...].reshape(refs[-1].shape[1:])


def weights_kernel(bucket, table, out):
    rows = bucket.shape[1]
    onehot = (lax.broadcasted_iota(jnp.int32, (table.shape[0], rows), 0) == bucket[...]).astype(F32)
    out[...] = lax.dot_general(
        onehot, table[...], (((0,), (0,)), ((), ())),
        precision=lax.Precision.HIGHEST, preferred_element_type=F32,
    )


def features_kernel(train, table, out, sem):
    rows = out.shape[0] - table.shape[0]
    copy = pltpu.make_async_copy(train.at[pl.ds(0, rows)], out.at[pl.ds(0, rows)], sem)
    copy.start()
    rest = table[...]
    for part in range(3):
        term = rest.astype(BF16)
        out[rows:, part * LANES : (part + 1) * LANES] = term
        rest = rest - term.astype(F32)
    out[rows:, 3 * LANES :] = jnp.zeros((table.shape[0], out.shape[1] - 3 * LANES), BF16)
    copy.wait()


def choose(ensemble, k, outer, me, order, test):
    width = order.shape[0] * order.shape[2] // ensemble
    first = lax.rem(me[0] + k, ensemble) * width
    wanted = lax.broadcasted_iota(jnp.int32, (width, order.shape[2]), 0) + first
    onehot = (wanted == order[outer]).astype(BF16)
    return jnp.dot(onehot, test[...], preferred_element_type=F32).astype(BF16)


def unpack(offsets, dims, me, k, blocks, test, inverse):
    rows = blocks[0].shape[1]
    outer = outer_place(me[1], k, dims)
    for offset, block in zip(offsets, blocks):
        at = inner_place(me[1], offset, dims)
        test[aligned(at, rows), :] = block[0]
        inverse[aligned(outer * len(blocks) + at, rows), :] = block[1]
    return outer


def part_kernel(ensemble, offsets, dims, k, me, order, *rest):
    blocks = rest[: len(offsets)]
    inverse, chosen, test = rest[-3:]
    outer = unpack(offsets, dims, me, k, blocks, test, inverse)
    width = chosen.shape[0] // ensemble
    for j in range(ensemble):
        rows = pl.ds(j * width, width)
        picked = choose(ensemble, j, outer, me, order, test)
        chosen[rows, :] = picked if k == 0 else chosen[rows, :] + picked


def transformed(inverse, chosen):
    return lax.dot_general(
        inverse[...], chosen, (((1,), (1,)), ((), ())), preferred_element_type=F32
    ).astype(BF16)


def send_transform_kernel(ensemble, offsets, dims, k, me, order, *rest):
    blocks = rest[: len(offsets)]
    inverse, chosen, test, out = rest[-4:]
    outer = unpack(offsets, dims, me, k, blocks, test, inverse)
    width = chosen.shape[0] // ensemble
    for j in range(1, ensemble):
        rows = pl.ds(j * width, width)
        picked = choose(ensemble, j, outer, me, order, test)
        if k > 0:
            picked = chosen[rows, :] + picked
        out[j - 1] = transformed(inverse, picked)


def own_transform_kernel(ensemble, dims, k, me, order, inverse, chosen, test, *rest):
    picked = choose(ensemble, 0, outer_place(me[1], k, dims), me, order, test)
    if k > 0:
        picked = chosen[: picked.shape[0], :] + picked
    rest[-1][...] = transformed(inverse, picked)


def scaled(train, matrix, weight):
    tile = jnp.dot(train, matrix, preferred_element_type=F32)
    wide = jnp.concatenate([weight] * (tile.shape[1] // weight.shape[1]), axis=1)
    return (tile * wide).astype(BF16)


def send_kernel(first, j, train, matrices, weight, *rest):
    out = rest[-1]
    rows = pl.ds(first, out.shape[0])
    out[...] = scaled(train[rows, :], matrices[j], weight[rows, :])


def first_kernel(first, me, train, matrices, weight, out, shard):
    send_kernel(first, 0, train, matrices, weight, out)
    shard[...] = matrices[0, aligned(me[1], shard.shape[0]), :]


def relay_kernel(block, *rest):
    rest[-1][...] = block[...]


def store(out, first, buffer, sems, step, tile):
    copies = []
    for i in range(buffer.shape[0] // step):
        at = i * step
        buffer[pl.ds(at, step), :] = tile(at)
        copies.append(
            pltpu.make_async_copy(
                buffer.at[pl.ds(at, step)], out.at[pl.ds(first + at, step)], sems.at[i]
            )
        )
        copies[-1].start()
    for copy in copies:
        copy.wait()


def sum_kernel(ensemble, others, first, step, train, matrix, weight, *rest):
    got = rest[:others]
    out, token, buffer, sems = rest[-4:]
    token[...] = jnp.zeros_like(token)

    def tile(at):
        rows = pl.ds(first + at, step)
        total = scaled(train[rows, :], matrix[...], weight[rows, :]).astype(F32)
        for other in got:
            total = total + other[pl.ds(at, step), :].astype(F32)
        return total / ensemble

    store(out, first, buffer, sems, step, tile)


def both_kernel(ensemble, dims, offsets, step, me, train, matrix, weight, bucket, train2, *rest):
    pieces = rest[: len(offsets)]
    out, token, matrix2, weight2, buffer, sems = rest[-6:]
    token[...] = jnp.zeros_like(token)
    count = buffer.shape[0]
    table = jnp.zeros((train2.shape[0] - count, LANES), F32)
    for part in range(3):
        table = table + train2[count:, part * LANES : (part + 1) * LANES].astype(F32)
    onehot = (
        lax.broadcasted_iota(jnp.int32, (table.shape[0], count), 0) == bucket[:, :count]
    ).astype(F32)
    weight2[...] = lax.dot_general(
        onehot, table, (((0,), (0,)), ((), ())),
        precision=lax.Precision.HIGHEST, preferred_element_type=F32,
    )
    rows = pieces[0].shape[1]
    for offset, piece in zip(offsets, pieces):
        at = inner_place(me[1], offset, dims)
        for k in range(dims[0]):
            index = outer_place(me[1], k, dims) * len(offsets) + at
            matrix2[aligned(index, rows), :] = piece[k]

    def tile(at):
        rows = pl.ds(at, step)
        total = scaled(train[rows, :], matrix[...], weight[rows, :]).astype(F32)
        total = total + scaled(train2[rows, :], matrix2[...], weight2[rows, :]).astype(F32)
        return total / ensemble

    store(out, 0, buffer, sems, step, tile)


def shards(train_feat, test_feat, kernel_inv, bucket_weight, bucket, test_order):
    ensemble, n = lax.axis_size("ckpt"), lax.axis_size("train")
    dims = factors(n)
    train = train_feat[0]
    rows, size = train.shape
    count = test_order.shape[0]
    width = count // ensemble
    unit = rows // 16
    paired = ensemble == 2
    featured = 6 if paired else 0
    parts = [1, 2, 2, 2, 2, 1] if paired else [8, 8]
    buckets = bucket_weight.shape[1]
    table_rows = -(-buckets // 16) * 16

    me = jnp.stack([lax.axis_index("ckpt"), lax.axis_index("train")]).astype(jnp.int32)
    order = test_order.reshape(dims[0], 1, count // dims[0])
    bucket = bucket.reshape(1, rows)
    table = jnp.broadcast_to(bucket_weight.reshape(buckets, 1), (buckets, LANES))
    table = jnp.pad(table, ((0, table_rows - buckets), (0, 0)))

    own = call(
        stack_kernel, shape((2, test_feat.shape[1], size)), (test_feat, kernel_inv), [VMEM] * 2
    )
    early = []
    if paired:
        features = call(
            features_kernel, shape((featured * unit + table_rows, size)), (train, table),
            [ANY, VMEM], scratch=[pltpu.SemaphoreType.DMA],
        )
        train2 = lax.ppermute(features, "ckpt", ahead(1, ensemble))
        early = [train2]

    outer = [own] + [turn(own, dims, 0, k) for k in range(1, dims[0])]
    groups = [within(block, dims) for block in outer]
    weight = call(weights_kernel, shape((rows, LANES), F32), (bucket, table), [VMEM] * 2)

    half = 2 * size * size * width
    state, last = [], dims[0] - 1
    for k, (offsets, blocks) in enumerate(groups[:-1]):
        operands = [me, order, *blocks, *state]
        state = call(
            functools.partial(part_kernel, ensemble, offsets, dims, k),
            [shape((size, size)), shape((count, size))],
            operands, [SMEM] + [VMEM] * (len(operands) - 1),
            scratch=[pltpu.VMEM((count // dims[0], size), BF16)],
            aliases={len(operands) - 2: 0, len(operands) - 1: 1} if state else None,
            flops=4 * half, moved=4 * size * size,
        )
    offsets, blocks = groups[-1]
    operands = [me, order, *blocks, *state, *early]
    aliases = {2 + len(blocks): 0, 3 + len(blocks): 1} if state else None
    inverse, chosen, test, matrices = call(
        functools.partial(send_transform_kernel, ensemble, offsets, dims, last),
        [
            shape((size, size)), shape((count, size)), shape((count // dims[0], size)),
            shape((ensemble - 1, size, width)),
        ],
        operands, [SMEM] + [VMEM] * (1 + len(blocks) + len(state)) + [ANY] * len(early),
        aliases=aliases, flops=3 * half, moved=4 * size * size, mib=12,
    )

    def send(first, part, after):
        got = []
        for k in range(1, ensemble):
            tile = call(
                functools.partial(send_kernel, first * unit, k - 1),
                shape((part * unit, width)),
                (train, matrices, weight, *after), [VMEM] * 3 + [ANY] * len(after),
                flops=2 * part * unit * size * width, moved=2 * part * unit * (size + width),
            )
            after = [tile]
            got.append(lax.ppermute(tile, "ckpt", ahead(k, ensemble)))
        return got, after

    starts = [featured + sum(parts[:q]) for q in range(len(parts))]
    flying = 3
    received, after = [], []
    for q in range(min(flying, len(parts))):
        if q == 0 and paired:
            tile, shard = call(
                functools.partial(first_kernel, starts[0] * unit),
                [shape((parts[0] * unit, width)), shape((size // n, width))],
                (me, train, matrices, weight), [SMEM] + [VMEM] * 3,
                flops=2 * parts[0] * unit * size * width, moved=2 * parts[0] * unit * (size + width),
            )
            got, after = [lax.ppermute(tile, "ckpt", ahead(1, ensemble))], [tile]
        else:
            got, after = send(starts[q], parts[q], after)
        received.append(got)
        if q == 1 and paired:
            shard2 = lax.ppermute(shard, "ckpt", ahead(1, ensemble))
            shard2 = call(relay_kernel, shape(shard2.shape), (shard2, *after), [VMEM] + [ANY] * len(after))
            column = call(
                stack_kernel, shape((dims[0],) + shard.shape),
                [shard2] + [turn(shard2, dims, 0, k) for k in range(1, dims[0])],
                [VMEM] * dims[0],
            )
            piece_offsets, pieces = within(column, dims)
        if q == min(1, len(parts) - 1):
            matrix = call(
                functools.partial(own_transform_kernel, ensemble, dims, last),
                shape((size, width)), (me, order, inverse, chosen, test, *after),
                [SMEM] + [VMEM] * 4 + [ANY] * len(after), flops=3 * half, moved=4 * size * size, mib=12,
            )
            after = [matrix]

    out = None

    def put(kernel, first, part, step, operands, specs, scratch=()):
        held = [] if out is None else [out]
        return call(
            kernel, [shape((rows, width), F32), shape((8, LANES), F32)],
            (*operands, *held), specs + [ANY] * len(held),
            out_specs=[ANY, VMEM],
            scratch=[
                *scratch, pltpu.VMEM((part * unit, width), F32),
                pltpu.SemaphoreType.DMA((part * unit // step,)),
            ],
            aliases={len(operands): 0} if held else None, mib=16,
            flops=2 * part * unit * size * width, moved=2 * part * unit * (size + 3 * width),
        )

    for q, (first, part) in enumerate(zip(starts, parts)):
        if paired and q == max(len(parts) - 2, 0):
            out, token = put(
                functools.partial(both_kernel, ensemble, dims, piece_offsets, unit),
                0, featured, unit,
                (me, train, matrix, weight, bucket, train2, *pieces),
                [SMEM] + [VMEM] * (5 + len(pieces)),
                scratch=[
                    pltpu.VMEM((size, width), BF16), pltpu.VMEM((featured * unit, LANES), F32)
                ],
            )
        got = received[q]
        out, token = put(
            functools.partial(sum_kernel, ensemble, len(got), first * unit, unit),
            first, part, unit, (train, matrix, weight, *got), [VMEM] * (3 + len(got)),
        )
        if q + flying < len(parts):
            more, _ = send(starts[q + flying], parts[q + flying], [token])
            received.append(more)
    return out


def solution(mesh):
    return jax.shard_map(
        shards,
        mesh=mesh,
        in_specs=(
            P("ckpt", "train", None),
            P("ckpt", "train", None),
            P("ckpt", "train", None),
            P("ckpt", None),
            P("train"),
            P(),
        ),
        out_specs=P("train", "ckpt"),
        check_vma=False,
    )
```

time: 181 us -> 94.7 us (0.52)
  waiting for transfers between devices: 140 us -> 35 us
  Pallas kernels: 0 us -> 27.2 us
  starting transfers between devices: 0.11 us -> 26.9 us
  between operations: 13.2 us -> 0.44 us
  matrix products: 12.1 us -> 0 us
  local copies, waits for them, and re-layouts: 11.9 us -> 4.73 us
  other arithmetic: 4.09 us -> 0.08 us
    all_gather x2 -> x0, waiting for transfers between devices: 85.9 us -> none  [the longest x1 46.3 us: shards(): full_inverse = lax.all_gather(kernel_inv, 'train', axis=1, tiled=True)]
    reduce_scatter x1 -> x0, waiting for transfers between devices: 53.2 us -> none  [shards(): lax.psum_scatter(total.astype(jnp.bfloat16), 'ckpt', scatter_dimension=1,...]
    ppermute x0 -> x29, waiting for transfers between devices: none -> 35 us  [the longest x21 28.1 us: turn(): return lax.ppermute(block, 'train', pairs)]
    pallas_call x0 -> x23, Pallas kernels: none -> 27.2 us  [call(): pl.pallas_call(kernel, out_shape=outs, in_specs=specs, out_specs=out_spec...]
    ppermute x0 -> x29, starting transfers between devices: none -> 26.9 us  [the longest x21 16.4 us: turn(): return lax.ppermute(block, 'train', pairs)]
    dot_general x3 -> x0, matrix products: 12.1 us -> none  [the longest x1 8.38 us: shards(): jnp.dot(train_feat[0], ordered[0].T, preferred_element_type=jnp.float32)]
    scatter x1 -> x0, local copies, waits for them, and re-layouts: 6.58 us -> none  [shards(): ordered = jnp.zeros_like(stored).at[:, test_order, :].set(stored)]
    div x1 -> x0, local copies, waits for them, and re-layouts: 5.34 us -> none  [shards(): return summed / ensemble]
  transfers between devices with their start and end apart: 3 -> 29, of which waited for: 3 -> 10; matrix products, arithmetic and copies ran while one was open for 0% -> 1% of each run, Pallas kernels for 0% -> 23%
where the time goes in v2:
time: 94.7 us; the launch traced here: 94.4 us
  waiting for transfers between devices  35 us (37%)
  Pallas kernels  27.2 us (29%)
  starting transfers between devices  26.9 us (28%)
  local copies, waits for them, and re-layouts  4.73 us (5%)
    ppermute x21, waiting for transfers between devices, turn(): return lax.ppermute(block, 'train', pairs)  28.1 us
    pallas_call x23, Pallas kernels, call(): pl.pallas_call(kernel, out_shape=outs, in_specs=specs, out_specs=out_spec...  27.2 us
    ppermute x21, starting transfers between devices, turn(): return lax.ppermute(block, 'train', pairs)  16.4 us
    ppermute x5, starting transfers between devices, send(): got.append(lax.ppermute(tile, 'ckpt', ahead(k, ensemble)))  7.01 us
    ppermute x5, waiting for transfers between devices, send(): got.append(lax.ppermute(tile, 'ckpt', ahead(k, ensemble)))  4.32 us
    unnamed x12, local copies, waits for them, and re-layouts  4.01 us
    ppermute x1, waiting for transfers between devices, shards(): shard2 = lax.ppermute(shard, 'ckpt', ahead(1, ensemble))  2.52 us
  transfers between devices with their start and end apart: 29, of which 10 were waited for; matrix products, arithmetic and copies ran while one was open for 1% of the time, Pallas kernels for 23%

profile of v2, /device:TPU:0, one launch (start us, length us, event | category | flops | bytes accessed | tf_op | source)
XLA Modules:
  0.0 94.4 jit_solution(8989430312707005647)
XLA Ops:
  0.0 0.9 copy-done.2
  0.9 0.9 copy-done.3
  1.8 3.1 %collective-permute-start = (bf16[2,64,1024]{2,1,0:T(8,128)(2,1)S(1)}, bf16[2,64,1024]{2,1,0:T(8,128)(2,1)}, u32[]{:S(2)}, u32[]{:S(2)}) collective-permute-start(bf16[2,64,1024]{2,1,0:T(8,128)(2,1)S(1)} %shard_map.64.rest_0_), channel_id=1, source_target_pairs={{12,0},{13,1},{14,2},{15,3},{0,4},{1,5},{2,6},{3,7},{4,8},{5,9},{6... | collective-permute-start | bytes 786440 | tf_op jit(solution)/shard_map/ppermute | solution.py:35
  4.9 2.1 %collective-permute-start.8 = (bf16[2,64,1024]{2,1,0:T(8,128)(2,1)S(1)}, bf16[2,64,1024]{2,1,0:T(8,128)(2,1)}, u32[]{:S(2)}, u32[]{:S(2)}) collective-permute-start(bf16[2,64,1024]{2,1,0:T(8,128)(2,1)S(1)} %shard_map.64.rest_0_), channel_id=1, source_target_pairs={{4,0},{5,1},{6,2},{7,3},{8,4},{9,5},{10,6},{11,7},{12,8},{13,9},{1... | collective-permute-start | bytes 786440 | tf_op jit(solution)/shard_map/ppermute | solution.py:35
  7.0 1.7 %collective-permute-start.12 = (bf16[2,64,1024]{2,1,0:T(8,128)(2,1)S(1)}, bf16[2,64,1024]{2,1,0:T(8,128)(2,1)}, u32[]{:S(2)}, u32[]{:S(2)}) collective-permute-start(bf16[2,64,1024]{2,1,0:T(8,128)(2,1)S(1)} %shard_map.64.rest_0_), channel_id=1, source_target_pairs={{2,0},{3,1},{0,2},{1,3},{6,4},{7,5},{4,6},{5,7},{10,8},{11,9},{8,1... | collective-permute-start | bytes 786440 | tf_op jit(solution)/shard_map/ppermute | solution.py:35
  8.7 0.7 broadcast_in_dim.8.table
  9.4 2.2 %copy-done = bf16[1,2048,1024]{2,1,0:T(8,128)(2,1)S(1)} copy-done((bf16[1,2048,1024]{2,1,0:T(8,128)(2,1)S(1)}, bf16[1,2048,1024]{2,1,0:T(8,128)(2,1)}, u32[]{:S(2)}) %copy-start) | copy-done | bytes 4194328
  11.7 1.6 %collective-permute-start.15 = (bf16[784,1024]{1,0:T(8,128)(2,1)S(1)}, bf16[784,1024]{1,0:T(8,128)(2,1)S(1)}, u32[]{:S(2)}, u32[]{:S(2)}) collective-permute-start(bf16[784,1024]{1,0:T(8,128)(2,1)S(1)} %shard_map.68), channel_id=1, source_target_pairs={{0,16},{16,0},{1,17},{17,1},{2,18},{18,2},{3,19},{19,3},{4,20},{20... | collective-permute-start | bytes 4816904 | tf_op jit(solution)/shard_map/ppermute | solution.py:285
  13.3 0.8 collective-permute-start.4
  14.2 4.2 %collective-permute-done.8.rest_0_ = bf16[2,64,1024]{2,1,0:T(8,128)(2,1)} collective-permute-done((bf16[2,64,1024]{2,1,0:T(8,128)(2,1)S(1)}, bf16[2,64,1024]{2,1,0:T(8,128)(2,1)}, u32[]{:S(2)}, u32[]{:S(2)}) %collective-permute-start.8) | collective-permute-done | bytes 262176 | tf_op jit(solution)/shard_map/ppermute | solution.py:35
  18.4 1.5 %collective-permute-start.9 = (bf16[2,64,1024]{2,1,0:T(8,128)(2,1)}, bf16[2,64,1024]{2,1,0:T(8,128)(2,1)}, u32[]{:S(2)}, u32[]{:S(2)}) collective-permute-start(bf16[2,64,1024]{2,1,0:T(8,128)(2,1)} %collective-permute-done.8.rest_0_), channel_id=1, source_target_pairs={{2,0},{3,1},{0,2},{1,3},{6,4},{7,5},{4,6},{5,7},{10,8},{11,9},{8,1... | collective-permute-start | bytes 786440 | tf_op jit(solution)/shard_map/ppermute | solution.py:35
  19.9 1.0 %shard_map.70.weight = f32[2048,128]{1,0:T(8,128)S(1)} custom-call(s32[1,2048]{1,0:T(1,128)S(1)} %bitcast.20, f32[16,128]{1,0:T(8,128)S(1)} %broadcast_in_dim.8.table), custom_call_target="tpu_custom_call" | custom-call | tf_op jit(solution)/shard_map/pallas_call | solution.py:76
  21.0 9.2 %collective-permute-done.4.rest_0_ = bf16[2,64,1024]{2,1,0:T(8,128)(2,1)} collective-permute-done((bf16[2,64,1024]{2,1,0:T(8,128)(2,1)S(1)}, bf16[2,64,1024]{2,1,0:T(8,128)(2,1)}, u32[]{:S(2)}, u32[]{:S(2)}) %collective-permute-start.4) | collective-permute-done | bytes 262176 | tf_op jit(solution)/shard_map/ppermute | solution.py:35
  30.2 1.5 %collective-permute-start.1 = (bf16[2,64,1024]{2,1,0:T(8,128)(2,1)}, bf16[2,64,1024]{2,1,0:T(8,128)(2,1)S(1)}, u32[]{:S(2)}, u32[]{:S(2)}) collective-permute-start(bf16[2,64,1024]{2,1,0:T(8,128)(2,1)} %collective-permute-done.rest_0_), channel_id=1, source_target_pairs={{2,0},{3,1},{0,2},{1,3},{6,4},{7,5},{4,6},{5,7},{10,8},{11,9},{8,1... | collective-permute-start | bytes 786440 | tf_op jit(solution)/shard_map/ppermute | solution.py:35
  31.7 0.5 collective-permute-start.5
  32.3 1.9 %shard_map.65 = (bf16[1024,1024]{1,0:T(8,128)(2,1)S(1)}, bf16[1024,1024]{1,0:T(8,128)(2,1)S(1)}) custom-call(s32[2]{0:T(128)S(1)} %pad_add_fusion.me, s32[4,1,256]{2,1,0:T(1,128)S(1)} %bitcast.22, bf16[2,64,1024]{2,1,0:T(8,128)(2,1)S(1)} %shard_map.64.rest_0_, bf16[2,64,1024]{2,1,0:T(8,128)(2,1)} %collective-permute-done.12.rest_1_, ...), custom_call_target="tpu_custom_call" | custom-call | flops 4294967296 | bytes 4194304 | tf_op jit(solution)/shard_map/pallas_call | solution.py:76
  34.2 5.3 %collective-permute-done.1.rest_1_ = bf16[2,64,1024]{2,1,0:T(8,128)(2,1)S(1)} collective-permute-done((bf16[2,64,1024]{2,1,0:T(8,128)(2,1)}, bf16[2,64,1024]{2,1,0:T(8,128)(2,1)S(1)}, u32[]{:S(2)}, u32[]{:S(2)}) %collective-permute-start.1) | collective-permute-done | bytes 262176 | tf_op jit(solution)/shard_map/ppermute | solution.py:35
  39.5 5.2 %collective-permute-done.5.rest_1_ = bf16[2,64,1024]{2,1,0:T(8,128)(2,1)S(1)} collective-permute-done((bf16[2,64,1024]{2,1,0:T(8,128)(2,1)}, bf16[2,64,1024]{2,1,0:T(8,128)(2,1)S(1)}, u32[]{:S(2)}, u32[]{:S(2)}) %collective-permute-start.5) | collective-permute-done | bytes 262176 | tf_op jit(solution)/shard_map/ppermute | solution.py:35
  44.8 0.5 collective-permute-start.3
  45.3 1.9 %shard_map.66 = (bf16[1024,1024]{1,0:T(8,128)(2,1)S(1)}, bf16[1024,1024]{1,0:T(8,128)(2,1)S(1)}) custom-call(s32[2]{0:T(128)S(1)} %pad_add_fusion.me, s32[4,1,256]{2,1,0:T(1,128)S(1)} %bitcast.23, bf16[2,64,1024]{2,1,0:T(8,128)(2,1)} %collective-permute-done.8.rest_0_, ...), custom_call_target="tpu_custom_call", output_to_operand_aliasing={{0}: (6, {}), {1}: (7, {})} | custom-call | flops 4294967296 | bytes 4194304 | tf_op jit(solution)/shard_map/pallas_call | solution.py:76
  47.2 1.8 %shard_map.67 = (bf16[1024,1024]{1,0:T(8,128)(2,1)S(1)}, bf16[1024,1024]{1,0:T(8,128)(2,1)S(1)}) custom-call(s32[2]{0:T(128)S(1)} %pad_add_fusion.me, s32[4,1,256]{2,1,0:T(1,128)S(1)} %bitcast.24, bf16[2,64,1024]{2,1,0:T(8,128)(2,1)} %collective-permute-done.4.rest_0_, ...), custom_call_target="tpu_custom_call", output_to_operand_aliasing={{0}: (6, {}), {1}: (7, {})} | custom-call | flops 4294967296 | bytes 4194304 | tf_op jit(solution)/shard_map/pallas_call | solution.py:76
  49.1 2.7 %shard_map.69 = (bf16[1024,1024]{1,0:T(8,128)(2,1)S(1)}, bf16[1024,1024]{1,0:T(8,128)(2,1)S(1)}, bf16[256,1024]{1,0:T(8,128)(2,1)S(1)}, bf16[1,1024,512]{2,1,0:T(8,128)(2,1)S(1)}) custom-call(s32[2]{0:T(128)S(1)} %pad_add_fusion.me, s32[4,1,256]{2,1,0:T(1,128)S(1)} %bitcast.25, ...), custom_call_target="tpu_custom_call", output_to_operand_aliasing={{0}: (6, {}), {1}: (7, {})} | custom-call | flops 3221225472 | bytes 4194304 | tf_op jit(solution)/shard_map/pallas_call | solution.py:76
  51.8 0.9 shard_map.71
  52.7 1.5 %collective-permute-start.21 = (bf16[64,512]{1,0:T(8,128)(2,1)S(1)}, bf16[64,512]{1,0:T(8,128)(2,1)S(1)}, u32[]{:S(2)}, u32[]{:S(2)}) collective-permute-start(bf16[64,512]{1,0:T(8,128)(2,1)S(1)} %get-tuple-element.42), channel_id=1, source_target_pairs={{0,16},{16,0},{1,17},{17,1},{2,18},{18,2},{3,19},{19,3},{4,20},{20... | collective-permute-start | bytes 196616 | tf_op jit(solution)/shard_map/ppermute | solution.py:346
  54.6 2.5 %collective-permute-done.21.block = bf16[64,512]{1,0:T(8,128)(2,1)S(1)} collective-permute-done((bf16[64,512]{1,0:T(8,128)(2,1)S(1)}, bf16[64,512]{1,0:T(8,128)(2,1)S(1)}, u32[]{:S(2)}, u32[]{:S(2)}) %collective-permute-start.21) | collective-permute-done | bytes 65568 | tf_op jit(solution)/shard_map/ppermute | solution.py:346
  57.2 1.6 %collective-permute-start.22 = (bf16[64,512]{1,0:T(8,128)(2,1)S(1)}, bf16[64,512]{1,0:T(8,128)(2,1)S(1)}, u32[]{:S(2)}, u32[]{:S(2)}) collective-permute-start(bf16[64,512]{1,0:T(8,128)(2,1)S(1)} %shard_map.80.refs_0_), channel_id=1, source_target_pairs={{4,0},{5,1},{6,2},{7,3},{8,4},{9,5},{10,6},{11,7},{12,8},{13,9},{1... | collective-permute-start | bytes 196616 | tf_op jit(solution)/shard_map/ppermute | solution.py:35
  58.7 1.2 %collective-permute-start.24 = (bf16[64,512]{1,0:T(8,128)(2,1)S(1)}, bf16[64,512]{1,0:T(8,128)(2,1)S(1)}, u32[]{:S(2)}, u32[]{:S(2)}) collective-permute-start(bf16[64,512]{1,0:T(8,128)(2,1)S(1)} %shard_map.80.refs_0_), channel_id=1, source_target_pairs={{12,0},{13,1},{14,2},{15,3},{0,4},{1,5},{2,6},{3,7},{4,8},{5,9},{6... | collective-permute-start | bytes 196616 | tf_op jit(solution)/shard_map/ppermute | solution.py:35
  59.9 1.6 %collective-permute-start.17 = (bf16[256,512]{1,0:T(8,128)(2,1)S(1)}, bf16[256,512]{1,0:T(8,128)(2,1)S(1)}, u32[]{:S(2)}, u32[]{:S(2)}) collective-permute-start(bf16[256,512]{1,0:T(8,128)(2,1)S(1)} %shard_map.72.rest_0_), channel_id=1, source_target_pairs={{0,16},{16,0},{1,17},{17,1},{2,18},{18,2},{3,19},{19,3},{4,20},{20... | collective-permute-start | bytes 786440 | tf_op jit(solution)/shard_map/ppermute | solution.py:327
  61.5 0.4 collective-permute-start.18
  62.0 3.8 %collective-permute-done.23.refs_2_ = bf16[64,512]{1,0:T(8,128)(2,1)S(1)} collective-permute-done((bf16[64,512]{1,0:T(8,128)(2,1)S(1)}, bf16[64,512]{1,0:T(8,128)(2,1)S(1)}, u32[]{:S(2)}, u32[]{:S(2)}) %collective-permute-start.23) | collective-permute-done | bytes 65568 | tf_op jit(solution)/shard_map/ppermute | solution.py:35
  65.8 1.6 %collective-permute-start.25 = (bf16[4,64,512]{2,1,0:T(8,128)(2,1)S(1)}, bf16[4,64,512]{2,1,0:T(8,128)(2,1)S(1)}, u32[]{:S(2)}, u32[]{:S(2)}) collective-permute-start(bf16[4,64,512]{2,1,0:T(8,128)(2,1)S(1)} %shard_map.81.rest_0_), channel_id=1, source_target_pairs={{2,0},{3,1},{0,2},{1,3},{6,4},{7,5},{4,6},{5,7},{10,8},{11,9},{8,1... | collective-permute-start | bytes 786440 | tf_op jit(solution)/shard_map/ppermute | solution.py:35
  67.4 2.1 %shard_map.73.rest_0_.matrix = bf16[1024,512]{1,0:T(8,128)(2,1)S(1)} custom-call(s32[2]{0:T(128)S(1)} %pad_add_fusion.me, s32[4,1,256]{2,1,0:T(1,128)S(1)} %bitcast.26, bf16[1024,1024]{1,0:T(8,128)(2,1)S(1)} %get-tuple-element.33.inverse, bf16[1024,1024]{1,0:T(8,128)(2,1)S(1)} %get-tuple-element.34.chosen, bf16[256,1024]{1,0:T(8,128)(2,1)S(1)} %get-tuple-element.35.test, ...), custom_call_target="tpu_custom_call" | custom-call | flops 3221225472 | bytes 4194304 | tf_op jit(solution)/shard_map/pallas_call | solution.py:76
  69.5 0.4 shard_map.74
  69.9 1.6 %collective-permute-start.16 = (bf16[256,512]{1,0:T(8,128)(2,1)S(1)}, bf16[256,512]{1,0:T(8,128)(2,1)S(1)}, u32[]{:S(2)}, u32[]{:S(2)}) collective-permute-start(bf16[256,512]{1,0:T(8,128)(2,1)S(1)} %shard_map.74), channel_id=1, source_target_pairs={{0,16},{16,0},{1,17},{17,1},{2,18},{18,2},{3,19},{19,3},{4,20},{20... | collective-permute-start | bytes 786440 | tf_op jit(solution)/shard_map/ppermute | solution.py:327
  71.5 1.0 %shard_map.75 = (f32[2048,512]{1,0:T(8,128)}, f32[8,128]{1,0:T(8,128)S(1)}) custom-call(bf16[2048,1024]{1,0:T(8,128)(2,1)S(1)} %bitcast.10, bf16[1024,512]{1,0:T(8,128)(2,1)S(1)} %shard_map.73.rest_0_.matrix, f32[2048,128]{1,0:T(8,128)S(1)} %shard_map.70.weight, bf16[128,512]{1,0:T(8,128)(2,1)S(1)} %collective-permute-done.18.rest_0_), custom_call_target="tpu_custom_call" | custom-call | flops 134217728 | bytes 655360 | tf_op jit(solution)/shard_map/pallas_call | solution.py:76
  72.6 0.4 shard_map.82
  73.0 0.5 collective-permute-start.28
  74.1 1.2 %shard_map.76 = (f32[2048,512]{1,0:T(8,128)}, f32[8,128]{1,0:T(8,128)S(1)}) custom-call(bf16[2048,1024]{1,0:T(8,128)(2,1)S(1)} %bitcast.12, bf16[1024,512]{1,0:T(8,128)(2,1)S(1)} %shard_map.73.rest_0_.matrix, f32[2048,128]{1,0:T(8,128)S(1)} %shard_map.70.weight, ...), custom_call_target="tpu_custom_call", output_to_operand_aliasing={{0}: (4, {})} | custom-call | flops 268435456 | bytes 1310720 | tf_op jit(solution)/shard_map/pallas_call | solution.py:76
  75.3 0.4 shard_map.79
  75.7 1.6 %collective-permute-start.20 = (bf16[256,512]{1,0:T(8,128)(2,1)S(1)}, bf16[256,512]{1,0:T(8,128)(2,1)S(1)}, u32[]{:S(2)}, u32[]{:S(2)}) collective-permute-start(bf16[256,512]{1,0:T(8,128)(2,1)S(1)} %shard_map.79), channel_id=1, source_target_pairs={{0,16},{16,0},{1,17},{17,1},{2,18},{18,2},{3,19},{19,3},{4,20},{20... | collective-permute-start | bytes 786440 | tf_op jit(solution)/shard_map/ppermute | solution.py:327
  77.3 1.9 %collective-permute-done.16.rest_0_ = bf16[256,512]{1,0:T(8,128)(2,1)S(1)} collective-permute-done((bf16[256,512]{1,0:T(8,128)(2,1)S(1)}, bf16[256,512]{1,0:T(8,128)(2,1)S(1)}, u32[]{:S(2)}, u32[]{:S(2)}) %collective-permute-start.16) | collective-permute-done | bytes 262176 | tf_op jit(solution)/shard_map/ppermute | solution.py:327
  79.2 1.2 %shard_map.77 = (f32[2048,512]{1,0:T(8,128)}, f32[8,128]{1,0:T(8,128)S(1)}) custom-call(bf16[2048,1024]{1,0:T(8,128)(2,1)S(1)} %bitcast.14, bf16[1024,512]{1,0:T(8,128)(2,1)S(1)} %shard_map.73.rest_0_.matrix, f32[2048,128]{1,0:T(8,128)S(1)} %shard_map.70.weight, ...), custom_call_target="tpu_custom_call", output_to_operand_aliasing={{0}: (4, {})} | custom-call | flops 268435456 | bytes 1310720 | tf_op jit(solution)/shard_map/pallas_call | solution.py:76
  80.7 1.6 %collective-permute-start.19 = (bf16[128,512]{1,0:T(8,128)(2,1)S(1)}, bf16[128,512]{1,0:T(8,128)(2,1)S(1)}, u32[]{:S(2)}, u32[]{:S(2)}) collective-permute-start(bf16[128,512]{1,0:T(8,128)(2,1)S(1)} %shard_map.78), channel_id=1, source_target_pairs={{0,16},{16,0},{1,17},{17,1},{2,18},{18,2},{3,19},{19,3},{4,20},{20... | collective-permute-start | bytes 393224 | tf_op jit(solution)/shard_map/ppermute | solution.py:327
  82.4 2.5 %collective-permute-done.28.rest_0_ = bf16[256,512]{1,0:T(8,128)(2,1)S(1)} collective-permute-done((bf16[256,512]{1,0:T(8,128)(2,1)S(1)}, bf16[256,512]{1,0:T(8,128)(2,1)S(1)}, u32[]{:S(2)}, u32[]{:S(2)}) %collective-permute-start.28) | collective-permute-done | bytes 262176 | tf_op jit(solution)/shard_map/ppermute | solution.py:327
  84.8 1.8 %shard_map.83 = (f32[2048,512]{1,0:T(8,128)}, f32[8,128]{1,0:T(8,128)}) custom-call(bf16[2048,1024]{1,0:T(8,128)(2,1)S(1)} %bitcast.16, bf16[1024,512]{1,0:T(8,128)(2,1)S(1)} %shard_map.73.rest_0_.matrix, f32[2048,128]{1,0:T(8,128)S(1)} %shard_map.70.weight, bf16[256,512]{1,0:T(8,128)(2,1)S(1)} %collective-permute-done.28.rest_0_, ...), custom_call_target="tpu_custom_call", output_to_operand_aliasing={{0}: (4, {})} | custom-call | flops 268435456 | bytes 1310720 | tf_op jit(solution)/shard_map/pallas_call | solution.py:76
  86.6 4.1 %shard_map.84 = (f32[2048,512]{1,0:T(8,128)}, f32[8,128]{1,0:T(8,128)}) custom-call(s32[2]{0:T(128)S(1)} %pad_add_fusion.me, bf16[2048,1024]{1,0:T(8,128)(2,1)S(1)} %bitcast.17, bf16[1024,512]{1,0:T(8,128)(2,1)S(1)} %shard_map.73.rest_0_.matrix, f32[2048,128]{1,0:T(8,128)S(1)} %shard_map.70.weight, ...), custom_call_target="tpu_custom_call", output_to_operand_aliasing={{0}: (10, {})} | custom-call | flops 805306368 | bytes 3932160 | tf_op jit(solution)/shard_map/pallas_call | solution.py:76
  90.8 1.8 %shard_map.85 = (f32[2048,512]{1,0:T(8,128)}, f32[8,128]{1,0:T(8,128)}) custom-call(bf16[2048,1024]{1,0:T(8,128)(2,1)S(1)} %bitcast.18, bf16[1024,512]{1,0:T(8,128)(2,1)S(1)} %shard_map.73.rest_0_.matrix, f32[2048,128]{1,0:T(8,128)S(1)} %shard_map.70.weight, bf16[256,512]{1,0:T(8,128)(2,1)S(1)} %collective-permute-done.20.rest_0_, ...), custom_call_target="tpu_custom_call", output_to_operand_aliasing={{0}: (4, {})} | custom-call | flops 268435456 | bytes 1310720 | tf_op jit(solution)/shard_map/pallas_call | solution.py:76
  92.6 1.6 %shard_map.86 = (f32[2048,512]{1,0:T(8,128)}, f32[8,128]{1,0:T(8,128)}) custom-call(bf16[2048,1024]{1,0:T(8,128)(2,1)S(1)} %bitcast.19, bf16[1024,512]{1,0:T(8,128)(2,1)S(1)} %shard_map.73.rest_0_.matrix, f32[2048,128]{1,0:T(8,128)S(1)} %shard_map.70.weight, bf16[128,512]{1,0:T(8,128)(2,1)S(1)} %collective-permute-done.19.rest_0_, ...), custom_call_target="tpu_custom_call", output_to_operand_aliasing={{0}: (4, {})} | custom-call | flops 134217728 | bytes 655360 | tf_op jit(solution)/shard_map/pallas_call | solution.py:76
  (47 shorter events, 1.8 us)
Async XLA Ops:
  0.0 0.9 copy-start.2
  0.9 0.9 copy-start.3
  1.8 12.4 %collective-permute-start = (bf16[2,64,1024]{2,1,0:T(8,128)(2,1)S(1)}, bf16[2,64,1024]{2,1,0:T(8,128)(2,1)}, u32[]{:S(2)}, u32[]{:S(2)}) collective-permute-start(bf16[2,64,1024]{2,1,0:T(8,128)(2,1)S(1)} %shard_map.64.rest_0_), channel_id=1, source_target_pairs={{12,0},{13,1},{14,2},{15,3},{0,4},{1,5},{2,6},{3,7},{4,8},{5,9},{6... | collective-permute-start | bytes 786440 | tf_op jit(solution)/shard_map/ppermute | solution.py:35
  4.9 13.5 %collective-permute-start.8 = (bf16[2,64,1024]{2,1,0:T(8,128)(2,1)S(1)}, bf16[2,64,1024]{2,1,0:T(8,128)(2,1)}, u32[]{:S(2)}, u32[]{:S(2)}) collective-permute-start(bf16[2,64,1024]{2,1,0:T(8,128)(2,1)S(1)} %shard_map.64.rest_0_), channel_id=1, source_target_pairs={{4,0},{5,1},{6,2},{7,3},{8,4},{9,5},{10,6},{11,7},{12,8},{13,9},{1... | collective-permute-start | bytes 786440 | tf_op jit(solution)/shard_map/ppermute | solution.py:35
  7.0 12.9 %collective-permute-start.12 = (bf16[2,64,1024]{2,1,0:T(8,128)(2,1)S(1)}, bf16[2,64,1024]{2,1,0:T(8,128)(2,1)}, u32[]{:S(2)}, u32[]{:S(2)}) collective-permute-start(bf16[2,64,1024]{2,1,0:T(8,128)(2,1)S(1)} %shard_map.64.rest_0_), channel_id=1, source_target_pairs={{2,0},{3,1},{0,2},{1,3},{6,4},{7,5},{4,6},{5,7},{10,8},{11,9},{8,1... | collective-permute-start | bytes 786440 | tf_op jit(solution)/shard_map/ppermute | solution.py:35
  9.4 2.2 %copy-start = (bf16[1,2048,1024]{2,1,0:T(8,128)(2,1)S(1)}, bf16[1,2048,1024]{2,1,0:T(8,128)(2,1)}, u32[]{:S(2)}) copy-start(bf16[1,2048,1024]{2,1,0:T(8,128)(2,1)} %param.6) | copy-start | bytes 12582916
  11.6 8.3 %copy-start.4 = (s32[2048]{0:T(1024)S(1)}, s32[2048]{0:T(1024)}, u32[]{:S(2)}) copy-start(s32[2048]{0:T(1024)} %param.10) | copy-start | bytes 24580
  11.6 20.7 %copy-start.5 = (s32[1024]{0:T(1024)S(1)}, s32[1024]{0:T(1024)}, u32[]{:S(2)}) copy-start(s32[1024]{0:T(1024)} %param.11) | copy-start | bytes 12292
  11.7 37.3 %collective-permute-start.15 = (bf16[784,1024]{1,0:T(8,128)(2,1)S(1)}, bf16[784,1024]{1,0:T(8,128)(2,1)S(1)}, u32[]{:S(2)}, u32[]{:S(2)}) collective-permute-start(bf16[784,1024]{1,0:T(8,128)(2,1)S(1)} %shard_map.68), channel_id=1, source_target_pairs={{0,16},{16,0},{1,17},{17,1},{2,18},{18,2},{3,19},{19,3},{4,20},{20... | collective-permute-start | bytes 4816904 | tf_op jit(solution)/shard_map/ppermute | solution.py:285
  13.3 16.9 %collective-permute-start.4 = (bf16[2,64,1024]{2,1,0:T(8,128)(2,1)S(1)}, bf16[2,64,1024]{2,1,0:T(8,128)(2,1)}, u32[]{:S(2)}, u32[]{:S(2)}) collective-permute-start(bf16[2,64,1024]{2,1,0:T(8,128)(2,1)S(1)} %shard_map.64.rest_0_), channel_id=1, source_target_pairs={{8,0},{9,1},{10,2},{11,3},{12,4},{13,5},{14,6},{15,7},{0,8},{1,9},... | collective-permute-start | bytes 786440 | tf_op jit(solution)/shard_map/ppermute | solution.py:35
  14.2 16.0 %collective-permute-start.13 = (bf16[2,64,1024]{2,1,0:T(8,128)(2,1)S(1)}, bf16[2,64,1024]{2,1,0:T(8,128)(2,1)}, u32[]{:S(2)}, u32[]{:S(2)}) collective-permute-start(bf16[2,64,1024]{2,1,0:T(8,128)(2,1)S(1)} %shard_map.64.rest_0_), channel_id=1, source_target_pairs={{1,0},{0,1},{3,2},{2,3},{5,4},{4,5},{7,6},{6,7},{9,8},{8,9},{11,10... | collective-permute-start | bytes 786440 | tf_op jit(solution)/shard_map/ppermute | solution.py:35
  18.4 13.3 %collective-permute-start.9 = (bf16[2,64,1024]{2,1,0:T(8,128)(2,1)}, bf16[2,64,1024]{2,1,0:T(8,128)(2,1)}, u32[]{:S(2)}, u32[]{:S(2)}) collective-permute-start(bf16[2,64,1024]{2,1,0:T(8,128)(2,1)} %collective-permute-done.8.rest_0_), channel_id=1, source_target_pairs={{2,0},{3,1},{0,2},{1,3},{6,4},{7,5},{4,6},{5,7},{10,8},{11,9},{8,1... | collective-permute-start | bytes 786440 | tf_op jit(solution)/shard_map/ppermute | solution.py:35
  19.9 12.3 %collective-permute-start.14 = (bf16[2,64,1024]{2,1,0:T(8,128)(2,1)}, bf16[2,64,1024]{2,1,0:T(8,128)(2,1)}, u32[]{:S(2)}, u32[]{:S(2)}) collective-permute-start(bf16[2,64,1024]{2,1,0:T(8,128)(2,1)} %collective-permute-done.12.rest_1_), channel_id=1, source_target_pairs={{1,0},{0,1},{3,2},{2,3},{5,4},{4,5},{7,6},{6,7},{9,8},{8,9},{11,10... | collective-permute-start | bytes 786440 | tf_op jit(solution)/shard_map/ppermute | solution.py:35
  30.2 14.6 %collective-permute-start.10 = (bf16[2,64,1024]{2,1,0:T(8,128)(2,1)}, bf16[2,64,1024]{2,1,0:T(8,128)(2,1)S(1)}, u32[]{:S(2)}, u32[]{:S(2)}) collective-permute-start(bf16[2,64,1024]{2,1,0:T(8,128)(2,1)} %collective-permute-done.8.rest_0_), channel_id=1, source_target_pairs={{1,0},{0,1},{3,2},{2,3},{5,4},{4,5},{7,6},{6,7},{9,8},{8,9},{11,10... | collective-permute-start | bytes 786440 | tf_op jit(solution)/shard_map/ppermute | solution.py:35
  30.2 9.3 %collective-permute-start.1 = (bf16[2,64,1024]{2,1,0:T(8,128)(2,1)}, bf16[2,64,1024]{2,1,0:T(8,128)(2,1)S(1)}, u32[]{:S(2)}, u32[]{:S(2)}) collective-permute-start(bf16[2,64,1024]{2,1,0:T(8,128)(2,1)} %collective-permute-done.rest_0_), channel_id=1, source_target_pairs={{2,0},{3,1},{0,2},{1,3},{6,4},{7,5},{4,6},{5,7},{10,8},{11,9},{8,1... | collective-permute-start | bytes 786440 | tf_op jit(solution)/shard_map/ppermute | solution.py:35
  31.7 13.0 %collective-permute-start.5 = (bf16[2,64,1024]{2,1,0:T(8,128)(2,1)}, bf16[2,64,1024]{2,1,0:T(8,128)(2,1)S(1)}, u32[]{:S(2)}, u32[]{:S(2)}) collective-permute-start(bf16[2,64,1024]{2,1,0:T(8,128)(2,1)} %collective-permute-done.4.rest_0_), channel_id=1, source_target_pairs={{2,0},{3,1},{0,2},{1,3},{6,4},{7,5},{4,6},{5,7},{10,8},{11,9},{8,1... | collective-permute-start | bytes 786440 | tf_op jit(solution)/shard_map/ppermute | solution.py:35
  32.3 13.0 %collective-permute-start.11 = (bf16[2,64,1024]{2,1,0:T(8,128)(2,1)}, bf16[2,64,1024]{2,1,0:T(8,128)(2,1)S(1)}, u32[]{:S(2)}, u32[]{:S(2)}) collective-permute-start(bf16[2,64,1024]{2,1,0:T(8,128)(2,1)} %collective-permute-done.9.rest_1_), channel_id=1, source_target_pairs={{1,0},{0,1},{3,2},{2,3},{5,4},{4,5},{7,6},{6,7},{9,8},{8,9},{11,10... | collective-permute-start | bytes 786440 | tf_op jit(solution)/shard_map/ppermute | solution.py:35
  39.5 9.5 %collective-permute-start.2 = (bf16[2,64,1024]{2,1,0:T(8,128)(2,1)}, bf16[2,64,1024]{2,1,0:T(8,128)(2,1)S(1)}, u32[]{:S(2)}, u32[]{:S(2)}) collective-permute-start(bf16[2,64,1024]{2,1,0:T(8,128)(2,1)} %collective-permute-done.rest_0_), channel_id=1, source_target_pairs={{1,0},{0,1},{3,2},{2,3},{5,4},{4,5},{7,6},{6,7},{9,8},{8,9},{11,10... | collective-permute-start | bytes 786440 | tf_op jit(solution)/shard_map/ppermute | solution.py:35
  44.8 2.4 %collective-permute-start.6 = (bf16[2,64,1024]{2,1,0:T(8,128)(2,1)}, bf16[2,64,1024]{2,1,0:T(8,128)(2,1)S(1)}, u32[]{:S(2)}, u32[]{:S(2)}) collective-permute-start(bf16[2,64,1024]{2,1,0:T(8,128)(2,1)} %collective-permute-done.4.rest_0_), channel_id=1, source_target_pairs={{1,0},{0,1},{3,2},{2,3},{5,4},{4,5},{7,6},{6,7},{9,8},{8,9},{11,10... | collective-permute-start | bytes 786440 | tf_op jit(solution)/shard_map/ppermute | solution.py:35
  44.8 4.3 %collective-permute-start.3 = (bf16[2,64,1024]{2,1,0:T(8,128)(2,1)S(1)}, bf16[2,64,1024]{2,1,0:T(8,128)(2,1)S(1)}, u32[]{:S(2)}, u32[]{:S(2)}) collective-permute-start(bf16[2,64,1024]{2,1,0:T(8,128)(2,1)S(1)} %collective-permute-done.1.rest_1_), channel_id=1, source_target_pairs={{1,0},{0,1},{3,2},{2,3},{5,4},{4,5},{7,6},{6,7},{9,8},{8,9},{11,10... | collective-permute-start | bytes 786440 | tf_op jit(solution)/shard_map/ppermute | solution.py:35
  45.3 1.9 %collective-permute-start.7 = (bf16[2,64,1024]{2,1,0:T(8,128)(2,1)S(1)}, bf16[2,64,1024]{2,1,0:T(8,128)(2,1)S(1)}, u32[]{:S(2)}, u32[]{:S(2)}) collective-permute-start(bf16[2,64,1024]{2,1,0:T(8,128)(2,1)S(1)} %collective-permute-done.5.rest_1_), channel_id=1, source_target_pairs={{1,0},{0,1},{3,2},{2,3},{5,4},{4,5},{7,6},{6,7},{9,8},{8,9},{11,10... | collective-permute-start | bytes 786440 | tf_op jit(solution)/shard_map/ppermute | solution.py:35
  49.0 2.7 %copy-start.1 = (bf16[1,2048,1024]{2,1,0:T(8,128)(2,1)S(1)}, bf16[1,2048,1024]{2,1,0:T(8,128)(2,1)}, u32[]{:S(2)}) copy-start(bf16[1,2048,1024]{2,1,0:T(8,128)(2,1)} %param.6) | copy-start | bytes 12582916
  52.7 4.5 %collective-permute-start.21 = (bf16[64,512]{1,0:T(8,128)(2,1)S(1)}, bf16[64,512]{1,0:T(8,128)(2,1)S(1)}, u32[]{:S(2)}, u32[]{:S(2)}) collective-permute-start(bf16[64,512]{1,0:T(8,128)(2,1)S(1)} %get-tuple-element.42), channel_id=1, source_target_pairs={{0,16},{16,0},{1,17},{17,1},{2,18},{18,2},{3,19},{19,3},{4,20},{20... | collective-permute-start | bytes 196616 | tf_op jit(solution)/shard_map/ppermute | solution.py:346
  57.2 4.8 %collective-permute-start.22 = (bf16[64,512]{1,0:T(8,128)(2,1)S(1)}, bf16[64,512]{1,0:T(8,128)(2,1)S(1)}, u32[]{:S(2)}, u32[]{:S(2)}) collective-permute-start(bf16[64,512]{1,0:T(8,128)(2,1)S(1)} %shard_map.80.refs_0_), channel_id=1, source_target_pairs={{4,0},{5,1},{6,2},{7,3},{8,4},{9,5},{10,6},{11,7},{12,8},{13,9},{1... | collective-permute-start | bytes 196616 | tf_op jit(solution)/shard_map/ppermute | solution.py:35
  58.7 7.0 %collective-permute-start.23 = (bf16[64,512]{1,0:T(8,128)(2,1)S(1)}, bf16[64,512]{1,0:T(8,128)(2,1)S(1)}, u32[]{:S(2)}, u32[]{:S(2)}) collective-permute-start(bf16[64,512]{1,0:T(8,128)(2,1)S(1)} %shard_map.80.refs_0_), channel_id=1, source_target_pairs={{8,0},{9,1},{10,2},{11,3},{12,4},{13,5},{14,6},{15,7},{0,8},{1,9},... | collective-permute-start | bytes 196616 | tf_op jit(solution)/shard_map/ppermute | solution.py:35
  58.7 7.0 %collective-permute-start.24 = (bf16[64,512]{1,0:T(8,128)(2,1)S(1)}, bf16[64,512]{1,0:T(8,128)(2,1)S(1)}, u32[]{:S(2)}, u32[]{:S(2)}) collective-permute-start(bf16[64,512]{1,0:T(8,128)(2,1)S(1)} %shard_map.80.refs_0_), channel_id=1, source_target_pairs={{12,0},{13,1},{14,2},{15,3},{0,4},{1,5},{2,6},{3,7},{4,8},{5,9},{6... | collective-permute-start | bytes 196616 | tf_op jit(solution)/shard_map/ppermute | solution.py:35
  59.9 14.1 %collective-permute-start.17 = (bf16[256,512]{1,0:T(8,128)(2,1)S(1)}, bf16[256,512]{1,0:T(8,128)(2,1)S(1)}, u32[]{:S(2)}, u32[]{:S(2)}) collective-permute-start(bf16[256,512]{1,0:T(8,128)(2,1)S(1)} %shard_map.72.rest_0_), channel_id=1, source_target_pairs={{0,16},{16,0},{1,17},{17,1},{2,18},{18,2},{3,19},{19,3},{4,20},{20... | collective-permute-start | bytes 786440 | tf_op jit(solution)/shard_map/ppermute | solution.py:327
  61.5 10.0 %collective-permute-start.18 = (bf16[128,512]{1,0:T(8,128)(2,1)S(1)}, bf16[128,512]{1,0:T(8,128)(2,1)S(1)}, u32[]{:S(2)}, u32[]{:S(2)}) collective-permute-start(bf16[128,512]{1,0:T(8,128)(2,1)S(1)} %get-tuple-element.37.rest_0_), channel_id=1, source_target_pairs={{0,16},{16,0},{1,17},{17,1},{2,18},{18,2},{3,19},{19,3},{4,20},{20... | collective-permute-start | bytes 393224 | tf_op jit(solution)/shard_map/ppermute | solution.py:341
  65.8 8.1 %collective-permute-start.25 = (bf16[4,64,512]{2,1,0:T(8,128)(2,1)S(1)}, bf16[4,64,512]{2,1,0:T(8,128)(2,1)S(1)}, u32[]{:S(2)}, u32[]{:S(2)}) collective-permute-start(bf16[4,64,512]{2,1,0:T(8,128)(2,1)S(1)} %shard_map.81.rest_0_), channel_id=1, source_target_pairs={{2,0},{3,1},{0,2},{1,3},{6,4},{7,5},{4,6},{5,7},{10,8},{11,9},{8,1... | collective-permute-start | bytes 786440 | tf_op jit(solution)/shard_map/ppermute | solution.py:35
  69.9 9.3 %collective-permute-start.16 = (bf16[256,512]{1,0:T(8,128)(2,1)S(1)}, bf16[256,512]{1,0:T(8,128)(2,1)S(1)}, u32[]{:S(2)}, u32[]{:S(2)}) collective-permute-start(bf16[256,512]{1,0:T(8,128)(2,1)S(1)} %shard_map.74), channel_id=1, source_target_pairs={{0,16},{16,0},{1,17},{17,1},{2,18},{18,2},{3,19},{19,3},{4,20},{20... | collective-permute-start | bytes 786440 | tf_op jit(solution)/shard_map/ppermute | solution.py:327
  73.0 11.8 %collective-permute-start.28 = (bf16[256,512]{1,0:T(8,128)(2,1)S(1)}, bf16[256,512]{1,0:T(8,128)(2,1)S(1)}, u32[]{:S(2)}, u32[]{:S(2)}) collective-permute-start(bf16[256,512]{1,0:T(8,128)(2,1)S(1)} %shard_map.82), channel_id=1, source_target_pairs={{0,16},{16,0},{1,17},{17,1},{2,18},{18,2},{3,19},{19,3},{4,20},{20... | collective-permute-start | bytes 786440 | tf_op jit(solution)/shard_map/ppermute | solution.py:327
  73.6 13.1 %collective-permute-start.26 = (bf16[4,64,512]{2,1,0:T(8,128)(2,1)S(1)}, bf16[4,64,512]{2,1,0:T(8,128)(2,1)S(1)}, u32[]{:S(2)}, u32[]{:S(2)}) collective-permute-start(bf16[4,64,512]{2,1,0:T(8,128)(2,1)S(1)} %shard_map.81.rest_0_), channel_id=1, source_target_pairs={{1,0},{0,1},{3,2},{2,3},{5,4},{4,5},{7,6},{6,7},{9,8},{8,9},{11,10... | collective-permute-start | bytes 786440 | tf_op jit(solution)/shard_map/ppermute | solution.py:35
  73.9 12.8 %collective-permute-start.27 = (bf16[4,64,512]{2,1,0:T(8,128)(2,1)S(1)}, bf16[4,64,512]{2,1,0:T(8,128)(2,1)S(1)}, u32[]{:S(2)}, u32[]{:S(2)}) collective-permute-start(bf16[4,64,512]{2,1,0:T(8,128)(2,1)S(1)} %collective-permute-done.25.rest_1_), channel_id=1, source_target_pairs={{1,0},{0,1},{3,2},{2,3},{5,4},{4,5},{7,6},{6,7},{9,8},{8,9},{11,10... | collective-permute-start | bytes 786440 | tf_op jit(solution)/shard_map/ppermute | solution.py:35
  75.7 15.1 %collective-permute-start.20 = (bf16[256,512]{1,0:T(8,128)(2,1)S(1)}, bf16[256,512]{1,0:T(8,128)(2,1)S(1)}, u32[]{:S(2)}, u32[]{:S(2)}) collective-permute-start(bf16[256,512]{1,0:T(8,128)(2,1)S(1)} %shard_map.79), channel_id=1, source_target_pairs={{0,16},{16,0},{1,17},{17,1},{2,18},{18,2},{3,19},{19,3},{4,20},{20... | collective-permute-start | bytes 786440 | tf_op jit(solution)/shard_map/ppermute | solution.py:327
  80.7 11.9 %collective-permute-start.19 = (bf16[128,512]{1,0:T(8,128)(2,1)S(1)}, bf16[128,512]{1,0:T(8,128)(2,1)S(1)}, u32[]{:S(2)}, u32[]{:S(2)}) collective-permute-start(bf16[128,512]{1,0:T(8,128)(2,1)S(1)} %shard_map.78), channel_id=1, source_target_pairs={{0,16},{16,0},{1,17},{17,1},{2,18},{18,2},{3,19},{19,3},{4,20},{20... | collective-permute-start | bytes 393224 | tf_op jit(solution)/shard_map/ppermute | solution.py:327

commit v3 on v0

v3 whole, which is shorter than its diff:
```python
import functools
import jax
import jax.numpy as jnp
from jax import lax
from jax.experimental import pallas as pl
from jax.experimental.pallas import tpu as pltpu
from jax.sharding import PartitionSpec as P

VMEM = pl.BlockSpec(memory_space=pltpu.VMEM)
SMEM = pl.BlockSpec(memory_space=pltpu.SMEM)
ANY = pl.BlockSpec(memory_space=pl.ANY)
F32 = jnp.float32
BF16 = jnp.bfloat16
MIB = 1024 * 1024
LANES = 128


def bits_of(n):
    bits = [1 << i for i in reversed(range(n.bit_length() - 1))]
    assert n == 1 << len(bits)
    core = bits[-1:]
    rest = bits[:-1]
    cut = (len(rest) + 1) // 2
    return rest[:cut], rest[cut:], core


def swap(block, mask, n):
    return lax.ppermute(block, "train", [(d ^ mask, d) for d in range(n)])


def spread(block, bits, n, start=0):
    return spread_on([(start, block)], bits, n)


def spread_on(held, bits, n):
    for bit in bits:
        held += [(mask ^ bit, swap(b, bit, n)) for mask, b in held]
    return sorted(held, key=lambda entry: entry[0])


def masks_of(bits):
    masks = [0]
    for bit in bits:
        masks += [mask ^ bit for mask in masks]
    return sorted(masks)


def ahead(k, n):
    return [(d, (d + k) % n) for d in range(n)]


def aligned(index, rows):
    return pl.ds(pl.multiple_of(index * rows, rows), rows)


def call(kernel, outs, operands, specs, mib=8, flops=0, moved=0, scratch=(), aliases=None, out_specs=None):
    several = isinstance(outs, list)
    out_specs = out_specs or [VMEM] * (len(outs) if several else 1)
    return pl.pallas_call(
        kernel,
        out_shape=outs,
        in_specs=specs,
        out_specs=out_specs if several else out_specs[0],
        scratch_shapes=list(scratch),
        input_output_aliases=aliases or {},
        compiler_params=pltpu.CompilerParams(vmem_limit_bytes=mib * MIB),
        cost_estimate=pl.CostEstimate(flops=flops, bytes_accessed=moved, transcendentals=0),
    )(*operands)


def shape(dims, dtype=BF16):
    return jax.ShapeDtypeStruct(dims, dtype)


def table_of(bucket_weight, rows):
    count = bucket_weight.shape[1]
    at = lax.broadcasted_iota(jnp.int32, (rows, count), 0)
    lane = lax.broadcasted_iota(jnp.int32, (rows, count), 1)
    column = jnp.sum(jnp.where(at == lane, bucket_weight, 0.0), axis=1, keepdims=True)
    return jnp.broadcast_to(column, (rows, LANES))


def weights_of(bucket, table):
    onehot = lax.broadcasted_iota(jnp.int32, (table.shape[0], bucket.shape[1]), 0) == bucket
    return lax.dot_general(
        onehot.astype(F32), table, (((0,), (0,)), ((), ())),
        precision=lax.Precision.HIGHEST, preferred_element_type=F32,
    )


def weights_kernel(table_rows, bucket, bucket_weight, out):
    out[...] = weights_of(bucket[...], table_of(bucket_weight[...], table_rows))


def start_kernel(steps, test_feat, kernel_inv, train, bucket_weight, own, *rest):
    batches, (pair, held, below, sems) = rest[:-4], rest[-4:]
    moves = [(test_feat.at[0], pair.at[0], own.at[0]), (kernel_inv.at[0], pair.at[1], own.at[1])]
    count = below.shape[0]
    first = 0
    for i, batch in enumerate(batches):
        step = (batch.shape[0] - (0 if i else count)) // steps
        for i in range(steps):
            span = pl.ds(first + i * step, step)
            moves.append((train.at[span], held.at[span], batch.at[pl.ds(i * step, step)]))
        first += steps * step
    ins = [
        pltpu.make_async_copy(source, middle, sems.at[0, i])
        for i, (source, middle, _) in enumerate(moves)
    ]
    outs = [
        pltpu.make_async_copy(middle, target, sems.at[1, i])
        for i, (_, middle, target) in enumerate(moves)
    ]
    for copy in ins:
        copy.start()
    if batches:
        left = table_of(bucket_weight[...], count)
        for part in range(3):
            term = left.astype(BF16)
            below[:, part * LANES : (part + 1) * LANES] = term
            left = left - term.astype(F32)
        below[:, 3 * LANES :] = jnp.zeros((count, below.shape[1] - 3 * LANES), BF16)
        span = pl.ds(batches[0].shape[0] - count, count)
        outs.append(pltpu.make_async_copy(below, batches[0].at[span], sems.at[1, len(moves)]))
        outs[-1].start()
    for inward, outward in zip(ins, outs):
        inward.wait()
        outward.start()
    for copy in outs:
        copy.wait()


def choose(ensemble, k, outer, ckpt, order, test):
    width = order.shape[0] * order.shape[2] // ensemble
    first = lax.rem(ckpt[0] + k, ensemble) * width
    wanted = lax.broadcasted_iota(jnp.int32, (width, order.shape[2]), 0) + first
    onehot = (wanted == order[outer]).astype(BF16)
    return jnp.dot(onehot, test[...], preferred_element_type=F32).astype(BF16)


def unpack(masks, me, blocks, test, inverse):
    rows = blocks[0].shape[1]
    for mask, block in zip(masks, blocks):
        at = lax.bitwise_xor(me[0], mask)
        test[aligned(lax.rem(at, len(masks)), rows), :] = block[0]
        inverse[aligned(at, rows), :] = block[1]
    return lax.div(lax.bitwise_xor(me[0], masks[0]), len(masks))


def part_kernel(ensemble, masks, ckpt, me, order, *rest):
    blocks = rest[: len(masks)]
    inverse, chosen, test = rest[-3:]
    outer = unpack(masks, me, blocks, test, inverse)
    width = chosen.shape[0] // ensemble
    for j in range(ensemble):
        rows = pl.ds(j * width, width)
        picked = choose(ensemble, j, outer, ckpt, order, test)
        chosen[rows, :] = picked if masks[0] == 0 else chosen[rows, :] + picked


def transformed(inverse, chosen):
    return lax.dot_general(
        inverse[...], chosen, (((1,), (1,)), ((), ())), preferred_element_type=F32
    ).astype(BF16)


def send_transform_kernel(ensemble, masks, ckpt, me, order, *rest):
    blocks = rest[: len(masks)]
    inverse, chosen, test, out = rest[-4:]
    outer = unpack(masks, me, blocks, test, inverse)
    width = chosen.shape[0] // ensemble
    for j in range(1, ensemble):
        picked = choose(ensemble, j, outer, ckpt, order, test)
        out[j - 1] = transformed(inverse, chosen[pl.ds(j * width, width), :] + picked)


def own_transform_kernel(ensemble, masks, ckpt, me, order, inverse, chosen, test, *rest):
    outer = lax.div(lax.bitwise_xor(me[0], masks[0]), len(masks))
    picked = choose(ensemble, 0, outer, ckpt, order, test)
    rest[-1][...] = transformed(inverse, chosen[: picked.shape[0], :] + picked)


def scaled(train, matrix, weight):
    tile = jnp.dot(train, matrix, preferred_element_type=F32)
    wide = jnp.concatenate([weight] * (tile.shape[1] // weight.shape[1]), axis=1)
    return (tile * wide).astype(BF16)


def send_kernel(first, length, j, train, matrices, weight, *rest):
    rows = pl.ds(first, length)
    rest[-1][:length, :] = scaled(train[rows, :], matrices[j], weight[rows, :])


def first_kernel(first, length, me, train, matrices, weight, out):
    send_kernel(first, length, 0, train, matrices, weight, out)
    out[length:, :] = matrices[0, aligned(me[0], out.shape[0] - length), :]


def tail_kernel(first, block, *rest):
    rest[-1][...] = block[first:, :]


def relay_kernel(block, *rest):
    rest[-1][...] = block[...]


def stack_kernel(count, *refs):
    for i, ref in enumerate(refs[:count]):
        refs[-1][i] = ref[...]


def store(out, first, at, buffer, sems, tile):
    rows = tile.shape[0] // len(sems)
    copies = []
    for i, sem in enumerate(sems):
        span = pl.ds(at + i * rows, rows)
        buffer[span, :] = tile[i * rows : (i + 1) * rows]
        copies.append(
            pltpu.make_async_copy(buffer.at[span], out.at[pl.ds(first + at + i * rows, rows)], sem)
        )
        copies[-1].start()
    return copies


def sums(ensemble, first, at, train, matrix, weight, got, out, buffer, sems, length):
    rows = pl.ds(first, length)
    total = scaled(train[rows, :], matrix[...], weight[rows, :]).astype(F32)
    for other in got:
        total = total + other[:length, :].astype(F32)
    return store(out, first - at, at, buffer, sems, total / ensemble)


def sum_kernel(ensemble, first, lengths, train, matrix, weight, *rest):
    out, buffer, sems = rest[-3:]
    copies, at, others = [], 0, ensemble - 1
    for i, length in enumerate(lengths):
        got = rest[i * others : (i + 1) * others]
        two = [sems.at[2 * i], sems.at[2 * i + 1]]
        copies += sums(
            ensemble, first + at, at, train, matrix, weight, got, out, buffer, two, length
        )
        at += length
    for copy in copies:
        copy.wait()


def both_kernel(ensemble, masks, outers, batches, me, train, matrix, weight, bucket, *rest):
    features, pieces = rest[:batches], rest[batches : batches + len(masks)]
    out, matrix2, weight2, buffer, sems = rest[-5:]
    count = buffer.shape[0]
    extra = sum(batch.shape[0] for batch in features) - count
    table = jnp.zeros((extra, LANES), F32)
    for part in range(3):
        lanes = pl.ds(part * LANES, LANES)
        table = table + features[0][features[0].shape[0] - extra :, lanes].astype(F32)
    weight2[...] = weights_of(bucket[:, :count], table)
    rows = pieces[0].shape[1]
    for mask, piece in zip(masks, pieces):
        for i, outer in enumerate(outers):
            at = lax.bitwise_xor(me[0], mask ^ outer)
            matrix2[aligned(at, rows), :] = piece[i]
    copies, first = [], 0
    for i, batch in enumerate(features):
        each = batch.shape[0] - (0 if i else extra)
        rows = pl.ds(first, each)
        total = scaled(train[rows, :], matrix[...], weight[rows, :]).astype(F32)
        total = total + scaled(batch[:each, :], matrix2[...], weight2[rows, :]).astype(F32)
        two = [sems.at[2 * i], sems.at[2 * i + 1]]
        copies += store(out, 0, first, buffer, two, total / ensemble)
        first += each
    for copy in copies:
        copy.wait()


def shards(train_feat, test_feat, kernel_inv, bucket_weight, bucket, test_order):
    ensemble, n = lax.axis_size("ckpt"), lax.axis_size("train")
    outer_bits, inner_bits, core_bits = bits_of(n)
    outers = masks_of(outer_bits)
    inners = masks_of(inner_bits + core_bits)
    train = train_feat[0]
    rows, size = train.shape
    count = test_order.shape[0]
    width = count // ensemble
    share = size // n
    unit = rows // 32
    paired = ensemble == 2
    batches = [6, 6] if paired else []
    featured = sum(batches)
    parts = [1, 10, 5, 4] if paired else [16, 16]
    flying = 2
    table_rows = -(-bucket_weight.shape[1] // 16) * 16

    ckpt = lax.axis_index("ckpt").astype(jnp.int32).reshape(1)
    me = lax.axis_index("train").astype(jnp.int32).reshape(1)
    order = test_order.reshape(len(outers), 1, count // len(outers))
    bucket = bucket.reshape(1, rows)

    sent = [shape((part * unit + (0 if i else table_rows), size)) for i, part in enumerate(batches)]
    steps = 2
    own, *features = call(
        functools.partial(start_kernel, steps),
        [shape((2, test_feat.shape[1], size)), *sent],
        (test_feat, kernel_inv, train, bucket_weight), [ANY] * 3 + [VMEM],
        out_specs=[ANY] * (1 + len(sent)), mib=60,
        scratch=[
            pltpu.VMEM((2, test_feat.shape[1], size), BF16),
            pltpu.VMEM((max(featured, 1) * unit, size), BF16),
            pltpu.VMEM((table_rows, size), BF16),
            pltpu.SemaphoreType.DMA((2, 3 + steps * len(sent))),
        ],
    )
    features = [lax.ppermute(batch, "ckpt", ahead(1, ensemble)) for batch in features]

    groups = []
    for mask, block in sorted(spread(own, outer_bits, n), key=lambda e: e[0]):
        held = [(mask, block)]
        inner = spread(block, inner_bits, n, mask)[1:]
        held = spread_on(held + inner, core_bits, n)
        groups.append(([m for m, _ in held], [b for _, b in held]))
    weight = call(
        functools.partial(weights_kernel, table_rows), shape((rows, LANES), F32),
        (bucket, bucket_weight), [VMEM] * 2,
    )

    half = 2 * size * size * width
    state = []
    for masks, blocks in groups[:-1]:
        operands = [ckpt, me, order, *blocks, *state]
        after = features[:1] if not state else []
        state = call(
            functools.partial(part_kernel, ensemble, masks),
            [shape((size, size)), shape((count, size))],
            [*operands, *after], [SMEM] * 2 + [VMEM] * (len(operands) - 2) + [ANY] * len(after),
            scratch=[pltpu.VMEM((count // len(outers), size), BF16)],
            aliases={len(operands) - 2: 0, len(operands) - 1: 1} if state else None,
            flops=4 * half, moved=4 * size * size,
        )
    masks, blocks = groups[-1]
    inverse, chosen, test, matrices = call(
        functools.partial(send_transform_kernel, ensemble, masks),
        [
            shape((size, size)), shape((count, size)), shape((count // len(outers), size)),
            shape((ensemble - 1, size, width)),
        ],
        [ckpt, me, order, *blocks, *state],
        [SMEM] * 2 + [VMEM] * (3 + len(blocks)),
        aliases={3 + len(blocks): 0, 4 + len(blocks): 1},
        flops=3 * half, moved=4 * size * size, mib=12,
    )

    def send(first, part, after):
        got = []
        for k in range(1, ensemble):
            tile = call(
                functools.partial(send_kernel, first * unit, part * unit, k - 1),
                shape((part * unit, width)),
                (train, matrices, weight, *after), [VMEM] * 3 + [ANY] * len(after),
            )
            after = [tile]
            got.append(lax.ppermute(tile, "ckpt", ahead(k, ensemble)))
        return got, after

    starts = [featured + sum(parts[:q]) for q in range(len(parts))]
    received, after = [], []
    if paired:
        tile = call(
            functools.partial(first_kernel, starts[0] * unit, parts[0] * unit),
            shape((parts[0] * unit + share, width)),
            (me, train, matrices, weight), [SMEM] + [VMEM] * 3,
        )
        received.append([lax.ppermute(tile, "ckpt", ahead(1, ensemble))])
        after = [tile]
    for q in range(len(received), min(flying, len(parts))):
        got, after = send(starts[q], parts[q], after)
        received.append(got)
    if paired:
        piece = call(
            functools.partial(tail_kernel, parts[0] * unit), shape((share, width)),
            (*received[0], *after), [VMEM, ANY],
        )
        after = [piece]

    matrix = call(
        functools.partial(own_transform_kernel, ensemble, masks),
        shape((size, width)), (ckpt, me, order, inverse, chosen, test, *after, *features[1:]),
        [SMEM] * 2 + [VMEM] * 4 + [ANY] * (len(after) + len(features[1:])), flops=3 * half, mib=12,
    )
    if paired:
        got, after = send(starts[flying], parts[flying], after)
        received.append(got)
        column = call(
            functools.partial(stack_kernel, len(outers)), shape((len(outers), share, width)),
            [piece] + [swap(piece, mask, n) for mask in outers[1:]] + [matrix],
            [VMEM] * len(outers) + [ANY],
        )
        for q in range(flying + 1, len(parts)):
            got, after = send(starts[q], parts[q], [column])
            received.append(got)
        held = [(0, column)]
        for bit in inner_bits:
            held += [(mask ^ bit, swap(b, bit, n)) for mask, b in held]
        held = held[:1] + [
            (mask, call(relay_kernel, shape(b.shape), (b, *received[1]), [VMEM, ANY]))
            for mask, b in held[1:]
        ]
        for bit in core_bits:
            held += [(mask ^ bit, swap(b, bit, n)) for mask, b in held]
        pieces = [b for _, b in sorted(held, key=lambda entry: entry[0])]

    out = None

    def put(kernel, part, copies, operands, specs, scratch=()):
        held = [] if out is None else [out]
        return call(
            kernel, shape((rows, width), F32),
            (*operands, *held), specs + [ANY] * len(held),
            out_specs=[ANY],
            scratch=[
                *scratch, pltpu.VMEM((part * unit, width), F32), pltpu.SemaphoreType.DMA((copies,)),
            ],
            aliases={len(operands): 0} if held else None, mib=24,
        )

    together = [[0, 1], [], [2, 3]] if paired else [[q] for q in range(len(parts))]
    for chunks in together:
        if chunks:
            part = sum(parts[q] for q in chunks)
            got = [tile for q in chunks for tile in received[q]]
            lengths = [parts[q] * unit for q in chunks]
            out = put(
                functools.partial(sum_kernel, ensemble, starts[chunks[0]] * unit, lengths),
                part, 2 * len(chunks), (train, matrix, weight, *got), [VMEM] * (3 + len(got)),
            )
        else:
            out = put(
                functools.partial(both_kernel, ensemble, inners, outers, len(batches)),
                featured, 2 * len(batches),
                (me, train, matrix, weight, bucket, *features, *pieces),
                [SMEM] + [VMEM] * (4 + len(features) + len(pieces)),
                scratch=[
                    pltpu.VMEM((size, width), BF16), pltpu.VMEM((featured * unit, LANES), F32)
                ],
            )
    return out


def solution(mesh):
    return jax.shard_map(
        shards,
        mesh=mesh,
        in_specs=(
            P("ckpt", "train", None),
            P("ckpt", "train", None),
            P("ckpt", "train", None),
            P("ckpt", None),
            P("train"),
            P(),
        ),
        out_specs=P("train", "ckpt"),
        check_vma=False,
    )
```

time: 181 us -> 81 us (0.45)
  waiting for transfers between devices: 140 us -> 34.3 us
  starting transfers between devices: 0.11 us -> 25.8 us
  Pallas kernels: 0 us -> 18.8 us
  between operations: 13.2 us -> 0.22 us
  matrix products: 12.1 us -> 0 us
  local copies, waits for them, and re-layouts: 11.9 us -> 1.55 us
  other arithmetic: 4.09 us -> 0 us
    all_gather x2 -> x0, waiting for transfers between devices: 85.9 us -> none  [the longest x1 46.3 us: shards(): full_inverse = lax.all_gather(kernel_inv, 'train', axis=1, tiled=True)]
    reduce_scatter x1 -> x0, waiting for transfers between devices: 53.2 us -> none  [shards(): lax.psum_scatter(total.astype(jnp.bfloat16), 'ckpt', scatter_dimension=1,...]
    ppermute x0 -> x27, waiting for transfers between devices: none -> 34.3 us  [the longest x21 27.9 us: swap(): return lax.ppermute(block, 'train', [(d ^ mask, d) for d in range(n)])]
    ppermute x0 -> x27, starting transfers between devices: none -> 25.8 us  [the longest x21 19.2 us: swap(): return lax.ppermute(block, 'train', [(d ^ mask, d) for d in range(n)])]
    pallas_call x0 -> x17, Pallas kernels: none -> 18.8 us  [call(): pl.pallas_call(kernel, out_shape=outs, in_specs=specs, out_specs=out_spec...]
    dot_general x3 -> x0, matrix products: 12.1 us -> none  [the longest x1 8.38 us: shards(): jnp.dot(train_feat[0], ordered[0].T, preferred_element_type=jnp.float32)]
    scatter x1 -> x0, local copies, waits for them, and re-layouts: 6.58 us -> none  [shards(): ordered = jnp.zeros_like(stored).at[:, test_order, :].set(stored)]
    div x1 -> x0, local copies, waits for them, and re-layouts: 5.34 us -> none  [shards(): return summed / ensemble]
  transfers between devices with their start and end apart: 3 -> 27, of which waited for: 3 -> 11; matrix products, arithmetic and copies ran while one was open for 0% -> 0% of each run, Pallas kernels for 0% -> 17%
where the time goes in v3:
time: 81 us; the launch traced here: 80.7 us
  waiting for transfers between devices  34.3 us (42%)
  starting transfers between devices  25.8 us (32%)
  Pallas kernels  18.8 us (23%)
  local copies, waits for them, and re-layouts  1.55 us (2%)
    ppermute x21, waiting for transfers between devices, swap(): return lax.ppermute(block, 'train', [(d ^ mask, d) for d in range(n)])  27.9 us
    ppermute x21, starting transfers between devices, swap(): return lax.ppermute(block, 'train', [(d ^ mask, d) for d in range(n)])  19.2 us
    pallas_call x17, Pallas kernels, call(): pl.pallas_call(kernel, out_shape=outs, in_specs=specs, out_specs=out_spec...  18.8 us
    ppermute x2, starting transfers between devices, shards(): lax.ppermute(batch, 'ckpt', ahead(1, ensemble))  3.6 us
    ppermute x1, waiting for transfers between devices, shards(): received.append([lax.ppermute(tile, 'ckpt', ahead(1, ensemble))])  3.41 us
    ppermute x3, waiting for transfers between devices, send(): got.append(lax.ppermute(tile, 'ckpt', ahead(k, ensemble)))  3.04 us
    ppermute x3, starting transfers between devices, send(): got.append(lax.ppermute(tile, 'ckpt', ahead(k, ensemble)))  2.44 us
  transfers between devices with their start and end apart: 27, of which 11 were waited for; matrix products, arithmetic and copies ran while one was open for 0% of the time, Pallas kernels for 17%

profile of v3, /device:TPU:0, one launch (start us, length us, event | category | flops | bytes accessed | tf_op | source)
XLA Modules:
  0.0 80.7 jit_solution(12687169991956537887)
XLA Ops:
  0.0 3.1 %shard_map.64 = (bf16[2,64,1024]{2,1,0:T(8,128)(2,1)}, bf16[400,1024]{1,0:T(8,128)(2,1)}, bf16[384,1024]{1,0:T(8,128)(2,1)}) custom-call(bf16[1,64,1024]{2,1,0:T(8,128)(2,1)} %test_feat.1, bf16[1,64,1024]{2,1,0:T(8,128)(2,1)} %kernel_inv.1, bf16[2048,1024]{1,0:T(8,128)(2,1)} %bitcast.5, f32[1,16]{1,0:T(1,128)} %bucket_weight.3), custom_call_target="tpu_custom_call" | custom-call | tf_op jit(solution)/shard_map/pallas_call | solution.py:59
  3.1 3.0 %collective-permute-start.15 = (bf16[400,1024]{1,0:T(8,128)(2,1)}, bf16[400,1024]{1,0:T(8,128)(2,1)S(1)}, u32[]{:S(2)}, u32[]{:S(2)}) collective-permute-start(bf16[400,1024]{1,0:T(8,128)(2,1)} %get-tuple-element.19), channel_id=1, source_target_pairs={{0,16},{16,0},{1,17},{17,1},{2,18},{18,2},{3,19},{19,3},{4,20},{20... | collective-permute-start | bytes 2457608 | tf_op jit(solution)/shard_map/ppermute | solution.py:312
  6.1 2.6 %collective-permute-start = (bf16[2,64,1024]{2,1,0:T(8,128)(2,1)}, bf16[2,64,1024]{2,1,0:T(8,128)(2,1)S(1)}, u32[]{:S(2)}, u32[]{:S(2)}) collective-permute-start(bf16[2,64,1024]{2,1,0:T(8,128)(2,1)} %get-tuple-element.18.rest_0_), channel_id=1, source_target_pairs={{8,0},{9,1},{10,2},{11,3},{12,4},{13,5},{14,6},{15,7},{0,8},{1,9},... | collective-permute-start | bytes 786440 | tf_op jit(solution)/shard_map/ppermute | solution.py:28
  8.7 1.6 %collective-permute-start.8 = (bf16[2,64,1024]{2,1,0:T(8,128)(2,1)}, bf16[2,64,1024]{2,1,0:T(8,128)(2,1)S(1)}, u32[]{:S(2)}, u32[]{:S(2)}) collective-permute-start(bf16[2,64,1024]{2,1,0:T(8,128)(2,1)} %get-tuple-element.18.rest_0_), channel_id=1, source_target_pairs={{4,0},{5,1},{6,2},{7,3},{0,4},{1,5},{2,6},{3,7},{12,8},{13,9},{14,... | collective-permute-start | bytes 786440 | tf_op jit(solution)/shard_map/ppermute | solution.py:28
  10.3 1.5 %collective-permute-start.13 = (bf16[2,64,1024]{2,1,0:T(8,128)(2,1)}, bf16[2,64,1024]{2,1,0:T(8,128)(2,1)S(1)}, u32[]{:S(2)}, u32[]{:S(2)}) collective-permute-start(bf16[2,64,1024]{2,1,0:T(8,128)(2,1)} %get-tuple-element.18.rest_0_), channel_id=1, source_target_pairs={{2,0},{3,1},{0,2},{1,3},{6,4},{7,5},{4,6},{5,7},{10,8},{11,9},{8,1... | collective-permute-start | bytes 786440 | tf_op jit(solution)/shard_map/ppermute | solution.py:28
  11.8 8.9 %collective-permute-done.rest_0_ = bf16[2,64,1024]{2,1,0:T(8,128)(2,1)S(1)} collective-permute-done((bf16[2,64,1024]{2,1,0:T(8,128)(2,1)}, bf16[2,64,1024]{2,1,0:T(8,128)(2,1)S(1)}, u32[]{:S(2)}, u32[]{:S(2)}) %collective-permute-start) | collective-permute-done | bytes 262176 | tf_op jit(solution)/shard_map/ppermute | solution.py:28
  20.7 0.7 collective-permute-start.1
  21.4 1.5 %collective-permute-start.10 = (bf16[2,64,1024]{2,1,0:T(8,128)(2,1)S(1)}, bf16[2,64,1024]{2,1,0:T(8,128)(2,1)S(1)}, u32[]{:S(2)}, u32[]{:S(2)}) collective-permute-start(bf16[2,64,1024]{2,1,0:T(8,128)(2,1)S(1)} %collective-permute-done.8.rest_0_), channel_id=1, source_target_pairs={{2,0},{3,1},{0,2},{1,3},{6,4},{7,5},{4,6},{5,7},{10,8},{11,9},{8,1... | collective-permute-start | bytes 786440 | tf_op jit(solution)/shard_map/ppermute | solution.py:28
  23.0 1.1 %shard_map.69.weight = f32[2048,128]{1,0:T(8,128)S(1)} custom-call(s32[1,2048]{1,0:T(1,128)S(1)} %bitcast.13, f32[1,16]{1,0:T(1,128)S(1)} %copy-done.2), custom_call_target="tpu_custom_call" | custom-call | tf_op jit(solution)/shard_map/pallas_call | solution.py:59
  24.0 0.6 collective-permute-start.17
  24.6 3.3 %collective-permute-done.1.rest_0_ = bf16[2,64,1024]{2,1,0:T(8,128)(2,1)S(1)} collective-permute-done((bf16[2,64,1024]{2,1,0:T(8,128)(2,1)S(1)}, bf16[2,64,1024]{2,1,0:T(8,128)(2,1)S(1)}, u32[]{:S(2)}, u32[]{:S(2)}) %collective-permute-start.1) | collective-permute-done | bytes 262176 | tf_op jit(solution)/shard_map/ppermute | solution.py:28
  27.9 1.5 %collective-permute-start.6 = (bf16[2,64,1024]{2,1,0:T(8,128)(2,1)S(1)}, bf16[2,64,1024]{2,1,0:T(8,128)(2,1)S(1)}, u32[]{:S(2)}, u32[]{:S(2)}) collective-permute-start(bf16[2,64,1024]{2,1,0:T(8,128)(2,1)S(1)} %collective-permute-done.rest_0_), channel_id=1, source_target_pairs={{2,0},{3,1},{0,2},{1,3},{6,4},{7,5},{4,6},{5,7},{10,8},{11,9},{8,1... | collective-permute-start | bytes 786440 | tf_op jit(solution)/shard_map/ppermute | solution.py:28
  29.4 0.3 collective-permute-done.10.rest_2_
  29.7 1.5 %collective-permute-start.3 = (bf16[2,64,1024]{2,1,0:T(8,128)(2,1)S(1)}, bf16[2,64,1024]{2,1,0:T(8,128)(2,1)S(1)}, u32[]{:S(2)}, u32[]{:S(2)}) collective-permute-start(bf16[2,64,1024]{2,1,0:T(8,128)(2,1)S(1)} %collective-permute-done.1.rest_0_), channel_id=1, source_target_pairs={{2,0},{3,1},{0,2},{1,3},{6,4},{7,5},{4,6},{5,7},{10,8},{11,9},{8,1... | collective-permute-start | bytes 786440 | tf_op jit(solution)/shard_map/ppermute | solution.py:28
  31.3 0.2 collective-permute-start.11
  31.5 0.9 %copy-done.3 = bf16[2,64,1024]{2,1,0:T(8,128)(2,1)S(1)} copy-done((bf16[2,64,1024]{2,1,0:T(8,128)(2,1)S(1)}, bf16[2,64,1024]{2,1,0:T(8,128)(2,1)}, u32[]{:S(2)}) %copy-start.3) | copy-done | bytes 262168
  32.5 0.8 %shard_map.65 = (bf16[1024,1024]{1,0:T(8,128)(2,1)S(1)}, bf16[1024,1024]{1,0:T(8,128)(2,1)S(1)}) custom-call(s32[1]{0:T(128)} %bitcast.1.ckpt, s32[1]{0:T(128)} %bitcast.2.me, s32[4,1,256]{2,1,0:T(1,128)S(1)} %bitcast.15, bf16[2,64,1024]{2,1,0:T(8,128)(2,1)S(1)} %copy-done.3, bf16[2,64,1024]{2,1,0:T(8,128)(2,1)S(1)} %collective-permute-done.12.rest_1_, ...), custom_call_target="tpu_custom_call" | custom-call | flops 4294967296 | bytes 4194304 | tf_op jit(solution)/shard_map/pallas_call | solution.py:59
  33.3 3.8 %collective-permute-done.6.rest_2_ = bf16[2,64,1024]{2,1,0:T(8,128)(2,1)S(1)} collective-permute-done((bf16[2,64,1024]{2,1,0:T(8,128)(2,1)S(1)}, bf16[2,64,1024]{2,1,0:T(8,128)(2,1)S(1)}, u32[]{:S(2)}, u32[]{:S(2)}) %collective-permute-start.6) | collective-permute-done | bytes 262176 | tf_op jit(solution)/shard_map/ppermute | solution.py:28
  37.1 0.5 collective-permute-start.2
  37.6 3.0 %collective-permute-done.3.rest_2_ = bf16[2,64,1024]{2,1,0:T(8,128)(2,1)S(1)} collective-permute-done((bf16[2,64,1024]{2,1,0:T(8,128)(2,1)S(1)}, bf16[2,64,1024]{2,1,0:T(8,128)(2,1)S(1)}, u32[]{:S(2)}, u32[]{:S(2)}) %collective-permute-start.3) | collective-permute-done | bytes 262176 | tf_op jit(solution)/shard_map/ppermute | solution.py:28
  40.6 0.5 collective-permute-start.4
  41.1 0.8 %shard_map.66 = (bf16[1024,1024]{1,0:T(8,128)(2,1)S(1)}, bf16[1024,1024]{1,0:T(8,128)(2,1)S(1)}) custom-call(s32[1]{0:T(128)} %bitcast.1.ckpt, s32[1]{0:T(128)} %bitcast.2.me, s32[4,1,256]{2,1,0:T(1,128)S(1)} %bitcast.16, bf16[2,64,1024]{2,1,0:T(8,128)(2,1)S(1)} %collective-permute-done.8.rest_0_, ...), custom_call_target="tpu_custom_call", output_to_operand_aliasing={{0}: (7, {}), {1}: (8, {})} | custom-call | flops 4294967296 | bytes 4194304 | tf_op jit(solution)/shard_map/pallas_call | solution.py:59
  42.0 0.2 collective-permute-done.7.rest_3_
  42.1 0.8 %shard_map.67 = (bf16[1024,1024]{1,0:T(8,128)(2,1)S(1)}, bf16[1024,1024]{1,0:T(8,128)(2,1)S(1)}) custom-call(s32[1]{0:T(128)} %bitcast.1.ckpt, s32[1]{0:T(128)} %bitcast.2.me, s32[4,1,256]{2,1,0:T(1,128)S(1)} %bitcast.17, bf16[2,64,1024]{2,1,0:T(8,128)(2,1)S(1)} %collective-permute-done.rest_0_, ...), custom_call_target="tpu_custom_call", output_to_operand_aliasing={{0}: (7, {}), {1}: (8, {})} | custom-call | flops 4294967296 | bytes 4194304 | tf_op jit(solution)/shard_map/pallas_call | solution.py:59
  43.0 1.6 %shard_map.68 = (bf16[1024,1024]{1,0:T(8,128)(2,1)S(1)}, bf16[1024,1024]{1,0:T(8,128)(2,1)S(1)}, bf16[256,1024]{1,0:T(8,128)(2,1)S(1)}, bf16[1,1024,512]{2,1,0:T(8,128)(2,1)S(1)}) custom-call(s32[1]{0:T(128)} %bitcast.1.ckpt, s32[1]{0:T(128)} %bitcast.2.me, s32[4,1,256]{2,1,0:T(1,128)S(1)} %bitcast.18, ...), custom_call_target="tpu_custom_call", output_to_operand_aliasing={{0}: (7, {}), {1}: (8, {})} | custom-call | flops 3221225472 | bytes 4194304 | tf_op jit(solution)/shard_map/pallas_call | solution.py:59
  44.6 0.6 copy-done
  45.2 0.3 shard_map.70.rest_0_
  45.5 0.6 collective-permute-start.16
  46.1 0.8 %shard_map.71.rest_0_ = bf16[640,512]{1,0:T(8,128)(2,1)S(1)} custom-call(bf16[2048,1024]{1,0:T(8,128)(2,1)S(1)} %bitcast.7, bf16[1,1024,512]{2,1,0:T(8,128)(2,1)S(1)} %get-tuple-element.29.matrices, f32[2048,128]{1,0:T(8,128)S(1)} %shard_map.69.weight, bf16[128,512]{1,0:T(8,128)(2,1)S(1)} %shard_map.70.rest_0_), custom_call_target="tpu_custom_call" | custom-call | tf_op jit(solution)/shard_map/pallas_call | solution.py:59
  46.9 1.6 %collective-permute-start.25 = (bf16[640,512]{1,0:T(8,128)(2,1)S(1)}, bf16[640,512]{1,0:T(8,128)(2,1)S(1)}, u32[]{:S(2)}, u32[]{:S(2)}) collective-permute-start(bf16[640,512]{1,0:T(8,128)(2,1)S(1)} %shard_map.71.rest_0_), channel_id=1, source_target_pairs={{0,16},{16,0},{1,17},{17,1},{2,18},{18,2},{3,19},{19,3},{4,20},{20... | collective-permute-start | bytes 1966088 | tf_op jit(solution)/shard_map/ppermute | solution.py:360
  48.5 3.4 %collective-permute-done.16.block.rest_0_ = bf16[128,512]{1,0:T(8,128)(2,1)S(1)} collective-permute-done((bf16[128,512]{1,0:T(8,128)(2,1)S(1)}, bf16[128,512]{1,0:T(8,128)(2,1)S(1)}, u32[]{:S(2)}, u32[]{:S(2)}) %collective-permute-start.16) | collective-permute-done | bytes 131104 | tf_op jit(solution)/shard_map/ppermute | solution.py:371
  51.9 2.0 %collective-permute-start.19 = (bf16[64,512]{1,0:T(8,128)(2,1)S(1)}, bf16[64,512]{1,0:T(8,128)(2,1)S(1)}, u32[]{:S(2)}, u32[]{:S(2)}) collective-permute-start(bf16[64,512]{1,0:T(8,128)(2,1)S(1)} %shard_map.72.rest_0_.refs_0_), channel_id=1, source_target_pairs={{4,0},{5,1},{6,2},{7,3},{0,4},{1,5},{2,6},{3,7},{12,8},{13,9},{14,... | collective-permute-start | bytes 196616 | tf_op jit(solution)/shard_map/ppermute | solution.py:28
  53.9 3.3 %collective-permute-start.20 = (bf16[64,512]{1,0:T(8,128)(2,1)S(1)}, bf16[64,512]{1,0:T(8,128)(2,1)S(1)}, u32[]{:S(2)}, u32[]{:S(2)}) collective-permute-start(bf16[64,512]{1,0:T(8,128)(2,1)S(1)} %shard_map.72.rest_0_.refs_0_), channel_id=1, source_target_pairs={{8,0},{9,1},{10,2},{11,3},{12,4},{13,5},{14,6},{15,7},{0,8},{1,9},... | collective-permute-start | bytes 196616 | tf_op jit(solution)/shard_map/ppermute | solution.py:28
  57.2 0.0 collective-permute-start.21
  57.3 1.5 %shard_map.73.refs_4_.matrix = bf16[1024,512]{1,0:T(8,128)(2,1)S(1)} custom-call(s32[1]{0:T(128)} %bitcast.1.ckpt, s32[1]{0:T(128)} %bitcast.2.me, s32[4,1,256]{2,1,0:T(1,128)S(1)} %bitcast.19, bf16[1024,1024]{1,0:T(8,128)(2,1)S(1)} %get-tuple-element.26.inverse, bf16[1024,1024]{1,0:T(8,128)(2,1)S(1)} %get-tuple-element.27.chosen, ...), custom_call_target="tpu_custom_call" | custom-call | flops 3221225472 | tf_op jit(solution)/shard_map/pallas_call | solution.py:59
  58.8 0.6 collective-permute-done.20.refs_2_
  59.5 3.8 %collective-permute-done.21.refs_3_ = bf16[64,512]{1,0:T(8,128)(2,1)S(1)} collective-permute-done((bf16[64,512]{1,0:T(8,128)(2,1)S(1)}, bf16[64,512]{1,0:T(8,128)(2,1)S(1)}, u32[]{:S(2)}, u32[]{:S(2)}) %collective-permute-start.21) | collective-permute-done | bytes 65568 | tf_op jit(solution)/shard_map/ppermute | solution.py:28
  63.3 1.6 %collective-permute-start.24 = (bf16[4,64,512]{2,1,0:T(8,128)(2,1)S(1)}, bf16[4,64,512]{2,1,0:T(8,128)(2,1)S(1)}, u32[]{:S(2)}, u32[]{:S(2)}) collective-permute-start(bf16[4,64,512]{2,1,0:T(8,128)(2,1)S(1)} %shard_map.75.rest_0_.rest_2_), channel_id=1, source_target_pairs={{2,0},{3,1},{0,2},{1,3},{6,4},{7,5},{4,6},{5,7},{10,8},{11,9},{8,1... | collective-permute-start | bytes 786440 | tf_op jit(solution)/shard_map/ppermute | solution.py:28
  64.9 0.5 shard_map.74
  65.4 0.4 collective-permute-start.18
  65.8 3.9 %collective-permute-done.24.block = bf16[4,64,512]{2,1,0:T(8,128)(2,1)S(1)} collective-permute-done((bf16[4,64,512]{2,1,0:T(8,128)(2,1)S(1)}, bf16[4,64,512]{2,1,0:T(8,128)(2,1)S(1)}, u32[]{:S(2)}, u32[]{:S(2)}) %collective-permute-start.24) | collective-permute-done | bytes 262176 | tf_op jit(solution)/shard_map/ppermute | solution.py:28
  69.8 0.1 collective-permute-start.26
  69.8 0.4 shard_map.76
  70.3 0.4 collective-permute-start.22
  70.7 2.1 %shard_map.78.rest_6_ = f32[2048,512]{1,0:T(8,128)} custom-call(bf16[2048,1024]{1,0:T(8,128)(2,1)S(1)} %bitcast.10, bf16[1024,512]{1,0:T(8,128)(2,1)S(1)} %shard_map.73.refs_4_.matrix, f32[2048,128]{1,0:T(8,128)S(1)} %shard_map.69.weight, bf16[128,512]{1,0:T(8,128)(2,1)S(1)} %collective-permute-done.16.block.rest_0_, ...), custom_call_target="tpu_custom_call" | custom-call | tf_op jit(solution)/shard_map/pallas_call | solution.py:59
  72.8 3.2 %shard_map.79.rest_2_ = f32[2048,512]{1,0:T(8,128)} custom-call(s32[1]{0:T(128)} %bitcast.2.me, bf16[2048,1024]{1,0:T(8,128)(2,1)S(1)} %bitcast.11, bf16[1024,512]{1,0:T(8,128)(2,1)S(1)} %shard_map.73.refs_4_.matrix, f32[2048,128]{1,0:T(8,128)S(1)} %shard_map.69.weight, s32[1,2048]{1,0:T(1,128)S(1)} %bitcast.14, ...), custom_call_target="tpu_custom_call", output_to_operand_aliasing={{}: (11, {})} | custom-call | tf_op jit(solution)/shard_map/pallas_call | solution.py:59
  76.0 3.0 %collective-permute-done.22.rest_1_ = bf16[256,512]{1,0:T(8,128)(2,1)S(1)} collective-permute-done((bf16[256,512]{1,0:T(8,128)(2,1)S(1)}, bf16[256,512]{1,0:T(8,128)(2,1)S(1)}, u32[]{:S(2)}, u32[]{:S(2)}) %collective-permute-start.22) | collective-permute-done | bytes 262176 | tf_op jit(solution)/shard_map/ppermute | solution.py:360
  79.1 1.7 %shard_map.80 = f32[2048,512]{1,0:T(8,128)} custom-call(bf16[2048,1024]{1,0:T(8,128)(2,1)S(1)} %bitcast.12, bf16[1024,512]{1,0:T(8,128)(2,1)S(1)} %shard_map.73.refs_4_.matrix, f32[2048,128]{1,0:T(8,128)S(1)} %shard_map.69.weight, bf16[320,512]{1,0:T(8,128)(2,1)S(1)} %collective-permute-done.18.rest_0_, ...), custom_call_target="tpu_custom_call", output_to_operand_aliasing={{}: (5, {})} | custom-call | tf_op jit(solution)/shard_map/pallas_call | solution.py:59
  (33 shorter events, 0.1 us)
Async XLA Ops:
  0.0 23.0 %copy-start.1 = (s32[2048]{0:T(1024)S(1)}, s32[2048]{0:T(1024)}, u32[]{:S(2)}) copy-start(s32[2048]{0:T(1024)} %param.10) | copy-start | bytes 24580
  0.0 23.0 %copy-start.2 = (f32[1,16]{1,0:T(1,128)S(1)}, f32[1,16]{1,0:T(1,128)}, u32[]{:S(2)}) copy-start(f32[1,16]{1,0:T(1,128)} %bucket_weight.3) | copy-start | bytes 196
  0.0 31.5 %copy-start.4 = (s32[1024]{0:T(1024)S(1)}, s32[1024]{0:T(1024)}, u32[]{:S(2)}) copy-start(s32[1024]{0:T(1024)} %param.11) | copy-start | bytes 12292
  3.1 28.1 %collective-permute-start.15 = (bf16[400,1024]{1,0:T(8,128)(2,1)}, bf16[400,1024]{1,0:T(8,128)(2,1)S(1)}, u32[]{:S(2)}, u32[]{:S(2)}) collective-permute-start(bf16[400,1024]{1,0:T(8,128)(2,1)} %get-tuple-element.19), channel_id=1, source_target_pairs={{0,16},{16,0},{1,17},{17,1},{2,18},{18,2},{3,19},{19,3},{4,20},{20... | collective-permute-start | bytes 2457608 | tf_op jit(solution)/shard_map/ppermute | solution.py:312
  6.1 14.6 %collective-permute-start = (bf16[2,64,1024]{2,1,0:T(8,128)(2,1)}, bf16[2,64,1024]{2,1,0:T(8,128)(2,1)S(1)}, u32[]{:S(2)}, u32[]{:S(2)}) collective-permute-start(bf16[2,64,1024]{2,1,0:T(8,128)(2,1)} %get-tuple-element.18.rest_0_), channel_id=1, source_target_pairs={{8,0},{9,1},{10,2},{11,3},{12,4},{13,5},{14,6},{15,7},{0,8},{1,9},... | collective-permute-start | bytes 786440 | tf_op jit(solution)/shard_map/ppermute | solution.py:28
  8.7 12.7 %collective-permute-start.8 = (bf16[2,64,1024]{2,1,0:T(8,128)(2,1)}, bf16[2,64,1024]{2,1,0:T(8,128)(2,1)S(1)}, u32[]{:S(2)}, u32[]{:S(2)}) collective-permute-start(bf16[2,64,1024]{2,1,0:T(8,128)(2,1)} %get-tuple-element.18.rest_0_), channel_id=1, source_target_pairs={{4,0},{5,1},{6,2},{7,3},{0,4},{1,5},{2,6},{3,7},{12,8},{13,9},{14,... | collective-permute-start | bytes 786440 | tf_op jit(solution)/shard_map/ppermute | solution.py:28
  10.3 12.6 %collective-permute-start.13 = (bf16[2,64,1024]{2,1,0:T(8,128)(2,1)}, bf16[2,64,1024]{2,1,0:T(8,128)(2,1)S(1)}, u32[]{:S(2)}, u32[]{:S(2)}) collective-permute-start(bf16[2,64,1024]{2,1,0:T(8,128)(2,1)} %get-tuple-element.18.rest_0_), channel_id=1, source_target_pairs={{2,0},{3,1},{0,2},{1,3},{6,4},{7,5},{4,6},{5,7},{10,8},{11,9},{8,1... | collective-permute-start | bytes 786440 | tf_op jit(solution)/shard_map/ppermute | solution.py:28
  11.8 12.2 %collective-permute-start.12 = (bf16[2,64,1024]{2,1,0:T(8,128)(2,1)}, bf16[2,64,1024]{2,1,0:T(8,128)(2,1)S(1)}, u32[]{:S(2)}, u32[]{:S(2)}) collective-permute-start(bf16[2,64,1024]{2,1,0:T(8,128)(2,1)} %get-tuple-element.18.rest_0_), channel_id=1, source_target_pairs={{1,0},{0,1},{3,2},{2,3},{5,4},{4,5},{7,6},{6,7},{9,8},{8,9},{11,10... | collective-permute-start | bytes 786440 | tf_op jit(solution)/shard_map/ppermute | solution.py:28
  20.7 7.2 %collective-permute-start.1 = (bf16[2,64,1024]{2,1,0:T(8,128)(2,1)S(1)}, bf16[2,64,1024]{2,1,0:T(8,128)(2,1)S(1)}, u32[]{:S(2)}, u32[]{:S(2)}) collective-permute-start(bf16[2,64,1024]{2,1,0:T(8,128)(2,1)S(1)} %collective-permute-done.rest_0_), channel_id=1, source_target_pairs={{4,0},{5,1},{6,2},{7,3},{0,4},{1,5},{2,6},{3,7},{12,8},{13,9},{14,... | collective-permute-start | bytes 786440 | tf_op jit(solution)/shard_map/ppermute | solution.py:28
  21.4 8.3 %collective-permute-start.10 = (bf16[2,64,1024]{2,1,0:T(8,128)(2,1)S(1)}, bf16[2,64,1024]{2,1,0:T(8,128)(2,1)S(1)}, u32[]{:S(2)}, u32[]{:S(2)}) collective-permute-start(bf16[2,64,1024]{2,1,0:T(8,128)(2,1)S(1)} %collective-permute-done.8.rest_0_), channel_id=1, source_target_pairs={{2,0},{3,1},{0,2},{1,3},{6,4},{7,5},{4,6},{5,7},{10,8},{11,9},{8,1... | collective-permute-start | bytes 786440 | tf_op jit(solution)/shard_map/ppermute | solution.py:28
  22.9 6.8 %collective-permute-start.14 = (bf16[2,64,1024]{2,1,0:T(8,128)(2,1)S(1)}, bf16[2,64,1024]{2,1,0:T(8,128)(2,1)S(1)}, u32[]{:S(2)}, u32[]{:S(2)}) collective-permute-start(bf16[2,64,1024]{2,1,0:T(8,128)(2,1)S(1)} %collective-permute-done.13.rest_2_), channel_id=1, source_target_pairs={{1,0},{0,1},{3,2},{2,3},{5,4},{4,5},{7,6},{6,7},{9,8},{8,9},{11,10... | collective-permute-start | bytes 786440 | tf_op jit(solution)/shard_map/ppermute | solution.py:28
  24.0 33.2 %collective-permute-start.17 = (bf16[384,1024]{1,0:T(8,128)(2,1)}, bf16[384,1024]{1,0:T(8,128)(2,1)S(1)}, u32[]{:S(2)}, u32[]{:S(2)}) collective-permute-start(bf16[384,1024]{1,0:T(8,128)(2,1)} %get-tuple-element.30), channel_id=1, source_target_pairs={{0,16},{16,0},{1,17},{17,1},{2,18},{18,2},{3,19},{19,3},{4,20},{20... | collective-permute-start | bytes 2359304 | tf_op jit(solution)/shard_map/ppermute | solution.py:312
  27.9 9.2 %collective-permute-start.6 = (bf16[2,64,1024]{2,1,0:T(8,128)(2,1)S(1)}, bf16[2,64,1024]{2,1,0:T(8,128)(2,1)S(1)}, u32[]{:S(2)}, u32[]{:S(2)}) collective-permute-start(bf16[2,64,1024]{2,1,0:T(8,128)(2,1)S(1)} %collective-permute-done.rest_0_), channel_id=1, source_target_pairs={{2,0},{3,1},{0,2},{1,3},{6,4},{7,5},{4,6},{5,7},{10,8},{11,9},{8,1... | collective-permute-start | bytes 786440 | tf_op jit(solution)/shard_map/ppermute | solution.py:28
  29.7 7.3 %collective-permute-start.9 = (bf16[2,64,1024]{2,1,0:T(8,128)(2,1)S(1)}, bf16[2,64,1024]{2,1,0:T(8,128)(2,1)S(1)}, u32[]{:S(2)}, u32[]{:S(2)}) collective-permute-start(bf16[2,64,1024]{2,1,0:T(8,128)(2,1)S(1)} %collective-permute-done.8.rest_0_), channel_id=1, source_target_pairs={{1,0},{0,1},{3,2},{2,3},{5,4},{4,5},{7,6},{6,7},{9,8},{8,9},{11,10... | collective-permute-start | bytes 786440 | tf_op jit(solution)/shard_map/ppermute | solution.py:28
  29.7 10.9 %collective-permute-start.3 = (bf16[2,64,1024]{2,1,0:T(8,128)(2,1)S(1)}, bf16[2,64,1024]{2,1,0:T(8,128)(2,1)S(1)}, u32[]{:S(2)}, u32[]{:S(2)}) collective-permute-start(bf16[2,64,1024]{2,1,0:T(8,128)(2,1)S(1)} %collective-permute-done.1.rest_0_), channel_id=1, source_target_pairs={{2,0},{3,1},{0,2},{1,3},{6,4},{7,5},{4,6},{5,7},{10,8},{11,9},{8,1... | collective-permute-start | bytes 786440 | tf_op jit(solution)/shard_map/ppermute | solution.py:28
  31.3 9.3 %collective-permute-start.11 = (bf16[2,64,1024]{2,1,0:T(8,128)(2,1)S(1)}, bf16[2,64,1024]{2,1,0:T(8,128)(2,1)S(1)}, u32[]{:S(2)}, u32[]{:S(2)}) collective-permute-start(bf16[2,64,1024]{2,1,0:T(8,128)(2,1)S(1)} %collective-permute-done.10.rest_2_), channel_id=1, source_target_pairs={{1,0},{0,1},{3,2},{2,3},{5,4},{4,5},{7,6},{6,7},{9,8},{8,9},{11,10... | collective-permute-start | bytes 786440 | tf_op jit(solution)/shard_map/ppermute | solution.py:28
  31.5 1.0 %copy-start.3 = (bf16[2,64,1024]{2,1,0:T(8,128)(2,1)S(1)}, bf16[2,64,1024]{2,1,0:T(8,128)(2,1)}, u32[]{:S(2)}) copy-start(bf16[2,64,1024]{2,1,0:T(8,128)(2,1)} %get-tuple-element.18.rest_0_) | copy-start | bytes 786436
  37.1 4.9 %collective-permute-start.5 = (bf16[2,64,1024]{2,1,0:T(8,128)(2,1)S(1)}, bf16[2,64,1024]{2,1,0:T(8,128)(2,1)S(1)}, u32[]{:S(2)}, u32[]{:S(2)}) collective-permute-start(bf16[2,64,1024]{2,1,0:T(8,128)(2,1)S(1)} %collective-permute-done.rest_0_), channel_id=1, source_target_pairs={{1,0},{0,1},{3,2},{2,3},{5,4},{4,5},{7,6},{6,7},{9,8},{8,9},{11,10... | collective-permute-start | bytes 786440 | tf_op jit(solution)/shard_map/ppermute | solution.py:28
  37.1 5.9 %collective-permute-start.2 = (bf16[2,64,1024]{2,1,0:T(8,128)(2,1)S(1)}, bf16[2,64,1024]{2,1,0:T(8,128)(2,1)S(1)}, u32[]{:S(2)}, u32[]{:S(2)}) collective-permute-start(bf16[2,64,1024]{2,1,0:T(8,128)(2,1)S(1)} %collective-permute-done.1.rest_0_), channel_id=1, source_target_pairs={{1,0},{0,1},{3,2},{2,3},{5,4},{4,5},{7,6},{6,7},{9,8},{8,9},{11,10... | collective-permute-start | bytes 786440 | tf_op jit(solution)/shard_map/ppermute | solution.py:28
  40.6 1.5 %collective-permute-start.7 = (bf16[2,64,1024]{2,1,0:T(8,128)(2,1)S(1)}, bf16[2,64,1024]{2,1,0:T(8,128)(2,1)S(1)}, u32[]{:S(2)}, u32[]{:S(2)}) collective-permute-start(bf16[2,64,1024]{2,1,0:T(8,128)(2,1)S(1)} %collective-permute-done.6.rest_2_), channel_id=1, source_target_pairs={{1,0},{0,1},{3,2},{2,3},{5,4},{4,5},{7,6},{6,7},{9,8},{8,9},{11,10... | collective-permute-start | bytes 786440 | tf_op jit(solution)/shard_map/ppermute | solution.py:28
  40.6 2.4 %collective-permute-start.4 = (bf16[2,64,1024]{2,1,0:T(8,128)(2,1)S(1)}, bf16[2,64,1024]{2,1,0:T(8,128)(2,1)S(1)}, u32[]{:S(2)}, u32[]{:S(2)}) collective-permute-start(bf16[2,64,1024]{2,1,0:T(8,128)(2,1)S(1)} %collective-permute-done.3.rest_2_), channel_id=1, source_target_pairs={{1,0},{0,1},{3,2},{2,3},{5,4},{4,5},{7,6},{6,7},{9,8},{8,9},{11,10... | collective-permute-start | bytes 786440 | tf_op jit(solution)/shard_map/ppermute | solution.py:28
  43.0 2.2 %copy-start = (bf16[1,2048,1024]{2,1,0:T(8,128)(2,1)S(1)}, bf16[1,2048,1024]{2,1,0:T(8,128)(2,1)}, u32[]{:S(2)}) copy-start(bf16[1,2048,1024]{2,1,0:T(8,128)(2,1)} %param.6) | copy-start | bytes 12582916
  45.5 6.4 %collective-permute-start.16 = (bf16[128,512]{1,0:T(8,128)(2,1)S(1)}, bf16[128,512]{1,0:T(8,128)(2,1)S(1)}, u32[]{:S(2)}, u32[]{:S(2)}) collective-permute-start(bf16[128,512]{1,0:T(8,128)(2,1)S(1)} %shard_map.70.rest_0_), channel_id=1, source_target_pairs={{0,16},{16,0},{1,17},{17,1},{2,18},{18,2},{3,19},{19,3},{4,20},{20... | collective-permute-start | bytes 393224 | tf_op jit(solution)/shard_map/ppermute | solution.py:371
  46.9 22.8 %collective-permute-start.25 = (bf16[640,512]{1,0:T(8,128)(2,1)S(1)}, bf16[640,512]{1,0:T(8,128)(2,1)S(1)}, u32[]{:S(2)}, u32[]{:S(2)}) collective-permute-start(bf16[640,512]{1,0:T(8,128)(2,1)S(1)} %shard_map.71.rest_0_), channel_id=1, source_target_pairs={{0,16},{16,0},{1,17},{17,1},{2,18},{18,2},{3,19},{19,3},{4,20},{20... | collective-permute-start | bytes 1966088 | tf_op jit(solution)/shard_map/ppermute | solution.py:360
  51.9 6.9 %collective-permute-start.19 = (bf16[64,512]{1,0:T(8,128)(2,1)S(1)}, bf16[64,512]{1,0:T(8,128)(2,1)S(1)}, u32[]{:S(2)}, u32[]{:S(2)}) collective-permute-start(bf16[64,512]{1,0:T(8,128)(2,1)S(1)} %shard_map.72.rest_0_.refs_0_), channel_id=1, source_target_pairs={{4,0},{5,1},{6,2},{7,3},{0,4},{1,5},{2,6},{3,7},{12,8},{13,9},{14,... | collective-permute-start | bytes 196616 | tf_op jit(solution)/shard_map/ppermute | solution.py:28
  53.9 5.5 %collective-permute-start.20 = (bf16[64,512]{1,0:T(8,128)(2,1)S(1)}, bf16[64,512]{1,0:T(8,128)(2,1)S(1)}, u32[]{:S(2)}, u32[]{:S(2)}) collective-permute-start(bf16[64,512]{1,0:T(8,128)(2,1)S(1)} %shard_map.72.rest_0_.refs_0_), channel_id=1, source_target_pairs={{8,0},{9,1},{10,2},{11,3},{12,4},{13,5},{14,6},{15,7},{0,8},{1,9},... | collective-permute-start | bytes 196616 | tf_op jit(solution)/shard_map/ppermute | solution.py:28
  57.2 6.1 %collective-permute-start.21 = (bf16[64,512]{1,0:T(8,128)(2,1)S(1)}, bf16[64,512]{1,0:T(8,128)(2,1)S(1)}, u32[]{:S(2)}, u32[]{:S(2)}) collective-permute-start(bf16[64,512]{1,0:T(8,128)(2,1)S(1)} %shard_map.72.rest_0_.refs_0_), channel_id=1, source_target_pairs={{12,0},{13,1},{14,2},{15,3},{8,4},{9,5},{10,6},{11,7},{4,8},{5,9},... | collective-permute-start | bytes 196616 | tf_op jit(solution)/shard_map/ppermute | solution.py:28
  63.3 6.4 %collective-permute-start.24 = (bf16[4,64,512]{2,1,0:T(8,128)(2,1)S(1)}, bf16[4,64,512]{2,1,0:T(8,128)(2,1)S(1)}, u32[]{:S(2)}, u32[]{:S(2)}) collective-permute-start(bf16[4,64,512]{2,1,0:T(8,128)(2,1)S(1)} %shard_map.75.rest_0_.rest_2_), channel_id=1, source_target_pairs={{2,0},{3,1},{0,2},{1,3},{6,4},{7,5},{4,6},{5,7},{10,8},{11,9},{8,1... | collective-permute-start | bytes 786440 | tf_op jit(solution)/shard_map/ppermute | solution.py:28
  65.4 10.6 %collective-permute-start.18 = (bf16[320,512]{1,0:T(8,128)(2,1)S(1)}, bf16[320,512]{1,0:T(8,128)(2,1)S(1)}, u32[]{:S(2)}, u32[]{:S(2)}) collective-permute-start(bf16[320,512]{1,0:T(8,128)(2,1)S(1)} %shard_map.74), channel_id=1, source_target_pairs={{0,16},{16,0},{1,17},{17,1},{2,18},{18,2},{3,19},{19,3},{4,20},{20... | collective-permute-start | bytes 983048 | tf_op jit(solution)/shard_map/ppermute | solution.py:360
  65.8 7.0 %collective-permute-start.23 = (bf16[4,64,512]{2,1,0:T(8,128)(2,1)S(1)}, bf16[4,64,512]{2,1,0:T(8,128)(2,1)S(1)}, u32[]{:S(2)}, u32[]{:S(2)}) collective-permute-start(bf16[4,64,512]{2,1,0:T(8,128)(2,1)S(1)} %shard_map.75.rest_0_.rest_2_), channel_id=1, source_target_pairs={{1,0},{0,1},{3,2},{2,3},{5,4},{4,5},{7,6},{6,7},{9,8},{8,9},{11,10... | collective-permute-start | bytes 786440 | tf_op jit(solution)/shard_map/ppermute | solution.py:28
  69.8 3.0 %collective-permute-start.26 = (bf16[4,64,512]{2,1,0:T(8,128)(2,1)S(1)}, bf16[4,64,512]{2,1,0:T(8,128)(2,1)S(1)}, u32[]{:S(2)}, u32[]{:S(2)}) collective-permute-start(bf16[4,64,512]{2,1,0:T(8,128)(2,1)S(1)} %shard_map.77.rest_4_), channel_id=1, source_target_pairs={{1,0},{0,1},{3,2},{2,3},{5,4},{4,5},{7,6},{6,7},{9,8},{8,9},{11,10... | collective-permute-start | bytes 786440 | tf_op jit(solution)/shard_map/ppermute | solution.py:28
  70.3 8.8 %collective-permute-start.22 = (bf16[256,512]{1,0:T(8,128)(2,1)S(1)}, bf16[256,512]{1,0:T(8,128)(2,1)S(1)}, u32[]{:S(2)}, u32[]{:S(2)}) collective-permute-start(bf16[256,512]{1,0:T(8,128)(2,1)S(1)} %shard_map.76), channel_id=1, source_target_pairs={{0,16},{16,0},{1,17},{17,1},{2,18},{18,2},{3,19},{19,3},{4,20},{20... | collective-permute-start | bytes 786440 | tf_op jit(solution)/shard_map/ppermute | solution.py:360

commit v4 on v3

--- a/solution.py
+++ b/solution.py
@@ -284,9 +284,9 @@
     share = size // n
     unit = rows // 32
     paired = ensemble == 2
-    batches = [6, 6] if paired else []
+    batches = [7, 6] if paired else []
     featured = sum(batches)
-    parts = [1, 10, 5, 4] if paired else [16, 16]
+    parts = [1, 8, 5, 5] if paired else [16, 16]
     flying = 2
     table_rows = -(-bucket_weight.shape[1] // 16) * 16
 
@@ -400,7 +400,7 @@
         for bit in inner_bits:
             held += [(mask ^ bit, swap(b, bit, n)) for mask, b in held]
         held = held[:1] + [
-            (mask, call(relay_kernel, shape(b.shape), (b, *received[1]), [VMEM, ANY]))
+            (mask, call(relay_kernel, shape(b.shape), (b, *received[1], *received[2]), [VMEM, ANY, ANY]))
             for mask, b in held[1:]
         ]
         for bit in core_bits:
@@ -421,7 +421,7 @@
             aliases={len(operands): 0} if held else None, mib=24,
         )
 
-    together = [[0, 1], [], [2, 3]] if paired else [[q] for q in range(len(parts))]
+    together = [[0, 1, 2], [], [3]] if paired else [[q] for q in range(len(parts))]
     for chunks in together:
         if chunks:
             part = sum(parts[q] for q in chunks)

time: 81 us -> 78 us (0.963)
  waiting for transfers between devices: 34.3 us -> 31.2 us
    ppermute x21, waiting for transfers between devices: 27.9 us -> 22.9 us  [swap(): return lax.ppermute(block, 'train', [(d ^ mask, d) for d in range(n)])]
    ppermute x3, waiting for transfers between devices: 3.04 us -> 4.76 us  [send(): got.append(lax.ppermute(tile, 'ckpt', ahead(k, ensemble)))]
  transfers between devices with their start and end apart: 27 -> 27, of which waited for: 11 -> 10; matrix products, arithmetic and copies ran while one was open for 0% -> 0% of each run, Pallas kernels for 17% -> 18%
where the time goes in v4:
time: 78 us; the launch traced here: 77.8 us
  waiting for transfers between devices  31.2 us (40%)
  starting transfers between devices  26.2 us (34%)
  Pallas kernels  18.7 us (24%)
  local copies, waits for them, and re-layouts  1.55 us (2%)
    ppermute x21, waiting for transfers between devices, swap(): return lax.ppermute(block, 'train', [(d ^ mask, d) for d in range(n)])  22.9 us
    ppermute x21, starting transfers between devices, swap(): return lax.ppermute(block, 'train', [(d ^ mask, d) for d in range(n)])  19.2 us
    pallas_call x17, Pallas kernels, call(): pl.pallas_call(kernel, out_shape=outs, in_specs=specs, out_specs=out_spec...  18.7 us
    ppermute x3, waiting for transfers between devices, send(): got.append(lax.ppermute(tile, 'ckpt', ahead(k, ensemble)))  4.76 us
    ppermute x2, starting transfers between devices, shards(): lax.ppermute(batch, 'ckpt', ahead(1, ensemble))  3.6 us
    ppermute x1, waiting for transfers between devices, shards(): received.append([lax.ppermute(tile, 'ckpt', ahead(1, ensemble))])  3.54 us
    ppermute x3, starting transfers between devices, send(): got.append(lax.ppermute(tile, 'ckpt', ahead(k, ensemble)))  2.75 us
  transfers between devices with their start and end apart: 27, of which 10 were waited for; matrix products, arithmetic and copies ran while one was open for 0% of the time, Pallas kernels for 18%

profile of v4, /device:TPU:0, one launch (start us, length us, event | category | flops | bytes accessed | tf_op | source)
XLA Modules:
  0.0 77.8 jit_solution(9114302143902339964)
XLA Ops:
  0.0 3.2 %shard_map.64 = (bf16[2,64,1024]{2,1,0:T(8,128)(2,1)}, bf16[464,1024]{1,0:T(8,128)(2,1)}, bf16[384,1024]{1,0:T(8,128)(2,1)}) custom-call(bf16[1,64,1024]{2,1,0:T(8,128)(2,1)} %test_feat.1, bf16[1,64,1024]{2,1,0:T(8,128)(2,1)} %kernel_inv.1, bf16[2048,1024]{1,0:T(8,128)(2,1)} %bitcast.5, f32[1,16]{1,0:T(1,128)} %bucket_weight.3), custom_call_target="tpu_custom_call" | custom-call | tf_op jit(solution)/shard_map/pallas_call | solution.py:59
  3.2 3.0 %collective-permute-start.15 = (bf16[464,1024]{1,0:T(8,128)(2,1)}, bf16[464,1024]{1,0:T(8,128)(2,1)S(1)}, u32[]{:S(2)}, u32[]{:S(2)}) collective-permute-start(bf16[464,1024]{1,0:T(8,128)(2,1)} %get-tuple-element.19), channel_id=1, source_target_pairs={{0,16},{16,0},{1,17},{17,1},{2,18},{18,2},{3,19},{19,3},{4,20},{20... | collective-permute-start | bytes 2850824 | tf_op jit(solution)/shard_map/ppermute | solution.py:312
  6.2 2.6 %collective-permute-start = (bf16[2,64,1024]{2,1,0:T(8,128)(2,1)}, bf16[2,64,1024]{2,1,0:T(8,128)(2,1)S(1)}, u32[]{:S(2)}, u32[]{:S(2)}) collective-permute-start(bf16[2,64,1024]{2,1,0:T(8,128)(2,1)} %get-tuple-element.18.rest_0_), channel_id=1, source_target_pairs={{8,0},{9,1},{10,2},{11,3},{12,4},{13,5},{14,6},{15,7},{0,8},{1,9},... | collective-permute-start | bytes 786440 | tf_op jit(solution)/shard_map/ppermute | solution.py:28
  8.8 1.6 %collective-permute-start.8 = (bf16[2,64,1024]{2,1,0:T(8,128)(2,1)}, bf16[2,64,1024]{2,1,0:T(8,128)(2,1)S(1)}, u32[]{:S(2)}, u32[]{:S(2)}) collective-permute-start(bf16[2,64,1024]{2,1,0:T(8,128)(2,1)} %get-tuple-element.18.rest_0_), channel_id=1, source_target_pairs={{4,0},{5,1},{6,2},{7,3},{0,4},{1,5},{2,6},{3,7},{12,8},{13,9},{14,... | collective-permute-start | bytes 786440 | tf_op jit(solution)/shard_map/ppermute | solution.py:28
  10.4 1.5 %collective-permute-start.13 = (bf16[2,64,1024]{2,1,0:T(8,128)(2,1)}, bf16[2,64,1024]{2,1,0:T(8,128)(2,1)S(1)}, u32[]{:S(2)}, u32[]{:S(2)}) collective-permute-start(bf16[2,64,1024]{2,1,0:T(8,128)(2,1)} %get-tuple-element.18.rest_0_), channel_id=1, source_target_pairs={{2,0},{3,1},{0,2},{1,3},{6,4},{7,5},{4,6},{5,7},{10,8},{11,9},{8,1... | collective-permute-start | bytes 786440 | tf_op jit(solution)/shard_map/ppermute | solution.py:28
  11.9 8.9 %collective-permute-done.rest_0_ = bf16[2,64,1024]{2,1,0:T(8,128)(2,1)S(1)} collective-permute-done((bf16[2,64,1024]{2,1,0:T(8,128)(2,1)}, bf16[2,64,1024]{2,1,0:T(8,128)(2,1)S(1)}, u32[]{:S(2)}, u32[]{:S(2)}) %collective-permute-start) | collective-permute-done | bytes 262176 | tf_op jit(solution)/shard_map/ppermute | solution.py:28
  20.8 0.7 collective-permute-start.1
  21.5 1.5 %collective-permute-start.10 = (bf16[2,64,1024]{2,1,0:T(8,128)(2,1)S(1)}, bf16[2,64,1024]{2,1,0:T(8,128)(2,1)S(1)}, u32[]{:S(2)}, u32[]{:S(2)}) collective-permute-start(bf16[2,64,1024]{2,1,0:T(8,128)(2,1)S(1)} %collective-permute-done.8.rest_0_), channel_id=1, source_target_pairs={{2,0},{3,1},{0,2},{1,3},{6,4},{7,5},{4,6},{5,7},{10,8},{11,9},{8,1... | collective-permute-start | bytes 786440 | tf_op jit(solution)/shard_map/ppermute | solution.py:28
  23.0 1.1 %shard_map.69.weight = f32[2048,128]{1,0:T(8,128)S(1)} custom-call(s32[1,2048]{1,0:T(1,128)S(1)} %bitcast.13, f32[1,16]{1,0:T(1,128)S(1)} %copy-done.2), custom_call_target="tpu_custom_call" | custom-call | tf_op jit(solution)/shard_map/pallas_call | solution.py:59
  24.1 0.6 collective-permute-start.17
  24.7 3.3 %collective-permute-done.1.rest_0_ = bf16[2,64,1024]{2,1,0:T(8,128)(2,1)S(1)} collective-permute-done((bf16[2,64,1024]{2,1,0:T(8,128)(2,1)S(1)}, bf16[2,64,1024]{2,1,0:T(8,128)(2,1)S(1)}, u32[]{:S(2)}, u32[]{:S(2)}) %collective-permute-start.1) | collective-permute-done | bytes 262176 | tf_op jit(solution)/shard_map/ppermute | solution.py:28
  28.0 1.5 %collective-permute-start.6 = (bf16[2,64,1024]{2,1,0:T(8,128)(2,1)S(1)}, bf16[2,64,1024]{2,1,0:T(8,128)(2,1)S(1)}, u32[]{:S(2)}, u32[]{:S(2)}) collective-permute-start(bf16[2,64,1024]{2,1,0:T(8,128)(2,1)S(1)} %collective-permute-done.rest_0_), channel_id=1, source_target_pairs={{2,0},{3,1},{0,2},{1,3},{6,4},{7,5},{4,6},{5,7},{10,8},{11,9},{8,1... | collective-permute-start | bytes 786440 | tf_op jit(solution)/shard_map/ppermute | solution.py:28
  29.5 0.3 collective-permute-done.10.rest_2_
  29.8 1.5 %collective-permute-start.3 = (bf16[2,64,1024]{2,1,0:T(8,128)(2,1)S(1)}, bf16[2,64,1024]{2,1,0:T(8,128)(2,1)S(1)}, u32[]{:S(2)}, u32[]{:S(2)}) collective-permute-start(bf16[2,64,1024]{2,1,0:T(8,128)(2,1)S(1)} %collective-permute-done.1.rest_0_), channel_id=1, source_target_pairs={{2,0},{3,1},{0,2},{1,3},{6,4},{7,5},{4,6},{5,7},{10,8},{11,9},{8,1... | collective-permute-start | bytes 786440 | tf_op jit(solution)/shard_map/ppermute | solution.py:28
  31.3 0.2 collective-permute-start.11
  31.6 0.9 %copy-done.3 = bf16[2,64,1024]{2,1,0:T(8,128)(2,1)S(1)} copy-done((bf16[2,64,1024]{2,1,0:T(8,128)(2,1)S(1)}, bf16[2,64,1024]{2,1,0:T(8,128)(2,1)}, u32[]{:S(2)}) %copy-start.3) | copy-done | bytes 262168
  32.5 0.8 %shard_map.65 = (bf16[1024,1024]{1,0:T(8,128)(2,1)S(1)}, bf16[1024,1024]{1,0:T(8,128)(2,1)S(1)}) custom-call(s32[1]{0:T(128)} %bitcast.1.ckpt, s32[1]{0:T(128)} %bitcast.2.me, s32[4,1,256]{2,1,0:T(1,128)S(1)} %bitcast.15, bf16[2,64,1024]{2,1,0:T(8,128)(2,1)S(1)} %copy-done.3, bf16[2,64,1024]{2,1,0:T(8,128)(2,1)S(1)} %collective-permute-done.12.rest_1_, ...), custom_call_target="tpu_custom_call" | custom-call | flops 4294967296 | bytes 4194304 | tf_op jit(solution)/shard_map/pallas_call | solution.py:59
  33.3 3.8 %collective-permute-done.6.rest_2_ = bf16[2,64,1024]{2,1,0:T(8,128)(2,1)S(1)} collective-permute-done((bf16[2,64,1024]{2,1,0:T(8,128)(2,1)S(1)}, bf16[2,64,1024]{2,1,0:T(8,128)(2,1)S(1)}, u32[]{:S(2)}, u32[]{:S(2)}) %collective-permute-start.6) | collective-permute-done | bytes 262176 | tf_op jit(solution)/shard_map/ppermute | solution.py:28
  37.2 0.5 collective-permute-start.2
  37.7 3.0 %collective-permute-done.3.rest_2_ = bf16[2,64,1024]{2,1,0:T(8,128)(2,1)S(1)} collective-permute-done((bf16[2,64,1024]{2,1,0:T(8,128)(2,1)S(1)}, bf16[2,64,1024]{2,1,0:T(8,128)(2,1)S(1)}, u32[]{:S(2)}, u32[]{:S(2)}) %collective-permute-start.3) | collective-permute-done | bytes 262176 | tf_op jit(solution)/shard_map/ppermute | solution.py:28
  40.7 0.5 collective-permute-start.4
  41.2 0.8 %shard_map.66 = (bf16[1024,1024]{1,0:T(8,128)(2,1)S(1)}, bf16[1024,1024]{1,0:T(8,128)(2,1)S(1)}) custom-call(s32[1]{0:T(128)} %bitcast.1.ckpt, s32[1]{0:T(128)} %bitcast.2.me, s32[4,1,256]{2,1,0:T(1,128)S(1)} %bitcast.16, bf16[2,64,1024]{2,1,0:T(8,128)(2,1)S(1)} %collective-permute-done.8.rest_0_, ...), custom_call_target="tpu_custom_call", output_to_operand_aliasing={{0}: (7, {}), {1}: (8, {})} | custom-call | flops 4294967296 | bytes 4194304 | tf_op jit(solution)/shard_map/pallas_call | solution.py:59
  42.0 0.2 collective-permute-done.7.rest_3_
  42.2 0.8 %shard_map.67 = (bf16[1024,1024]{1,0:T(8,128)(2,1)S(1)}, bf16[1024,1024]{1,0:T(8,128)(2,1)S(1)}) custom-call(s32[1]{0:T(128)} %bitcast.1.ckpt, s32[1]{0:T(128)} %bitcast.2.me, s32[4,1,256]{2,1,0:T(1,128)S(1)} %bitcast.17, bf16[2,64,1024]{2,1,0:T(8,128)(2,1)S(1)} %collective-permute-done.rest_0_, ...), custom_call_target="tpu_custom_call", output_to_operand_aliasing={{0}: (7, {}), {1}: (8, {})} | custom-call | flops 4294967296 | bytes 4194304 | tf_op jit(solution)/shard_map/pallas_call | solution.py:59
  43.1 0.0 copy-start
  43.1 1.6 %shard_map.68 = (bf16[1024,1024]{1,0:T(8,128)(2,1)S(1)}, bf16[1024,1024]{1,0:T(8,128)(2,1)S(1)}, bf16[256,1024]{1,0:T(8,128)(2,1)S(1)}, bf16[1,1024,512]{2,1,0:T(8,128)(2,1)S(1)}) custom-call(s32[1]{0:T(128)} %bitcast.1.ckpt, s32[1]{0:T(128)} %bitcast.2.me, s32[4,1,256]{2,1,0:T(1,128)S(1)} %bitcast.18, ...), custom_call_target="tpu_custom_call", output_to_operand_aliasing={{0}: (7, {}), {1}: (8, {})} | custom-call | flops 3221225472 | bytes 4194304 | tf_op jit(solution)/shard_map/pallas_call | solution.py:59
  44.7 0.6 copy-done
  45.3 0.3 shard_map.70.rest_0_
  45.6 0.6 collective-permute-start.16
  46.2 0.7 shard_map.71.rest_0_
  46.9 1.6 %collective-permute-start.24 = (bf16[512,512]{1,0:T(8,128)(2,1)S(1)}, bf16[512,512]{1,0:T(8,128)(2,1)S(1)}, u32[]{:S(2)}, u32[]{:S(2)}) collective-permute-start(bf16[512,512]{1,0:T(8,128)(2,1)S(1)} %shard_map.71.rest_0_), channel_id=1, source_target_pairs={{0,16},{16,0},{1,17},{17,1},{2,18},{18,2},{3,19},{19,3},{4,20},{20... | collective-permute-start | bytes 1572872 | tf_op jit(solution)/shard_map/ppermute | solution.py:360
  48.4 3.5 %collective-permute-done.16.block.rest_0_ = bf16[128,512]{1,0:T(8,128)(2,1)S(1)} collective-permute-done((bf16[128,512]{1,0:T(8,128)(2,1)S(1)}, bf16[128,512]{1,0:T(8,128)(2,1)S(1)}, u32[]{:S(2)}, u32[]{:S(2)}) %collective-permute-start.16) | collective-permute-done | bytes 131104 | tf_op jit(solution)/shard_map/ppermute | solution.py:371
  52.0 2.0 %collective-permute-start.18 = (bf16[64,512]{1,0:T(8,128)(2,1)S(1)}, bf16[64,512]{1,0:T(8,128)(2,1)S(1)}, u32[]{:S(2)}, u32[]{:S(2)}) collective-permute-start(bf16[64,512]{1,0:T(8,128)(2,1)S(1)} %shard_map.72.rest_0_.refs_0_), channel_id=1, source_target_pairs={{4,0},{5,1},{6,2},{7,3},{0,4},{1,5},{2,6},{3,7},{12,8},{13,9},{14,... | collective-permute-start | bytes 196616 | tf_op jit(solution)/shard_map/ppermute | solution.py:28
  54.0 3.3 %collective-permute-start.19 = (bf16[64,512]{1,0:T(8,128)(2,1)S(1)}, bf16[64,512]{1,0:T(8,128)(2,1)S(1)}, u32[]{:S(2)}, u32[]{:S(2)}) collective-permute-start(bf16[64,512]{1,0:T(8,128)(2,1)S(1)} %shard_map.72.rest_0_.refs_0_), channel_id=1, source_target_pairs={{8,0},{9,1},{10,2},{11,3},{12,4},{13,5},{14,6},{15,7},{0,8},{1,9},... | collective-permute-start | bytes 196616 | tf_op jit(solution)/shard_map/ppermute | solution.py:28
  57.3 0.0 collective-permute-start.20
  57.3 0.5 shard_map.76
  57.8 0.6 collective-permute-start.25
  58.4 1.5 %shard_map.73.refs_4_.matrix = bf16[1024,512]{1,0:T(8,128)(2,1)S(1)} custom-call(s32[1]{0:T(128)} %bitcast.1.ckpt, s32[1]{0:T(128)} %bitcast.2.me, s32[4,1,256]{2,1,0:T(1,128)S(1)} %bitcast.19, bf16[1024,1024]{1,0:T(8,128)(2,1)S(1)} %get-tuple-element.26.inverse, bf16[1024,1024]{1,0:T(8,128)(2,1)S(1)} %get-tuple-element.27.chosen, ...), custom_call_target="tpu_custom_call" | custom-call | flops 3221225472 | tf_op jit(solution)/shard_map/pallas_call | solution.py:59
  60.0 3.4 %collective-permute-done.20.refs_3_ = bf16[64,512]{1,0:T(8,128)(2,1)S(1)} collective-permute-done((bf16[64,512]{1,0:T(8,128)(2,1)S(1)}, bf16[64,512]{1,0:T(8,128)(2,1)S(1)}, u32[]{:S(2)}, u32[]{:S(2)}) %collective-permute-start.20) | collective-permute-done | bytes 65568 | tf_op jit(solution)/shard_map/ppermute | solution.py:28
  63.4 1.6 %collective-permute-start.23 = (bf16[4,64,512]{2,1,0:T(8,128)(2,1)S(1)}, bf16[4,64,512]{2,1,0:T(8,128)(2,1)S(1)}, u32[]{:S(2)}, u32[]{:S(2)}) collective-permute-start(bf16[4,64,512]{2,1,0:T(8,128)(2,1)S(1)} %shard_map.74.rest_0_.rest_2_), channel_id=1, source_target_pairs={{2,0},{3,1},{0,2},{1,3},{6,4},{7,5},{4,6},{5,7},{10,8},{11,9},{8,1... | collective-permute-start | bytes 786440 | tf_op jit(solution)/shard_map/ppermute | solution.py:28
  65.0 0.5 shard_map.75
  65.5 0.6 collective-permute-start.21
  66.1 4.2 %collective-permute-done.25.rest_1_.rest_2_ = bf16[320,512]{1,0:T(8,128)(2,1)S(1)} collective-permute-done((bf16[320,512]{1,0:T(8,128)(2,1)S(1)}, bf16[320,512]{1,0:T(8,128)(2,1)S(1)}, u32[]{:S(2)}, u32[]{:S(2)}) %collective-permute-start.25) | collective-permute-done | bytes 327712 | tf_op jit(solution)/shard_map/ppermute | solution.py:360
  70.2 0.1 collective-permute-start.26
  70.3 2.2 %shard_map.78.rest_6_ = f32[2048,512]{1,0:T(8,128)} custom-call(bf16[2048,1024]{1,0:T(8,128)(2,1)S(1)} %bitcast.10, bf16[1024,512]{1,0:T(8,128)(2,1)S(1)} %shard_map.73.refs_4_.matrix, f32[2048,128]{1,0:T(8,128)S(1)} %shard_map.69.weight, bf16[128,512]{1,0:T(8,128)(2,1)S(1)} %collective-permute-done.16.block.rest_0_, ...), custom_call_target="tpu_custom_call" | custom-call | tf_op jit(solution)/shard_map/pallas_call | solution.py:59
  72.5 3.3 %shard_map.79.rest_1_ = f32[2048,512]{1,0:T(8,128)} custom-call(s32[1]{0:T(128)} %bitcast.2.me, bf16[2048,1024]{1,0:T(8,128)(2,1)S(1)} %bitcast.11, bf16[1024,512]{1,0:T(8,128)(2,1)S(1)} %shard_map.73.refs_4_.matrix, f32[2048,128]{1,0:T(8,128)S(1)} %shard_map.69.weight, s32[1,2048]{1,0:T(1,128)S(1)} %bitcast.14, ...), custom_call_target="tpu_custom_call", output_to_operand_aliasing={{}: (11, {})} | custom-call | tf_op jit(solution)/shard_map/pallas_call | solution.py:59
  75.8 0.6 collective-permute-done.21.rest_0_
  76.4 1.3 %shard_map.80 = f32[2048,512]{1,0:T(8,128)} custom-call(bf16[2048,1024]{1,0:T(8,128)(2,1)S(1)} %bitcast.12, bf16[1024,512]{1,0:T(8,128)(2,1)S(1)} %shard_map.73.refs_4_.matrix, f32[2048,128]{1,0:T(8,128)S(1)} %shard_map.69.weight, bf16[320,512]{1,0:T(8,128)(2,1)S(1)} %collective-permute-done.21.rest_0_, ...), custom_call_target="tpu_custom_call", output_to_operand_aliasing={{}: (4, {})} | custom-call | tf_op jit(solution)/shard_map/pallas_call | solution.py:59
  (33 shorter events, 0.1 us)
Async XLA Ops:
  0.0 23.0 %copy-start.1 = (s32[2048]{0:T(1024)S(1)}, s32[2048]{0:T(1024)}, u32[]{:S(2)}) copy-start(s32[2048]{0:T(1024)} %param.10) | copy-start | bytes 24580
  0.0 23.0 %copy-start.2 = (f32[1,16]{1,0:T(1,128)S(1)}, f32[1,16]{1,0:T(1,128)}, u32[]{:S(2)}) copy-start(f32[1,16]{1,0:T(1,128)} %bucket_weight.3) | copy-start | bytes 196
  0.0 31.6 %copy-start.4 = (s32[1024]{0:T(1024)S(1)}, s32[1024]{0:T(1024)}, u32[]{:S(2)}) copy-start(s32[1024]{0:T(1024)} %param.11) | copy-start | bytes 12292
  3.2 28.1 %collective-permute-start.15 = (bf16[464,1024]{1,0:T(8,128)(2,1)}, bf16[464,1024]{1,0:T(8,128)(2,1)S(1)}, u32[]{:S(2)}, u32[]{:S(2)}) collective-permute-start(bf16[464,1024]{1,0:T(8,128)(2,1)} %get-tuple-element.19), channel_id=1, source_target_pairs={{0,16},{16,0},{1,17},{17,1},{2,18},{18,2},{3,19},{19,3},{4,20},{20... | collective-permute-start | bytes 2850824 | tf_op jit(solution)/shard_map/ppermute | solution.py:312
  6.2 14.6 %collective-permute-start = (bf16[2,64,1024]{2,1,0:T(8,128)(2,1)}, bf16[2,64,1024]{2,1,0:T(8,128)(2,1)S(1)}, u32[]{:S(2)}, u32[]{:S(2)}) collective-permute-start(bf16[2,64,1024]{2,1,0:T(8,128)(2,1)} %get-tuple-element.18.rest_0_), channel_id=1, source_target_pairs={{8,0},{9,1},{10,2},{11,3},{12,4},{13,5},{14,6},{15,7},{0,8},{1,9},... | collective-permute-start | bytes 786440 | tf_op jit(solution)/shard_map/ppermute | solution.py:28
  8.8 12.7 %collective-permute-start.8 = (bf16[2,64,1024]{2,1,0:T(8,128)(2,1)}, bf16[2,64,1024]{2,1,0:T(8,128)(2,1)S(1)}, u32[]{:S(2)}, u32[]{:S(2)}) collective-permute-start(bf16[2,64,1024]{2,1,0:T(8,128)(2,1)} %get-tuple-element.18.rest_0_), channel_id=1, source_target_pairs={{4,0},{5,1},{6,2},{7,3},{0,4},{1,5},{2,6},{3,7},{12,8},{13,9},{14,... | collective-permute-start | bytes 786440 | tf_op jit(solution)/shard_map/ppermute | solution.py:28
  10.4 12.6 %collective-permute-start.13 = (bf16[2,64,1024]{2,1,0:T(8,128)(2,1)}, bf16[2,64,1024]{2,1,0:T(8,128)(2,1)S(1)}, u32[]{:S(2)}, u32[]{:S(2)}) collective-permute-start(bf16[2,64,1024]{2,1,0:T(8,128)(2,1)} %get-tuple-element.18.rest_0_), channel_id=1, source_target_pairs={{2,0},{3,1},{0,2},{1,3},{6,4},{7,5},{4,6},{5,7},{10,8},{11,9},{8,1... | collective-permute-start | bytes 786440 | tf_op jit(solution)/shard_map/ppermute | solution.py:28
  11.9 12.2 %collective-permute-start.12 = (bf16[2,64,1024]{2,1,0:T(8,128)(2,1)}, bf16[2,64,1024]{2,1,0:T(8,128)(2,1)S(1)}, u32[]{:S(2)}, u32[]{:S(2)}) collective-permute-start(bf16[2,64,1024]{2,1,0:T(8,128)(2,1)} %get-tuple-element.18.rest_0_), channel_id=1, source_target_pairs={{1,0},{0,1},{3,2},{2,3},{5,4},{4,5},{7,6},{6,7},{9,8},{8,9},{11,10... | collective-permute-start | bytes 786440 | tf_op jit(solution)/shard_map/ppermute | solution.py:28
  20.8 7.2 %collective-permute-start.1 = (bf16[2,64,1024]{2,1,0:T(8,128)(2,1)S(1)}, bf16[2,64,1024]{2,1,0:T(8,128)(2,1)S(1)}, u32[]{:S(2)}, u32[]{:S(2)}) collective-permute-start(bf16[2,64,1024]{2,1,0:T(8,128)(2,1)S(1)} %collective-permute-done.rest_0_), channel_id=1, source_target_pairs={{4,0},{5,1},{6,2},{7,3},{0,4},{1,5},{2,6},{3,7},{12,8},{13,9},{14,... | collective-permute-start | bytes 786440 | tf_op jit(solution)/shard_map/ppermute | solution.py:28
  21.5 8.3 %collective-permute-start.10 = (bf16[2,64,1024]{2,1,0:T(8,128)(2,1)S(1)}, bf16[2,64,1024]{2,1,0:T(8,128)(2,1)S(1)}, u32[]{:S(2)}, u32[]{:S(2)}) collective-permute-start(bf16[2,64,1024]{2,1,0:T(8,128)(2,1)S(1)} %collective-permute-done.8.rest_0_), channel_id=1, source_target_pairs={{2,0},{3,1},{0,2},{1,3},{6,4},{7,5},{4,6},{5,7},{10,8},{11,9},{8,1... | collective-permute-start | bytes 786440 | tf_op jit(solution)/shard_map/ppermute | solution.py:28
  23.0 6.8 %collective-permute-start.14 = (bf16[2,64,1024]{2,1,0:T(8,128)(2,1)S(1)}, bf16[2,64,1024]{2,1,0:T(8,128)(2,1)S(1)}, u32[]{:S(2)}, u32[]{:S(2)}) collective-permute-start(bf16[2,64,1024]{2,1,0:T(8,128)(2,1)S(1)} %collective-permute-done.13.rest_2_), channel_id=1, source_target_pairs={{1,0},{0,1},{3,2},{2,3},{5,4},{4,5},{7,6},{6,7},{9,8},{8,9},{11,10... | collective-permute-start | bytes 786440 | tf_op jit(solution)/shard_map/ppermute | solution.py:28
  24.1 33.7 %collective-permute-start.17 = (bf16[384,1024]{1,0:T(8,128)(2,1)}, bf16[384,1024]{1,0:T(8,128)(2,1)S(1)}, u32[]{:S(2)}, u32[]{:S(2)}) collective-permute-start(bf16[384,1024]{1,0:T(8,128)(2,1)} %get-tuple-element.30), channel_id=1, source_target_pairs={{0,16},{16,0},{1,17},{17,1},{2,18},{18,2},{3,19},{19,3},{4,20},{20... | collective-permute-start | bytes 2359304 | tf_op jit(solution)/shard_map/ppermute | solution.py:312
  28.0 9.2 %collective-permute-start.6 = (bf16[2,64,1024]{2,1,0:T(8,128)(2,1)S(1)}, bf16[2,64,1024]{2,1,0:T(8,128)(2,1)S(1)}, u32[]{:S(2)}, u32[]{:S(2)}) collective-permute-start(bf16[2,64,1024]{2,1,0:T(8,128)(2,1)S(1)} %collective-permute-done.rest_0_), channel_id=1, source_target_pairs={{2,0},{3,1},{0,2},{1,3},{6,4},{7,5},{4,6},{5,7},{10,8},{11,9},{8,1... | collective-permute-start | bytes 786440 | tf_op jit(solution)/shard_map/ppermute | solution.py:28
  29.8 7.3 %collective-permute-start.9 = (bf16[2,64,1024]{2,1,0:T(8,128)(2,1)S(1)}, bf16[2,64,1024]{2,1,0:T(8,128)(2,1)S(1)}, u32[]{:S(2)}, u32[]{:S(2)}) collective-permute-start(bf16[2,64,1024]{2,1,0:T(8,128)(2,1)S(1)} %collective-permute-done.8.rest_0_), channel_id=1, source_target_pairs={{1,0},{0,1},{3,2},{2,3},{5,4},{4,5},{7,6},{6,7},{9,8},{8,9},{11,10... | collective-permute-start | bytes 786440 | tf_op jit(solution)/shard_map/ppermute | solution.py:28
  29.8 10.9 %collective-permute-start.3 = (bf16[2,64,1024]{2,1,0:T(8,128)(2,1)S(1)}, bf16[2,64,1024]{2,1,0:T(8,128)(2,1)S(1)}, u32[]{:S(2)}, u32[]{:S(2)}) collective-permute-start(bf16[2,64,1024]{2,1,0:T(8,128)(2,1)S(1)} %collective-permute-done.1.rest_0_), channel_id=1, source_target_pairs={{2,0},{3,1},{0,2},{1,3},{6,4},{7,5},{4,6},{5,7},{10,8},{11,9},{8,1... | collective-permute-start | bytes 786440 | tf_op jit(solution)/shard_map/ppermute | solution.py:28
  31.3 9.3 %collective-permute-start.11 = (bf16[2,64,1024]{2,1,0:T(8,128)(2,1)S(1)}, bf16[2,64,1024]{2,1,0:T(8,128)(2,1)S(1)}, u32[]{:S(2)}, u32[]{:S(2)}) collective-permute-start(bf16[2,64,1024]{2,1,0:T(8,128)(2,1)S(1)} %collective-permute-done.10.rest_2_), channel_id=1, source_target_pairs={{1,0},{0,1},{3,2},{2,3},{5,4},{4,5},{7,6},{6,7},{9,8},{8,9},{11,10... | collective-permute-start | bytes 786440 | tf_op jit(solution)/shard_map/ppermute | solution.py:28
  31.6 1.0 %copy-start.3 = (bf16[2,64,1024]{2,1,0:T(8,128)(2,1)S(1)}, bf16[2,64,1024]{2,1,0:T(8,128)(2,1)}, u32[]{:S(2)}) copy-start(bf16[2,64,1024]{2,1,0:T(8,128)(2,1)} %get-tuple-element.18.rest_0_) | copy-start | bytes 786436
  37.1 4.9 %collective-permute-start.5 = (bf16[2,64,1024]{2,1,0:T(8,128)(2,1)S(1)}, bf16[2,64,1024]{2,1,0:T(8,128)(2,1)S(1)}, u32[]{:S(2)}, u32[]{:S(2)}) collective-permute-start(bf16[2,64,1024]{2,1,0:T(8,128)(2,1)S(1)} %collective-permute-done.rest_0_), channel_id=1, source_target_pairs={{1,0},{0,1},{3,2},{2,3},{5,4},{4,5},{7,6},{6,7},{9,8},{8,9},{11,10... | collective-permute-start | bytes 786440 | tf_op jit(solution)/shard_map/ppermute | solution.py:28
  37.2 5.9 %collective-permute-start.2 = (bf16[2,64,1024]{2,1,0:T(8,128)(2,1)S(1)}, bf16[2,64,1024]{2,1,0:T(8,128)(2,1)S(1)}, u32[]{:S(2)}, u32[]{:S(2)}) collective-permute-start(bf16[2,64,1024]{2,1,0:T(8,128)(2,1)S(1)} %collective-permute-done.1.rest_0_), channel_id=1, source_target_pairs={{1,0},{0,1},{3,2},{2,3},{5,4},{4,5},{7,6},{6,7},{9,8},{8,9},{11,10... | collective-permute-start | bytes 786440 | tf_op jit(solution)/shard_map/ppermute | solution.py:28
  40.7 1.5 %collective-permute-start.7 = (bf16[2,64,1024]{2,1,0:T(8,128)(2,1)S(1)}, bf16[2,64,1024]{2,1,0:T(8,128)(2,1)S(1)}, u32[]{:S(2)}, u32[]{:S(2)}) collective-permute-start(bf16[2,64,1024]{2,1,0:T(8,128)(2,1)S(1)} %collective-permute-done.6.rest_2_), channel_id=1, source_target_pairs={{1,0},{0,1},{3,2},{2,3},{5,4},{4,5},{7,6},{6,7},{9,8},{8,9},{11,10... | collective-permute-start | bytes 786440 | tf_op jit(solution)/shard_map/ppermute | solution.py:28
  40.7 2.4 %collective-permute-start.4 = (bf16[2,64,1024]{2,1,0:T(8,128)(2,1)S(1)}, bf16[2,64,1024]{2,1,0:T(8,128)(2,1)S(1)}, u32[]{:S(2)}, u32[]{:S(2)}) collective-permute-start(bf16[2,64,1024]{2,1,0:T(8,128)(2,1)S(1)} %collective-permute-done.3.rest_2_), channel_id=1, source_target_pairs={{1,0},{0,1},{3,2},{2,3},{5,4},{4,5},{7,6},{6,7},{9,8},{8,9},{11,10... | collective-permute-start | bytes 786440 | tf_op jit(solution)/shard_map/ppermute | solution.py:28
  43.1 2.2 %copy-start = (bf16[1,2048,1024]{2,1,0:T(8,128)(2,1)S(1)}, bf16[1,2048,1024]{2,1,0:T(8,128)(2,1)}, u32[]{:S(2)}) copy-start(bf16[1,2048,1024]{2,1,0:T(8,128)(2,1)} %param.6) | copy-start | bytes 12582916
  45.6 6.4 %collective-permute-start.16 = (bf16[128,512]{1,0:T(8,128)(2,1)S(1)}, bf16[128,512]{1,0:T(8,128)(2,1)S(1)}, u32[]{:S(2)}, u32[]{:S(2)}) collective-permute-start(bf16[128,512]{1,0:T(8,128)(2,1)S(1)} %shard_map.70.rest_0_), channel_id=1, source_target_pairs={{0,16},{16,0},{1,17},{17,1},{2,18},{18,2},{3,19},{19,3},{4,20},{20... | collective-permute-start | bytes 393224 | tf_op jit(solution)/shard_map/ppermute | solution.py:371
  46.9 23.4 %collective-permute-start.24 = (bf16[512,512]{1,0:T(8,128)(2,1)S(1)}, bf16[512,512]{1,0:T(8,128)(2,1)S(1)}, u32[]{:S(2)}, u32[]{:S(2)}) collective-permute-start(bf16[512,512]{1,0:T(8,128)(2,1)S(1)} %shard_map.71.rest_0_), channel_id=1, source_target_pairs={{0,16},{16,0},{1,17},{17,1},{2,18},{18,2},{3,19},{19,3},{4,20},{20... | collective-permute-start | bytes 1572872 | tf_op jit(solution)/shard_map/ppermute | solution.py:360
  52.0 8.0 %collective-permute-start.18 = (bf16[64,512]{1,0:T(8,128)(2,1)S(1)}, bf16[64,512]{1,0:T(8,128)(2,1)S(1)}, u32[]{:S(2)}, u32[]{:S(2)}) collective-permute-start(bf16[64,512]{1,0:T(8,128)(2,1)S(1)} %shard_map.72.rest_0_.refs_0_), channel_id=1, source_target_pairs={{4,0},{5,1},{6,2},{7,3},{0,4},{1,5},{2,6},{3,7},{12,8},{13,9},{14,... | collective-permute-start | bytes 196616 | tf_op jit(solution)/shard_map/ppermute | solution.py:28
  54.0 6.0 %collective-permute-start.19 = (bf16[64,512]{1,0:T(8,128)(2,1)S(1)}, bf16[64,512]{1,0:T(8,128)(2,1)S(1)}, u32[]{:S(2)}, u32[]{:S(2)}) collective-permute-start(bf16[64,512]{1,0:T(8,128)(2,1)S(1)} %shard_map.72.rest_0_.refs_0_), channel_id=1, source_target_pairs={{8,0},{9,1},{10,2},{11,3},{12,4},{13,5},{14,6},{15,7},{0,8},{1,9},... | collective-permute-start | bytes 196616 | tf_op jit(solution)/shard_map/ppermute | solution.py:28
  57.3 6.1 %collective-permute-start.20 = (bf16[64,512]{1,0:T(8,128)(2,1)S(1)}, bf16[64,512]{1,0:T(8,128)(2,1)S(1)}, u32[]{:S(2)}, u32[]{:S(2)}) collective-permute-start(bf16[64,512]{1,0:T(8,128)(2,1)S(1)} %shard_map.72.rest_0_.refs_0_), channel_id=1, source_target_pairs={{12,0},{13,1},{14,2},{15,3},{8,4},{9,5},{10,6},{11,7},{4,8},{5,9},... | collective-permute-start | bytes 196616 | tf_op jit(solution)/shard_map/ppermute | solution.py:28
  57.8 12.4 %collective-permute-start.25 = (bf16[320,512]{1,0:T(8,128)(2,1)S(1)}, bf16[320,512]{1,0:T(8,128)(2,1)S(1)}, u32[]{:S(2)}, u32[]{:S(2)}) collective-permute-start(bf16[320,512]{1,0:T(8,128)(2,1)S(1)} %shard_map.76), channel_id=1, source_target_pairs={{0,16},{16,0},{1,17},{17,1},{2,18},{18,2},{3,19},{19,3},{4,20},{20... | collective-permute-start | bytes 983048 | tf_op jit(solution)/shard_map/ppermute | solution.py:360
  63.4 6.9 %collective-permute-start.23 = (bf16[4,64,512]{2,1,0:T(8,128)(2,1)S(1)}, bf16[4,64,512]{2,1,0:T(8,128)(2,1)S(1)}, u32[]{:S(2)}, u32[]{:S(2)}) collective-permute-start(bf16[4,64,512]{2,1,0:T(8,128)(2,1)S(1)} %shard_map.74.rest_0_.rest_2_), channel_id=1, source_target_pairs={{2,0},{3,1},{0,2},{1,3},{6,4},{7,5},{4,6},{5,7},{10,8},{11,9},{8,1... | collective-permute-start | bytes 786440 | tf_op jit(solution)/shard_map/ppermute | solution.py:28
  65.5 11.0 %collective-permute-start.21 = (bf16[320,512]{1,0:T(8,128)(2,1)S(1)}, bf16[320,512]{1,0:T(8,128)(2,1)S(1)}, u32[]{:S(2)}, u32[]{:S(2)}) collective-permute-start(bf16[320,512]{1,0:T(8,128)(2,1)S(1)} %shard_map.75), channel_id=1, source_target_pairs={{0,16},{16,0},{1,17},{17,1},{2,18},{18,2},{3,19},{19,3},{4,20},{20... | collective-permute-start | bytes 983048 | tf_op jit(solution)/shard_map/ppermute | solution.py:360
  66.1 6.5 %collective-permute-start.22 = (bf16[4,64,512]{2,1,0:T(8,128)(2,1)S(1)}, bf16[4,64,512]{2,1,0:T(8,128)(2,1)S(1)}, u32[]{:S(2)}, u32[]{:S(2)}) collective-permute-start(bf16[4,64,512]{2,1,0:T(8,128)(2,1)S(1)} %shard_map.74.rest_0_.rest_2_), channel_id=1, source_target_pairs={{1,0},{0,1},{3,2},{2,3},{5,4},{4,5},{7,6},{6,7},{9,8},{8,9},{11,10... | collective-permute-start | bytes 786440 | tf_op jit(solution)/shard_map/ppermute | solution.py:28
  70.2 2.3 %collective-permute-start.26 = (bf16[4,64,512]{2,1,0:T(8,128)(2,1)S(1)}, bf16[4,64,512]{2,1,0:T(8,128)(2,1)S(1)}, u32[]{:S(2)}, u32[]{:S(2)}) collective-permute-start(bf16[4,64,512]{2,1,0:T(8,128)(2,1)S(1)} %shard_map.77.rest_4_), channel_id=1, source_target_pairs={{1,0},{0,1},{3,2},{2,3},{5,4},{4,5},{7,6},{6,7},{9,8},{8,9},{11,10... | collective-permute-start | bytes 786440 | tf_op jit(solution)/shard_map/ppermute | solution.py:28

commit v5 on v4

--- a/solution.py
+++ b/solution.py
@@ -166,12 +166,13 @@
 
 def send_transform_kernel(ensemble, masks, ckpt, me, order, *rest):
     blocks = rest[: len(masks)]
-    inverse, chosen, test, out = rest[-4:]
+    inverse, chosen, test, out, shard = rest[-5:]
     outer = unpack(masks, me, blocks, test, inverse)
     width = chosen.shape[0] // ensemble
     for j in range(1, ensemble):
         picked = choose(ensemble, j, outer, ckpt, order, test)
         out[j - 1] = transformed(inverse, chosen[pl.ds(j * width, width), :] + picked)
+    shard[...] = out[0, aligned(me[0], shard.shape[0]), :]
 
 
 def own_transform_kernel(ensemble, masks, ckpt, me, order, inverse, chosen, test, *rest):
@@ -189,15 +190,6 @@
 def send_kernel(first, length, j, train, matrices, weight, *rest):
     rows = pl.ds(first, length)
     rest[-1][:length, :] = scaled(train[rows, :], matrices[j], weight[rows, :])
-
-
-def first_kernel(first, length, me, train, matrices, weight, out):
-    send_kernel(first, length, 0, train, matrices, weight, out)
-    out[length:, :] = matrices[0, aligned(me[0], out.shape[0] - length), :]
-
-
-def tail_kernel(first, block, *rest):
-    rest[-1][...] = block[first:, :]
 
 
 def relay_kernel(block, *rest):
@@ -284,10 +276,10 @@
     share = size // n
     unit = rows // 32
     paired = ensemble == 2
-    batches = [7, 6] if paired else []
+    batches = [7, 7] if paired else []
     featured = sum(batches)
-    parts = [1, 8, 5, 5] if paired else [16, 16]
-    flying = 2
+    parts = [7, 6, 5] if paired else [16, 16]
+    flying = 1 if paired else 2
     table_rows = -(-bucket_weight.shape[1] // 16) * 16
 
     ckpt = lax.axis_index("ckpt").astype(jnp.int32).reshape(1)
@@ -295,7 +287,10 @@
     order = test_order.reshape(len(outers), 1, count // len(outers))
     bucket = bucket.reshape(1, rows)
 
-    sent = [shape((part * unit + (0 if i else table_rows), size)) for i, part in enumerate(batches)]
+    sent = [
+        shape((part * unit + (0 if i else table_rows), size))
+        for i, part in enumerate(batches)
+    ]
     steps = 2
     own, *features = call(
         functools.partial(start_kernel, steps),
@@ -326,7 +321,7 @@
     state = []
     for masks, blocks in groups[:-1]:
         operands = [ckpt, me, order, *blocks, *state]
-        after = features[:1] if not state else []
+        after = features[:1] if not state else [weight]
         state = call(
             functools.partial(part_kernel, ensemble, masks),
             [shape((size, size)), shape((count, size))],
@@ -336,14 +331,14 @@
             flops=4 * half, moved=4 * size * size,
         )
     masks, blocks = groups[-1]
-    inverse, chosen, test, matrices = call(
+    starts = [featured + sum(parts[:q]) for q in range(len(parts))]
+    inverse, chosen, test, matrices, shard = call(
         functools.partial(send_transform_kernel, ensemble, masks),
         [
             shape((size, size)), shape((count, size)), shape((count // len(outers), size)),
-            shape((ensemble - 1, size, width)),
+            shape((ensemble - 1, size, width)), shape((share, width)),
         ],
-        [ckpt, me, order, *blocks, *state],
-        [SMEM] * 2 + [VMEM] * (3 + len(blocks)),
+        [ckpt, me, order, *blocks, *state], [SMEM] * 2 + [VMEM] * (3 + len(blocks)),
         aliases={3 + len(blocks): 0, 4 + len(blocks): 1},
         flops=3 * half, moved=4 * size * size, mib=12,
     )
@@ -360,24 +355,14 @@
             got.append(lax.ppermute(tile, "ckpt", ahead(k, ensemble)))
         return got, after
 
-    starts = [featured + sum(parts[:q]) for q in range(len(parts))]
     received, after = [], []
     if paired:
-        tile = call(
-            functools.partial(first_kernel, starts[0] * unit, parts[0] * unit),
-            shape((parts[0] * unit + share, width)),
-            (me, train, matrices, weight), [SMEM] + [VMEM] * 3,
-        )
-        received.append([lax.ppermute(tile, "ckpt", ahead(1, ensemble))])
-        after = [tile]
-    for q in range(len(received), min(flying, len(parts))):
+        shard2 = lax.ppermute(shard, "ckpt", ahead(1, ensemble))
+    for q in range(min(flying, len(parts))):
         got, after = send(starts[q], parts[q], after)
         received.append(got)
     if paired:
-        piece = call(
-            functools.partial(tail_kernel, parts[0] * unit), shape((share, width)),
-            (*received[0], *after), [VMEM, ANY],
-        )
+        piece = call(relay_kernel, shape(shard2.shape), (shard2, *after), [VMEM, ANY])
         after = [piece]
 
     matrix = call(
@@ -400,7 +385,7 @@
         for bit in inner_bits:
             held += [(mask ^ bit, swap(b, bit, n)) for mask, b in held]
         held = held[:1] + [
-            (mask, call(relay_kernel, shape(b.shape), (b, *received[1], *received[2]), [VMEM, ANY, ANY]))
+            (mask, call(relay_kernel, shape(b.shape), (b, *received[0], *received[1]), [VMEM, ANY, ANY]))
             for mask, b in held[1:]
         ]
         for bit in core_bits:
@@ -421,7 +406,7 @@
             aliases={len(operands): 0} if held else None, mib=24,
         )
 
-    together = [[0, 1, 2], [], [3]] if paired else [[q] for q in range(len(parts))]
+    together = [[0, 1], [], [2]] if paired else [[q] for q in range(len(parts))]
     for chunks in together:
         if chunks:
             part = sum(parts[q] for q in chunks)

time: 78 us -> 75.5 us (0.968)
  starting transfers between devices: 26.2 us -> 24.3 us
    ppermute x21, waiting for transfers between devices: 22.9 us -> 27.4 us  [swap(): return lax.ppermute(block, 'train', [(d ^ mask, d) for d in range(n)])]
    ppermute x3, waiting for transfers between devices: 4.76 us -> 0.83 us  [send(): got.append(lax.ppermute(tile, 'ckpt', ahead(k, ensemble)))]
    ppermute x21, starting transfers between devices: 19.2 us -> 15.3 us  [swap(): return lax.ppermute(block, 'train', [(d ^ mask, d) for d in range(n)])]
    ppermute x3, starting transfers between devices: 2.75 us -> 3.77 us  [send(): got.append(lax.ppermute(tile, 'ckpt', ahead(k, ensemble)))]
    ppermute x1, starting transfers between devices: 0.6 us -> 1.56 us  [shards(): shard2 = lax.ppermute(shard, 'ckpt', ahead(1, ensemble))]
    pallas_call x17 -> x16, Pallas kernels: 18.7 us -> 18.6 us  [call(): pl.pallas_call(kernel, out_shape=outs, in_specs=specs, out_specs=out_spec...]
  transfers between devices with their start and end apart: 27 -> 27, of which waited for: 10 -> 12; matrix products, arithmetic and copies ran while one was open for 0% -> 0% of each run, Pallas kernels for 18% -> 19%
where the time goes in v5:
time: 75.5 us; the launch traced here: 75.2 us
  waiting for transfers between devices  31.2 us (41%)
  starting transfers between devices  24.3 us (32%)
  Pallas kernels  18.6 us (25%)
  local copies, waits for them, and re-layouts  0.97 us (1%)
    ppermute x21, waiting for transfers between devices, swap(): return lax.ppermute(block, 'train', [(d ^ mask, d) for d in range(n)])  27.4 us
    pallas_call x16, Pallas kernels, call(): pl.pallas_call(kernel, out_shape=outs, in_specs=specs, out_specs=out_spec...  18.6 us
    ppermute x21, starting transfers between devices, swap(): return lax.ppermute(block, 'train', [(d ^ mask, d) for d in range(n)])  15.3 us
    ppermute x3, starting transfers between devices, send(): got.append(lax.ppermute(tile, 'ckpt', ahead(k, ensemble)))  3.77 us
    ppermute x2, starting transfers between devices, shards(): lax.ppermute(batch, 'ckpt', ahead(1, ensemble))  3.6 us
    ppermute x1, waiting for transfers between devices, shards(): shard2 = lax.ppermute(shard, 'ckpt', ahead(1, ensemble))  2.94 us
    ppermute x1, starting transfers between devices, shards(): shard2 = lax.ppermute(shard, 'ckpt', ahead(1, ensemble))  1.56 us
  transfers between devices with their start and end apart: 27, of which 12 were waited for; matrix products, arithmetic and copies ran while one was open for 0% of the time, Pallas kernels for 19%

profile of v5, /device:TPU:0, one launch (start us, length us, event | category | flops | bytes accessed | tf_op | source)
XLA Modules:
  0.0 75.2 jit_solution(3274232520321241905)
XLA Ops:
  0.0 3.3 %shard_map.64 = (bf16[2,64,1024]{2,1,0:T(8,128)(2,1)}, bf16[464,1024]{1,0:T(8,128)(2,1)}, bf16[448,1024]{1,0:T(8,128)(2,1)}) custom-call(bf16[1,64,1024]{2,1,0:T(8,128)(2,1)} %test_feat.1, bf16[1,64,1024]{2,1,0:T(8,128)(2,1)} %kernel_inv.1, bf16[2048,1024]{1,0:T(8,128)(2,1)} %bitcast.5, f32[1,16]{1,0:T(1,128)} %bucket_weight.3), custom_call_target="tpu_custom_call" | custom-call | tf_op jit(solution)/shard_map/pallas_call | solution.py:59
  3.3 3.0 %collective-permute-start.15 = (bf16[464,1024]{1,0:T(8,128)(2,1)}, bf16[464,1024]{1,0:T(8,128)(2,1)S(1)}, u32[]{:S(2)}, u32[]{:S(2)}) collective-permute-start(bf16[464,1024]{1,0:T(8,128)(2,1)} %get-tuple-element.20), channel_id=1, source_target_pairs={{0,16},{16,0},{1,17},{17,1},{2,18},{18,2},{3,19},{19,3},{4,20},{20... | collective-permute-start | bytes 2850824 | tf_op jit(solution)/shard_map/ppermute | solution.py:307
  6.3 1.5 %collective-permute-start.13 = (bf16[2,64,1024]{2,1,0:T(8,128)(2,1)}, bf16[2,64,1024]{2,1,0:T(8,128)(2,1)S(1)}, u32[]{:S(2)}, u32[]{:S(2)}) collective-permute-start(bf16[2,64,1024]{2,1,0:T(8,128)(2,1)} %get-tuple-element.19.rest_0_), channel_id=1, source_target_pairs={{2,0},{3,1},{0,2},{1,3},{6,4},{7,5},{4,6},{5,7},{10,8},{11,9},{8,1... | collective-permute-start | bytes 786440 | tf_op jit(solution)/shard_map/ppermute | solution.py:28
  7.8 1.6 %collective-permute-start.8 = (bf16[2,64,1024]{2,1,0:T(8,128)(2,1)}, bf16[2,64,1024]{2,1,0:T(8,128)(2,1)S(1)}, u32[]{:S(2)}, u32[]{:S(2)}) collective-permute-start(bf16[2,64,1024]{2,1,0:T(8,128)(2,1)} %get-tuple-element.19.rest_0_), channel_id=1, source_target_pairs={{4,0},{5,1},{6,2},{7,3},{0,4},{1,5},{2,6},{3,7},{12,8},{13,9},{14,... | collective-permute-start | bytes 786440 | tf_op jit(solution)/shard_map/ppermute | solution.py:28
  9.4 2.6 %collective-permute-start = (bf16[2,64,1024]{2,1,0:T(8,128)(2,1)}, bf16[2,64,1024]{2,1,0:T(8,128)(2,1)S(1)}, u32[]{:S(2)}, u32[]{:S(2)}) collective-permute-start(bf16[2,64,1024]{2,1,0:T(8,128)(2,1)} %get-tuple-element.19.rest_0_), channel_id=1, source_target_pairs={{8,0},{9,1},{10,2},{11,3},{12,4},{13,5},{14,6},{15,7},{0,8},{1,9},... | collective-permute-start | bytes 786440 | tf_op jit(solution)/shard_map/ppermute | solution.py:28
  12.0 2.3 %collective-permute-done.13.rest_2_ = bf16[2,64,1024]{2,1,0:T(8,128)(2,1)S(1)} collective-permute-done((bf16[2,64,1024]{2,1,0:T(8,128)(2,1)}, bf16[2,64,1024]{2,1,0:T(8,128)(2,1)S(1)}, u32[]{:S(2)}, u32[]{:S(2)}) %collective-permute-start.13) | collective-permute-done | bytes 262176 | tf_op jit(solution)/shard_map/ppermute | solution.py:28
  14.3 0.0 collective-permute-start.14
  14.3 6.7 %collective-permute-done.8.rest_0_ = bf16[2,64,1024]{2,1,0:T(8,128)(2,1)S(1)} collective-permute-done((bf16[2,64,1024]{2,1,0:T(8,128)(2,1)}, bf16[2,64,1024]{2,1,0:T(8,128)(2,1)S(1)}, u32[]{:S(2)}, u32[]{:S(2)}) %collective-permute-start.8) | collective-permute-done | bytes 262176 | tf_op jit(solution)/shard_map/ppermute | solution.py:28
  21.0 0.5 collective-permute-start.10
  21.5 2.0 %collective-permute-done.rest_0_ = bf16[2,64,1024]{2,1,0:T(8,128)(2,1)S(1)} collective-permute-done((bf16[2,64,1024]{2,1,0:T(8,128)(2,1)}, bf16[2,64,1024]{2,1,0:T(8,128)(2,1)S(1)}, u32[]{:S(2)}, u32[]{:S(2)}) %collective-permute-start) | collective-permute-done | bytes 262176 | tf_op jit(solution)/shard_map/ppermute | solution.py:28
  23.5 0.3 collective-permute-start.1
  23.8 1.0 %shard_map.66.rest_6_.weight = f32[2048,128]{1,0:T(8,128)S(1)} custom-call(s32[1,2048]{1,0:T(1,128)S(1)} %bitcast.12, f32[1,16]{1,0:T(1,128)S(1)} %copy-done.2), custom_call_target="tpu_custom_call" | custom-call | tf_op jit(solution)/shard_map/pallas_call | solution.py:59
  24.9 0.6 collective-permute-start.17
  25.5 0.0 collective-permute-start.9
  25.5 1.9 %collective-permute-done.10.rest_2_ = bf16[2,64,1024]{2,1,0:T(8,128)(2,1)S(1)} collective-permute-done((bf16[2,64,1024]{2,1,0:T(8,128)(2,1)S(1)}, bf16[2,64,1024]{2,1,0:T(8,128)(2,1)S(1)}, u32[]{:S(2)}, u32[]{:S(2)}) %collective-permute-start.10) | collective-permute-done | bytes 262176 | tf_op jit(solution)/shard_map/ppermute | solution.py:28
  27.4 0.5 collective-permute-start.6
  27.9 2.0 %collective-permute-done.1.rest_0_ = bf16[2,64,1024]{2,1,0:T(8,128)(2,1)S(1)} collective-permute-done((bf16[2,64,1024]{2,1,0:T(8,128)(2,1)S(1)}, bf16[2,64,1024]{2,1,0:T(8,128)(2,1)S(1)}, u32[]{:S(2)}, u32[]{:S(2)}) %collective-permute-start.1) | collective-permute-done | bytes 262176 | tf_op jit(solution)/shard_map/ppermute | solution.py:28
  29.9 0.6 collective-permute-start.3
  30.5 0.9 %copy-done.3 = bf16[2,64,1024]{2,1,0:T(8,128)(2,1)S(1)} copy-done((bf16[2,64,1024]{2,1,0:T(8,128)(2,1)S(1)}, bf16[2,64,1024]{2,1,0:T(8,128)(2,1)}, u32[]{:S(2)}) %copy-start.3) | copy-done | bytes 262168
  31.4 0.8 %shard_map.65 = (bf16[1024,1024]{1,0:T(8,128)(2,1)S(1)}, bf16[1024,1024]{1,0:T(8,128)(2,1)S(1)}) custom-call(s32[1]{0:T(128)} %bitcast.1.ckpt, s32[1]{0:T(128)} %bitcast.2.me, s32[4,1,256]{2,1,0:T(1,128)S(1)} %bitcast.14, bf16[2,64,1024]{2,1,0:T(8,128)(2,1)S(1)} %copy-done.3, bf16[2,64,1024]{2,1,0:T(8,128)(2,1)S(1)} %collective-permute-done.12.rest_1_, ...), custom_call_target="tpu_custom_call" | custom-call | flops 4294967296 | bytes 4194304 | tf_op jit(solution)/shard_map/pallas_call | solution.py:59
  32.3 0.2 collective-permute-start.5
  32.5 2.9 %collective-permute-done.6.rest_2_ = bf16[2,64,1024]{2,1,0:T(8,128)(2,1)S(1)} collective-permute-done((bf16[2,64,1024]{2,1,0:T(8,128)(2,1)S(1)}, bf16[2,64,1024]{2,1,0:T(8,128)(2,1)S(1)}, u32[]{:S(2)}, u32[]{:S(2)}) %collective-permute-start.6) | collective-permute-done | bytes 262176 | tf_op jit(solution)/shard_map/ppermute | solution.py:28
  35.4 0.5 collective-permute-start.7
  35.9 3.9 %collective-permute-done.3.rest_2_ = bf16[2,64,1024]{2,1,0:T(8,128)(2,1)S(1)} collective-permute-done((bf16[2,64,1024]{2,1,0:T(8,128)(2,1)S(1)}, bf16[2,64,1024]{2,1,0:T(8,128)(2,1)S(1)}, u32[]{:S(2)}, u32[]{:S(2)}) %collective-permute-start.3) | collective-permute-done | bytes 262176 | tf_op jit(solution)/shard_map/ppermute | solution.py:28
  39.8 0.8 %shard_map.67 = (bf16[1024,1024]{1,0:T(8,128)(2,1)S(1)}, bf16[1024,1024]{1,0:T(8,128)(2,1)S(1)}) custom-call(s32[1]{0:T(128)} %bitcast.1.ckpt, s32[1]{0:T(128)} %bitcast.2.me, s32[4,1,256]{2,1,0:T(1,128)S(1)} %bitcast.15, bf16[2,64,1024]{2,1,0:T(8,128)(2,1)S(1)} %collective-permute-done.8.rest_0_, ...), custom_call_target="tpu_custom_call", output_to_operand_aliasing={{0}: (7, {}), {1}: (8, {})} | custom-call | flops 4294967296 | bytes 4194304 | tf_op jit(solution)/shard_map/pallas_call | solution.py:59
  40.7 0.8 %shard_map.68 = (bf16[1024,1024]{1,0:T(8,128)(2,1)S(1)}, bf16[1024,1024]{1,0:T(8,128)(2,1)S(1)}) custom-call(s32[1]{0:T(128)} %bitcast.1.ckpt, s32[1]{0:T(128)} %bitcast.2.me, s32[4,1,256]{2,1,0:T(1,128)S(1)} %bitcast.16, bf16[2,64,1024]{2,1,0:T(8,128)(2,1)S(1)} %collective-permute-done.rest_0_, ...), custom_call_target="tpu_custom_call", output_to_operand_aliasing={{0}: (7, {}), {1}: (8, {})} | custom-call | flops 4294967296 | bytes 4194304 | tf_op jit(solution)/shard_map/pallas_call | solution.py:59
  41.5 0.0 copy-start
  41.6 1.6 %shard_map.69 = (bf16[1024,1024]{1,0:T(8,128)(2,1)S(1)}, bf16[1024,1024]{1,0:T(8,128)(2,1)S(1)}, bf16[256,1024]{1,0:T(8,128)(2,1)S(1)}, bf16[1,1024,512]{2,1,0:T(8,128)(2,1)S(1)}, bf16[64,512]{1,0:T(8,128)(2,1)S(1)}) custom-call(s32[1]{0:T(128)} %bitcast.1.ckpt, s32[1]{0:T(128)} %bitcast.2.me, ...), custom_call_target="tpu_custom_call", output_to_operand_aliasing={{0}: (7, {}), {1}: (8, {})} | custom-call | flops 3221225472 | bytes 4194304 | tf_op jit(solution)/shard_map/pallas_call | solution.py:59
  43.2 1.6 %collective-permute-start.16 = (bf16[64,512]{1,0:T(8,128)(2,1)S(1)}, bf16[64,512]{1,0:T(8,128)(2,1)S(1)}, u32[]{:S(2)}, u32[]{:S(2)}) collective-permute-start(bf16[64,512]{1,0:T(8,128)(2,1)S(1)} %get-tuple-element.30), channel_id=1, source_target_pairs={{0,16},{16,0},{1,17},{17,1},{2,18},{18,2},{3,19},{19,3},{4,20},{20... | collective-permute-start | bytes 196616 | tf_op jit(solution)/shard_map/ppermute | solution.py:360
  44.7 0.6 shard_map.70.rest_0_
  45.4 0.6 collective-permute-start.24
  46.0 2.9 %collective-permute-done.16.block = bf16[64,512]{1,0:T(8,128)(2,1)S(1)} collective-permute-done((bf16[64,512]{1,0:T(8,128)(2,1)S(1)}, bf16[64,512]{1,0:T(8,128)(2,1)S(1)}, u32[]{:S(2)}, u32[]{:S(2)}) %collective-permute-start.16) | collective-permute-done | bytes 65568 | tf_op jit(solution)/shard_map/ppermute | solution.py:360
  48.9 0.6 shard_map.75
  49.5 2.0 %collective-permute-start.18 = (bf16[64,512]{1,0:T(8,128)(2,1)S(1)}, bf16[64,512]{1,0:T(8,128)(2,1)S(1)}, u32[]{:S(2)}, u32[]{:S(2)}) collective-permute-start(bf16[64,512]{1,0:T(8,128)(2,1)S(1)} %shard_map.71.rest_0_.refs_0_), channel_id=1, source_target_pairs={{4,0},{5,1},{6,2},{7,3},{0,4},{1,5},{2,6},{3,7},{12,8},{13,9},{14,... | collective-permute-start | bytes 196616 | tf_op jit(solution)/shard_map/ppermute | solution.py:28
  51.5 3.3 %collective-permute-start.19 = (bf16[64,512]{1,0:T(8,128)(2,1)S(1)}, bf16[64,512]{1,0:T(8,128)(2,1)S(1)}, u32[]{:S(2)}, u32[]{:S(2)}) collective-permute-start(bf16[64,512]{1,0:T(8,128)(2,1)S(1)} %shard_map.71.rest_0_.refs_0_), channel_id=1, source_target_pairs={{8,0},{9,1},{10,2},{11,3},{12,4},{13,5},{14,6},{15,7},{0,8},{1,9},... | collective-permute-start | bytes 196616 | tf_op jit(solution)/shard_map/ppermute | solution.py:28
  54.8 1.6 %collective-permute-start.25 = (bf16[384,512]{1,0:T(8,128)(2,1)S(1)}, bf16[384,512]{1,0:T(8,128)(2,1)S(1)}, u32[]{:S(2)}, u32[]{:S(2)}) collective-permute-start(bf16[384,512]{1,0:T(8,128)(2,1)S(1)} %shard_map.75), channel_id=1, source_target_pairs={{0,16},{16,0},{1,17},{17,1},{2,18},{18,2},{3,19},{19,3},{4,20},{20... | collective-permute-start | bytes 1179656 | tf_op jit(solution)/shard_map/ppermute | solution.py:355
  56.4 1.5 %shard_map.72.refs_4_.matrix = bf16[1024,512]{1,0:T(8,128)(2,1)S(1)} custom-call(s32[1]{0:T(128)} %bitcast.1.ckpt, s32[1]{0:T(128)} %bitcast.2.me, s32[4,1,256]{2,1,0:T(1,128)S(1)} %bitcast.18, bf16[1024,1024]{1,0:T(8,128)(2,1)S(1)} %get-tuple-element.27.inverse, bf16[1024,1024]{1,0:T(8,128)(2,1)S(1)} %get-tuple-element.28.chosen, ...), custom_call_target="tpu_custom_call" | custom-call | flops 3221225472 | tf_op jit(solution)/shard_map/pallas_call | solution.py:59
  58.0 0.5 collective-permute-done.19.refs_2_
  58.5 2.4 %collective-permute-done.20.refs_3_ = bf16[64,512]{1,0:T(8,128)(2,1)S(1)} collective-permute-done((bf16[64,512]{1,0:T(8,128)(2,1)S(1)}, bf16[64,512]{1,0:T(8,128)(2,1)S(1)}, u32[]{:S(2)}, u32[]{:S(2)}) %collective-permute-start.20) | collective-permute-done | bytes 65568 | tf_op jit(solution)/shard_map/ppermute | solution.py:28
  60.9 1.6 %collective-permute-start.23 = (bf16[4,64,512]{2,1,0:T(8,128)(2,1)S(1)}, bf16[4,64,512]{2,1,0:T(8,128)(2,1)S(1)}, u32[]{:S(2)}, u32[]{:S(2)}) collective-permute-start(bf16[4,64,512]{2,1,0:T(8,128)(2,1)S(1)} %shard_map.73.rest_0_.rest_2_), channel_id=1, source_target_pairs={{2,0},{3,1},{0,2},{1,3},{6,4},{7,5},{4,6},{5,7},{10,8},{11,9},{8,1... | collective-permute-start | bytes 786440 | tf_op jit(solution)/shard_map/ppermute | solution.py:28
  62.5 0.5 shard_map.74
  63.0 1.6 %collective-permute-start.21 = (bf16[320,512]{1,0:T(8,128)(2,1)S(1)}, bf16[320,512]{1,0:T(8,128)(2,1)S(1)}, u32[]{:S(2)}, u32[]{:S(2)}) collective-permute-start(bf16[320,512]{1,0:T(8,128)(2,1)S(1)} %shard_map.74), channel_id=1, source_target_pairs={{0,16},{16,0},{1,17},{17,1},{2,18},{18,2},{3,19},{19,3},{4,20},{20... | collective-permute-start | bytes 983048 | tf_op jit(solution)/shard_map/ppermute | solution.py:355
  64.6 2.8 %collective-permute-done.23.block = bf16[4,64,512]{2,1,0:T(8,128)(2,1)S(1)} collective-permute-done((bf16[4,64,512]{2,1,0:T(8,128)(2,1)S(1)}, bf16[4,64,512]{2,1,0:T(8,128)(2,1)S(1)}, u32[]{:S(2)}, u32[]{:S(2)}) %collective-permute-start.23) | collective-permute-done | bytes 262176 | tf_op jit(solution)/shard_map/ppermute | solution.py:28
  67.4 0.1 collective-permute-start.26
  67.5 2.0 %shard_map.77.rest_6_ = f32[2048,512]{1,0:T(8,128)} custom-call(bf16[2048,1024]{1,0:T(8,128)(2,1)S(1)} %bitcast.9, bf16[1024,512]{1,0:T(8,128)(2,1)S(1)} %shard_map.72.refs_4_.matrix, f32[2048,128]{1,0:T(8,128)S(1)} %shard_map.66.rest_6_.weight, bf16[448,512]{1,0:T(8,128)(2,1)S(1)} %collective-permute-done.24.rest_0_, ...), custom_call_target="tpu_custom_call" | custom-call | tf_op jit(solution)/shard_map/pallas_call | solution.py:59
  69.5 3.6 %shard_map.78.rest_1_ = f32[2048,512]{1,0:T(8,128)} custom-call(s32[1]{0:T(128)} %bitcast.2.me, bf16[2048,1024]{1,0:T(8,128)(2,1)S(1)} %bitcast.10, bf16[1024,512]{1,0:T(8,128)(2,1)S(1)} %shard_map.72.refs_4_.matrix, f32[2048,128]{1,0:T(8,128)S(1)} %shard_map.66.rest_6_.weight, s32[1,2048]{1,0:T(1,128)S(1)} %bitcast.13, ...), custom_call_target="tpu_custom_call", output_to_operand_aliasing={{}: (11, {})} | custom-call | tf_op jit(solution)/shard_map/pallas_call | solution.py:59
  73.1 0.8 %collective-permute-done.21.rest_0_ = bf16[320,512]{1,0:T(8,128)(2,1)S(1)} collective-permute-done((bf16[320,512]{1,0:T(8,128)(2,1)S(1)}, bf16[320,512]{1,0:T(8,128)(2,1)S(1)}, u32[]{:S(2)}, u32[]{:S(2)}) %collective-permute-start.21) | collective-permute-done | bytes 327712 | tf_op jit(solution)/shard_map/ppermute | solution.py:355
  73.9 1.4 %shard_map.79 = f32[2048,512]{1,0:T(8,128)} custom-call(bf16[2048,1024]{1,0:T(8,128)(2,1)S(1)} %bitcast.11, bf16[1024,512]{1,0:T(8,128)(2,1)S(1)} %shard_map.72.refs_4_.matrix, f32[2048,128]{1,0:T(8,128)S(1)} %shard_map.66.rest_6_.weight, bf16[320,512]{1,0:T(8,128)(2,1)S(1)} %collective-permute-done.21.rest_0_, ...), custom_call_target="tpu_custom_call", output_to_operand_aliasing={{}: (4, {})} | custom-call | tf_op jit(solution)/shard_map/pallas_call | solution.py:59
  (32 shorter events, 0.1 us)
Async XLA Ops:
  0.0 23.8 %copy-start.1 = (s32[2048]{0:T(1024)S(1)}, s32[2048]{0:T(1024)}, u32[]{:S(2)}) copy-start(s32[2048]{0:T(1024)} %param.10) | copy-start | bytes 24580
  0.0 23.8 %copy-start.2 = (f32[1,16]{1,0:T(1,128)S(1)}, f32[1,16]{1,0:T(1,128)}, u32[]{:S(2)}) copy-start(f32[1,16]{1,0:T(1,128)} %bucket_weight.3) | copy-start | bytes 196
  0.0 30.5 %copy-start.4 = (s32[1024]{0:T(1024)S(1)}, s32[1024]{0:T(1024)}, u32[]{:S(2)}) copy-start(s32[1024]{0:T(1024)} %param.11) | copy-start | bytes 12292
  3.3 26.6 %collective-permute-start.15 = (bf16[464,1024]{1,0:T(8,128)(2,1)}, bf16[464,1024]{1,0:T(8,128)(2,1)S(1)}, u32[]{:S(2)}, u32[]{:S(2)}) collective-permute-start(bf16[464,1024]{1,0:T(8,128)(2,1)} %get-tuple-element.20), channel_id=1, source_target_pairs={{0,16},{16,0},{1,17},{17,1},{2,18},{18,2},{3,19},{19,3},{4,20},{20... | collective-permute-start | bytes 2850824 | tf_op jit(solution)/shard_map/ppermute | solution.py:307
  6.3 8.0 %collective-permute-start.13 = (bf16[2,64,1024]{2,1,0:T(8,128)(2,1)}, bf16[2,64,1024]{2,1,0:T(8,128)(2,1)S(1)}, u32[]{:S(2)}, u32[]{:S(2)}) collective-permute-start(bf16[2,64,1024]{2,1,0:T(8,128)(2,1)} %get-tuple-element.19.rest_0_), channel_id=1, source_target_pairs={{2,0},{3,1},{0,2},{1,3},{6,4},{7,5},{4,6},{5,7},{10,8},{11,9},{8,1... | collective-permute-start | bytes 786440 | tf_op jit(solution)/shard_map/ppermute | solution.py:28
  7.8 13.2 %collective-permute-start.8 = (bf16[2,64,1024]{2,1,0:T(8,128)(2,1)}, bf16[2,64,1024]{2,1,0:T(8,128)(2,1)S(1)}, u32[]{:S(2)}, u32[]{:S(2)}) collective-permute-start(bf16[2,64,1024]{2,1,0:T(8,128)(2,1)} %get-tuple-element.19.rest_0_), channel_id=1, source_target_pairs={{4,0},{5,1},{6,2},{7,3},{0,4},{1,5},{2,6},{3,7},{12,8},{13,9},{14,... | collective-permute-start | bytes 786440 | tf_op jit(solution)/shard_map/ppermute | solution.py:28
  9.4 14.1 %collective-permute-start = (bf16[2,64,1024]{2,1,0:T(8,128)(2,1)}, bf16[2,64,1024]{2,1,0:T(8,128)(2,1)S(1)}, u32[]{:S(2)}, u32[]{:S(2)}) collective-permute-start(bf16[2,64,1024]{2,1,0:T(8,128)(2,1)} %get-tuple-element.19.rest_0_), channel_id=1, source_target_pairs={{8,0},{9,1},{10,2},{11,3},{12,4},{13,5},{14,6},{15,7},{0,8},{1,9},... | collective-permute-start | bytes 786440 | tf_op jit(solution)/shard_map/ppermute | solution.py:28
  12.0 12.9 %collective-permute-start.12 = (bf16[2,64,1024]{2,1,0:T(8,128)(2,1)}, bf16[2,64,1024]{2,1,0:T(8,128)(2,1)S(1)}, u32[]{:S(2)}, u32[]{:S(2)}) collective-permute-start(bf16[2,64,1024]{2,1,0:T(8,128)(2,1)} %get-tuple-element.19.rest_0_), channel_id=1, source_target_pairs={{1,0},{0,1},{3,2},{2,3},{5,4},{4,5},{7,6},{6,7},{9,8},{8,9},{11,10... | collective-permute-start | bytes 786440 | tf_op jit(solution)/shard_map/ppermute | solution.py:28
  14.3 11.2 %collective-permute-start.14 = (bf16[2,64,1024]{2,1,0:T(8,128)(2,1)S(1)}, bf16[2,64,1024]{2,1,0:T(8,128)(2,1)S(1)}, u32[]{:S(2)}, u32[]{:S(2)}) collective-permute-start(bf16[2,64,1024]{2,1,0:T(8,128)(2,1)S(1)} %collective-permute-done.13.rest_2_), channel_id=1, source_target_pairs={{1,0},{0,1},{3,2},{2,3},{5,4},{4,5},{7,6},{6,7},{9,8},{8,9},{11,10... | collective-permute-start | bytes 786440 | tf_op jit(solution)/shard_map/ppermute | solution.py:28
  21.0 6.4 %collective-permute-start.10 = (bf16[2,64,1024]{2,1,0:T(8,128)(2,1)S(1)}, bf16[2,64,1024]{2,1,0:T(8,128)(2,1)S(1)}, u32[]{:S(2)}, u32[]{:S(2)}) collective-permute-start(bf16[2,64,1024]{2,1,0:T(8,128)(2,1)S(1)} %collective-permute-done.8.rest_0_), channel_id=1, source_target_pairs={{2,0},{3,1},{0,2},{1,3},{6,4},{7,5},{4,6},{5,7},{10,8},{11,9},{8,1... | collective-permute-start | bytes 786440 | tf_op jit(solution)/shard_map/ppermute | solution.py:28
  23.5 6.4 %collective-permute-start.1 = (bf16[2,64,1024]{2,1,0:T(8,128)(2,1)S(1)}, bf16[2,64,1024]{2,1,0:T(8,128)(2,1)S(1)}, u32[]{:S(2)}, u32[]{:S(2)}) collective-permute-start(bf16[2,64,1024]{2,1,0:T(8,128)(2,1)S(1)} %collective-permute-done.rest_0_), channel_id=1, source_target_pairs={{4,0},{5,1},{6,2},{7,3},{0,4},{1,5},{2,6},{3,7},{12,8},{13,9},{14,... | collective-permute-start | bytes 786440 | tf_op jit(solution)/shard_map/ppermute | solution.py:28
  24.9 29.9 %collective-permute-start.17 = (bf16[448,1024]{1,0:T(8,128)(2,1)}, bf16[448,1024]{1,0:T(8,128)(2,1)S(1)}, u32[]{:S(2)}, u32[]{:S(2)}) collective-permute-start(bf16[448,1024]{1,0:T(8,128)(2,1)} %get-tuple-element.32), channel_id=1, source_target_pairs={{0,16},{16,0},{1,17},{17,1},{2,18},{18,2},{3,19},{19,3},{4,20},{20... | collective-permute-start | bytes 2752520 | tf_op jit(solution)/shard_map/ppermute | solution.py:307
  25.5 6.8 %collective-permute-start.9 = (bf16[2,64,1024]{2,1,0:T(8,128)(2,1)S(1)}, bf16[2,64,1024]{2,1,0:T(8,128)(2,1)S(1)}, u32[]{:S(2)}, u32[]{:S(2)}) collective-permute-start(bf16[2,64,1024]{2,1,0:T(8,128)(2,1)S(1)} %collective-permute-done.8.rest_0_), channel_id=1, source_target_pairs={{1,0},{0,1},{3,2},{2,3},{5,4},{4,5},{7,6},{6,7},{9,8},{8,9},{11,10... | collective-permute-start | bytes 786440 | tf_op jit(solution)/shard_map/ppermute | solution.py:28
  27.4 8.0 %collective-permute-start.6 = (bf16[2,64,1024]{2,1,0:T(8,128)(2,1)S(1)}, bf16[2,64,1024]{2,1,0:T(8,128)(2,1)S(1)}, u32[]{:S(2)}, u32[]{:S(2)}) collective-permute-start(bf16[2,64,1024]{2,1,0:T(8,128)(2,1)S(1)} %collective-permute-done.rest_0_), channel_id=1, source_target_pairs={{2,0},{3,1},{0,2},{1,3},{6,4},{7,5},{4,6},{5,7},{10,8},{11,9},{8,1... | collective-permute-start | bytes 786440 | tf_op jit(solution)/shard_map/ppermute | solution.py:28
  29.9 5.5 %collective-permute-start.11 = (bf16[2,64,1024]{2,1,0:T(8,128)(2,1)S(1)}, bf16[2,64,1024]{2,1,0:T(8,128)(2,1)S(1)}, u32[]{:S(2)}, u32[]{:S(2)}) collective-permute-start(bf16[2,64,1024]{2,1,0:T(8,128)(2,1)S(1)} %collective-permute-done.10.rest_2_), channel_id=1, source_target_pairs={{1,0},{0,1},{3,2},{2,3},{5,4},{4,5},{7,6},{6,7},{9,8},{8,9},{11,10... | collective-permute-start | bytes 786440 | tf_op jit(solution)/shard_map/ppermute | solution.py:28
  29.9 10.0 %collective-permute-start.3 = (bf16[2,64,1024]{2,1,0:T(8,128)(2,1)S(1)}, bf16[2,64,1024]{2,1,0:T(8,128)(2,1)S(1)}, u32[]{:S(2)}, u32[]{:S(2)}) collective-permute-start(bf16[2,64,1024]{2,1,0:T(8,128)(2,1)S(1)} %collective-permute-done.1.rest_0_), channel_id=1, source_target_pairs={{2,0},{3,1},{0,2},{1,3},{6,4},{7,5},{4,6},{5,7},{10,8},{11,9},{8,1... | collective-permute-start | bytes 786440 | tf_op jit(solution)/shard_map/ppermute | solution.py:28
  30.5 1.0 %copy-start.3 = (bf16[2,64,1024]{2,1,0:T(8,128)(2,1)S(1)}, bf16[2,64,1024]{2,1,0:T(8,128)(2,1)}, u32[]{:S(2)}) copy-start(bf16[2,64,1024]{2,1,0:T(8,128)(2,1)} %get-tuple-element.19.rest_0_) | copy-start | bytes 786436
  32.3 8.4 %collective-permute-start.5 = (bf16[2,64,1024]{2,1,0:T(8,128)(2,1)S(1)}, bf16[2,64,1024]{2,1,0:T(8,128)(2,1)S(1)}, u32[]{:S(2)}, u32[]{:S(2)}) collective-permute-start(bf16[2,64,1024]{2,1,0:T(8,128)(2,1)S(1)} %collective-permute-done.rest_0_), channel_id=1, source_target_pairs={{1,0},{0,1},{3,2},{2,3},{5,4},{4,5},{7,6},{6,7},{9,8},{8,9},{11,10... | collective-permute-start | bytes 786440 | tf_op jit(solution)/shard_map/ppermute | solution.py:28
  35.4 6.1 %collective-permute-start.2 = (bf16[2,64,1024]{2,1,0:T(8,128)(2,1)S(1)}, bf16[2,64,1024]{2,1,0:T(8,128)(2,1)S(1)}, u32[]{:S(2)}, u32[]{:S(2)}) collective-permute-start(bf16[2,64,1024]{2,1,0:T(8,128)(2,1)S(1)} %collective-permute-done.1.rest_0_), channel_id=1, source_target_pairs={{1,0},{0,1},{3,2},{2,3},{5,4},{4,5},{7,6},{6,7},{9,8},{8,9},{11,10... | collective-permute-start | bytes 786440 | tf_op jit(solution)/shard_map/ppermute | solution.py:28
  35.4 5.3 %collective-permute-start.7 = (bf16[2,64,1024]{2,1,0:T(8,128)(2,1)S(1)}, bf16[2,64,1024]{2,1,0:T(8,128)(2,1)S(1)}, u32[]{:S(2)}, u32[]{:S(2)}) collective-permute-start(bf16[2,64,1024]{2,1,0:T(8,128)(2,1)S(1)} %collective-permute-done.6.rest_2_), channel_id=1, source_target_pairs={{1,0},{0,1},{3,2},{2,3},{5,4},{4,5},{7,6},{6,7},{9,8},{8,9},{11,10... | collective-permute-start | bytes 786440 | tf_op jit(solution)/shard_map/ppermute | solution.py:28
  39.8 1.7 %collective-permute-start.4 = (bf16[2,64,1024]{2,1,0:T(8,128)(2,1)S(1)}, bf16[2,64,1024]{2,1,0:T(8,128)(2,1)S(1)}, u32[]{:S(2)}, u32[]{:S(2)}) collective-permute-start(bf16[2,64,1024]{2,1,0:T(8,128)(2,1)S(1)} %collective-permute-done.3.rest_2_), channel_id=1, source_target_pairs={{1,0},{0,1},{3,2},{2,3},{5,4},{4,5},{7,6},{6,7},{9,8},{8,9},{11,10... | collective-permute-start | bytes 786440 | tf_op jit(solution)/shard_map/ppermute | solution.py:28
  41.5 3.2 %copy-start = (bf16[1,2048,1024]{2,1,0:T(8,128)(2,1)S(1)}, bf16[1,2048,1024]{2,1,0:T(8,128)(2,1)}, u32[]{:S(2)}) copy-start(bf16[1,2048,1024]{2,1,0:T(8,128)(2,1)} %param.6) | copy-start | bytes 12582916
  43.2 5.7 %collective-permute-start.16 = (bf16[64,512]{1,0:T(8,128)(2,1)S(1)}, bf16[64,512]{1,0:T(8,128)(2,1)S(1)}, u32[]{:S(2)}, u32[]{:S(2)}) collective-permute-start(bf16[64,512]{1,0:T(8,128)(2,1)S(1)} %get-tuple-element.30), channel_id=1, source_target_pairs={{0,16},{16,0},{1,17},{17,1},{2,18},{18,2},{3,19},{19,3},{4,20},{20... | collective-permute-start | bytes 196616 | tf_op jit(solution)/shard_map/ppermute | solution.py:360
  45.4 22.0 %collective-permute-start.24 = (bf16[448,512]{1,0:T(8,128)(2,1)S(1)}, bf16[448,512]{1,0:T(8,128)(2,1)S(1)}, u32[]{:S(2)}, u32[]{:S(2)}) collective-permute-start(bf16[448,512]{1,0:T(8,128)(2,1)S(1)} %shard_map.70.rest_0_), channel_id=1, source_target_pairs={{0,16},{16,0},{1,17},{17,1},{2,18},{18,2},{3,19},{19,3},{4,20},{20... | collective-permute-start | bytes 1376264 | tf_op jit(solution)/shard_map/ppermute | solution.py:355
  49.5 8.5 %collective-permute-start.18 = (bf16[64,512]{1,0:T(8,128)(2,1)S(1)}, bf16[64,512]{1,0:T(8,128)(2,1)S(1)}, u32[]{:S(2)}, u32[]{:S(2)}) collective-permute-start(bf16[64,512]{1,0:T(8,128)(2,1)S(1)} %shard_map.71.rest_0_.refs_0_), channel_id=1, source_target_pairs={{4,0},{5,1},{6,2},{7,3},{0,4},{1,5},{2,6},{3,7},{12,8},{13,9},{14,... | collective-permute-start | bytes 196616 | tf_op jit(solution)/shard_map/ppermute | solution.py:28
  51.5 7.0 %collective-permute-start.19 = (bf16[64,512]{1,0:T(8,128)(2,1)S(1)}, bf16[64,512]{1,0:T(8,128)(2,1)S(1)}, u32[]{:S(2)}, u32[]{:S(2)}) collective-permute-start(bf16[64,512]{1,0:T(8,128)(2,1)S(1)} %shard_map.71.rest_0_.refs_0_), channel_id=1, source_target_pairs={{8,0},{9,1},{10,2},{11,3},{12,4},{13,5},{14,6},{15,7},{0,8},{1,9},... | collective-permute-start | bytes 196616 | tf_op jit(solution)/shard_map/ppermute | solution.py:28
  54.8 6.1 %collective-permute-start.20 = (bf16[64,512]{1,0:T(8,128)(2,1)S(1)}, bf16[64,512]{1,0:T(8,128)(2,1)S(1)}, u32[]{:S(2)}, u32[]{:S(2)}) collective-permute-start(bf16[64,512]{1,0:T(8,128)(2,1)S(1)} %shard_map.71.rest_0_.refs_0_), channel_id=1, source_target_pairs={{12,0},{13,1},{14,2},{15,3},{8,4},{9,5},{10,6},{11,7},{4,8},{5,9},... | collective-permute-start | bytes 196616 | tf_op jit(solution)/shard_map/ppermute | solution.py:28
  54.8 12.5 %collective-permute-start.25 = (bf16[384,512]{1,0:T(8,128)(2,1)S(1)}, bf16[384,512]{1,0:T(8,128)(2,1)S(1)}, u32[]{:S(2)}, u32[]{:S(2)}) collective-permute-start(bf16[384,512]{1,0:T(8,128)(2,1)S(1)} %shard_map.75), channel_id=1, source_target_pairs={{0,16},{16,0},{1,17},{17,1},{2,18},{18,2},{3,19},{19,3},{4,20},{20... | collective-permute-start | bytes 1179656 | tf_op jit(solution)/shard_map/ppermute | solution.py:355
  60.9 6.4 %collective-permute-start.23 = (bf16[4,64,512]{2,1,0:T(8,128)(2,1)S(1)}, bf16[4,64,512]{2,1,0:T(8,128)(2,1)S(1)}, u32[]{:S(2)}, u32[]{:S(2)}) collective-permute-start(bf16[4,64,512]{2,1,0:T(8,128)(2,1)S(1)} %shard_map.73.rest_0_.rest_2_), channel_id=1, source_target_pairs={{2,0},{3,1},{0,2},{1,3},{6,4},{7,5},{4,6},{5,7},{10,8},{11,9},{8,1... | collective-permute-start | bytes 786440 | tf_op jit(solution)/shard_map/ppermute | solution.py:28
  63.0 10.9 %collective-permute-start.21 = (bf16[320,512]{1,0:T(8,128)(2,1)S(1)}, bf16[320,512]{1,0:T(8,128)(2,1)S(1)}, u32[]{:S(2)}, u32[]{:S(2)}) collective-permute-start(bf16[320,512]{1,0:T(8,128)(2,1)S(1)} %shard_map.74), channel_id=1, source_target_pairs={{0,16},{16,0},{1,17},{17,1},{2,18},{18,2},{3,19},{19,3},{4,20},{20... | collective-permute-start | bytes 983048 | tf_op jit(solution)/shard_map/ppermute | solution.py:355
  64.6 4.9 %collective-permute-start.22 = (bf16[4,64,512]{2,1,0:T(8,128)(2,1)S(1)}, bf16[4,64,512]{2,1,0:T(8,128)(2,1)S(1)}, u32[]{:S(2)}, u32[]{:S(2)}) collective-permute-start(bf16[4,64,512]{2,1,0:T(8,128)(2,1)S(1)} %shard_map.73.rest_0_.rest_2_), channel_id=1, source_target_pairs={{1,0},{0,1},{3,2},{2,3},{5,4},{4,5},{7,6},{6,7},{9,8},{8,9},{11,10... | collective-permute-start | bytes 786440 | tf_op jit(solution)/shard_map/ppermute | solution.py:28
  67.4 2.1 %collective-permute-start.26 = (bf16[4,64,512]{2,1,0:T(8,128)(2,1)S(1)}, bf16[4,64,512]{2,1,0:T(8,128)(2,1)S(1)}, u32[]{:S(2)}, u32[]{:S(2)}) collective-permute-start(bf16[4,64,512]{2,1,0:T(8,128)(2,1)S(1)} %shard_map.76.rest_4_), channel_id=1, source_target_pairs={{1,0},{0,1},{3,2},{2,3},{5,4},{4,5},{7,6},{6,7},{9,8},{8,9},{11,10... | collective-permute-start | bytes 786440 | tf_op jit(solution)/shard_map/ppermute | solution.py:28

commit v6 on v5

--- a/solution.py
+++ b/solution.py
@@ -236,26 +236,40 @@
         copy.wait()
 
 
-def both_kernel(ensemble, masks, outers, batches, me, train, matrix, weight, bucket, *rest):
-    features, pieces = rest[:batches], rest[batches : batches + len(masks)]
-    out, matrix2, weight2, buffer, sems = rest[-5:]
-    count = buffer.shape[0]
-    extra = sum(batch.shape[0] for batch in features) - count
-    table = jnp.zeros((extra, LANES), F32)
+def ahead_kernel(last, first, train, matrix, weight, bucket, features, _, own, final, weight2):
+    count = own.shape[0]
+    own[...] = scaled(train[:count, :], matrix[...], weight[:count, :])
+    rows = pl.ds(last, final.shape[0])
+    final[...] = scaled(train[rows, :], matrix[...], weight[rows, :])
+    table = jnp.zeros((features.shape[0] - first, LANES), F32)
     for part in range(3):
         lanes = pl.ds(part * LANES, LANES)
-        table = table + features[0][features[0].shape[0] - extra :, lanes].astype(F32)
+        table = table + features[first:, lanes].astype(F32)
     weight2[...] = weights_of(bucket[:, :count], table)
+
+
+def last_kernel(ensemble, first, own, *rest):
+    out, buffer, sems = rest[-3:]
+    total = own[...].astype(F32)
+    for other in rest[: ensemble - 1]:
+        total = total + other[...].astype(F32)
+    two = [sems.at[0], sems.at[1]]
+    for copy in store(out, first, 0, buffer, two, total / ensemble):
+        copy.wait()
+
+
+def both_kernel(ensemble, masks, outers, batches, lengths, me, own, weight2, *rest):
+    features, pieces = rest[:batches], rest[batches : batches + len(masks)]
+    out, matrix2, buffer, sems = rest[-4:]
     rows = pieces[0].shape[1]
     for mask, piece in zip(masks, pieces):
         for i, outer in enumerate(outers):
             at = lax.bitwise_xor(me[0], mask ^ outer)
             matrix2[aligned(at, rows), :] = piece[i]
     copies, first = [], 0
-    for i, batch in enumerate(features):
-        each = batch.shape[0] - (0 if i else extra)
+    for i, (batch, each) in enumerate(zip(features, lengths)):
         rows = pl.ds(first, each)
-        total = scaled(train[rows, :], matrix[...], weight[rows, :]).astype(F32)
+        total = own[rows, :].astype(F32)
         total = total + scaled(batch[:each, :], matrix2[...], weight2[rows, :]).astype(F32)
         two = [sems.at[2 * i], sems.at[2 * i + 1]]
         copies += store(out, 0, first, buffer, two, total / ensemble)
@@ -274,11 +288,11 @@
     count = test_order.shape[0]
     width = count // ensemble
     share = size // n
-    unit = rows // 32
+    unit = rows // 64
     paired = ensemble == 2
-    batches = [7, 7] if paired else []
+    batches = [14, 14] if paired else []
     featured = sum(batches)
-    parts = [7, 6, 5] if paired else [16, 16]
+    parts = [16, 10, 10] if paired else [32, 32]
     flying = 1 if paired else 2
     table_rows = -(-bucket_weight.shape[1] // 16) * 16
 
@@ -381,11 +395,19 @@
         for q in range(flying + 1, len(parts)):
             got, after = send(starts[q], parts[q], [column])
             received.append(got)
+        own_rows, last_rows, weight2 = call(
+            functools.partial(ahead_kernel, starts[-1] * unit, batches[0] * unit),
+            [
+                shape((featured * unit, width)), shape((parts[-1] * unit, width)),
+                shape((featured * unit, LANES), F32),
+            ],
+            (train, matrix, weight, bucket, features[0], column), [VMEM] * 5 + [ANY], mib=16,
+        )
         held = [(0, column)]
         for bit in inner_bits:
             held += [(mask ^ bit, swap(b, bit, n)) for mask, b in held]
         held = held[:1] + [
-            (mask, call(relay_kernel, shape(b.shape), (b, *received[0], *received[1]), [VMEM, ANY, ANY]))
+            (mask, call(relay_kernel, shape(b.shape), (b, *received[0], *received[1], own_rows), [VMEM] + [ANY] * 3))
             for mask, b in held[1:]
         ]
         for bit in core_bits:
@@ -408,23 +430,26 @@
 
     together = [[0, 1], [], [2]] if paired else [[q] for q in range(len(parts))]
     for chunks in together:
-        if chunks:
-            part = sum(parts[q] for q in chunks)
-            got = [tile for q in chunks for tile in received[q]]
+        part = sum(parts[q] for q in chunks)
+        got = [tile for q in chunks for tile in received[q]]
+        if paired and not chunks:
+            lengths = [part * unit for part in batches]
+            out = put(
+                functools.partial(both_kernel, ensemble, inners, outers, len(batches), lengths),
+                featured, 2 * len(batches), (me, own_rows, weight2, *features, *pieces),
+                [SMEM] + [VMEM] * (2 + len(features) + len(pieces)),
+                scratch=[pltpu.VMEM((size, width), BF16)],
+            )
+        elif paired and chunks == together[-1]:
+            out = put(
+                functools.partial(last_kernel, ensemble, starts[chunks[0]] * unit),
+                part, 2, (last_rows, *got), [VMEM] * (1 + len(got)),
+            )
+        else:
             lengths = [parts[q] * unit for q in chunks]
             out = put(
                 functools.partial(sum_kernel, ensemble, starts[chunks[0]] * unit, lengths),
                 part, 2 * len(chunks), (train, matrix, weight, *got), [VMEM] * (3 + len(got)),
-            )
-        else:
-            out = put(
-                functools.partial(both_kernel, ensemble, inners, outers, len(batches)),
-                featured, 2 * len(batches),
-                (me, train, matrix, weight, bucket, *features, *pieces),
-                [SMEM] + [VMEM] * (4 + len(features) + len(pieces)),
-                scratch=[
-                    pltpu.VMEM((size, width), BF16), pltpu.VMEM((featured * unit, LANES), F32)
-                ],
             )
     return out
 

time: 75.5 us -> 75 us (level)
    ppermute x21, waiting for transfers between devices: 27.4 us -> 23.8 us  [swap(): return lax.ppermute(block, 'train', [(d ^ mask, d) for d in range(n)])]
    ppermute x3, waiting for transfers between devices: 0.83 us -> 4.04 us  [send(): got.append(lax.ppermute(tile, 'ckpt', ahead(k, ensemble)))]
    pallas_call x16 -> x17, Pallas kernels: 18.6 us -> 18.6 us  [call(): pl.pallas_call(kernel, out_shape=outs, in_specs=specs, out_specs=out_spec...]
where the time goes in v6:
time: 75 us; the launch traced here: 74.8 us
  waiting for transfers between devices  30.7 us (41%)
  starting transfers between devices  24.3 us (32%)
  Pallas kernels  18.6 us (25%)
  local copies, waits for them, and re-layouts  0.97 us (1%)
    ppermute x21, waiting for transfers between devices, swap(): return lax.ppermute(block, 'train', [(d ^ mask, d) for d in range(n)])  23.8 us
    pallas_call x17, Pallas kernels, call(): pl.pallas_call(kernel, out_shape=outs, in_specs=specs, out_specs=out_spec...  18.6 us
    ppermute x21, starting transfers between devices, swap(): return lax.ppermute(block, 'train', [(d ^ mask, d) for d in range(n)])  15.3 us
    ppermute x3, waiting for transfers between devices, send(): got.append(lax.ppermute(tile, 'ckpt', ahead(k, ensemble)))  4.04 us
    ppermute x3, starting transfers between devices, send(): got.append(lax.ppermute(tile, 'ckpt', ahead(k, ensemble)))  3.76 us
    ppermute x2, starting transfers between devices, shards(): lax.ppermute(batch, 'ckpt', ahead(1, ensemble))  3.6 us
    ppermute x1, waiting for transfers between devices, shards(): shard2 = lax.ppermute(shard, 'ckpt', ahead(1, ensemble))  2.88 us
    ppermute x1, starting transfers between devices, shards(): shard2 = lax.ppermute(shard, 'ckpt', ahead(1, ensemble))  1.56 us
  transfers between devices with their start and end apart: 27, of which 12 were waited for; matrix products, arithmetic and copies ran while one was open for 0% of the time, Pallas kernels for 19%

profile of v6, /device:TPU:0, one launch (start us, length us, event | category | flops | bytes accessed | tf_op | source)
XLA Modules:
  0.0 74.8 jit_solution(8384228048213836907)
XLA Ops:
  0.0 3.3 %shard_map.64 = (bf16[2,64,1024]{2,1,0:T(8,128)(2,1)}, bf16[464,1024]{1,0:T(8,128)(2,1)}, bf16[448,1024]{1,0:T(8,128)(2,1)}) custom-call(bf16[1,64,1024]{2,1,0:T(8,128)(2,1)} %test_feat.1, bf16[1,64,1024]{2,1,0:T(8,128)(2,1)} %kernel_inv.1, bf16[2048,1024]{1,0:T(8,128)(2,1)} %bitcast.5, f32[1,16]{1,0:T(1,128)} %bucket_weight.3), custom_call_target="tpu_custom_call" | custom-call | tf_op jit(solution)/shard_map/pallas_call | solution.py:59
  3.3 3.0 %collective-permute-start.15 = (bf16[464,1024]{1,0:T(8,128)(2,1)}, bf16[464,1024]{1,0:T(8,128)(2,1)S(1)}, u32[]{:S(2)}, u32[]{:S(2)}) collective-permute-start(bf16[464,1024]{1,0:T(8,128)(2,1)} %get-tuple-element.23), channel_id=1, source_target_pairs={{0,16},{16,0},{1,17},{17,1},{2,18},{18,2},{3,19},{19,3},{4,20},{20... | collective-permute-start | bytes 2850824 | tf_op jit(solution)/shard_map/ppermute | solution.py:321
  6.3 1.5 %collective-permute-start.13 = (bf16[2,64,1024]{2,1,0:T(8,128)(2,1)}, bf16[2,64,1024]{2,1,0:T(8,128)(2,1)S(1)}, u32[]{:S(2)}, u32[]{:S(2)}) collective-permute-start(bf16[2,64,1024]{2,1,0:T(8,128)(2,1)} %get-tuple-element.22.rest_0_), channel_id=1, source_target_pairs={{2,0},{3,1},{0,2},{1,3},{6,4},{7,5},{4,6},{5,7},{10,8},{11,9},{8,1... | collective-permute-start | bytes 786440 | tf_op jit(solution)/shard_map/ppermute | solution.py:28
  7.8 1.6 %collective-permute-start.8 = (bf16[2,64,1024]{2,1,0:T(8,128)(2,1)}, bf16[2,64,1024]{2,1,0:T(8,128)(2,1)S(1)}, u32[]{:S(2)}, u32[]{:S(2)}) collective-permute-start(bf16[2,64,1024]{2,1,0:T(8,128)(2,1)} %get-tuple-element.22.rest_0_), channel_id=1, source_target_pairs={{4,0},{5,1},{6,2},{7,3},{0,4},{1,5},{2,6},{3,7},{12,8},{13,9},{14,... | collective-permute-start | bytes 786440 | tf_op jit(solution)/shard_map/ppermute | solution.py:28
  9.4 2.6 %collective-permute-start = (bf16[2,64,1024]{2,1,0:T(8,128)(2,1)}, bf16[2,64,1024]{2,1,0:T(8,128)(2,1)S(1)}, u32[]{:S(2)}, u32[]{:S(2)}) collective-permute-start(bf16[2,64,1024]{2,1,0:T(8,128)(2,1)} %get-tuple-element.22.rest_0_), channel_id=1, source_target_pairs={{8,0},{9,1},{10,2},{11,3},{12,4},{13,5},{14,6},{15,7},{0,8},{1,9},... | collective-permute-start | bytes 786440 | tf_op jit(solution)/shard_map/ppermute | solution.py:28
  12.0 0.0 collective-permute-start.12
  12.0 2.3 %collective-permute-done.13.rest_2_ = bf16[2,64,1024]{2,1,0:T(8,128)(2,1)S(1)} collective-permute-done((bf16[2,64,1024]{2,1,0:T(8,128)(2,1)}, bf16[2,64,1024]{2,1,0:T(8,128)(2,1)S(1)}, u32[]{:S(2)}, u32[]{:S(2)}) %collective-permute-start.13) | collective-permute-done | bytes 262176 | tf_op jit(solution)/shard_map/ppermute | solution.py:28
  14.3 6.7 %collective-permute-done.8.rest_0_ = bf16[2,64,1024]{2,1,0:T(8,128)(2,1)S(1)} collective-permute-done((bf16[2,64,1024]{2,1,0:T(8,128)(2,1)}, bf16[2,64,1024]{2,1,0:T(8,128)(2,1)S(1)}, u32[]{:S(2)}, u32[]{:S(2)}) %collective-permute-start.8) | collective-permute-done | bytes 262176 | tf_op jit(solution)/shard_map/ppermute | solution.py:28
  21.0 0.5 collective-permute-start.10
  21.5 2.0 %collective-permute-done.rest_0_ = bf16[2,64,1024]{2,1,0:T(8,128)(2,1)S(1)} collective-permute-done((bf16[2,64,1024]{2,1,0:T(8,128)(2,1)}, bf16[2,64,1024]{2,1,0:T(8,128)(2,1)S(1)}, u32[]{:S(2)}, u32[]{:S(2)}) %collective-permute-start) | collective-permute-done | bytes 262176 | tf_op jit(solution)/shard_map/ppermute | solution.py:28
  23.5 0.3 collective-permute-start.1
  23.8 1.1 %shard_map.66.rest_6_.weight = f32[2048,128]{1,0:T(8,128)S(1)} custom-call(s32[1,2048]{1,0:T(1,128)S(1)} %bitcast.11, f32[1,16]{1,0:T(1,128)S(1)} %copy-done.2), custom_call_target="tpu_custom_call" | custom-call | tf_op jit(solution)/shard_map/pallas_call | solution.py:59
  24.9 0.6 collective-permute-start.17
  25.5 1.9 %collective-permute-done.10.rest_2_ = bf16[2,64,1024]{2,1,0:T(8,128)(2,1)S(1)} collective-permute-done((bf16[2,64,1024]{2,1,0:T(8,128)(2,1)S(1)}, bf16[2,64,1024]{2,1,0:T(8,128)(2,1)S(1)}, u32[]{:S(2)}, u32[]{:S(2)}) %collective-permute-start.10) | collective-permute-done | bytes 262176 | tf_op jit(solution)/shard_map/ppermute | solution.py:28
  27.4 0.5 collective-permute-start.6
  27.9 2.0 %collective-permute-done.1.rest_0_ = bf16[2,64,1024]{2,1,0:T(8,128)(2,1)S(1)} collective-permute-done((bf16[2,64,1024]{2,1,0:T(8,128)(2,1)S(1)}, bf16[2,64,1024]{2,1,0:T(8,128)(2,1)S(1)}, u32[]{:S(2)}, u32[]{:S(2)}) %collective-permute-start.1) | collective-permute-done | bytes 262176 | tf_op jit(solution)/shard_map/ppermute | solution.py:28
  29.9 0.6 collective-permute-start.3
  30.5 0.9 %copy-done.3 = bf16[2,64,1024]{2,1,0:T(8,128)(2,1)S(1)} copy-done((bf16[2,64,1024]{2,1,0:T(8,128)(2,1)S(1)}, bf16[2,64,1024]{2,1,0:T(8,128)(2,1)}, u32[]{:S(2)}) %copy-start.3) | copy-done | bytes 262168
  31.4 0.8 %shard_map.65 = (bf16[1024,1024]{1,0:T(8,128)(2,1)S(1)}, bf16[1024,1024]{1,0:T(8,128)(2,1)S(1)}) custom-call(s32[1]{0:T(128)} %bitcast.1.ckpt, s32[1]{0:T(128)} %bitcast.2.me, s32[4,1,256]{2,1,0:T(1,128)S(1)} %bitcast.13, bf16[2,64,1024]{2,1,0:T(8,128)(2,1)S(1)} %copy-done.3, bf16[2,64,1024]{2,1,0:T(8,128)(2,1)S(1)} %collective-permute-done.12.rest_1_, ...), custom_call_target="tpu_custom_call" | custom-call | flops 4294967296 | bytes 4194304 | tf_op jit(solution)/shard_map/pallas_call | solution.py:59
  32.2 0.2 collective-permute-start.5
  32.5 2.9 %collective-permute-done.6.rest_2_ = bf16[2,64,1024]{2,1,0:T(8,128)(2,1)S(1)} collective-permute-done((bf16[2,64,1024]{2,1,0:T(8,128)(2,1)S(1)}, bf16[2,64,1024]{2,1,0:T(8,128)(2,1)S(1)}, u32[]{:S(2)}, u32[]{:S(2)}) %collective-permute-start.6) | collective-permute-done | bytes 262176 | tf_op jit(solution)/shard_map/ppermute | solution.py:28
  35.4 0.5 collective-permute-start.7
  35.9 3.9 %collective-permute-done.3.rest_2_ = bf16[2,64,1024]{2,1,0:T(8,128)(2,1)S(1)} collective-permute-done((bf16[2,64,1024]{2,1,0:T(8,128)(2,1)S(1)}, bf16[2,64,1024]{2,1,0:T(8,128)(2,1)S(1)}, u32[]{:S(2)}, u32[]{:S(2)}) %collective-permute-start.3) | collective-permute-done | bytes 262176 | tf_op jit(solution)/shard_map/ppermute | solution.py:28
  39.8 0.8 %shard_map.67 = (bf16[1024,1024]{1,0:T(8,128)(2,1)S(1)}, bf16[1024,1024]{1,0:T(8,128)(2,1)S(1)}) custom-call(s32[1]{0:T(128)} %bitcast.1.ckpt, s32[1]{0:T(128)} %bitcast.2.me, s32[4,1,256]{2,1,0:T(1,128)S(1)} %bitcast.14, bf16[2,64,1024]{2,1,0:T(8,128)(2,1)S(1)} %collective-permute-done.8.rest_0_, ...), custom_call_target="tpu_custom_call", output_to_operand_aliasing={{0}: (7, {}), {1}: (8, {})} | custom-call | flops 4294967296 | bytes 4194304 | tf_op jit(solution)/shard_map/pallas_call | solution.py:59
  40.7 0.8 %shard_map.68 = (bf16[1024,1024]{1,0:T(8,128)(2,1)S(1)}, bf16[1024,1024]{1,0:T(8,128)(2,1)S(1)}) custom-call(s32[1]{0:T(128)} %bitcast.1.ckpt, s32[1]{0:T(128)} %bitcast.2.me, s32[4,1,256]{2,1,0:T(1,128)S(1)} %bitcast.15, bf16[2,64,1024]{2,1,0:T(8,128)(2,1)S(1)} %collective-permute-done.rest_0_, ...), custom_call_target="tpu_custom_call", output_to_operand_aliasing={{0}: (7, {}), {1}: (8, {})} | custom-call | flops 4294967296 | bytes 4194304 | tf_op jit(solution)/shard_map/pallas_call | solution.py:59
  41.5 0.0 copy-start
  41.5 1.6 %shard_map.69 = (bf16[1024,1024]{1,0:T(8,128)(2,1)S(1)}, bf16[1024,1024]{1,0:T(8,128)(2,1)S(1)}, bf16[256,1024]{1,0:T(8,128)(2,1)S(1)}, bf16[1,1024,512]{2,1,0:T(8,128)(2,1)S(1)}, bf16[64,512]{1,0:T(8,128)(2,1)S(1)}) custom-call(s32[1]{0:T(128)} %bitcast.1.ckpt, s32[1]{0:T(128)} %bitcast.2.me, ...), custom_call_target="tpu_custom_call", output_to_operand_aliasing={{0}: (7, {}), {1}: (8, {})} | custom-call | flops 3221225472 | bytes 4194304 | tf_op jit(solution)/shard_map/pallas_call | solution.py:59
  43.2 1.6 %collective-permute-start.16 = (bf16[64,512]{1,0:T(8,128)(2,1)S(1)}, bf16[64,512]{1,0:T(8,128)(2,1)S(1)}, u32[]{:S(2)}, u32[]{:S(2)}) collective-permute-start(bf16[64,512]{1,0:T(8,128)(2,1)S(1)} %get-tuple-element.33), channel_id=1, source_target_pairs={{0,16},{16,0},{1,17},{17,1},{2,18},{18,2},{3,19},{19,3},{4,20},{20... | collective-permute-start | bytes 196616 | tf_op jit(solution)/shard_map/ppermute | solution.py:374
  44.7 0.7 shard_map.70.rest_0_
  45.4 0.6 collective-permute-start.24
  46.0 2.9 %collective-permute-done.16.block = bf16[64,512]{1,0:T(8,128)(2,1)S(1)} collective-permute-done((bf16[64,512]{1,0:T(8,128)(2,1)S(1)}, bf16[64,512]{1,0:T(8,128)(2,1)S(1)}, u32[]{:S(2)}, u32[]{:S(2)}) %collective-permute-start.16) | collective-permute-done | bytes 65568 | tf_op jit(solution)/shard_map/ppermute | solution.py:374
  48.9 4.7 %collective-permute-start.20 = (bf16[64,512]{1,0:T(8,128)(2,1)S(1)}, bf16[64,512]{1,0:T(8,128)(2,1)S(1)}, u32[]{:S(2)}, u32[]{:S(2)}) collective-permute-start(bf16[64,512]{1,0:T(8,128)(2,1)S(1)} %shard_map.71.rest_0_.refs_0_), channel_id=1, source_target_pairs={{12,0},{13,1},{14,2},{15,3},{8,4},{9,5},{10,6},{11,7},{4,8},{5,9},... | collective-permute-start | bytes 196616 | tf_op jit(solution)/shard_map/ppermute | solution.py:28
  53.6 0.6 collective-permute-start.18
  54.2 0.5 shard_map.76
  54.8 1.6 %collective-permute-start.25 = (bf16[320,512]{1,0:T(8,128)(2,1)S(1)}, bf16[320,512]{1,0:T(8,128)(2,1)S(1)}, u32[]{:S(2)}, u32[]{:S(2)}) collective-permute-start(bf16[320,512]{1,0:T(8,128)(2,1)S(1)} %shard_map.76), channel_id=1, source_target_pairs={{0,16},{16,0},{1,17},{17,1},{2,18},{18,2},{3,19},{19,3},{4,20},{20... | collective-permute-start | bytes 983048 | tf_op jit(solution)/shard_map/ppermute | solution.py:369
  56.4 1.5 %shard_map.72.refs_4_.matrix = bf16[1024,512]{1,0:T(8,128)(2,1)S(1)} custom-call(s32[1]{0:T(128)} %bitcast.1.ckpt, s32[1]{0:T(128)} %bitcast.2.me, s32[4,1,256]{2,1,0:T(1,128)S(1)} %bitcast.17, bf16[1024,1024]{1,0:T(8,128)(2,1)S(1)} %get-tuple-element.30.inverse, bf16[1024,1024]{1,0:T(8,128)(2,1)S(1)} %get-tuple-element.31.chosen, ...), custom_call_target="tpu_custom_call" | custom-call | flops 3221225472 | tf_op jit(solution)/shard_map/pallas_call | solution.py:59
  57.9 0.8 %collective-permute-done.19.refs_2_ = bf16[64,512]{1,0:T(8,128)(2,1)S(1)} collective-permute-done((bf16[64,512]{1,0:T(8,128)(2,1)S(1)}, bf16[64,512]{1,0:T(8,128)(2,1)S(1)}, u32[]{:S(2)}, u32[]{:S(2)}) %collective-permute-start.19) | collective-permute-done | bytes 65568 | tf_op jit(solution)/shard_map/ppermute | solution.py:28
  58.8 1.6 %collective-permute-start.23 = (bf16[4,64,512]{2,1,0:T(8,128)(2,1)S(1)}, bf16[4,64,512]{2,1,0:T(8,128)(2,1)S(1)}, u32[]{:S(2)}, u32[]{:S(2)}) collective-permute-start(bf16[4,64,512]{2,1,0:T(8,128)(2,1)S(1)} %shard_map.73._.rest_0_.rest_2_), channel_id=1, source_target_pairs={{2,0},{3,1},{0,2},{1,3},{6,4},{7,5},{4,6},{5,7},{10,8},{11,9},{8,1... | collective-permute-start | bytes 786440 | tf_op jit(solution)/shard_map/ppermute | solution.py:28
  60.4 0.5 shard_map.75
  60.9 1.6 %collective-permute-start.21 = (bf16[320,512]{1,0:T(8,128)(2,1)S(1)}, bf16[320,512]{1,0:T(8,128)(2,1)S(1)}, u32[]{:S(2)}, u32[]{:S(2)}) collective-permute-start(bf16[320,512]{1,0:T(8,128)(2,1)S(1)} %shard_map.75), channel_id=1, source_target_pairs={{0,16},{16,0},{1,17},{17,1},{2,18},{18,2},{3,19},{19,3},{4,20},{20... | collective-permute-start | bytes 983048 | tf_op jit(solution)/shard_map/ppermute | solution.py:369
  62.5 1.8 %shard_map.74 = (bf16[896,512]{1,0:T(8,128)(2,1)S(1)}, bf16[320,512]{1,0:T(8,128)(2,1)S(1)}, f32[896,128]{1,0:T(8,128)S(1)}) custom-call(bf16[2048,1024]{1,0:T(8,128)(2,1)S(1)} %bitcast.9, bf16[1024,512]{1,0:T(8,128)(2,1)S(1)} %shard_map.72.refs_4_.matrix, f32[2048,128]{1,0:T(8,128)S(1)} %shard_map.66.rest_6_.weight, s32[1,2048]{1,0:T(1,128)S(1)} %bitcast.12, ...), custom_call_target="tpu_custom_call" | custom-call | tf_op jit(solution)/shard_map/pallas_call | solution.py:59
  64.3 1.2 %collective-permute-done.23.block = bf16[4,64,512]{2,1,0:T(8,128)(2,1)S(1)} collective-permute-done((bf16[4,64,512]{2,1,0:T(8,128)(2,1)S(1)}, bf16[4,64,512]{2,1,0:T(8,128)(2,1)S(1)}, u32[]{:S(2)}, u32[]{:S(2)}) %collective-permute-start.23) | collective-permute-done | bytes 262176 | tf_op jit(solution)/shard_map/ppermute | solution.py:28
  65.5 1.8 %collective-permute-done.25.rest_1_ = bf16[320,512]{1,0:T(8,128)(2,1)S(1)} collective-permute-done((bf16[320,512]{1,0:T(8,128)(2,1)S(1)}, bf16[320,512]{1,0:T(8,128)(2,1)S(1)}, u32[]{:S(2)}, u32[]{:S(2)}) %collective-permute-start.25) | collective-permute-done | bytes 327712 | tf_op jit(solution)/shard_map/ppermute | solution.py:369
  67.3 0.1 collective-permute-start.26
  67.4 2.0 %shard_map.78.rest_6_ = f32[2048,512]{1,0:T(8,128)} custom-call(bf16[2048,1024]{1,0:T(8,128)(2,1)S(1)} %bitcast.10, bf16[1024,512]{1,0:T(8,128)(2,1)S(1)} %shard_map.72.refs_4_.matrix, f32[2048,128]{1,0:T(8,128)S(1)} %shard_map.66.rest_6_.weight, bf16[512,512]{1,0:T(8,128)(2,1)S(1)} %collective-permute-done.24.rest_0_, ...), custom_call_target="tpu_custom_call" | custom-call | tf_op jit(solution)/shard_map/pallas_call | solution.py:59
  69.4 2.2 %shard_map.79.rest_1_ = f32[2048,512]{1,0:T(8,128)} custom-call(s32[1]{0:T(128)} %bitcast.2.me, bf16[896,512]{1,0:T(8,128)(2,1)S(1)} %get-tuple-element.37.rest_2_.own, f32[896,128]{1,0:T(8,128)S(1)} %get-tuple-element.38.weight2, bf16[464,1024]{1,0:T(8,128)(2,1)S(1)} %collective-permute-done.15.rest_4_.features.rest_0_, ...), custom_call_target="tpu_custom_call", output_to_operand_aliasing={{}: (9, {})} | custom-call | tf_op jit(solution)/shard_map/pallas_call | solution.py:59
  71.6 2.3 %collective-permute-done.21.rest_0_ = bf16[320,512]{1,0:T(8,128)(2,1)S(1)} collective-permute-done((bf16[320,512]{1,0:T(8,128)(2,1)S(1)}, bf16[320,512]{1,0:T(8,128)(2,1)S(1)}, u32[]{:S(2)}, u32[]{:S(2)}) %collective-permute-start.21) | collective-permute-done | bytes 327712 | tf_op jit(solution)/shard_map/ppermute | solution.py:369
  73.9 0.9 %shard_map.80 = f32[2048,512]{1,0:T(8,128)} custom-call(bf16[320,512]{1,0:T(8,128)(2,1)S(1)} %get-tuple-element.36.own, bf16[320,512]{1,0:T(8,128)(2,1)S(1)} %collective-permute-done.21.rest_0_, f32[2048,512]{1,0:T(8,128)} %shard_map.79.rest_1_), custom_call_target="tpu_custom_call", output_to_operand_aliasing={{}: (2, {})} | custom-call | tf_op jit(solution)/shard_map/pallas_call | solution.py:59
  (33 shorter events, 0.1 us)
Async XLA Ops:
  0.0 23.8 %copy-start.1 = (s32[2048]{0:T(1024)S(1)}, s32[2048]{0:T(1024)}, u32[]{:S(2)}) copy-start(s32[2048]{0:T(1024)} %param.10) | copy-start | bytes 24580
  0.0 23.8 %copy-start.2 = (f32[1,16]{1,0:T(1,128)S(1)}, f32[1,16]{1,0:T(1,128)}, u32[]{:S(2)}) copy-start(f32[1,16]{1,0:T(1,128)} %bucket_weight.3) | copy-start | bytes 196
  0.0 30.5 %copy-start.4 = (s32[1024]{0:T(1024)S(1)}, s32[1024]{0:T(1024)}, u32[]{:S(2)}) copy-start(s32[1024]{0:T(1024)} %param.11) | copy-start | bytes 12292
  3.3 26.6 %collective-permute-start.15 = (bf16[464,1024]{1,0:T(8,128)(2,1)}, bf16[464,1024]{1,0:T(8,128)(2,1)S(1)}, u32[]{:S(2)}, u32[]{:S(2)}) collective-permute-start(bf16[464,1024]{1,0:T(8,128)(2,1)} %get-tuple-element.23), channel_id=1, source_target_pairs={{0,16},{16,0},{1,17},{17,1},{2,18},{18,2},{3,19},{19,3},{4,20},{20... | collective-permute-start | bytes 2850824 | tf_op jit(solution)/shard_map/ppermute | solution.py:321
  6.3 8.0 %collective-permute-start.13 = (bf16[2,64,1024]{2,1,0:T(8,128)(2,1)}, bf16[2,64,1024]{2,1,0:T(8,128)(2,1)S(1)}, u32[]{:S(2)}, u32[]{:S(2)}) collective-permute-start(bf16[2,64,1024]{2,1,0:T(8,128)(2,1)} %get-tuple-element.22.rest_0_), channel_id=1, source_target_pairs={{2,0},{3,1},{0,2},{1,3},{6,4},{7,5},{4,6},{5,7},{10,8},{11,9},{8,1... | collective-permute-start | bytes 786440 | tf_op jit(solution)/shard_map/ppermute | solution.py:28
  7.8 13.2 %collective-permute-start.8 = (bf16[2,64,1024]{2,1,0:T(8,128)(2,1)}, bf16[2,64,1024]{2,1,0:T(8,128)(2,1)S(1)}, u32[]{:S(2)}, u32[]{:S(2)}) collective-permute-start(bf16[2,64,1024]{2,1,0:T(8,128)(2,1)} %get-tuple-element.22.rest_0_), channel_id=1, source_target_pairs={{4,0},{5,1},{6,2},{7,3},{0,4},{1,5},{2,6},{3,7},{12,8},{13,9},{14,... | collective-permute-start | bytes 786440 | tf_op jit(solution)/shard_map/ppermute | solution.py:28
  9.4 14.1 %collective-permute-start = (bf16[2,64,1024]{2,1,0:T(8,128)(2,1)}, bf16[2,64,1024]{2,1,0:T(8,128)(2,1)S(1)}, u32[]{:S(2)}, u32[]{:S(2)}) collective-permute-start(bf16[2,64,1024]{2,1,0:T(8,128)(2,1)} %get-tuple-element.22.rest_0_), channel_id=1, source_target_pairs={{8,0},{9,1},{10,2},{11,3},{12,4},{13,5},{14,6},{15,7},{0,8},{1,9},... | collective-permute-start | bytes 786440 | tf_op jit(solution)/shard_map/ppermute | solution.py:28
  12.0 12.9 %collective-permute-start.12 = (bf16[2,64,1024]{2,1,0:T(8,128)(2,1)}, bf16[2,64,1024]{2,1,0:T(8,128)(2,1)S(1)}, u32[]{:S(2)}, u32[]{:S(2)}) collective-permute-start(bf16[2,64,1024]{2,1,0:T(8,128)(2,1)} %get-tuple-element.22.rest_0_), channel_id=1, source_target_pairs={{1,0},{0,1},{3,2},{2,3},{5,4},{4,5},{7,6},{6,7},{9,8},{8,9},{11,10... | collective-permute-start | bytes 786440 | tf_op jit(solution)/shard_map/ppermute | solution.py:28
  14.3 11.2 %collective-permute-start.14 = (bf16[2,64,1024]{2,1,0:T(8,128)(2,1)S(1)}, bf16[2,64,1024]{2,1,0:T(8,128)(2,1)S(1)}, u32[]{:S(2)}, u32[]{:S(2)}) collective-permute-start(bf16[2,64,1024]{2,1,0:T(8,128)(2,1)S(1)} %collective-permute-done.13.rest_2_), channel_id=1, source_target_pairs={{1,0},{0,1},{3,2},{2,3},{5,4},{4,5},{7,6},{6,7},{9,8},{8,9},{11,10... | collective-permute-start | bytes 786440 | tf_op jit(solution)/shard_map/ppermute | solution.py:28
  21.0 6.4 %collective-permute-start.10 = (bf16[2,64,1024]{2,1,0:T(8,128)(2,1)S(1)}, bf16[2,64,1024]{2,1,0:T(8,128)(2,1)S(1)}, u32[]{:S(2)}, u32[]{:S(2)}) collective-permute-start(bf16[2,64,1024]{2,1,0:T(8,128)(2,1)S(1)} %collective-permute-done.8.rest_0_), channel_id=1, source_target_pairs={{2,0},{3,1},{0,2},{1,3},{6,4},{7,5},{4,6},{5,7},{10,8},{11,9},{8,1... | collective-permute-start | bytes 786440 | tf_op jit(solution)/shard_map/ppermute | solution.py:28
  23.5 6.4 %collective-permute-start.1 = (bf16[2,64,1024]{2,1,0:T(8,128)(2,1)S(1)}, bf16[2,64,1024]{2,1,0:T(8,128)(2,1)S(1)}, u32[]{:S(2)}, u32[]{:S(2)}) collective-permute-start(bf16[2,64,1024]{2,1,0:T(8,128)(2,1)S(1)} %collective-permute-done.rest_0_), channel_id=1, source_target_pairs={{4,0},{5,1},{6,2},{7,3},{0,4},{1,5},{2,6},{3,7},{12,8},{13,9},{14,... | collective-permute-start | bytes 786440 | tf_op jit(solution)/shard_map/ppermute | solution.py:28
  24.9 29.9 %collective-permute-start.17 = (bf16[448,1024]{1,0:T(8,128)(2,1)}, bf16[448,1024]{1,0:T(8,128)(2,1)S(1)}, u32[]{:S(2)}, u32[]{:S(2)}) collective-permute-start(bf16[448,1024]{1,0:T(8,128)(2,1)} %get-tuple-element.35), channel_id=1, source_target_pairs={{0,16},{16,0},{1,17},{17,1},{2,18},{18,2},{3,19},{19,3},{4,20},{20... | collective-permute-start | bytes 2752520 | tf_op jit(solution)/shard_map/ppermute | solution.py:321
  25.5 6.8 %collective-permute-start.9 = (bf16[2,64,1024]{2,1,0:T(8,128)(2,1)S(1)}, bf16[2,64,1024]{2,1,0:T(8,128)(2,1)S(1)}, u32[]{:S(2)}, u32[]{:S(2)}) collective-permute-start(bf16[2,64,1024]{2,1,0:T(8,128)(2,1)S(1)} %collective-permute-done.8.rest_0_), channel_id=1, source_target_pairs={{1,0},{0,1},{3,2},{2,3},{5,4},{4,5},{7,6},{6,7},{9,8},{8,9},{11,10... | collective-permute-start | bytes 786440 | tf_op jit(solution)/shard_map/ppermute | solution.py:28
  27.4 8.0 %collective-permute-start.6 = (bf16[2,64,1024]{2,1,0:T(8,128)(2,1)S(1)}, bf16[2,64,1024]{2,1,0:T(8,128)(2,1)S(1)}, u32[]{:S(2)}, u32[]{:S(2)}) collective-permute-start(bf16[2,64,1024]{2,1,0:T(8,128)(2,1)S(1)} %collective-permute-done.rest_0_), channel_id=1, source_target_pairs={{2,0},{3,1},{0,2},{1,3},{6,4},{7,5},{4,6},{5,7},{10,8},{11,9},{8,1... | collective-permute-start | bytes 786440 | tf_op jit(solution)/shard_map/ppermute | solution.py:28
  29.9 5.5 %collective-permute-start.11 = (bf16[2,64,1024]{2,1,0:T(8,128)(2,1)S(1)}, bf16[2,64,1024]{2,1,0:T(8,128)(2,1)S(1)}, u32[]{:S(2)}, u32[]{:S(2)}) collective-permute-start(bf16[2,64,1024]{2,1,0:T(8,128)(2,1)S(1)} %collective-permute-done.10.rest_2_), channel_id=1, source_target_pairs={{1,0},{0,1},{3,2},{2,3},{5,4},{4,5},{7,6},{6,7},{9,8},{8,9},{11,10... | collective-permute-start | bytes 786440 | tf_op jit(solution)/shard_map/ppermute | solution.py:28
  29.9 10.0 %collective-permute-start.3 = (bf16[2,64,1024]{2,1,0:T(8,128)(2,1)S(1)}, bf16[2,64,1024]{2,1,0:T(8,128)(2,1)S(1)}, u32[]{:S(2)}, u32[]{:S(2)}) collective-permute-start(bf16[2,64,1024]{2,1,0:T(8,128)(2,1)S(1)} %collective-permute-done.1.rest_0_), channel_id=1, source_target_pairs={{2,0},{3,1},{0,2},{1,3},{6,4},{7,5},{4,6},{5,7},{10,8},{11,9},{8,1... | collective-permute-start | bytes 786440 | tf_op jit(solution)/shard_map/ppermute | solution.py:28
  30.5 1.0 %copy-start.3 = (bf16[2,64,1024]{2,1,0:T(8,128)(2,1)S(1)}, bf16[2,64,1024]{2,1,0:T(8,128)(2,1)}, u32[]{:S(2)}) copy-start(bf16[2,64,1024]{2,1,0:T(8,128)(2,1)} %get-tuple-element.22.rest_0_) | copy-start | bytes 786436
  32.2 8.4 %collective-permute-start.5 = (bf16[2,64,1024]{2,1,0:T(8,128)(2,1)S(1)}, bf16[2,64,1024]{2,1,0:T(8,128)(2,1)S(1)}, u32[]{:S(2)}, u32[]{:S(2)}) collective-permute-start(bf16[2,64,1024]{2,1,0:T(8,128)(2,1)S(1)} %collective-permute-done.rest_0_), channel_id=1, source_target_pairs={{1,0},{0,1},{3,2},{2,3},{5,4},{4,5},{7,6},{6,7},{9,8},{8,9},{11,10... | collective-permute-start | bytes 786440 | tf_op jit(solution)/shard_map/ppermute | solution.py:28
  35.4 6.1 %collective-permute-start.2 = (bf16[2,64,1024]{2,1,0:T(8,128)(2,1)S(1)}, bf16[2,64,1024]{2,1,0:T(8,128)(2,1)S(1)}, u32[]{:S(2)}, u32[]{:S(2)}) collective-permute-start(bf16[2,64,1024]{2,1,0:T(8,128)(2,1)S(1)} %collective-permute-done.1.rest_0_), channel_id=1, source_target_pairs={{1,0},{0,1},{3,2},{2,3},{5,4},{4,5},{7,6},{6,7},{9,8},{8,9},{11,10... | collective-permute-start | bytes 786440 | tf_op jit(solution)/shard_map/ppermute | solution.py:28
  35.4 5.3 %collective-permute-start.7 = (bf16[2,64,1024]{2,1,0:T(8,128)(2,1)S(1)}, bf16[2,64,1024]{2,1,0:T(8,128)(2,1)S(1)}, u32[]{:S(2)}, u32[]{:S(2)}) collective-permute-start(bf16[2,64,1024]{2,1,0:T(8,128)(2,1)S(1)} %collective-permute-done.6.rest_2_), channel_id=1, source_target_pairs={{1,0},{0,1},{3,2},{2,3},{5,4},{4,5},{7,6},{6,7},{9,8},{8,9},{11,10... | collective-permute-start | bytes 786440 | tf_op jit(solution)/shard_map/ppermute | solution.py:28
  39.8 1.7 %collective-permute-start.4 = (bf16[2,64,1024]{2,1,0:T(8,128)(2,1)S(1)}, bf16[2,64,1024]{2,1,0:T(8,128)(2,1)S(1)}, u32[]{:S(2)}, u32[]{:S(2)}) collective-permute-start(bf16[2,64,1024]{2,1,0:T(8,128)(2,1)S(1)} %collective-permute-done.3.rest_2_), channel_id=1, source_target_pairs={{1,0},{0,1},{3,2},{2,3},{5,4},{4,5},{7,6},{6,7},{9,8},{8,9},{11,10... | collective-permute-start | bytes 786440 | tf_op jit(solution)/shard_map/ppermute | solution.py:28
  41.5 3.2 %copy-start = (bf16[1,2048,1024]{2,1,0:T(8,128)(2,1)S(1)}, bf16[1,2048,1024]{2,1,0:T(8,128)(2,1)}, u32[]{:S(2)}) copy-start(bf16[1,2048,1024]{2,1,0:T(8,128)(2,1)} %param.6) | copy-start | bytes 12582916
  43.2 5.8 %collective-permute-start.16 = (bf16[64,512]{1,0:T(8,128)(2,1)S(1)}, bf16[64,512]{1,0:T(8,128)(2,1)S(1)}, u32[]{:S(2)}, u32[]{:S(2)}) collective-permute-start(bf16[64,512]{1,0:T(8,128)(2,1)S(1)} %get-tuple-element.33), channel_id=1, source_target_pairs={{0,16},{16,0},{1,17},{17,1},{2,18},{18,2},{3,19},{19,3},{4,20},{20... | collective-permute-start | bytes 196616 | tf_op jit(solution)/shard_map/ppermute | solution.py:374
  45.4 21.8 %collective-permute-start.24 = (bf16[512,512]{1,0:T(8,128)(2,1)S(1)}, bf16[512,512]{1,0:T(8,128)(2,1)S(1)}, u32[]{:S(2)}, u32[]{:S(2)}) collective-permute-start(bf16[512,512]{1,0:T(8,128)(2,1)S(1)} %shard_map.70.rest_0_), channel_id=1, source_target_pairs={{0,16},{16,0},{1,17},{17,1},{2,18},{18,2},{3,19},{19,3},{4,20},{20... | collective-permute-start | bytes 1572872 | tf_op jit(solution)/shard_map/ppermute | solution.py:369
  48.9 9.0 %collective-permute-start.20 = (bf16[64,512]{1,0:T(8,128)(2,1)S(1)}, bf16[64,512]{1,0:T(8,128)(2,1)S(1)}, u32[]{:S(2)}, u32[]{:S(2)}) collective-permute-start(bf16[64,512]{1,0:T(8,128)(2,1)S(1)} %shard_map.71.rest_0_.refs_0_), channel_id=1, source_target_pairs={{12,0},{13,1},{14,2},{15,3},{8,4},{9,5},{10,6},{11,7},{4,8},{5,9},... | collective-permute-start | bytes 196616 | tf_op jit(solution)/shard_map/ppermute | solution.py:28
  53.6 5.2 %collective-permute-start.19 = (bf16[64,512]{1,0:T(8,128)(2,1)S(1)}, bf16[64,512]{1,0:T(8,128)(2,1)S(1)}, u32[]{:S(2)}, u32[]{:S(2)}) collective-permute-start(bf16[64,512]{1,0:T(8,128)(2,1)S(1)} %shard_map.71.rest_0_.refs_0_), channel_id=1, source_target_pairs={{8,0},{9,1},{10,2},{11,3},{12,4},{13,5},{14,6},{15,7},{0,8},{1,9},... | collective-permute-start | bytes 196616 | tf_op jit(solution)/shard_map/ppermute | solution.py:28
  53.6 5.2 %collective-permute-start.18 = (bf16[64,512]{1,0:T(8,128)(2,1)S(1)}, bf16[64,512]{1,0:T(8,128)(2,1)S(1)}, u32[]{:S(2)}, u32[]{:S(2)}) collective-permute-start(bf16[64,512]{1,0:T(8,128)(2,1)S(1)} %shard_map.71.rest_0_.refs_0_), channel_id=1, source_target_pairs={{4,0},{5,1},{6,2},{7,3},{0,4},{1,5},{2,6},{3,7},{12,8},{13,9},{14,... | collective-permute-start | bytes 196616 | tf_op jit(solution)/shard_map/ppermute | solution.py:28
  54.8 12.5 %collective-permute-start.25 = (bf16[320,512]{1,0:T(8,128)(2,1)S(1)}, bf16[320,512]{1,0:T(8,128)(2,1)S(1)}, u32[]{:S(2)}, u32[]{:S(2)}) collective-permute-start(bf16[320,512]{1,0:T(8,128)(2,1)S(1)} %shard_map.76), channel_id=1, source_target_pairs={{0,16},{16,0},{1,17},{17,1},{2,18},{18,2},{3,19},{19,3},{4,20},{20... | collective-permute-start | bytes 983048 | tf_op jit(solution)/shard_map/ppermute | solution.py:369
  58.8 6.7 %collective-permute-start.23 = (bf16[4,64,512]{2,1,0:T(8,128)(2,1)S(1)}, bf16[4,64,512]{2,1,0:T(8,128)(2,1)S(1)}, u32[]{:S(2)}, u32[]{:S(2)}) collective-permute-start(bf16[4,64,512]{2,1,0:T(8,128)(2,1)S(1)} %shard_map.73._.rest_0_.rest_2_), channel_id=1, source_target_pairs={{2,0},{3,1},{0,2},{1,3},{6,4},{7,5},{4,6},{5,7},{10,8},{11,9},{8,1... | collective-permute-start | bytes 786440 | tf_op jit(solution)/shard_map/ppermute | solution.py:28
  60.9 13.0 %collective-permute-start.21 = (bf16[320,512]{1,0:T(8,128)(2,1)S(1)}, bf16[320,512]{1,0:T(8,128)(2,1)S(1)}, u32[]{:S(2)}, u32[]{:S(2)}) collective-permute-start(bf16[320,512]{1,0:T(8,128)(2,1)S(1)} %shard_map.75), channel_id=1, source_target_pairs={{0,16},{16,0},{1,17},{17,1},{2,18},{18,2},{3,19},{19,3},{4,20},{20... | collective-permute-start | bytes 983048 | tf_op jit(solution)/shard_map/ppermute | solution.py:369
  62.4 6.9 %collective-permute-start.22 = (bf16[4,64,512]{2,1,0:T(8,128)(2,1)S(1)}, bf16[4,64,512]{2,1,0:T(8,128)(2,1)S(1)}, u32[]{:S(2)}, u32[]{:S(2)}) collective-permute-start(bf16[4,64,512]{2,1,0:T(8,128)(2,1)S(1)} %shard_map.73._.rest_0_.rest_2_), channel_id=1, source_target_pairs={{1,0},{0,1},{3,2},{2,3},{5,4},{4,5},{7,6},{6,7},{9,8},{8,9},{11,10... | collective-permute-start | bytes 786440 | tf_op jit(solution)/shard_map/ppermute | solution.py:28
  67.3 2.1 %collective-permute-start.26 = (bf16[4,64,512]{2,1,0:T(8,128)(2,1)S(1)}, bf16[4,64,512]{2,1,0:T(8,128)(2,1)S(1)}, u32[]{:S(2)}, u32[]{:S(2)}) collective-permute-start(bf16[4,64,512]{2,1,0:T(8,128)(2,1)S(1)} %shard_map.77.rest_4_), channel_id=1, source_target_pairs={{1,0},{0,1},{3,2},{2,3},{5,4},{4,5},{7,6},{6,7},{9,8},{8,9},{11,10... | collective-permute-start | bytes 786440 | tf_op jit(solution)/shard_map/ppermute | solution.py:28

commit v7 on v6

--- a/solution.py
+++ b/solution.py
@@ -92,13 +92,12 @@
     out[...] = weights_of(bucket[...], table_of(bucket_weight[...], table_rows))
 
 
-def start_kernel(steps, test_feat, kernel_inv, train, bucket_weight, own, *rest):
-    batches, (pair, held, below, sems) = rest[:-4], rest[-4:]
+def start_kernel(steps, test_feat, kernel_inv, train, own, *rest):
+    batches, (pair, held, sems) = rest[:-3], rest[-3:]
     moves = [(test_feat.at[0], pair.at[0], own.at[0]), (kernel_inv.at[0], pair.at[1], own.at[1])]
-    count = below.shape[0]
     first = 0
-    for i, batch in enumerate(batches):
-        step = (batch.shape[0] - (0 if i else count)) // steps
+    for batch in batches:
+        step = batch.shape[0] // steps
         for i in range(steps):
             span = pl.ds(first + i * step, step)
             moves.append((train.at[span], held.at[span], batch.at[pl.ds(i * step, step)]))
@@ -113,16 +112,6 @@
     ]
     for copy in ins:
         copy.start()
-    if batches:
-        left = table_of(bucket_weight[...], count)
-        for part in range(3):
-            term = left.astype(BF16)
-            below[:, part * LANES : (part + 1) * LANES] = term
-            left = left - term.astype(F32)
-        below[:, 3 * LANES :] = jnp.zeros((count, below.shape[1] - 3 * LANES), BF16)
-        span = pl.ds(batches[0].shape[0] - count, count)
-        outs.append(pltpu.make_async_copy(below, batches[0].at[span], sems.at[1, len(moves)]))
-        outs[-1].start()
     for inward, outward in zip(ins, outs):
         inward.wait()
         outward.start()
@@ -164,7 +153,7 @@
     ).astype(BF16)
 
 
-def send_transform_kernel(ensemble, masks, ckpt, me, order, *rest):
+def send_transform_kernel(ensemble, masks, share, ckpt, me, order, bucket_weight, *rest):
     blocks = rest[: len(masks)]
     inverse, chosen, test, out, shard = rest[-5:]
     outer = unpack(masks, me, blocks, test, inverse)
@@ -172,7 +161,12 @@
     for j in range(1, ensemble):
         picked = choose(ensemble, j, outer, ckpt, order, test)
         out[j - 1] = transformed(inverse, chosen[pl.ds(j * width, width), :] + picked)
-    shard[...] = out[0, aligned(me[0], shard.shape[0]), :]
+    shard[:share, :] = out[0, aligned(me[0], share), :]
+    left = table_of(bucket_weight[...], shard.shape[0] - share)
+    for part in range(shard.shape[1] // LANES):
+        term = left.astype(BF16)
+        shard[share:, part * LANES : (part + 1) * LANES] = term
+        left = left - term.astype(F32)
 
 
 def own_transform_kernel(ensemble, masks, ckpt, me, order, inverse, chosen, test, *rest):
@@ -190,6 +184,10 @@
 def send_kernel(first, length, j, train, matrices, weight, *rest):
     rows = pl.ds(first, length)
     rest[-1][:length, :] = scaled(train[rows, :], matrices[j], weight[rows, :])
+
+
+def head_kernel(block, *rest):
+    rest[-1][...] = block[: rest[-1].shape[0], :]
 
 
 def relay_kernel(block, *rest):
@@ -236,15 +234,15 @@
         copy.wait()
 
 
-def ahead_kernel(last, first, train, matrix, weight, bucket, features, _, own, final, weight2):
+def ahead_kernel(last, first, train, matrix, weight, bucket, shared, _, own, final, weight2):
     count = own.shape[0]
     own[...] = scaled(train[:count, :], matrix[...], weight[:count, :])
     rows = pl.ds(last, final.shape[0])
     final[...] = scaled(train[rows, :], matrix[...], weight[rows, :])
-    table = jnp.zeros((features.shape[0] - first, LANES), F32)
+    table = jnp.zeros((shared.shape[0] - first, LANES), F32)
     for part in range(3):
         lanes = pl.ds(part * LANES, LANES)
-        table = table + features[first:, lanes].astype(F32)
+        table = table + shared[first:, lanes].astype(F32)
     weight2[...] = weights_of(bucket[:, :count], table)
 
 
@@ -289,7 +287,7 @@
     width = count // ensemble
     share = size // n
     unit = rows // 64
-    paired = ensemble == 2
+    paired = ensemble == 2 and width >= 3 * LANES
     batches = [14, 14] if paired else []
     featured = sum(batches)
     parts = [16, 10, 10] if paired else [32, 32]
@@ -302,19 +300,18 @@
     bucket = bucket.reshape(1, rows)
 
     sent = [
-        shape((part * unit + (0 if i else table_rows), size))
-        for i, part in enumerate(batches)
+        shape((part * unit, size))
+        for part in batches
     ]
     steps = 2
     own, *features = call(
         functools.partial(start_kernel, steps),
         [shape((2, test_feat.shape[1], size)), *sent],
-        (test_feat, kernel_inv, train, bucket_weight), [ANY] * 3 + [VMEM],
+        (test_feat, kernel_inv, train), [ANY] * 3,
         out_specs=[ANY] * (1 + len(sent)), mib=60,
         scratch=[
             pltpu.VMEM((2, test_feat.shape[1], size), BF16),
             pltpu.VMEM((max(featured, 1) * unit, size), BF16),
-            pltpu.VMEM((table_rows, size), BF16),
             pltpu.SemaphoreType.DMA((2, 3 + steps * len(sent))),
         ],
     )
@@ -347,13 +344,14 @@
     masks, blocks = groups[-1]
     starts = [featured + sum(parts[:q]) for q in range(len(parts))]
     inverse, chosen, test, matrices, shard = call(
-        functools.partial(send_transform_kernel, ensemble, masks),
+        functools.partial(send_transform_kernel, ensemble, masks, share),
         [
             shape((size, size)), shape((count, size)), shape((count // len(outers), size)),
-            shape((ensemble - 1, size, width)), shape((share, width)),
+            shape((ensemble - 1, size, width)), shape((share + table_rows, width)),
         ],
-        [ckpt, me, order, *blocks, *state], [SMEM] * 2 + [VMEM] * (3 + len(blocks)),
-        aliases={3 + len(blocks): 0, 4 + len(blocks): 1},
+        [ckpt, me, order, bucket_weight, *blocks, *state],
+        [SMEM] * 2 + [VMEM] * (4 + len(blocks)),
+        aliases={4 + len(blocks): 0, 5 + len(blocks): 1},
         flops=3 * half, moved=4 * size * size, mib=12,
     )
 
@@ -376,7 +374,7 @@
         got, after = send(starts[q], parts[q], after)
         received.append(got)
     if paired:
-        piece = call(relay_kernel, shape(shard2.shape), (shard2, *after), [VMEM, ANY])
+        piece = call(head_kernel, shape((share, width)), (shard2, *after), [VMEM, ANY])
         after = [piece]
 
     matrix = call(
@@ -396,12 +394,12 @@
             got, after = send(starts[q], parts[q], [column])
             received.append(got)
         own_rows, last_rows, weight2 = call(
-            functools.partial(ahead_kernel, starts[-1] * unit, batches[0] * unit),
+            functools.partial(ahead_kernel, starts[-1] * unit, share),
             [
                 shape((featured * unit, width)), shape((parts[-1] * unit, width)),
                 shape((featured * unit, LANES), F32),
             ],
-            (train, matrix, weight, bucket, features[0], column), [VMEM] * 5 + [ANY], mib=16,
+            (train, matrix, weight, bucket, shard2, column), [VMEM] * 5 + [ANY], mib=16,
         )
         held = [(0, column)]
         for bit in inner_bits:

time: 75 us -> 74 us (0.987)
  transfers between devices with their start and end apart: 27 -> 27, of which waited for: 12 -> 12; matrix products, arithmetic and copies ran while one was open for 0% -> 0% of each run, Pallas kernels for 19% -> 20%
where the time goes in v7:
time: 74 us; the launch traced here: 73.8 us
  waiting for transfers between devices  30.2 us (41%)
  starting transfers between devices  24.5 us (33%)
  Pallas kernels  17.9 us (24%)
  local copies, waits for them, and re-layouts  0.97 us (1%)
    ppermute x21, waiting for transfers between devices, swap(): return lax.ppermute(block, 'train', [(d ^ mask, d) for d in range(n)])  23.7 us
    pallas_call x17, Pallas kernels, call(): pl.pallas_call(kernel, out_shape=outs, in_specs=specs, out_specs=out_spec...  17.9 us
    ppermute x21, starting transfers between devices, swap(): return lax.ppermute(block, 'train', [(d ^ mask, d) for d in range(n)])  15.6 us
    ppermute x3, waiting for transfers between devices, send(): got.append(lax.ppermute(tile, 'ckpt', ahead(k, ensemble)))  4.35 us
    ppermute x3, starting transfers between devices, send(): got.append(lax.ppermute(tile, 'ckpt', ahead(k, ensemble)))  3.71 us
    ppermute x2, starting transfers between devices, shards(): lax.ppermute(batch, 'ckpt', ahead(1, ensemble))  3.61 us
    ppermute x1, waiting for transfers between devices, shards(): shard2 = lax.ppermute(shard, 'ckpt', ahead(1, ensemble))  2.21 us
    ppermute x1, starting transfers between devices, shards(): shard2 = lax.ppermute(shard, 'ckpt', ahead(1, ensemble))  1.55 us
  transfers between devices with their start and end apart: 27, of which 12 were waited for; matrix products, arithmetic and copies ran while one was open for 0% of the time, Pallas kernels for 20%

profile of v7, /device:TPU:0, one launch (start us, length us, event | category | flops | bytes accessed | tf_op | source)
XLA Modules:
  0.0 73.8 jit_solution(9596507844970012296)
XLA Ops:
  0.0 2.5 %shard_map.64 = (bf16[2,64,1024]{2,1,0:T(8,128)(2,1)}, bf16[448,1024]{1,0:T(8,128)(2,1)}, bf16[448,1024]{1,0:T(8,128)(2,1)}) custom-call(bf16[1,64,1024]{2,1,0:T(8,128)(2,1)} %test_feat.1, bf16[1,64,1024]{2,1,0:T(8,128)(2,1)} %kernel_inv.1, bf16[2048,1024]{1,0:T(8,128)(2,1)} %bitcast.5), custom_call_target="tpu_custom_call" | custom-call | tf_op jit(solution)/shard_map/pallas_call | solution.py:59
  2.6 3.0 %collective-permute-start.15 = (bf16[448,1024]{1,0:T(8,128)(2,1)}, bf16[448,1024]{1,0:T(8,128)(2,1)S(1)}, u32[]{:S(2)}, u32[]{:S(2)}) collective-permute-start(bf16[448,1024]{1,0:T(8,128)(2,1)} %get-tuple-element.23), channel_id=1, source_target_pairs={{0,16},{16,0},{1,17},{17,1},{2,18},{18,2},{3,19},{19,3},{4,20},{20... | collective-permute-start | bytes 2752520 | tf_op jit(solution)/shard_map/ppermute | solution.py:318
  5.6 1.5 %collective-permute-start.13 = (bf16[2,64,1024]{2,1,0:T(8,128)(2,1)}, bf16[2,64,1024]{2,1,0:T(8,128)(2,1)S(1)}, u32[]{:S(2)}, u32[]{:S(2)}) collective-permute-start(bf16[2,64,1024]{2,1,0:T(8,128)(2,1)} %get-tuple-element.22.rest_0_), channel_id=1, source_target_pairs={{2,0},{3,1},{0,2},{1,3},{6,4},{7,5},{4,6},{5,7},{10,8},{11,9},{8,1... | collective-permute-start | bytes 786440 | tf_op jit(solution)/shard_map/ppermute | solution.py:28
  7.1 1.6 %collective-permute-start.8 = (bf16[2,64,1024]{2,1,0:T(8,128)(2,1)}, bf16[2,64,1024]{2,1,0:T(8,128)(2,1)S(1)}, u32[]{:S(2)}, u32[]{:S(2)}) collective-permute-start(bf16[2,64,1024]{2,1,0:T(8,128)(2,1)} %get-tuple-element.22.rest_0_), channel_id=1, source_target_pairs={{4,0},{5,1},{6,2},{7,3},{0,4},{1,5},{2,6},{3,7},{12,8},{13,9},{14,... | collective-permute-start | bytes 786440 | tf_op jit(solution)/shard_map/ppermute | solution.py:28
  8.7 2.6 %collective-permute-start = (bf16[2,64,1024]{2,1,0:T(8,128)(2,1)}, bf16[2,64,1024]{2,1,0:T(8,128)(2,1)S(1)}, u32[]{:S(2)}, u32[]{:S(2)}) collective-permute-start(bf16[2,64,1024]{2,1,0:T(8,128)(2,1)} %get-tuple-element.22.rest_0_), channel_id=1, source_target_pairs={{8,0},{9,1},{10,2},{11,3},{12,4},{13,5},{14,6},{15,7},{0,8},{1,9},... | collective-permute-start | bytes 786440 | tf_op jit(solution)/shard_map/ppermute | solution.py:28
  11.3 2.3 %collective-permute-done.13.rest_2_ = bf16[2,64,1024]{2,1,0:T(8,128)(2,1)S(1)} collective-permute-done((bf16[2,64,1024]{2,1,0:T(8,128)(2,1)}, bf16[2,64,1024]{2,1,0:T(8,128)(2,1)S(1)}, u32[]{:S(2)}, u32[]{:S(2)}) %collective-permute-start.13) | collective-permute-done | bytes 262176 | tf_op jit(solution)/shard_map/ppermute | solution.py:28
  13.5 6.7 %collective-permute-done.8.rest_0_ = bf16[2,64,1024]{2,1,0:T(8,128)(2,1)S(1)} collective-permute-done((bf16[2,64,1024]{2,1,0:T(8,128)(2,1)}, bf16[2,64,1024]{2,1,0:T(8,128)(2,1)S(1)}, u32[]{:S(2)}, u32[]{:S(2)}) %collective-permute-start.8) | collective-permute-done | bytes 262176 | tf_op jit(solution)/shard_map/ppermute | solution.py:28
  20.3 0.5 collective-permute-start.10
  20.8 2.0 %collective-permute-done.rest_0_ = bf16[2,64,1024]{2,1,0:T(8,128)(2,1)S(1)} collective-permute-done((bf16[2,64,1024]{2,1,0:T(8,128)(2,1)}, bf16[2,64,1024]{2,1,0:T(8,128)(2,1)S(1)}, u32[]{:S(2)}, u32[]{:S(2)}) %collective-permute-start) | collective-permute-done | bytes 262176 | tf_op jit(solution)/shard_map/ppermute | solution.py:28
  22.8 0.3 collective-permute-start.1
  23.1 1.1 %shard_map.66.rest_6_.weight = f32[2048,128]{1,0:T(8,128)S(1)} custom-call(s32[1,2048]{1,0:T(1,128)S(1)} %bitcast.11, f32[1,16]{1,0:T(1,128)S(1)} %copy-done.2), custom_call_target="tpu_custom_call" | custom-call | tf_op jit(solution)/shard_map/pallas_call | solution.py:59
  24.2 0.6 collective-permute-start.17
  24.8 1.9 %collective-permute-done.10.rest_2_ = bf16[2,64,1024]{2,1,0:T(8,128)(2,1)S(1)} collective-permute-done((bf16[2,64,1024]{2,1,0:T(8,128)(2,1)S(1)}, bf16[2,64,1024]{2,1,0:T(8,128)(2,1)S(1)}, u32[]{:S(2)}, u32[]{:S(2)}) %collective-permute-start.10) | collective-permute-done | bytes 262176 | tf_op jit(solution)/shard_map/ppermute | solution.py:28
  26.6 0.5 collective-permute-start.6
  27.2 2.0 %collective-permute-done.1.rest_0_ = bf16[2,64,1024]{2,1,0:T(8,128)(2,1)S(1)} collective-permute-done((bf16[2,64,1024]{2,1,0:T(8,128)(2,1)S(1)}, bf16[2,64,1024]{2,1,0:T(8,128)(2,1)S(1)}, u32[]{:S(2)}, u32[]{:S(2)}) %collective-permute-start.1) | collective-permute-done | bytes 262176 | tf_op jit(solution)/shard_map/ppermute | solution.py:28
  29.1 0.0 collective-permute-start.11
  29.2 0.5 collective-permute-start.3
  29.7 0.9 %copy-done.3 = bf16[2,64,1024]{2,1,0:T(8,128)(2,1)S(1)} copy-done((bf16[2,64,1024]{2,1,0:T(8,128)(2,1)S(1)}, bf16[2,64,1024]{2,1,0:T(8,128)(2,1)}, u32[]{:S(2)}) %copy-start.3) | copy-done | bytes 262168
  30.6 0.8 %shard_map.65 = (bf16[1024,1024]{1,0:T(8,128)(2,1)S(1)}, bf16[1024,1024]{1,0:T(8,128)(2,1)S(1)}) custom-call(s32[1]{0:T(128)} %bitcast.1.ckpt, s32[1]{0:T(128)} %bitcast.2.me, s32[4,1,256]{2,1,0:T(1,128)S(1)} %bitcast.13, bf16[2,64,1024]{2,1,0:T(8,128)(2,1)S(1)} %copy-done.3, bf16[2,64,1024]{2,1,0:T(8,128)(2,1)S(1)} %collective-permute-done.12.rest_1_, ...), custom_call_target="tpu_custom_call" | custom-call | flops 4294967296 | bytes 4194304 | tf_op jit(solution)/shard_map/pallas_call | solution.py:59
  31.5 0.3 collective-permute-start.5
  31.7 2.9 %collective-permute-done.6.rest_2_ = bf16[2,64,1024]{2,1,0:T(8,128)(2,1)S(1)} collective-permute-done((bf16[2,64,1024]{2,1,0:T(8,128)(2,1)S(1)}, bf16[2,64,1024]{2,1,0:T(8,128)(2,1)S(1)}, u32[]{:S(2)}, u32[]{:S(2)}) %collective-permute-start.6) | collective-permute-done | bytes 262176 | tf_op jit(solution)/shard_map/ppermute | solution.py:28
  34.7 0.5 collective-permute-start.7
  35.2 3.9 %collective-permute-done.3.rest_2_ = bf16[2,64,1024]{2,1,0:T(8,128)(2,1)S(1)} collective-permute-done((bf16[2,64,1024]{2,1,0:T(8,128)(2,1)S(1)}, bf16[2,64,1024]{2,1,0:T(8,128)(2,1)S(1)}, u32[]{:S(2)}, u32[]{:S(2)}) %collective-permute-start.3) | collective-permute-done | bytes 262176 | tf_op jit(solution)/shard_map/ppermute | solution.py:28
  39.1 0.8 %shard_map.67 = (bf16[1024,1024]{1,0:T(8,128)(2,1)S(1)}, bf16[1024,1024]{1,0:T(8,128)(2,1)S(1)}) custom-call(s32[1]{0:T(128)} %bitcast.1.ckpt, s32[1]{0:T(128)} %bitcast.2.me, s32[4,1,256]{2,1,0:T(1,128)S(1)} %bitcast.14, bf16[2,64,1024]{2,1,0:T(8,128)(2,1)S(1)} %collective-permute-done.8.rest_0_, ...), custom_call_target="tpu_custom_call", output_to_operand_aliasing={{0}: (7, {}), {1}: (8, {})} | custom-call | flops 4294967296 | bytes 4194304 | tf_op jit(solution)/shard_map/pallas_call | solution.py:59
  40.0 0.8 %shard_map.68 = (bf16[1024,1024]{1,0:T(8,128)(2,1)S(1)}, bf16[1024,1024]{1,0:T(8,128)(2,1)S(1)}) custom-call(s32[1]{0:T(128)} %bitcast.1.ckpt, s32[1]{0:T(128)} %bitcast.2.me, s32[4,1,256]{2,1,0:T(1,128)S(1)} %bitcast.15, bf16[2,64,1024]{2,1,0:T(8,128)(2,1)S(1)} %collective-permute-done.rest_0_, ...), custom_call_target="tpu_custom_call", output_to_operand_aliasing={{0}: (7, {}), {1}: (8, {})} | custom-call | flops 4294967296 | bytes 4194304 | tf_op jit(solution)/shard_map/pallas_call | solution.py:59
  40.8 0.0 copy-start
  40.8 1.6 %shard_map.69 = (bf16[1024,1024]{1,0:T(8,128)(2,1)S(1)}, bf16[1024,1024]{1,0:T(8,128)(2,1)S(1)}, bf16[256,1024]{1,0:T(8,128)(2,1)S(1)}, bf16[1,1024,512]{2,1,0:T(8,128)(2,1)S(1)}, bf16[80,512]{1,0:T(8,128)(2,1)S(1)}) custom-call(s32[1]{0:T(128)} %bitcast.1.ckpt, s32[1]{0:T(128)} %bitcast.2.me, ...), custom_call_target="tpu_custom_call", output_to_operand_aliasing={{0}: (8, {}), {1}: (9, {})} | custom-call | flops 3221225472 | bytes 4194304 | tf_op jit(solution)/shard_map/pallas_call | solution.py:59
  42.5 1.6 %collective-permute-start.16 = (bf16[80,512]{1,0:T(8,128)(2,1)S(1)}, bf16[80,512]{1,0:T(8,128)(2,1)S(1)}, u32[]{:S(2)}, u32[]{:S(2)}) collective-permute-start(bf16[80,512]{1,0:T(8,128)(2,1)S(1)} %get-tuple-element.33), channel_id=1, source_target_pairs={{0,16},{16,0},{1,17},{17,1},{2,18},{18,2},{3,19},{19,3},{4,20},{20... | collective-permute-start | bytes 245768 | tf_op jit(solution)/shard_map/ppermute | solution.py:372
  44.0 0.7 shard_map.70.rest_0_
  44.7 0.6 collective-permute-start.24
  45.3 2.2 %collective-permute-done.16.block.shared = bf16[80,512]{1,0:T(8,128)(2,1)S(1)} collective-permute-done((bf16[80,512]{1,0:T(8,128)(2,1)S(1)}, bf16[80,512]{1,0:T(8,128)(2,1)S(1)}, u32[]{:S(2)}, u32[]{:S(2)}) %collective-permute-start.16) | collective-permute-done | bytes 81952 | tf_op jit(solution)/shard_map/ppermute | solution.py:372
  47.6 5.0 %collective-permute-start.20 = (bf16[64,512]{1,0:T(8,128)(2,1)S(1)}, bf16[64,512]{1,0:T(8,128)(2,1)S(1)}, u32[]{:S(2)}, u32[]{:S(2)}) collective-permute-start(bf16[64,512]{1,0:T(8,128)(2,1)S(1)} %shard_map.71.rest_0_.refs_0_), channel_id=1, source_target_pairs={{12,0},{13,1},{14,2},{15,3},{8,4},{9,5},{10,6},{11,7},{4,8},{5,9},... | collective-permute-start | bytes 196616 | tf_op jit(solution)/shard_map/ppermute | solution.py:28
  52.6 0.6 collective-permute-start.18
  53.2 0.5 shard_map.76
  53.7 1.6 %collective-permute-start.25 = (bf16[320,512]{1,0:T(8,128)(2,1)S(1)}, bf16[320,512]{1,0:T(8,128)(2,1)S(1)}, u32[]{:S(2)}, u32[]{:S(2)}) collective-permute-start(bf16[320,512]{1,0:T(8,128)(2,1)S(1)} %shard_map.76), channel_id=1, source_target_pairs={{0,16},{16,0},{1,17},{17,1},{2,18},{18,2},{3,19},{19,3},{4,20},{20... | collective-permute-start | bytes 983048 | tf_op jit(solution)/shard_map/ppermute | solution.py:367
  55.3 1.6 %shard_map.72.refs_4_.matrix = bf16[1024,512]{1,0:T(8,128)(2,1)S(1)} custom-call(s32[1]{0:T(128)} %bitcast.1.ckpt, s32[1]{0:T(128)} %bitcast.2.me, s32[4,1,256]{2,1,0:T(1,128)S(1)} %bitcast.17, bf16[1024,1024]{1,0:T(8,128)(2,1)S(1)} %get-tuple-element.30.inverse, bf16[1024,1024]{1,0:T(8,128)(2,1)S(1)} %get-tuple-element.31.chosen, ...), custom_call_target="tpu_custom_call" | custom-call | flops 3221225472 | tf_op jit(solution)/shard_map/pallas_call | solution.py:59
  56.8 0.9 %collective-permute-done.19.refs_2_ = bf16[64,512]{1,0:T(8,128)(2,1)S(1)} collective-permute-done((bf16[64,512]{1,0:T(8,128)(2,1)S(1)}, bf16[64,512]{1,0:T(8,128)(2,1)S(1)}, u32[]{:S(2)}, u32[]{:S(2)}) %collective-permute-start.19) | collective-permute-done | bytes 65568 | tf_op jit(solution)/shard_map/ppermute | solution.py:28
  57.7 1.6 %collective-permute-start.23 = (bf16[4,64,512]{2,1,0:T(8,128)(2,1)S(1)}, bf16[4,64,512]{2,1,0:T(8,128)(2,1)S(1)}, u32[]{:S(2)}, u32[]{:S(2)}) collective-permute-start(bf16[4,64,512]{2,1,0:T(8,128)(2,1)S(1)} %shard_map.73._.rest_0_.rest_2_), channel_id=1, source_target_pairs={{2,0},{3,1},{0,2},{1,3},{6,4},{7,5},{4,6},{5,7},{10,8},{11,9},{8,1... | collective-permute-start | bytes 786440 | tf_op jit(solution)/shard_map/ppermute | solution.py:28
  59.3 0.5 shard_map.75
  59.8 1.6 %collective-permute-start.21 = (bf16[320,512]{1,0:T(8,128)(2,1)S(1)}, bf16[320,512]{1,0:T(8,128)(2,1)S(1)}, u32[]{:S(2)}, u32[]{:S(2)}) collective-permute-start(bf16[320,512]{1,0:T(8,128)(2,1)S(1)} %shard_map.75), channel_id=1, source_target_pairs={{0,16},{16,0},{1,17},{17,1},{2,18},{18,2},{3,19},{19,3},{4,20},{20... | collective-permute-start | bytes 983048 | tf_op jit(solution)/shard_map/ppermute | solution.py:367
  61.4 1.8 %shard_map.74 = (bf16[896,512]{1,0:T(8,128)(2,1)S(1)}, bf16[320,512]{1,0:T(8,128)(2,1)S(1)}, f32[896,128]{1,0:T(8,128)S(1)}) custom-call(bf16[2048,1024]{1,0:T(8,128)(2,1)S(1)} %bitcast.9, bf16[1024,512]{1,0:T(8,128)(2,1)S(1)} %shard_map.72.refs_4_.matrix, f32[2048,128]{1,0:T(8,128)S(1)} %shard_map.66.rest_6_.weight, s32[1,2048]{1,0:T(1,128)S(1)} %bitcast.12, ...), custom_call_target="tpu_custom_call" | custom-call | tf_op jit(solution)/shard_map/pallas_call | solution.py:59
  63.2 1.0 %collective-permute-done.23.block = bf16[4,64,512]{2,1,0:T(8,128)(2,1)S(1)} collective-permute-done((bf16[4,64,512]{2,1,0:T(8,128)(2,1)S(1)}, bf16[4,64,512]{2,1,0:T(8,128)(2,1)S(1)}, u32[]{:S(2)}, u32[]{:S(2)}) %collective-permute-start.23) | collective-permute-done | bytes 262176 | tf_op jit(solution)/shard_map/ppermute | solution.py:28
  64.2 2.3 %collective-permute-done.25.rest_1_ = bf16[320,512]{1,0:T(8,128)(2,1)S(1)} collective-permute-done((bf16[320,512]{1,0:T(8,128)(2,1)S(1)}, bf16[320,512]{1,0:T(8,128)(2,1)S(1)}, u32[]{:S(2)}, u32[]{:S(2)}) %collective-permute-start.25) | collective-permute-done | bytes 327712 | tf_op jit(solution)/shard_map/ppermute | solution.py:367
  66.6 0.1 collective-permute-start.26
  66.7 2.0 %shard_map.78.rest_6_ = f32[2048,512]{1,0:T(8,128)} custom-call(bf16[2048,1024]{1,0:T(8,128)(2,1)S(1)} %bitcast.10, bf16[1024,512]{1,0:T(8,128)(2,1)S(1)} %shard_map.72.refs_4_.matrix, f32[2048,128]{1,0:T(8,128)S(1)} %shard_map.66.rest_6_.weight, bf16[512,512]{1,0:T(8,128)(2,1)S(1)} %collective-permute-done.24.rest_0_, ...), custom_call_target="tpu_custom_call" | custom-call | tf_op jit(solution)/shard_map/pallas_call | solution.py:59
  68.7 2.2 %shard_map.79.rest_1_ = f32[2048,512]{1,0:T(8,128)} custom-call(s32[1]{0:T(128)} %bitcast.2.me, bf16[896,512]{1,0:T(8,128)(2,1)S(1)} %get-tuple-element.37.rest_2_.own, f32[896,128]{1,0:T(8,128)S(1)} %get-tuple-element.38.weight2, bf16[448,1024]{1,0:T(8,128)(2,1)S(1)} %collective-permute-done.15.rest_4_.rest_0_, ...), custom_call_target="tpu_custom_call", output_to_operand_aliasing={{}: (9, {})} | custom-call | tf_op jit(solution)/shard_map/pallas_call | solution.py:59
  70.9 2.0 %collective-permute-done.21.rest_0_ = bf16[320,512]{1,0:T(8,128)(2,1)S(1)} collective-permute-done((bf16[320,512]{1,0:T(8,128)(2,1)S(1)}, bf16[320,512]{1,0:T(8,128)(2,1)S(1)}, u32[]{:S(2)}, u32[]{:S(2)}) %collective-permute-start.21) | collective-permute-done | bytes 327712 | tf_op jit(solution)/shard_map/ppermute | solution.py:367
  72.9 0.9 %shard_map.80 = f32[2048,512]{1,0:T(8,128)} custom-call(bf16[320,512]{1,0:T(8,128)(2,1)S(1)} %get-tuple-element.36.own, bf16[320,512]{1,0:T(8,128)(2,1)S(1)} %collective-permute-done.21.rest_0_, f32[2048,512]{1,0:T(8,128)} %shard_map.79.rest_1_), custom_call_target="tpu_custom_call", output_to_operand_aliasing={{}: (2, {})} | custom-call | tf_op jit(solution)/shard_map/pallas_call | solution.py:59
  (33 shorter events, 0.1 us)
Async XLA Ops:
  0.0 23.1 %copy-start.1 = (s32[2048]{0:T(1024)S(1)}, s32[2048]{0:T(1024)}, u32[]{:S(2)}) copy-start(s32[2048]{0:T(1024)} %param.10) | copy-start | bytes 24580
  0.0 23.1 %copy-start.2 = (f32[1,16]{1,0:T(1,128)S(1)}, f32[1,16]{1,0:T(1,128)}, u32[]{:S(2)}) copy-start(f32[1,16]{1,0:T(1,128)} %bucket_weight.3) | copy-start | bytes 196
  0.0 29.7 %copy-start.4 = (s32[1024]{0:T(1024)S(1)}, s32[1024]{0:T(1024)}, u32[]{:S(2)}) copy-start(s32[1024]{0:T(1024)} %param.11) | copy-start | bytes 12292
  2.6 26.6 %collective-permute-start.15 = (bf16[448,1024]{1,0:T(8,128)(2,1)}, bf16[448,1024]{1,0:T(8,128)(2,1)S(1)}, u32[]{:S(2)}, u32[]{:S(2)}) collective-permute-start(bf16[448,1024]{1,0:T(8,128)(2,1)} %get-tuple-element.23), channel_id=1, source_target_pairs={{0,16},{16,0},{1,17},{17,1},{2,18},{18,2},{3,19},{19,3},{4,20},{20... | collective-permute-start | bytes 2752520 | tf_op jit(solution)/shard_map/ppermute | solution.py:318
  5.6 8.0 %collective-permute-start.13 = (bf16[2,64,1024]{2,1,0:T(8,128)(2,1)}, bf16[2,64,1024]{2,1,0:T(8,128)(2,1)S(1)}, u32[]{:S(2)}, u32[]{:S(2)}) collective-permute-start(bf16[2,64,1024]{2,1,0:T(8,128)(2,1)} %get-tuple-element.22.rest_0_), channel_id=1, source_target_pairs={{2,0},{3,1},{0,2},{1,3},{6,4},{7,5},{4,6},{5,7},{10,8},{11,9},{8,1... | collective-permute-start | bytes 786440 | tf_op jit(solution)/shard_map/ppermute | solution.py:28
  7.1 13.2 %collective-permute-start.8 = (bf16[2,64,1024]{2,1,0:T(8,128)(2,1)}, bf16[2,64,1024]{2,1,0:T(8,128)(2,1)S(1)}, u32[]{:S(2)}, u32[]{:S(2)}) collective-permute-start(bf16[2,64,1024]{2,1,0:T(8,128)(2,1)} %get-tuple-element.22.rest_0_), channel_id=1, source_target_pairs={{4,0},{5,1},{6,2},{7,3},{0,4},{1,5},{2,6},{3,7},{12,8},{13,9},{14,... | collective-permute-start | bytes 786440 | tf_op jit(solution)/shard_map/ppermute | solution.py:28
  8.7 14.1 %collective-permute-start = (bf16[2,64,1024]{2,1,0:T(8,128)(2,1)}, bf16[2,64,1024]{2,1,0:T(8,128)(2,1)S(1)}, u32[]{:S(2)}, u32[]{:S(2)}) collective-permute-start(bf16[2,64,1024]{2,1,0:T(8,128)(2,1)} %get-tuple-element.22.rest_0_), channel_id=1, source_target_pairs={{8,0},{9,1},{10,2},{11,3},{12,4},{13,5},{14,6},{15,7},{0,8},{1,9},... | collective-permute-start | bytes 786440 | tf_op jit(solution)/shard_map/ppermute | solution.py:28
  11.3 12.9 %collective-permute-start.12 = (bf16[2,64,1024]{2,1,0:T(8,128)(2,1)}, bf16[2,64,1024]{2,1,0:T(8,128)(2,1)S(1)}, u32[]{:S(2)}, u32[]{:S(2)}) collective-permute-start(bf16[2,64,1024]{2,1,0:T(8,128)(2,1)} %get-tuple-element.22.rest_0_), channel_id=1, source_target_pairs={{1,0},{0,1},{3,2},{2,3},{5,4},{4,5},{7,6},{6,7},{9,8},{8,9},{11,10... | collective-permute-start | bytes 786440 | tf_op jit(solution)/shard_map/ppermute | solution.py:28
  13.5 11.2 %collective-permute-start.14 = (bf16[2,64,1024]{2,1,0:T(8,128)(2,1)S(1)}, bf16[2,64,1024]{2,1,0:T(8,128)(2,1)S(1)}, u32[]{:S(2)}, u32[]{:S(2)}) collective-permute-start(bf16[2,64,1024]{2,1,0:T(8,128)(2,1)S(1)} %collective-permute-done.13.rest_2_), channel_id=1, source_target_pairs={{1,0},{0,1},{3,2},{2,3},{5,4},{4,5},{7,6},{6,7},{9,8},{8,9},{11,10... | collective-permute-start | bytes 786440 | tf_op jit(solution)/shard_map/ppermute | solution.py:28
  20.3 6.4 %collective-permute-start.10 = (bf16[2,64,1024]{2,1,0:T(8,128)(2,1)S(1)}, bf16[2,64,1024]{2,1,0:T(8,128)(2,1)S(1)}, u32[]{:S(2)}, u32[]{:S(2)}) collective-permute-start(bf16[2,64,1024]{2,1,0:T(8,128)(2,1)S(1)} %collective-permute-done.8.rest_0_), channel_id=1, source_target_pairs={{2,0},{3,1},{0,2},{1,3},{6,4},{7,5},{4,6},{5,7},{10,8},{11,9},{8,1... | collective-permute-start | bytes 786440 | tf_op jit(solution)/shard_map/ppermute | solution.py:28
  22.8 6.4 %collective-permute-start.1 = (bf16[2,64,1024]{2,1,0:T(8,128)(2,1)S(1)}, bf16[2,64,1024]{2,1,0:T(8,128)(2,1)S(1)}, u32[]{:S(2)}, u32[]{:S(2)}) collective-permute-start(bf16[2,64,1024]{2,1,0:T(8,128)(2,1)S(1)} %collective-permute-done.rest_0_), channel_id=1, source_target_pairs={{4,0},{5,1},{6,2},{7,3},{0,4},{1,5},{2,6},{3,7},{12,8},{13,9},{14,... | collective-permute-start | bytes 786440 | tf_op jit(solution)/shard_map/ppermute | solution.py:28
  24.2 29.5 %collective-permute-start.17 = (bf16[448,1024]{1,0:T(8,128)(2,1)}, bf16[448,1024]{1,0:T(8,128)(2,1)S(1)}, u32[]{:S(2)}, u32[]{:S(2)}) collective-permute-start(bf16[448,1024]{1,0:T(8,128)(2,1)} %get-tuple-element.35), channel_id=1, source_target_pairs={{0,16},{16,0},{1,17},{17,1},{2,18},{18,2},{3,19},{19,3},{4,20},{20... | collective-permute-start | bytes 2752520 | tf_op jit(solution)/shard_map/ppermute | solution.py:318
  24.8 6.7 %collective-permute-start.9 = (bf16[2,64,1024]{2,1,0:T(8,128)(2,1)S(1)}, bf16[2,64,1024]{2,1,0:T(8,128)(2,1)S(1)}, u32[]{:S(2)}, u32[]{:S(2)}) collective-permute-start(bf16[2,64,1024]{2,1,0:T(8,128)(2,1)S(1)} %collective-permute-done.8.rest_0_), channel_id=1, source_target_pairs={{1,0},{0,1},{3,2},{2,3},{5,4},{4,5},{7,6},{6,7},{9,8},{8,9},{11,10... | collective-permute-start | bytes 786440 | tf_op jit(solution)/shard_map/ppermute | solution.py:28
  26.6 8.0 %collective-permute-start.6 = (bf16[2,64,1024]{2,1,0:T(8,128)(2,1)S(1)}, bf16[2,64,1024]{2,1,0:T(8,128)(2,1)S(1)}, u32[]{:S(2)}, u32[]{:S(2)}) collective-permute-start(bf16[2,64,1024]{2,1,0:T(8,128)(2,1)S(1)} %collective-permute-done.rest_0_), channel_id=1, source_target_pairs={{2,0},{3,1},{0,2},{1,3},{6,4},{7,5},{4,6},{5,7},{10,8},{11,9},{8,1... | collective-permute-start | bytes 786440 | tf_op jit(solution)/shard_map/ppermute | solution.py:28
  29.1 5.5 %collective-permute-start.11 = (bf16[2,64,1024]{2,1,0:T(8,128)(2,1)S(1)}, bf16[2,64,1024]{2,1,0:T(8,128)(2,1)S(1)}, u32[]{:S(2)}, u32[]{:S(2)}) collective-permute-start(bf16[2,64,1024]{2,1,0:T(8,128)(2,1)S(1)} %collective-permute-done.10.rest_2_), channel_id=1, source_target_pairs={{1,0},{0,1},{3,2},{2,3},{5,4},{4,5},{7,6},{6,7},{9,8},{8,9},{11,10... | collective-permute-start | bytes 786440 | tf_op jit(solution)/shard_map/ppermute | solution.py:28
  29.2 10.0 %collective-permute-start.3 = (bf16[2,64,1024]{2,1,0:T(8,128)(2,1)S(1)}, bf16[2,64,1024]{2,1,0:T(8,128)(2,1)S(1)}, u32[]{:S(2)}, u32[]{:S(2)}) collective-permute-start(bf16[2,64,1024]{2,1,0:T(8,128)(2,1)S(1)} %collective-permute-done.1.rest_0_), channel_id=1, source_target_pairs={{2,0},{3,1},{0,2},{1,3},{6,4},{7,5},{4,6},{5,7},{10,8},{11,9},{8,1... | collective-permute-start | bytes 786440 | tf_op jit(solution)/shard_map/ppermute | solution.py:28
  29.7 1.0 %copy-start.3 = (bf16[2,64,1024]{2,1,0:T(8,128)(2,1)S(1)}, bf16[2,64,1024]{2,1,0:T(8,128)(2,1)}, u32[]{:S(2)}) copy-start(bf16[2,64,1024]{2,1,0:T(8,128)(2,1)} %get-tuple-element.22.rest_0_) | copy-start | bytes 786436
  31.5 8.5 %collective-permute-start.5 = (bf16[2,64,1024]{2,1,0:T(8,128)(2,1)S(1)}, bf16[2,64,1024]{2,1,0:T(8,128)(2,1)S(1)}, u32[]{:S(2)}, u32[]{:S(2)}) collective-permute-start(bf16[2,64,1024]{2,1,0:T(8,128)(2,1)S(1)} %collective-permute-done.rest_0_), channel_id=1, source_target_pairs={{1,0},{0,1},{3,2},{2,3},{5,4},{4,5},{7,6},{6,7},{9,8},{8,9},{11,10... | collective-permute-start | bytes 786440 | tf_op jit(solution)/shard_map/ppermute | solution.py:28
  34.7 6.1 %collective-permute-start.2 = (bf16[2,64,1024]{2,1,0:T(8,128)(2,1)S(1)}, bf16[2,64,1024]{2,1,0:T(8,128)(2,1)S(1)}, u32[]{:S(2)}, u32[]{:S(2)}) collective-permute-start(bf16[2,64,1024]{2,1,0:T(8,128)(2,1)S(1)} %collective-permute-done.1.rest_0_), channel_id=1, source_target_pairs={{1,0},{0,1},{3,2},{2,3},{5,4},{4,5},{7,6},{6,7},{9,8},{8,9},{11,10... | collective-permute-start | bytes 786440 | tf_op jit(solution)/shard_map/ppermute | solution.py:28
  34.7 5.3 %collective-permute-start.7 = (bf16[2,64,1024]{2,1,0:T(8,128)(2,1)S(1)}, bf16[2,64,1024]{2,1,0:T(8,128)(2,1)S(1)}, u32[]{:S(2)}, u32[]{:S(2)}) collective-permute-start(bf16[2,64,1024]{2,1,0:T(8,128)(2,1)S(1)} %collective-permute-done.6.rest_2_), channel_id=1, source_target_pairs={{1,0},{0,1},{3,2},{2,3},{5,4},{4,5},{7,6},{6,7},{9,8},{8,9},{11,10... | collective-permute-start | bytes 786440 | tf_op jit(solution)/shard_map/ppermute | solution.py:28
  39.1 1.7 %collective-permute-start.4 = (bf16[2,64,1024]{2,1,0:T(8,128)(2,1)S(1)}, bf16[2,64,1024]{2,1,0:T(8,128)(2,1)S(1)}, u32[]{:S(2)}, u32[]{:S(2)}) collective-permute-start(bf16[2,64,1024]{2,1,0:T(8,128)(2,1)S(1)} %collective-permute-done.3.rest_2_), channel_id=1, source_target_pairs={{1,0},{0,1},{3,2},{2,3},{5,4},{4,5},{7,6},{6,7},{9,8},{8,9},{11,10... | collective-permute-start | bytes 786440 | tf_op jit(solution)/shard_map/ppermute | solution.py:28
  40.8 3.2 %copy-start = (bf16[1,2048,1024]{2,1,0:T(8,128)(2,1)S(1)}, bf16[1,2048,1024]{2,1,0:T(8,128)(2,1)}, u32[]{:S(2)}) copy-start(bf16[1,2048,1024]{2,1,0:T(8,128)(2,1)} %param.6) | copy-start | bytes 12582916
  42.5 5.1 %collective-permute-start.16 = (bf16[80,512]{1,0:T(8,128)(2,1)S(1)}, bf16[80,512]{1,0:T(8,128)(2,1)S(1)}, u32[]{:S(2)}, u32[]{:S(2)}) collective-permute-start(bf16[80,512]{1,0:T(8,128)(2,1)S(1)} %get-tuple-element.33), channel_id=1, source_target_pairs={{0,16},{16,0},{1,17},{17,1},{2,18},{18,2},{3,19},{19,3},{4,20},{20... | collective-permute-start | bytes 245768 | tf_op jit(solution)/shard_map/ppermute | solution.py:372
  44.7 21.8 %collective-permute-start.24 = (bf16[512,512]{1,0:T(8,128)(2,1)S(1)}, bf16[512,512]{1,0:T(8,128)(2,1)S(1)}, u32[]{:S(2)}, u32[]{:S(2)}) collective-permute-start(bf16[512,512]{1,0:T(8,128)(2,1)S(1)} %shard_map.70.rest_0_), channel_id=1, source_target_pairs={{0,16},{16,0},{1,17},{17,1},{2,18},{18,2},{3,19},{19,3},{4,20},{20... | collective-permute-start | bytes 1572872 | tf_op jit(solution)/shard_map/ppermute | solution.py:367
  47.6 9.3 %collective-permute-start.20 = (bf16[64,512]{1,0:T(8,128)(2,1)S(1)}, bf16[64,512]{1,0:T(8,128)(2,1)S(1)}, u32[]{:S(2)}, u32[]{:S(2)}) collective-permute-start(bf16[64,512]{1,0:T(8,128)(2,1)S(1)} %shard_map.71.rest_0_.refs_0_), channel_id=1, source_target_pairs={{12,0},{13,1},{14,2},{15,3},{8,4},{9,5},{10,6},{11,7},{4,8},{5,9},... | collective-permute-start | bytes 196616 | tf_op jit(solution)/shard_map/ppermute | solution.py:28
  52.6 5.2 %collective-permute-start.19 = (bf16[64,512]{1,0:T(8,128)(2,1)S(1)}, bf16[64,512]{1,0:T(8,128)(2,1)S(1)}, u32[]{:S(2)}, u32[]{:S(2)}) collective-permute-start(bf16[64,512]{1,0:T(8,128)(2,1)S(1)} %shard_map.71.rest_0_.refs_0_), channel_id=1, source_target_pairs={{8,0},{9,1},{10,2},{11,3},{12,4},{13,5},{14,6},{15,7},{0,8},{1,9},... | collective-permute-start | bytes 196616 | tf_op jit(solution)/shard_map/ppermute | solution.py:28
  52.6 5.2 %collective-permute-start.18 = (bf16[64,512]{1,0:T(8,128)(2,1)S(1)}, bf16[64,512]{1,0:T(8,128)(2,1)S(1)}, u32[]{:S(2)}, u32[]{:S(2)}) collective-permute-start(bf16[64,512]{1,0:T(8,128)(2,1)S(1)} %shard_map.71.rest_0_.refs_0_), channel_id=1, source_target_pairs={{4,0},{5,1},{6,2},{7,3},{0,4},{1,5},{2,6},{3,7},{12,8},{13,9},{14,... | collective-permute-start | bytes 196616 | tf_op jit(solution)/shard_map/ppermute | solution.py:28
  53.7 12.9 %collective-permute-start.25 = (bf16[320,512]{1,0:T(8,128)(2,1)S(1)}, bf16[320,512]{1,0:T(8,128)(2,1)S(1)}, u32[]{:S(2)}, u32[]{:S(2)}) collective-permute-start(bf16[320,512]{1,0:T(8,128)(2,1)S(1)} %shard_map.76), channel_id=1, source_target_pairs={{0,16},{16,0},{1,17},{17,1},{2,18},{18,2},{3,19},{19,3},{4,20},{20... | collective-permute-start | bytes 983048 | tf_op jit(solution)/shard_map/ppermute | solution.py:367
  57.7 6.5 %collective-permute-start.23 = (bf16[4,64,512]{2,1,0:T(8,128)(2,1)S(1)}, bf16[4,64,512]{2,1,0:T(8,128)(2,1)S(1)}, u32[]{:S(2)}, u32[]{:S(2)}) collective-permute-start(bf16[4,64,512]{2,1,0:T(8,128)(2,1)S(1)} %shard_map.73._.rest_0_.rest_2_), channel_id=1, source_target_pairs={{2,0},{3,1},{0,2},{1,3},{6,4},{7,5},{4,6},{5,7},{10,8},{11,9},{8,1... | collective-permute-start | bytes 786440 | tf_op jit(solution)/shard_map/ppermute | solution.py:28
  59.8 13.1 %collective-permute-start.21 = (bf16[320,512]{1,0:T(8,128)(2,1)S(1)}, bf16[320,512]{1,0:T(8,128)(2,1)S(1)}, u32[]{:S(2)}, u32[]{:S(2)}) collective-permute-start(bf16[320,512]{1,0:T(8,128)(2,1)S(1)} %shard_map.75), channel_id=1, source_target_pairs={{0,16},{16,0},{1,17},{17,1},{2,18},{18,2},{3,19},{19,3},{4,20},{20... | collective-permute-start | bytes 983048 | tf_op jit(solution)/shard_map/ppermute | solution.py:367
  61.4 7.3 %collective-permute-start.22 = (bf16[4,64,512]{2,1,0:T(8,128)(2,1)S(1)}, bf16[4,64,512]{2,1,0:T(8,128)(2,1)S(1)}, u32[]{:S(2)}, u32[]{:S(2)}) collective-permute-start(bf16[4,64,512]{2,1,0:T(8,128)(2,1)S(1)} %shard_map.73._.rest_0_.rest_2_), channel_id=1, source_target_pairs={{1,0},{0,1},{3,2},{2,3},{5,4},{4,5},{7,6},{6,7},{9,8},{8,9},{11,10... | collective-permute-start | bytes 786440 | tf_op jit(solution)/shard_map/ppermute | solution.py:28
  66.6 2.1 %collective-permute-start.26 = (bf16[4,64,512]{2,1,0:T(8,128)(2,1)S(1)}, bf16[4,64,512]{2,1,0:T(8,128)(2,1)S(1)}, u32[]{:S(2)}, u32[]{:S(2)}) collective-permute-start(bf16[4,64,512]{2,1,0:T(8,128)(2,1)S(1)} %shard_map.77.rest_4_), channel_id=1, source_target_pairs={{1,0},{0,1},{3,2},{2,3},{5,4},{4,5},{7,6},{6,7},{9,8},{8,9},{11,10... | collective-permute-start | bytes 786440 | tf_op jit(solution)/shard_map/ppermute | solution.py:28

commit v8 on v7

--- a/solution.py
+++ b/solution.py
@@ -290,7 +290,7 @@
     paired = ensemble == 2 and width >= 3 * LANES
     batches = [14, 14] if paired else []
     featured = sum(batches)
-    parts = [16, 10, 10] if paired else [32, 32]
+    parts = [18, 8, 10] if paired else [32, 32]
     flying = 1 if paired else 2
     table_rows = -(-bucket_weight.shape[1] // 16) * 16
 

time: 74 us -> 74 us (level)
    ppermute x3, waiting for transfers between devices: 4.35 us -> 5.46 us  [send(): got.append(lax.ppermute(tile, 'ckpt', ahead(k, ensemble)))]
    ppermute x21, waiting for transfers between devices: 23.7 us -> 22.7 us  [swap(): return lax.ppermute(block, 'train', [(d ^ mask, d) for d in range(n)])]
  transfers between devices with their start and end apart: 27 -> 27, of which waited for: 12 -> 11; matrix products, arithmetic and copies ran while one was open for 0% -> 0% of each run, Pallas kernels for 20% -> 19%
where the time goes in v8:
time: 74 us; the launch traced here: 73.9 us
  waiting for transfers between devices  30.3 us (41%)
  starting transfers between devices  24.5 us (33%)
  Pallas kernels  17.8 us (24%)
  local copies, waits for them, and re-layouts  0.97 us (1%)
    ppermute x21, waiting for transfers between devices, swap(): return lax.ppermute(block, 'train', [(d ^ mask, d) for d in range(n)])  22.7 us
    pallas_call x17, Pallas kernels, call(): pl.pallas_call(kernel, out_shape=outs, in_specs=specs, out_specs=out_spec...  17.8 us
    ppermute x21, starting transfers between devices, swap(): return lax.ppermute(block, 'train', [(d ^ mask, d) for d in range(n)])  15.6 us
    ppermute x3, waiting for transfers between devices, send(): got.append(lax.ppermute(tile, 'ckpt', ahead(k, ensemble)))  5.46 us
    ppermute x3, starting transfers between devices, send(): got.append(lax.ppermute(tile, 'ckpt', ahead(k, ensemble)))  3.71 us
    ppermute x2, starting transfers between devices, shards(): lax.ppermute(batch, 'ckpt', ahead(1, ensemble))  3.61 us
    ppermute x1, waiting for transfers between devices, shards(): shard2 = lax.ppermute(shard, 'ckpt', ahead(1, ensemble))  2.14 us
    ppermute x1, starting transfers between devices, shards(): shard2 = lax.ppermute(shard, 'ckpt', ahead(1, ensemble))  1.55 us
  transfers between devices with their start and end apart: 27, of which 11 were waited for; matrix products, arithmetic and copies ran while one was open for 0% of the time, Pallas kernels for 19%

profile of v8, /device:TPU:0, one launch (start us, length us, event | category | flops | bytes accessed | tf_op | source)
XLA Modules:
  0.0 73.9 jit_solution(17693500677080691505)
XLA Ops:
  0.0 2.5 %shard_map.64 = (bf16[2,64,1024]{2,1,0:T(8,128)(2,1)}, bf16[448,1024]{1,0:T(8,128)(2,1)}, bf16[448,1024]{1,0:T(8,128)(2,1)}) custom-call(bf16[1,64,1024]{2,1,0:T(8,128)(2,1)} %test_feat.1, bf16[1,64,1024]{2,1,0:T(8,128)(2,1)} %kernel_inv.1, bf16[2048,1024]{1,0:T(8,128)(2,1)} %bitcast.5), custom_call_target="tpu_custom_call" | custom-call | tf_op jit(solution)/shard_map/pallas_call | solution.py:59
  2.6 3.0 %collective-permute-start.15 = (bf16[448,1024]{1,0:T(8,128)(2,1)}, bf16[448,1024]{1,0:T(8,128)(2,1)S(1)}, u32[]{:S(2)}, u32[]{:S(2)}) collective-permute-start(bf16[448,1024]{1,0:T(8,128)(2,1)} %get-tuple-element.23), channel_id=1, source_target_pairs={{0,16},{16,0},{1,17},{17,1},{2,18},{18,2},{3,19},{19,3},{4,20},{20... | collective-permute-start | bytes 2752520 | tf_op jit(solution)/shard_map/ppermute | solution.py:318
  5.6 1.5 %collective-permute-start.13 = (bf16[2,64,1024]{2,1,0:T(8,128)(2,1)}, bf16[2,64,1024]{2,1,0:T(8,128)(2,1)S(1)}, u32[]{:S(2)}, u32[]{:S(2)}) collective-permute-start(bf16[2,64,1024]{2,1,0:T(8,128)(2,1)} %get-tuple-element.22.rest_0_), channel_id=1, source_target_pairs={{2,0},{3,1},{0,2},{1,3},{6,4},{7,5},{4,6},{5,7},{10,8},{11,9},{8,1... | collective-permute-start | bytes 786440 | tf_op jit(solution)/shard_map/ppermute | solution.py:28
  7.1 1.6 %collective-permute-start.8 = (bf16[2,64,1024]{2,1,0:T(8,128)(2,1)}, bf16[2,64,1024]{2,1,0:T(8,128)(2,1)S(1)}, u32[]{:S(2)}, u32[]{:S(2)}) collective-permute-start(bf16[2,64,1024]{2,1,0:T(8,128)(2,1)} %get-tuple-element.22.rest_0_), channel_id=1, source_target_pairs={{4,0},{5,1},{6,2},{7,3},{0,4},{1,5},{2,6},{3,7},{12,8},{13,9},{14,... | collective-permute-start | bytes 786440 | tf_op jit(solution)/shard_map/ppermute | solution.py:28
  8.7 2.6 %collective-permute-start = (bf16[2,64,1024]{2,1,0:T(8,128)(2,1)}, bf16[2,64,1024]{2,1,0:T(8,128)(2,1)S(1)}, u32[]{:S(2)}, u32[]{:S(2)}) collective-permute-start(bf16[2,64,1024]{2,1,0:T(8,128)(2,1)} %get-tuple-element.22.rest_0_), channel_id=1, source_target_pairs={{8,0},{9,1},{10,2},{11,3},{12,4},{13,5},{14,6},{15,7},{0,8},{1,9},... | collective-permute-start | bytes 786440 | tf_op jit(solution)/shard_map/ppermute | solution.py:28
  11.3 0.0 collective-permute-start.12
  11.3 2.3 %collective-permute-done.13.rest_2_ = bf16[2,64,1024]{2,1,0:T(8,128)(2,1)S(1)} collective-permute-done((bf16[2,64,1024]{2,1,0:T(8,128)(2,1)}, bf16[2,64,1024]{2,1,0:T(8,128)(2,1)S(1)}, u32[]{:S(2)}, u32[]{:S(2)}) %collective-permute-start.13) | collective-permute-done | bytes 262176 | tf_op jit(solution)/shard_map/ppermute | solution.py:28
  13.5 0.0 collective-permute-start.14
  13.5 6.7 %collective-permute-done.8.rest_0_ = bf16[2,64,1024]{2,1,0:T(8,128)(2,1)S(1)} collective-permute-done((bf16[2,64,1024]{2,1,0:T(8,128)(2,1)}, bf16[2,64,1024]{2,1,0:T(8,128)(2,1)S(1)}, u32[]{:S(2)}, u32[]{:S(2)}) %collective-permute-start.8) | collective-permute-done | bytes 262176 | tf_op jit(solution)/shard_map/ppermute | solution.py:28
  20.3 0.5 collective-permute-start.10
  20.8 2.0 %collective-permute-done.rest_0_ = bf16[2,64,1024]{2,1,0:T(8,128)(2,1)S(1)} collective-permute-done((bf16[2,64,1024]{2,1,0:T(8,128)(2,1)}, bf16[2,64,1024]{2,1,0:T(8,128)(2,1)S(1)}, u32[]{:S(2)}, u32[]{:S(2)}) %collective-permute-start) | collective-permute-done | bytes 262176 | tf_op jit(solution)/shard_map/ppermute | solution.py:28
  22.8 0.3 collective-permute-start.1
  23.1 1.1 %shard_map.66.rest_6_.weight = f32[2048,128]{1,0:T(8,128)S(1)} custom-call(s32[1,2048]{1,0:T(1,128)S(1)} %bitcast.11, f32[1,16]{1,0:T(1,128)S(1)} %copy-done.2), custom_call_target="tpu_custom_call" | custom-call | tf_op jit(solution)/shard_map/pallas_call | solution.py:59
  24.2 0.6 collective-permute-start.17
  24.8 1.9 %collective-permute-done.10.rest_2_ = bf16[2,64,1024]{2,1,0:T(8,128)(2,1)S(1)} collective-permute-done((bf16[2,64,1024]{2,1,0:T(8,128)(2,1)S(1)}, bf16[2,64,1024]{2,1,0:T(8,128)(2,1)S(1)}, u32[]{:S(2)}, u32[]{:S(2)}) %collective-permute-start.10) | collective-permute-done | bytes 262176 | tf_op jit(solution)/shard_map/ppermute | solution.py:28
  26.6 0.5 collective-permute-start.6
  27.2 2.0 %collective-permute-done.1.rest_0_ = bf16[2,64,1024]{2,1,0:T(8,128)(2,1)S(1)} collective-permute-done((bf16[2,64,1024]{2,1,0:T(8,128)(2,1)S(1)}, bf16[2,64,1024]{2,1,0:T(8,128)(2,1)S(1)}, u32[]{:S(2)}, u32[]{:S(2)}) %collective-permute-start.1) | collective-permute-done | bytes 262176 | tf_op jit(solution)/shard_map/ppermute | solution.py:28
  29.2 0.5 collective-permute-start.3
  29.7 0.9 %copy-done.3 = bf16[2,64,1024]{2,1,0:T(8,128)(2,1)S(1)} copy-done((bf16[2,64,1024]{2,1,0:T(8,128)(2,1)S(1)}, bf16[2,64,1024]{2,1,0:T(8,128)(2,1)}, u32[]{:S(2)}) %copy-start.3) | copy-done | bytes 262168
  30.6 0.8 %shard_map.65 = (bf16[1024,1024]{1,0:T(8,128)(2,1)S(1)}, bf16[1024,1024]{1,0:T(8,128)(2,1)S(1)}) custom-call(s32[1]{0:T(128)} %bitcast.1.ckpt, s32[1]{0:T(128)} %bitcast.2.me, s32[4,1,256]{2,1,0:T(1,128)S(1)} %bitcast.13, bf16[2,64,1024]{2,1,0:T(8,128)(2,1)S(1)} %copy-done.3, bf16[2,64,1024]{2,1,0:T(8,128)(2,1)S(1)} %collective-permute-done.12.rest_1_, ...), custom_call_target="tpu_custom_call" | custom-call | flops 4294967296 | bytes 4194304 | tf_op jit(solution)/shard_map/pallas_call | solution.py:59
  31.5 0.3 collective-permute-start.5
  31.7 2.9 %collective-permute-done.6.rest_2_ = bf16[2,64,1024]{2,1,0:T(8,128)(2,1)S(1)} collective-permute-done((bf16[2,64,1024]{2,1,0:T(8,128)(2,1)S(1)}, bf16[2,64,1024]{2,1,0:T(8,128)(2,1)S(1)}, u32[]{:S(2)}, u32[]{:S(2)}) %collective-permute-start.6) | collective-permute-done | bytes 262176 | tf_op jit(solution)/shard_map/ppermute | solution.py:28
  34.7 0.5 collective-permute-start.7
  35.2 3.9 %collective-permute-done.3.rest_2_ = bf16[2,64,1024]{2,1,0:T(8,128)(2,1)S(1)} collective-permute-done((bf16[2,64,1024]{2,1,0:T(8,128)(2,1)S(1)}, bf16[2,64,1024]{2,1,0:T(8,128)(2,1)S(1)}, u32[]{:S(2)}, u32[]{:S(2)}) %collective-permute-start.3) | collective-permute-done | bytes 262176 | tf_op jit(solution)/shard_map/ppermute | solution.py:28
  39.1 0.8 %shard_map.67 = (bf16[1024,1024]{1,0:T(8,128)(2,1)S(1)}, bf16[1024,1024]{1,0:T(8,128)(2,1)S(1)}) custom-call(s32[1]{0:T(128)} %bitcast.1.ckpt, s32[1]{0:T(128)} %bitcast.2.me, s32[4,1,256]{2,1,0:T(1,128)S(1)} %bitcast.14, bf16[2,64,1024]{2,1,0:T(8,128)(2,1)S(1)} %collective-permute-done.8.rest_0_, ...), custom_call_target="tpu_custom_call", output_to_operand_aliasing={{0}: (7, {}), {1}: (8, {})} | custom-call | flops 4294967296 | bytes 4194304 | tf_op jit(solution)/shard_map/pallas_call | solution.py:59
  40.0 0.8 %shard_map.68 = (bf16[1024,1024]{1,0:T(8,128)(2,1)S(1)}, bf16[1024,1024]{1,0:T(8,128)(2,1)S(1)}) custom-call(s32[1]{0:T(128)} %bitcast.1.ckpt, s32[1]{0:T(128)} %bitcast.2.me, s32[4,1,256]{2,1,0:T(1,128)S(1)} %bitcast.15, bf16[2,64,1024]{2,1,0:T(8,128)(2,1)S(1)} %collective-permute-done.rest_0_, ...), custom_call_target="tpu_custom_call", output_to_operand_aliasing={{0}: (7, {}), {1}: (8, {})} | custom-call | flops 4294967296 | bytes 4194304 | tf_op jit(solution)/shard_map/pallas_call | solution.py:59
  40.8 0.0 copy-start
  40.8 1.6 %shard_map.69 = (bf16[1024,1024]{1,0:T(8,128)(2,1)S(1)}, bf16[1024,1024]{1,0:T(8,128)(2,1)S(1)}, bf16[256,1024]{1,0:T(8,128)(2,1)S(1)}, bf16[1,1024,512]{2,1,0:T(8,128)(2,1)S(1)}, bf16[80,512]{1,0:T(8,128)(2,1)S(1)}) custom-call(s32[1]{0:T(128)} %bitcast.1.ckpt, s32[1]{0:T(128)} %bitcast.2.me, ...), custom_call_target="tpu_custom_call", output_to_operand_aliasing={{0}: (8, {}), {1}: (9, {})} | custom-call | flops 3221225472 | bytes 4194304 | tf_op jit(solution)/shard_map/pallas_call | solution.py:59
  42.5 1.6 %collective-permute-start.16 = (bf16[80,512]{1,0:T(8,128)(2,1)S(1)}, bf16[80,512]{1,0:T(8,128)(2,1)S(1)}, u32[]{:S(2)}, u32[]{:S(2)}) collective-permute-start(bf16[80,512]{1,0:T(8,128)(2,1)S(1)} %get-tuple-element.33), channel_id=1, source_target_pairs={{0,16},{16,0},{1,17},{17,1},{2,18},{18,2},{3,19},{19,3},{4,20},{20... | collective-permute-start | bytes 245768 | tf_op jit(solution)/shard_map/ppermute | solution.py:372
  44.0 0.8 %shard_map.70.rest_0_ = bf16[576,512]{1,0:T(8,128)(2,1)S(1)} custom-call(bf16[2048,1024]{1,0:T(8,128)(2,1)S(1)} %bitcast.6, bf16[1,1024,512]{2,1,0:T(8,128)(2,1)S(1)} %get-tuple-element.34.matrices, f32[2048,128]{1,0:T(8,128)S(1)} %shard_map.66.rest_6_.weight), custom_call_target="tpu_custom_call" | custom-call | tf_op jit(solution)/shard_map/pallas_call | solution.py:59
  44.8 0.6 collective-permute-start.24
  45.4 2.1 %collective-permute-done.16.block.shared = bf16[80,512]{1,0:T(8,128)(2,1)S(1)} collective-permute-done((bf16[80,512]{1,0:T(8,128)(2,1)S(1)}, bf16[80,512]{1,0:T(8,128)(2,1)S(1)}, u32[]{:S(2)}, u32[]{:S(2)}) %collective-permute-start.16) | collective-permute-done | bytes 81952 | tf_op jit(solution)/shard_map/ppermute | solution.py:372
  47.6 5.0 %collective-permute-start.20 = (bf16[64,512]{1,0:T(8,128)(2,1)S(1)}, bf16[64,512]{1,0:T(8,128)(2,1)S(1)}, u32[]{:S(2)}, u32[]{:S(2)}) collective-permute-start(bf16[64,512]{1,0:T(8,128)(2,1)S(1)} %shard_map.71.rest_0_.refs_0_), channel_id=1, source_target_pairs={{12,0},{13,1},{14,2},{15,3},{8,4},{9,5},{10,6},{11,7},{4,8},{5,9},... | collective-permute-start | bytes 196616 | tf_op jit(solution)/shard_map/ppermute | solution.py:28
  52.6 0.6 collective-permute-start.18
  53.2 0.4 shard_map.76
  53.6 1.6 %collective-permute-start.25 = (bf16[256,512]{1,0:T(8,128)(2,1)S(1)}, bf16[256,512]{1,0:T(8,128)(2,1)S(1)}, u32[]{:S(2)}, u32[]{:S(2)}) collective-permute-start(bf16[256,512]{1,0:T(8,128)(2,1)S(1)} %shard_map.76), channel_id=1, source_target_pairs={{0,16},{16,0},{1,17},{17,1},{2,18},{18,2},{3,19},{19,3},{4,20},{20... | collective-permute-start | bytes 786440 | tf_op jit(solution)/shard_map/ppermute | solution.py:367
  55.2 1.6 %shard_map.72.refs_4_.matrix = bf16[1024,512]{1,0:T(8,128)(2,1)S(1)} custom-call(s32[1]{0:T(128)} %bitcast.1.ckpt, s32[1]{0:T(128)} %bitcast.2.me, s32[4,1,256]{2,1,0:T(1,128)S(1)} %bitcast.17, bf16[1024,1024]{1,0:T(8,128)(2,1)S(1)} %get-tuple-element.30.inverse, bf16[1024,1024]{1,0:T(8,128)(2,1)S(1)} %get-tuple-element.31.chosen, ...), custom_call_target="tpu_custom_call" | custom-call | flops 3221225472 | tf_op jit(solution)/shard_map/pallas_call | solution.py:59
  56.8 1.0 %collective-permute-done.19.refs_2_ = bf16[64,512]{1,0:T(8,128)(2,1)S(1)} collective-permute-done((bf16[64,512]{1,0:T(8,128)(2,1)S(1)}, bf16[64,512]{1,0:T(8,128)(2,1)S(1)}, u32[]{:S(2)}, u32[]{:S(2)}) %collective-permute-start.19) | collective-permute-done | bytes 65568 | tf_op jit(solution)/shard_map/ppermute | solution.py:28
  57.7 1.6 %collective-permute-start.23 = (bf16[4,64,512]{2,1,0:T(8,128)(2,1)S(1)}, bf16[4,64,512]{2,1,0:T(8,128)(2,1)S(1)}, u32[]{:S(2)}, u32[]{:S(2)}) collective-permute-start(bf16[4,64,512]{2,1,0:T(8,128)(2,1)S(1)} %shard_map.73._.rest_0_.rest_2_), channel_id=1, source_target_pairs={{2,0},{3,1},{0,2},{1,3},{6,4},{7,5},{4,6},{5,7},{10,8},{11,9},{8,1... | collective-permute-start | bytes 786440 | tf_op jit(solution)/shard_map/ppermute | solution.py:28
  59.3 0.5 shard_map.75
  59.8 1.6 %collective-permute-start.21 = (bf16[320,512]{1,0:T(8,128)(2,1)S(1)}, bf16[320,512]{1,0:T(8,128)(2,1)S(1)}, u32[]{:S(2)}, u32[]{:S(2)}) collective-permute-start(bf16[320,512]{1,0:T(8,128)(2,1)S(1)} %shard_map.75), channel_id=1, source_target_pairs={{0,16},{16,0},{1,17},{17,1},{2,18},{18,2},{3,19},{19,3},{4,20},{20... | collective-permute-start | bytes 983048 | tf_op jit(solution)/shard_map/ppermute | solution.py:367
  61.4 1.8 %shard_map.74 = (bf16[896,512]{1,0:T(8,128)(2,1)S(1)}, bf16[320,512]{1,0:T(8,128)(2,1)S(1)}, f32[896,128]{1,0:T(8,128)S(1)}) custom-call(bf16[2048,1024]{1,0:T(8,128)(2,1)S(1)} %bitcast.9, bf16[1024,512]{1,0:T(8,128)(2,1)S(1)} %shard_map.72.refs_4_.matrix, f32[2048,128]{1,0:T(8,128)S(1)} %shard_map.66.rest_6_.weight, s32[1,2048]{1,0:T(1,128)S(1)} %bitcast.12, ...), custom_call_target="tpu_custom_call" | custom-call | tf_op jit(solution)/shard_map/pallas_call | solution.py:59
  63.2 3.4 %collective-permute-done.25.rest_1_ = bf16[256,512]{1,0:T(8,128)(2,1)S(1)} collective-permute-done((bf16[256,512]{1,0:T(8,128)(2,1)S(1)}, bf16[256,512]{1,0:T(8,128)(2,1)S(1)}, u32[]{:S(2)}, u32[]{:S(2)}) %collective-permute-start.25) | collective-permute-done | bytes 262176 | tf_op jit(solution)/shard_map/ppermute | solution.py:367
  66.7 0.1 collective-permute-start.26
  66.8 1.9 %shard_map.78.rest_6_ = f32[2048,512]{1,0:T(8,128)} custom-call(bf16[2048,1024]{1,0:T(8,128)(2,1)S(1)} %bitcast.10, bf16[1024,512]{1,0:T(8,128)(2,1)S(1)} %shard_map.72.refs_4_.matrix, f32[2048,128]{1,0:T(8,128)S(1)} %shard_map.66.rest_6_.weight, bf16[576,512]{1,0:T(8,128)(2,1)S(1)} %collective-permute-done.24.rest_0_, ...), custom_call_target="tpu_custom_call" | custom-call | tf_op jit(solution)/shard_map/pallas_call | solution.py:59
  68.7 2.2 %shard_map.79.rest_1_ = f32[2048,512]{1,0:T(8,128)} custom-call(s32[1]{0:T(128)} %bitcast.2.me, bf16[896,512]{1,0:T(8,128)(2,1)S(1)} %get-tuple-element.37.rest_2_.own, f32[896,128]{1,0:T(8,128)S(1)} %get-tuple-element.38.weight2, bf16[448,1024]{1,0:T(8,128)(2,1)S(1)} %collective-permute-done.15.rest_4_.rest_0_, ...), custom_call_target="tpu_custom_call", output_to_operand_aliasing={{}: (9, {})} | custom-call | tf_op jit(solution)/shard_map/pallas_call | solution.py:59
  70.9 2.0 %collective-permute-done.21.rest_0_ = bf16[320,512]{1,0:T(8,128)(2,1)S(1)} collective-permute-done((bf16[320,512]{1,0:T(8,128)(2,1)S(1)}, bf16[320,512]{1,0:T(8,128)(2,1)S(1)}, u32[]{:S(2)}, u32[]{:S(2)}) %collective-permute-start.21) | collective-permute-done | bytes 327712 | tf_op jit(solution)/shard_map/ppermute | solution.py:367
  73.0 0.9 %shard_map.80 = f32[2048,512]{1,0:T(8,128)} custom-call(bf16[320,512]{1,0:T(8,128)(2,1)S(1)} %get-tuple-element.36.own, bf16[320,512]{1,0:T(8,128)(2,1)S(1)} %collective-permute-done.21.rest_0_, f32[2048,512]{1,0:T(8,128)} %shard_map.79.rest_1_), custom_call_target="tpu_custom_call", output_to_operand_aliasing={{}: (2, {})} | custom-call | tf_op jit(solution)/shard_map/pallas_call | solution.py:59
  (33 shorter events, 0.1 us)
Async XLA Ops:
  0.0 23.1 %copy-start.1 = (s32[2048]{0:T(1024)S(1)}, s32[2048]{0:T(1024)}, u32[]{:S(2)}) copy-start(s32[2048]{0:T(1024)} %param.10) | copy-start | bytes 24580
  0.0 23.1 %copy-start.2 = (f32[1,16]{1,0:T(1,128)S(1)}, f32[1,16]{1,0:T(1,128)}, u32[]{:S(2)}) copy-start(f32[1,16]{1,0:T(1,128)} %bucket_weight.3) | copy-start | bytes 196
  0.0 29.7 %copy-start.4 = (s32[1024]{0:T(1024)S(1)}, s32[1024]{0:T(1024)}, u32[]{:S(2)}) copy-start(s32[1024]{0:T(1024)} %param.11) | copy-start | bytes 12292
  2.6 26.6 %collective-permute-start.15 = (bf16[448,1024]{1,0:T(8,128)(2,1)}, bf16[448,1024]{1,0:T(8,128)(2,1)S(1)}, u32[]{:S(2)}, u32[]{:S(2)}) collective-permute-start(bf16[448,1024]{1,0:T(8,128)(2,1)} %get-tuple-element.23), channel_id=1, source_target_pairs={{0,16},{16,0},{1,17},{17,1},{2,18},{18,2},{3,19},{19,3},{4,20},{20... | collective-permute-start | bytes 2752520 | tf_op jit(solution)/shard_map/ppermute | solution.py:318
  5.6 8.0 %collective-permute-start.13 = (bf16[2,64,1024]{2,1,0:T(8,128)(2,1)}, bf16[2,64,1024]{2,1,0:T(8,128)(2,1)S(1)}, u32[]{:S(2)}, u32[]{:S(2)}) collective-permute-start(bf16[2,64,1024]{2,1,0:T(8,128)(2,1)} %get-tuple-element.22.rest_0_), channel_id=1, source_target_pairs={{2,0},{3,1},{0,2},{1,3},{6,4},{7,5},{4,6},{5,7},{10,8},{11,9},{8,1... | collective-permute-start | bytes 786440 | tf_op jit(solution)/shard_map/ppermute | solution.py:28
  7.1 13.2 %collective-permute-start.8 = (bf16[2,64,1024]{2,1,0:T(8,128)(2,1)}, bf16[2,64,1024]{2,1,0:T(8,128)(2,1)S(1)}, u32[]{:S(2)}, u32[]{:S(2)}) collective-permute-start(bf16[2,64,1024]{2,1,0:T(8,128)(2,1)} %get-tuple-element.22.rest_0_), channel_id=1, source_target_pairs={{4,0},{5,1},{6,2},{7,3},{0,4},{1,5},{2,6},{3,7},{12,8},{13,9},{14,... | collective-permute-start | bytes 786440 | tf_op jit(solution)/shard_map/ppermute | solution.py:28
  8.7 14.1 %collective-permute-start = (bf16[2,64,1024]{2,1,0:T(8,128)(2,1)}, bf16[2,64,1024]{2,1,0:T(8,128)(2,1)S(1)}, u32[]{:S(2)}, u32[]{:S(2)}) collective-permute-start(bf16[2,64,1024]{2,1,0:T(8,128)(2,1)} %get-tuple-element.22.rest_0_), channel_id=1, source_target_pairs={{8,0},{9,1},{10,2},{11,3},{12,4},{13,5},{14,6},{15,7},{0,8},{1,9},... | collective-permute-start | bytes 786440 | tf_op jit(solution)/shard_map/ppermute | solution.py:28
  11.3 12.9 %collective-permute-start.12 = (bf16[2,64,1024]{2,1,0:T(8,128)(2,1)}, bf16[2,64,1024]{2,1,0:T(8,128)(2,1)S(1)}, u32[]{:S(2)}, u32[]{:S(2)}) collective-permute-start(bf16[2,64,1024]{2,1,0:T(8,128)(2,1)} %get-tuple-element.22.rest_0_), channel_id=1, source_target_pairs={{1,0},{0,1},{3,2},{2,3},{5,4},{4,5},{7,6},{6,7},{9,8},{8,9},{11,10... | collective-permute-start | bytes 786440 | tf_op jit(solution)/shard_map/ppermute | solution.py:28
  13.5 11.2 %collective-permute-start.14 = (bf16[2,64,1024]{2,1,0:T(8,128)(2,1)S(1)}, bf16[2,64,1024]{2,1,0:T(8,128)(2,1)S(1)}, u32[]{:S(2)}, u32[]{:S(2)}) collective-permute-start(bf16[2,64,1024]{2,1,0:T(8,128)(2,1)S(1)} %collective-permute-done.13.rest_2_), channel_id=1, source_target_pairs={{1,0},{0,1},{3,2},{2,3},{5,4},{4,5},{7,6},{6,7},{9,8},{8,9},{11,10... | collective-permute-start | bytes 786440 | tf_op jit(solution)/shard_map/ppermute | solution.py:28
  20.3 6.4 %collective-permute-start.10 = (bf16[2,64,1024]{2,1,0:T(8,128)(2,1)S(1)}, bf16[2,64,1024]{2,1,0:T(8,128)(2,1)S(1)}, u32[]{:S(2)}, u32[]{:S(2)}) collective-permute-start(bf16[2,64,1024]{2,1,0:T(8,128)(2,1)S(1)} %collective-permute-done.8.rest_0_), channel_id=1, source_target_pairs={{2,0},{3,1},{0,2},{1,3},{6,4},{7,5},{4,6},{5,7},{10,8},{11,9},{8,1... | collective-permute-start | bytes 786440 | tf_op jit(solution)/shard_map/ppermute | solution.py:28
  22.8 6.4 %collective-permute-start.1 = (bf16[2,64,1024]{2,1,0:T(8,128)(2,1)S(1)}, bf16[2,64,1024]{2,1,0:T(8,128)(2,1)S(1)}, u32[]{:S(2)}, u32[]{:S(2)}) collective-permute-start(bf16[2,64,1024]{2,1,0:T(8,128)(2,1)S(1)} %collective-permute-done.rest_0_), channel_id=1, source_target_pairs={{4,0},{5,1},{6,2},{7,3},{0,4},{1,5},{2,6},{3,7},{12,8},{13,9},{14,... | collective-permute-start | bytes 786440 | tf_op jit(solution)/shard_map/ppermute | solution.py:28
  24.2 29.5 %collective-permute-start.17 = (bf16[448,1024]{1,0:T(8,128)(2,1)}, bf16[448,1024]{1,0:T(8,128)(2,1)S(1)}, u32[]{:S(2)}, u32[]{:S(2)}) collective-permute-start(bf16[448,1024]{1,0:T(8,128)(2,1)} %get-tuple-element.35), channel_id=1, source_target_pairs={{0,16},{16,0},{1,17},{17,1},{2,18},{18,2},{3,19},{19,3},{4,20},{20... | collective-permute-start | bytes 2752520 | tf_op jit(solution)/shard_map/ppermute | solution.py:318
  24.8 6.7 %collective-permute-start.9 = (bf16[2,64,1024]{2,1,0:T(8,128)(2,1)S(1)}, bf16[2,64,1024]{2,1,0:T(8,128)(2,1)S(1)}, u32[]{:S(2)}, u32[]{:S(2)}) collective-permute-start(bf16[2,64,1024]{2,1,0:T(8,128)(2,1)S(1)} %collective-permute-done.8.rest_0_), channel_id=1, source_target_pairs={{1,0},{0,1},{3,2},{2,3},{5,4},{4,5},{7,6},{6,7},{9,8},{8,9},{11,10... | collective-permute-start | bytes 786440 | tf_op jit(solution)/shard_map/ppermute | solution.py:28
  26.6 8.0 %collective-permute-start.6 = (bf16[2,64,1024]{2,1,0:T(8,128)(2,1)S(1)}, bf16[2,64,1024]{2,1,0:T(8,128)(2,1)S(1)}, u32[]{:S(2)}, u32[]{:S(2)}) collective-permute-start(bf16[2,64,1024]{2,1,0:T(8,128)(2,1)S(1)} %collective-permute-done.rest_0_), channel_id=1, source_target_pairs={{2,0},{3,1},{0,2},{1,3},{6,4},{7,5},{4,6},{5,7},{10,8},{11,9},{8,1... | collective-permute-start | bytes 786440 | tf_op jit(solution)/shard_map/ppermute | solution.py:28
  29.1 5.5 %collective-permute-start.11 = (bf16[2,64,1024]{2,1,0:T(8,128)(2,1)S(1)}, bf16[2,64,1024]{2,1,0:T(8,128)(2,1)S(1)}, u32[]{:S(2)}, u32[]{:S(2)}) collective-permute-start(bf16[2,64,1024]{2,1,0:T(8,128)(2,1)S(1)} %collective-permute-done.10.rest_2_), channel_id=1, source_target_pairs={{1,0},{0,1},{3,2},{2,3},{5,4},{4,5},{7,6},{6,7},{9,8},{8,9},{11,10... | collective-permute-start | bytes 786440 | tf_op jit(solution)/shard_map/ppermute | solution.py:28
  29.2 10.0 %collective-permute-start.3 = (bf16[2,64,1024]{2,1,0:T(8,128)(2,1)S(1)}, bf16[2,64,1024]{2,1,0:T(8,128)(2,1)S(1)}, u32[]{:S(2)}, u32[]{:S(2)}) collective-permute-start(bf16[2,64,1024]{2,1,0:T(8,128)(2,1)S(1)} %collective-permute-done.1.rest_0_), channel_id=1, source_target_pairs={{2,0},{3,1},{0,2},{1,3},{6,4},{7,5},{4,6},{5,7},{10,8},{11,9},{8,1... | collective-permute-start | bytes 786440 | tf_op jit(solution)/shard_map/ppermute | solution.py:28
  29.7 1.0 %copy-start.3 = (bf16[2,64,1024]{2,1,0:T(8,128)(2,1)S(1)}, bf16[2,64,1024]{2,1,0:T(8,128)(2,1)}, u32[]{:S(2)}) copy-start(bf16[2,64,1024]{2,1,0:T(8,128)(2,1)} %get-tuple-element.22.rest_0_) | copy-start | bytes 786436
  31.5 8.5 %collective-permute-start.5 = (bf16[2,64,1024]{2,1,0:T(8,128)(2,1)S(1)}, bf16[2,64,1024]{2,1,0:T(8,128)(2,1)S(1)}, u32[]{:S(2)}, u32[]{:S(2)}) collective-permute-start(bf16[2,64,1024]{2,1,0:T(8,128)(2,1)S(1)} %collective-permute-done.rest_0_), channel_id=1, source_target_pairs={{1,0},{0,1},{3,2},{2,3},{5,4},{4,5},{7,6},{6,7},{9,8},{8,9},{11,10... | collective-permute-start | bytes 786440 | tf_op jit(solution)/shard_map/ppermute | solution.py:28
  34.7 6.1 %collective-permute-start.2 = (bf16[2,64,1024]{2,1,0:T(8,128)(2,1)S(1)}, bf16[2,64,1024]{2,1,0:T(8,128)(2,1)S(1)}, u32[]{:S(2)}, u32[]{:S(2)}) collective-permute-start(bf16[2,64,1024]{2,1,0:T(8,128)(2,1)S(1)} %collective-permute-done.1.rest_0_), channel_id=1, source_target_pairs={{1,0},{0,1},{3,2},{2,3},{5,4},{4,5},{7,6},{6,7},{9,8},{8,9},{11,10... | collective-permute-start | bytes 786440 | tf_op jit(solution)/shard_map/ppermute | solution.py:28
  34.7 5.3 %collective-permute-start.7 = (bf16[2,64,1024]{2,1,0:T(8,128)(2,1)S(1)}, bf16[2,64,1024]{2,1,0:T(8,128)(2,1)S(1)}, u32[]{:S(2)}, u32[]{:S(2)}) collective-permute-start(bf16[2,64,1024]{2,1,0:T(8,128)(2,1)S(1)} %collective-permute-done.6.rest_2_), channel_id=1, source_target_pairs={{1,0},{0,1},{3,2},{2,3},{5,4},{4,5},{7,6},{6,7},{9,8},{8,9},{11,10... | collective-permute-start | bytes 786440 | tf_op jit(solution)/shard_map/ppermute | solution.py:28
  39.1 1.7 %collective-permute-start.4 = (bf16[2,64,1024]{2,1,0:T(8,128)(2,1)S(1)}, bf16[2,64,1024]{2,1,0:T(8,128)(2,1)S(1)}, u32[]{:S(2)}, u32[]{:S(2)}) collective-permute-start(bf16[2,64,1024]{2,1,0:T(8,128)(2,1)S(1)} %collective-permute-done.3.rest_2_), channel_id=1, source_target_pairs={{1,0},{0,1},{3,2},{2,3},{5,4},{4,5},{7,6},{6,7},{9,8},{8,9},{11,10... | collective-permute-start | bytes 786440 | tf_op jit(solution)/shard_map/ppermute | solution.py:28
  40.8 3.2 %copy-start = (bf16[1,2048,1024]{2,1,0:T(8,128)(2,1)S(1)}, bf16[1,2048,1024]{2,1,0:T(8,128)(2,1)}, u32[]{:S(2)}) copy-start(bf16[1,2048,1024]{2,1,0:T(8,128)(2,1)} %param.6) | copy-start | bytes 12582916
  42.5 5.1 %collective-permute-start.16 = (bf16[80,512]{1,0:T(8,128)(2,1)S(1)}, bf16[80,512]{1,0:T(8,128)(2,1)S(1)}, u32[]{:S(2)}, u32[]{:S(2)}) collective-permute-start(bf16[80,512]{1,0:T(8,128)(2,1)S(1)} %get-tuple-element.33), channel_id=1, source_target_pairs={{0,16},{16,0},{1,17},{17,1},{2,18},{18,2},{3,19},{19,3},{4,20},{20... | collective-permute-start | bytes 245768 | tf_op jit(solution)/shard_map/ppermute | solution.py:372
  44.8 21.9 %collective-permute-start.24 = (bf16[576,512]{1,0:T(8,128)(2,1)S(1)}, bf16[576,512]{1,0:T(8,128)(2,1)S(1)}, u32[]{:S(2)}, u32[]{:S(2)}) collective-permute-start(bf16[576,512]{1,0:T(8,128)(2,1)S(1)} %shard_map.70.rest_0_), channel_id=1, source_target_pairs={{0,16},{16,0},{1,17},{17,1},{2,18},{18,2},{3,19},{19,3},{4,20},{20... | collective-permute-start | bytes 1769480 | tf_op jit(solution)/shard_map/ppermute | solution.py:367
  47.6 9.2 %collective-permute-start.20 = (bf16[64,512]{1,0:T(8,128)(2,1)S(1)}, bf16[64,512]{1,0:T(8,128)(2,1)S(1)}, u32[]{:S(2)}, u32[]{:S(2)}) collective-permute-start(bf16[64,512]{1,0:T(8,128)(2,1)S(1)} %shard_map.71.rest_0_.refs_0_), channel_id=1, source_target_pairs={{12,0},{13,1},{14,2},{15,3},{8,4},{9,5},{10,6},{11,7},{4,8},{5,9},... | collective-permute-start | bytes 196616 | tf_op jit(solution)/shard_map/ppermute | solution.py:28
  52.6 5.2 %collective-permute-start.19 = (bf16[64,512]{1,0:T(8,128)(2,1)S(1)}, bf16[64,512]{1,0:T(8,128)(2,1)S(1)}, u32[]{:S(2)}, u32[]{:S(2)}) collective-permute-start(bf16[64,512]{1,0:T(8,128)(2,1)S(1)} %shard_map.71.rest_0_.refs_0_), channel_id=1, source_target_pairs={{8,0},{9,1},{10,2},{11,3},{12,4},{13,5},{14,6},{15,7},{0,8},{1,9},... | collective-permute-start | bytes 196616 | tf_op jit(solution)/shard_map/ppermute | solution.py:28
  52.6 5.2 %collective-permute-start.18 = (bf16[64,512]{1,0:T(8,128)(2,1)S(1)}, bf16[64,512]{1,0:T(8,128)(2,1)S(1)}, u32[]{:S(2)}, u32[]{:S(2)}) collective-permute-start(bf16[64,512]{1,0:T(8,128)(2,1)S(1)} %shard_map.71.rest_0_.refs_0_), channel_id=1, source_target_pairs={{4,0},{5,1},{6,2},{7,3},{0,4},{1,5},{2,6},{3,7},{12,8},{13,9},{14,... | collective-permute-start | bytes 196616 | tf_op jit(solution)/shard_map/ppermute | solution.py:28
  53.6 13.0 %collective-permute-start.25 = (bf16[256,512]{1,0:T(8,128)(2,1)S(1)}, bf16[256,512]{1,0:T(8,128)(2,1)S(1)}, u32[]{:S(2)}, u32[]{:S(2)}) collective-permute-start(bf16[256,512]{1,0:T(8,128)(2,1)S(1)} %shard_map.76), channel_id=1, source_target_pairs={{0,16},{16,0},{1,17},{17,1},{2,18},{18,2},{3,19},{19,3},{4,20},{20... | collective-permute-start | bytes 786440 | tf_op jit(solution)/shard_map/ppermute | solution.py:367
  57.7 8.9 %collective-permute-start.23 = (bf16[4,64,512]{2,1,0:T(8,128)(2,1)S(1)}, bf16[4,64,512]{2,1,0:T(8,128)(2,1)S(1)}, u32[]{:S(2)}, u32[]{:S(2)}) collective-permute-start(bf16[4,64,512]{2,1,0:T(8,128)(2,1)S(1)} %shard_map.73._.rest_0_.rest_2_), channel_id=1, source_target_pairs={{2,0},{3,1},{0,2},{1,3},{6,4},{7,5},{4,6},{5,7},{10,8},{11,9},{8,1... | collective-permute-start | bytes 786440 | tf_op jit(solution)/shard_map/ppermute | solution.py:28
  59.8 13.1 %collective-permute-start.21 = (bf16[320,512]{1,0:T(8,128)(2,1)S(1)}, bf16[320,512]{1,0:T(8,128)(2,1)S(1)}, u32[]{:S(2)}, u32[]{:S(2)}) collective-permute-start(bf16[320,512]{1,0:T(8,128)(2,1)S(1)} %shard_map.75), channel_id=1, source_target_pairs={{0,16},{16,0},{1,17},{17,1},{2,18},{18,2},{3,19},{19,3},{4,20},{20... | collective-permute-start | bytes 983048 | tf_op jit(solution)/shard_map/ppermute | solution.py:367
  61.4 7.3 %collective-permute-start.22 = (bf16[4,64,512]{2,1,0:T(8,128)(2,1)S(1)}, bf16[4,64,512]{2,1,0:T(8,128)(2,1)S(1)}, u32[]{:S(2)}, u32[]{:S(2)}) collective-permute-start(bf16[4,64,512]{2,1,0:T(8,128)(2,1)S(1)} %shard_map.73._.rest_0_.rest_2_), channel_id=1, source_target_pairs={{1,0},{0,1},{3,2},{2,3},{5,4},{4,5},{7,6},{6,7},{9,8},{8,9},{11,10... | collective-permute-start | bytes 786440 | tf_op jit(solution)/shard_map/ppermute | solution.py:28
  66.7 2.0 %collective-permute-start.26 = (bf16[4,64,512]{2,1,0:T(8,128)(2,1)S(1)}, bf16[4,64,512]{2,1,0:T(8,128)(2,1)S(1)}, u32[]{:S(2)}, u32[]{:S(2)}) collective-permute-start(bf16[4,64,512]{2,1,0:T(8,128)(2,1)S(1)} %shard_map.77.rest_4_), channel_id=1, source_target_pairs={{1,0},{0,1},{3,2},{2,3},{5,4},{4,5},{7,6},{6,7},{9,8},{8,9},{11,10... | collective-permute-start | bytes 786440 | tf_op jit(solution)/shard_map/ppermute | solution.py:28
